TPU v7x, 32 devices: a whole 2x2x4 slice. The times are simulated.
32 devices in a mesh: dp: 8 (over y, x, core), mp: 4 (over z).
Axes of the slice: x: 2, y: 2, z: 4, core: 2. Of those that a mesh axis runs over, the one named last changes fastest.
Arguments:
- inputs: bfloat16 [16384, 1024], P(('dp', 'mp')), may hold values from -6 to 6
- documents: int32 [16, 1024], P('dp'), may hold values from 0 to 3, never falling along the last dimension, each value on 1 to 512 neighbouring positions
- cotangent: bfloat16 [16384, 1024], P(('dp', 'mp')), may hold values from -7.5 to 7.5
- qkv_weight: float32 [2, 1024, 3, 1024], P(None, 'dp', None, 'mp'), may hold values from -0.1875 to 0.1875
- qkv_moment: float32 [2, 1024, 3, 1024], P(None, 'dp', None, 'mp'), may hold values from -5.6969053e-05 to 5.6969053e-05
- qkv_square: float32 [2, 1024, 3, 1024], P(None, 'dp', None, 'mp'), may hold values from 3.7252904e-10 to 1.4901161e-09
- proj_weight: float32 [2, 1024, 1024], P(None, 'mp', 'dp'), may hold values from -0.75 to 0.75
- proj_moment: float32 [2, 1024, 1024], P(None, 'mp', 'dp'), may hold values from -5.6969053e-05 to 5.6969053e-05
- proj_square: float32 [2, 1024, 1024], P(None, 'mp', 'dp'), may hold values from 3.7252904e-10 to 1.4901161e-09
- upper_weight: float32 [2, 1024, 4096], P(None, 'dp', 'mp'), may hold values from -0.1875 to 0.1875
- upper_moment: float32 [2, 1024, 4096], P(None, 'dp', 'mp'), may hold values from -9.840109e-05 to 9.840109e-05
- upper_square: float32 [2, 1024, 4096], P(None, 'dp', 'mp'), may hold values from 1.1175871e-09 to 4.4703485e-09
- lower_weight: float32 [2, 4096, 1024], P(None, 'mp', 'dp'), may hold values from -0.09375 to 0.09375
- lower_moment: float32 [2, 4096, 1024], P(None, 'mp', 'dp'), may hold values from -0.00020198118 to 0.00020198118
- lower_square: float32 [2, 4096, 1024], P(None, 'mp', 'dp'), may hold values from 4.4703485e-09 to 1.7881394e-08
- hidden_bias: float32 [2, 4096], P(None, ('mp', 'dp')), may hold values from -3 to 3
- bias_moment: float32 [2, 4096], P(None, ('mp', 'dp')), may hold values from -9.840109e-05 to 9.840109e-05
- bias_square: float32 [2, 4096], P(None, ('mp', 'dp')), may hold values from 1.1175871e-09 to 4.4703485e-09
- norm_gains: float32 [2, 2, 1024], P(None, None, 'dp'), may hold values from 0.2 to 2.2
- gains_moment: float32 [2, 2, 1024], P(None, None, 'dp'), may hold values from -0.00028484527 to 0.00028484527
- gains_square: float32 [2, 2, 1024], P(None, None, 'dp'), may hold values from 9.313226e-09 to 3.7252903e-08
- shift_params: float32 [2, 3, 1024], P(None, None, 'dp'), may hold values from -1.2 to 1.2
- shifts_moment: float32 [2, 3, 1024], P(None, None, 'dp'), may hold values from -0.00028484527 to 0.00028484527
- shifts_square: float32 [2, 3, 1024], P(None, None, 'dp'), may hold values from 9.313226e-09 to 3.7252903e-08
Outputs:
- output_stream: float32 [16384, 1024], P(('dp', 'mp'))
- input_grad: float32 [16384, 1024], P(('dp', 'mp'))
- qkv_weight_new: float32 [2, 1024, 3, 1024], P(None, 'dp', None, 'mp')
- qkv_moment_new: float32 [2, 1024, 3, 1024], P(None, 'dp', None, 'mp')
- qkv_square_new: float32 [2, 1024, 3, 1024], P(None, 'dp', None, 'mp')
- proj_weight_new: float32 [2, 1024, 1024], P(None, 'mp', 'dp')
- proj_moment_new: float32 [2, 1024, 1024], P(None, 'mp', 'dp')
- proj_square_new: float32 [2, 1024, 1024], P(None, 'mp', 'dp')
- upper_weight_new: float32 [2, 1024, 4096], P(None, 'dp', 'mp')
- upper_moment_new: float32 [2, 1024, 4096], P(None, 'dp', 'mp')
- upper_square_new: float32 [2, 1024, 4096], P(None, 'dp', 'mp')
- lower_weight_new: float32 [2, 4096, 1024], P(None, 'mp', 'dp')
- lower_moment_new: float32 [2, 4096, 1024], P(None, 'mp', 'dp')
- lower_square_new: float32 [2, 4096, 1024], P(None, 'mp', 'dp')
- hidden_bias_new: float32 [2, 4096], P(None, ('mp', 'dp'))
- bias_moment_new: float32 [2, 4096], P(None, ('mp', 'dp'))
- bias_square_new: float32 [2, 4096], P(None, ('mp', 'dp'))
- norm_gains_new: float32 [2, 2, 1024], P(None, None, 'dp')
- gains_moment_new: float32 [2, 2, 1024], P(None, None, 'dp')
- gains_square_new: float32 [2, 2, 1024], P(None, None, 'dp')
- shift_params_new: float32 [2, 3, 1024], P(None, None, 'dp')
- shifts_moment_new: float32 [2, 3, 1024], P(None, None, 'dp')
- shifts_square_new: float32 [2, 3, 1024], P(None, None, 'dp')
- grad_norm: float32 [], replicated
Inputs may be any that keep to these rules, and one draw needn't show every extreme that they name: `documents`: ids never fall along a sequence; a document has at most 512 tokens, and the longest has exactly that many.
All inputs are finite; a program needn't handle non-finite values.
Results may differ from a plain program's by a relative error of at most 0.035.
Values may be sent and summed in bfloat16 or wider, within the bound.
A program may use at most 256 MiB of HBM per device.

v0:
```python
import math

import jax
import jax.numpy as jnp
import numpy as np
from jax import lax
from jax.sharding import PartitionSpec as P

H = 8
HD = 128
STEP = 5


norm_eps = 1e-05
clip_bound = 1.0
beta_first = 0.9
beta_second = 0.95
adam_eps = 1e-08
masked_score = -1e30
group_rates = (0.03, 0.12, 0.03, 0.015, 0.3, 0.7, 0.3)
group_decays = (0.1, 0.1, 0.1, 0.1, 0.0, 0.0, 0.0)
contract_rows = (((0,), (0,)), ((), ()))
contract_cols = (((1,), (1,)), ((), ()))


def gelu_tanh(values):
    return jax.nn.gelu(values, approximate=True)


def layer_norm(values, scale_vec, shift_vec):
    center = values - jnp.mean(values, axis=-1, keepdims=True)
    spread = jnp.mean(center * center, axis=-1, keepdims=True)
    return center * lax.rsqrt(spread + norm_eps) * scale_vec + shift_vec


def adam_update(master, moment, square, gradient, factor, step_rate, decay_rate):
    clipped = gradient * factor
    moment_new = beta_first * moment + (1.0 - beta_first) * clipped
    square_new = beta_second * square + (1.0 - beta_second) * clipped * clipped
    first_hat = moment_new / (1.0 - beta_first**STEP)
    second_hat = square_new / (1.0 - beta_second**STEP)
    master_new = master - step_rate * (
        first_hat / (jnp.sqrt(second_hat) + adam_eps) + decay_rate * master
    )
    return (master_new, moment_new, square_new)


def block_scores(query_heads, key_heads, query_docs, key_docs, first_row, slopes):
    scores = jnp.einsum(
        "qhd,khd->hqk", query_heads, key_heads, preferred_element_type=jnp.float32
    ) * (1.0 / math.sqrt(HD))
    row_ids = first_row + jnp.arange(query_heads.shape[0], dtype=jnp.int32)
    col_ids = jnp.arange(key_heads.shape[0], dtype=jnp.int32)
    distance = (row_ids[:, None] - col_ids[None, :]).astype(jnp.float32)
    scores = scores - slopes[:, None, None] * distance[None]
    allowed = (row_ids[:, None] >= col_ids[None, :]) & (query_docs[:, None] == key_docs[None, :])
    return jnp.where(allowed[None], scores, masked_score)


def attend_forward(qkv_rows, documents, slopes):
    seq_count, seq_len = documents.shape
    block_rows = min(512, seq_len)
    outputs = []
    row_maxes = []
    row_totals = []
    for sequence in range(seq_count):
        base_row = sequence * seq_len
        key_heads = qkv_rows[base_row : base_row + seq_len, 1].reshape(seq_len, -1, HD)
        value_heads = qkv_rows[base_row : base_row + seq_len, 2].reshape(seq_len, -1, HD)
        for first_row in range(0, seq_len, block_rows):
            lower_row = base_row + first_row
            query_heads = qkv_rows[lower_row : lower_row + block_rows, 0].reshape(
                block_rows, -1, HD
            )
            scores = block_scores(
                query_heads,
                key_heads,
                documents[sequence, first_row : first_row + block_rows],
                documents[sequence],
                first_row,
                slopes,
            )
            row_max = jnp.max(scores, axis=-1, keepdims=True)
            shifted = jnp.exp(scores - row_max)
            row_total = jnp.sum(shifted, axis=-1, keepdims=True)
            prob_low = (shifted / row_total).astype(jnp.bfloat16)
            block_out = jnp.einsum(
                "hqk,khd->qhd", prob_low, value_heads, preferred_element_type=jnp.float32
            )
            outputs.append(block_out.reshape(block_rows, -1))
            row_maxes.append(row_max)
            row_totals.append(row_total)
    return (jnp.concatenate(outputs, axis=0).astype(jnp.bfloat16), row_maxes, row_totals)


def attend_backward(qkv_rows, attended_grad, documents, row_maxes, row_totals, slopes):
    seq_count, seq_len = documents.shape
    block_rows = min(512, seq_len)
    scale_factor = 1.0 / math.sqrt(HD)
    pieces = []
    counter = 0
    for sequence in range(seq_count):
        base_row = sequence * seq_len
        key_heads = qkv_rows[base_row : base_row + seq_len, 1].reshape(seq_len, -1, HD)
        value_heads = qkv_rows[base_row : base_row + seq_len, 2].reshape(seq_len, -1, HD)
        key_grad = jnp.zeros(key_heads.shape, jnp.float32)
        value_grad = jnp.zeros(value_heads.shape, jnp.float32)
        query_grads = []
        for first_row in range(0, seq_len, block_rows):
            lower_row = base_row + first_row
            query_heads = qkv_rows[lower_row : lower_row + block_rows, 0].reshape(
                block_rows, -1, HD
            )
            scores = block_scores(
                query_heads,
                key_heads,
                documents[sequence, first_row : first_row + block_rows],
                documents[sequence],
                first_row,
                slopes,
            )
            probs = jnp.exp(scores - row_maxes[counter]) / row_totals[counter]
            prob_low = probs.astype(jnp.bfloat16)
            out_grad = attended_grad[lower_row : lower_row + block_rows].reshape(block_rows, -1, HD)
            value_grad = value_grad + jnp.einsum(
                "hqk,qhd->khd", prob_low, out_grad, preferred_element_type=jnp.float32
            )
            prob_grad = jnp.einsum(
                "qhd,khd->hqk", out_grad, value_heads, preferred_element_type=jnp.float32
            )
            inner = jnp.sum(probs * prob_grad, axis=-1, keepdims=True)
            score_grad = (probs * (prob_grad - inner)).astype(jnp.bfloat16)
            query_part = jnp.einsum(
                "hqk,khd->qhd", score_grad, key_heads, preferred_element_type=jnp.float32
            )
            query_grads.append(
                (query_part * scale_factor).astype(jnp.bfloat16).reshape(block_rows, -1)
            )
            key_grad = (
                key_grad
                + jnp.einsum(
                    "hqk,qhd->khd", score_grad, query_heads, preferred_element_type=jnp.float32
                )
                * scale_factor
            )
            counter += 1
        pieces.append(
            jnp.stack(
                [
                    jnp.concatenate(query_grads, axis=0),
                    key_grad.astype(jnp.bfloat16).reshape(seq_len, -1),
                    value_grad.astype(jnp.bfloat16).reshape(seq_len, -1),
                ],
                axis=1,
            )
        )
    return jnp.concatenate(pieces, axis=0)


def shards(
    inputs,
    documents,
    cotangent,
    qkv_weight,
    qkv_moment,
    qkv_square,
    proj_weight,
    proj_moment,
    proj_square,
    upper_weight,
    upper_moment,
    upper_square,
    lower_weight,
    lower_moment,
    lower_square,
    hidden_bias,
    bias_moment,
    bias_square,
    norm_gains,
    gains_moment,
    gains_square,
    shift_params,
    shifts_moment,
    shifts_square,
):
    layers = qkv_weight.shape[0]
    heads_here = qkv_weight.shape[3] // HD
    mp_index = lax.axis_index("mp")
    dp_index = lax.axis_index("dp")
    slope_table = jnp.asarray(0.5 ** (np.arange(H) + 1.0), dtype=jnp.float32)
    slopes = lax.dynamic_slice_in_dim(slope_table, mp_index * heads_here, heads_here)
    stream = inputs.astype(jnp.float32)
    stored = []
    for layer_index in range(layers):
        qkv_low, proj_low, upper_low, lower_low, bias_low, gains_low, shifts_low = (
            lax.all_gather(qkv_weight[layer_index].astype(jnp.bfloat16), "dp", axis=0, tiled=True),
            lax.all_gather(proj_weight[layer_index].astype(jnp.bfloat16), "dp", axis=1, tiled=True),
            lax.all_gather(
                upper_weight[layer_index].astype(jnp.bfloat16), "dp", axis=0, tiled=True
            ),
            lax.all_gather(
                lower_weight[layer_index].astype(jnp.bfloat16), "dp", axis=1, tiled=True
            ),
            lax.all_gather(hidden_bias[layer_index].astype(jnp.bfloat16), "dp", axis=0, tiled=True),
            lax.all_gather(norm_gains[layer_index].astype(jnp.bfloat16), "dp", axis=1, tiled=True),
            lax.all_gather(
                shift_params[layer_index].astype(jnp.bfloat16), "dp", axis=1, tiled=True
            ),
        )
        gain_rows = gains_low.astype(jnp.float32)
        shift_rows = shifts_low.astype(jnp.float32)
        normed = layer_norm(stream, gain_rows[0], shift_rows[0]).astype(jnp.bfloat16)
        full_normed = lax.all_gather(normed, "mp", axis=0, tiled=True)
        qkv_rows = jnp.einsum(
            "td,dcf->tcf", full_normed, qkv_low, preferred_element_type=jnp.float32
        ).astype(jnp.bfloat16)
        attended, row_maxes, row_totals = attend_forward(qkv_rows, documents, slopes)
        branch = lax.psum_scatter(
            jnp.dot(attended, proj_low, preferred_element_type=jnp.float32).astype(jnp.bfloat16),
            "mp",
            scatter_dimension=0,
            tiled=True,
        ).astype(jnp.float32)
        middle = stream + branch
        normed_two = layer_norm(middle, gain_rows[1], shift_rows[1]).astype(jnp.bfloat16)
        full_two = lax.all_gather(normed_two, "mp", axis=0, tiled=True)
        hidden = jnp.dot(full_two, upper_low, preferred_element_type=jnp.float32) + bias_low.astype(
            jnp.float32
        )
        active = gelu_tanh(hidden).astype(jnp.bfloat16)
        down = lax.psum_scatter(
            jnp.dot(active, lower_low, preferred_element_type=jnp.float32).astype(jnp.bfloat16),
            "mp",
            scatter_dimension=0,
            tiled=True,
        ).astype(jnp.float32)
        stored.append(
            (
                stream,
                middle,
                full_normed,
                qkv_rows,
                attended,
                row_maxes,
                row_totals,
                full_two,
                active,
                hidden,
                (qkv_low, proj_low, upper_low, lower_low, gains_low),
            )
        )
        stream = middle + down + shift_rows[2]
    grad_stream = cotangent.astype(jnp.float32)
    weight_grads = [None] * layers
    gain_grads = [None] * layers
    shift_grads = [None] * layers
    for layer_index in reversed(range(layers)):
        (
            stream_in,
            middle,
            full_normed,
            qkv_rows,
            attended,
            row_maxes,
            row_totals,
            full_two,
            active,
            hidden,
            kept_weights,
        ) = stored[layer_index]
        qkv_low, proj_low, upper_low, lower_low, gains_low = (
            lax.all_gather(qkv_weight[layer_index].astype(jnp.bfloat16), "dp", axis=0, tiled=True),
            lax.all_gather(proj_weight[layer_index].astype(jnp.bfloat16), "dp", axis=1, tiled=True),
            lax.all_gather(
                upper_weight[layer_index].astype(jnp.bfloat16), "dp", axis=0, tiled=True
            ),
            lax.all_gather(
                lower_weight[layer_index].astype(jnp.bfloat16), "dp", axis=1, tiled=True
            ),
            lax.all_gather(norm_gains[layer_index].astype(jnp.bfloat16), "dp", axis=1, tiled=True),
        )
        gain_rows = gains_low.astype(jnp.float32)
        zero_shift = jnp.zeros_like(gain_rows[0])
        out_shift_grad = jnp.sum(grad_stream, axis=0)
        full_down = lax.all_gather(grad_stream.astype(jnp.bfloat16), "mp", axis=0, tiled=True)
        lower_grad = lax.dot_general(
            active, full_down, contract_rows, preferred_element_type=jnp.float32
        )
        active_grad = lax.dot_general(
            full_down, lower_low, contract_cols, preferred_element_type=jnp.float32
        )
        _, pull_gelu = jax.vjp(gelu_tanh, hidden)
        hidden_grad = pull_gelu(active_grad)[0].astype(jnp.bfloat16)
        bias_grad = jnp.sum(hidden_grad, axis=0, dtype=jnp.float32)
        upper_grad = lax.dot_general(
            full_two, hidden_grad, contract_rows, preferred_element_type=jnp.float32
        )
        normed_two_grad = lax.psum_scatter(
            lax.dot_general(
                hidden_grad, upper_low, contract_cols, preferred_element_type=jnp.float32
            ).astype(jnp.bfloat16),
            "mp",
            scatter_dimension=0,
            tiled=True,
        ).astype(jnp.float32)
        _, pull_two = jax.vjp(layer_norm, middle, gain_rows[1], zero_shift)
        middle_part, gain_two, shift_two = pull_two(normed_two_grad)
        middle_grad = grad_stream + middle_part
        full_branch = lax.all_gather(middle_grad.astype(jnp.bfloat16), "mp", axis=0, tiled=True)
        proj_grad = lax.dot_general(
            attended, full_branch, contract_rows, preferred_element_type=jnp.float32
        )
        attended_grad = lax.dot_general(
            full_branch, proj_low, contract_cols, preferred_element_type=jnp.float32
        ).astype(jnp.bfloat16)
        qkv_rows_grad = attend_backward(
            qkv_rows, attended_grad, documents, row_maxes, row_totals, slopes
        )
        qkv_grad = jnp.einsum(
            "td,tcf->dcf", full_normed, qkv_rows_grad, preferred_element_type=jnp.float32
        )
        normed_grad = lax.psum_scatter(
            jnp.einsum(
                "tcf,dcf->td", qkv_rows_grad, qkv_low, preferred_element_type=jnp.float32
            ).astype(jnp.bfloat16),
            "mp",
            scatter_dimension=0,
            tiled=True,
        ).astype(jnp.float32)
        _, pull_one = jax.vjp(layer_norm, stream_in, gain_rows[0], zero_shift)
        stream_part, gain_one, shift_one = pull_one(normed_grad)
        grad_stream = middle_grad + stream_part
        weight_grads[layer_index] = (
            lax.psum_scatter(
                qkv_grad.astype(jnp.bfloat16), "dp", scatter_dimension=0, tiled=True
            ).astype(jnp.float32),
            lax.psum_scatter(
                proj_grad.astype(jnp.bfloat16), "dp", scatter_dimension=1, tiled=True
            ).astype(jnp.float32),
            lax.psum_scatter(
                upper_grad.astype(jnp.bfloat16), "dp", scatter_dimension=0, tiled=True
            ).astype(jnp.float32),
            lax.psum_scatter(
                lower_grad.astype(jnp.bfloat16), "dp", scatter_dimension=1, tiled=True
            ).astype(jnp.float32),
            lax.psum_scatter(
                bias_grad.astype(jnp.bfloat16), "dp", scatter_dimension=0, tiled=True
            ).astype(jnp.float32),
        )
        layer_gains = jnp.stack([gain_one, gain_two])
        layer_shifts = jnp.stack([shift_one, shift_two, out_shift_grad])
        gain_grads[layer_index], shift_grads[layer_index] = lax.psum(
            (layer_gains, layer_shifts), ("dp", "mp")
        )
    stacked = [
        jnp.stack([weight_grads[layer_at][member] for layer_at in range(layers)])
        for member in range(5)
    ]
    owned_squares = jnp.float32(0.0)
    for gradient in stacked:
        owned_squares = owned_squares + jnp.sum(gradient * gradient)
    gains_full = jnp.stack(gain_grads)
    shifts_full = jnp.stack(shift_grads)
    owned_total = lax.psum(owned_squares, ("dp", "mp"))
    sum_squares = (
        owned_total + jnp.sum(gains_full * gains_full) + jnp.sum(shifts_full * shifts_full)
    )
    grad_norm = jnp.sqrt(sum_squares)
    factor = jnp.minimum(1.0, clip_bound / grad_norm)
    shard_width = norm_gains.shape[2]
    gains_shard = lax.dynamic_slice_in_dim(gains_full, dp_index * shard_width, shard_width, 2)
    shifts_shard = lax.dynamic_slice_in_dim(shifts_full, dp_index * shard_width, shard_width, 2)
    masters = (
        qkv_weight,
        proj_weight,
        upper_weight,
        lower_weight,
        hidden_bias,
        norm_gains,
        shift_params,
    )
    moments = (
        qkv_moment,
        proj_moment,
        upper_moment,
        lower_moment,
        bias_moment,
        gains_moment,
        shifts_moment,
    )
    squares = (
        qkv_square,
        proj_square,
        upper_square,
        lower_square,
        bias_square,
        gains_square,
        shifts_square,
    )
    gradients = (
        stacked[0],
        stacked[1],
        stacked[2],
        stacked[3],
        stacked[4],
        gains_shard,
        shifts_shard,
    )
    results = [stream, grad_stream]
    for group_at in range(7):
        results.extend(
            adam_update(
                masters[group_at],
                moments[group_at],
                squares[group_at],
                gradients[group_at],
                factor,
                group_rates[group_at],
                group_decays[group_at],
            )
        )
    results.append(grad_norm)
    return tuple(results)


def solution(mesh):
    placed = (
        P(("dp", "mp"), None),
        P("dp", None),
        P(("dp", "mp"), None),
        P(None, "dp", None, "mp"),
        P(None, "dp", None, "mp"),
        P(None, "dp", None, "mp"),
        P(None, "mp", "dp"),
        P(None, "mp", "dp"),
        P(None, "mp", "dp"),
        P(None, "dp", "mp"),
        P(None, "dp", "mp"),
        P(None, "dp", "mp"),
        P(None, "mp", "dp"),
        P(None, "mp", "dp"),
        P(None, "mp", "dp"),
        P(None, ("mp", "dp")),
        P(None, ("mp", "dp")),
        P(None, ("mp", "dp")),
        P(None, None, "dp"),
        P(None, None, "dp"),
        P(None, None, "dp"),
        P(None, None, "dp"),
        P(None, None, "dp"),
        P(None, None, "dp"),
    )
    return jax.shard_map(
        shards,
        mesh=mesh,
        in_specs=placed,
        out_specs=(
            P(("dp", "mp"), None),
            P(("dp", "mp"), None),
            P(None, "dp", None, "mp"),
            P(None, "dp", None, "mp"),
            P(None, "dp", None, "mp"),
            P(None, "mp", "dp"),
            P(None, "mp", "dp"),
            P(None, "mp", "dp"),
            P(None, "dp", "mp"),
            P(None, "dp", "mp"),
            P(None, "dp", "mp"),
            P(None, "mp", "dp"),
            P(None, "mp", "dp"),
            P(None, "mp", "dp"),
            P(None, ("mp", "dp")),
            P(None, ("mp", "dp")),
            P(None, ("mp", "dp")),
            P(None, None, "dp"),
            P(None, None, "dp"),
            P(None, None, "dp"),
            P(None, None, "dp"),
            P(None, None, "dp"),
            P(None, None, "dp"),
            P(),
        ),
        check_vma=False,
    )
```

profile of v0, /device:TPU:1, one launch (start us, length us, event | category | flops | bytes accessed | tf_op | source)
XLA Modules:
  0.0 2159.1 jit_solution(9742032944842265570)
XLA Ops:
  10.9 10.1 all-gather
  21.0 8.8 all-gather.1
  35.3 10.2 all-gather.3
  52.0 69.5 %all-gather.29.cloned.1.call-done = bf16[2048,1024]{1,0:T(8,128)(2,1)} async-done(((bf16[512,1024]{1,0:T(8,128)(2,1)}), bf16[2048,1024]{1,0:T(8,128)(2,1)}) %all-gather.29.cloned.1.call-update) | async-done | bytes 4194320 | tf_op jit(solution)/shard_map/all_gather | solution.py:213
  121.5 6.1 fusion.38
  129.0 5.9 fusion.369
  139.7 5.6 fusion.370
  150.1 5.7 fusion.372
  160.6 5.4 fusion.371
  177.4 73.3 %reduce-scatter.25.cloned.1.call-done = bf16[512,1024]{1,0:T(8,128)(2,1)} async-done(((bf16[2048,1024]{1,0:T(8,128)(2,1)}), bf16[512,1024]{1,0:T(8,128)(2,1)}) %reduce-scatter.25.cloned.1.call-update) | async-done | bytes 1048592 | tf_op jit(solution)/shard_map/reduce_scatter | solution.py:218
  256.8 9.4 all-gather.5
  266.2 15.8 all-gather.47.cloned.1.call-done
  282.0 82.4 %all-gather.31.cloned.1.call-done = bf16[2048,1024]{1,0:T(8,128)(2,1)} async-done(((bf16[512,1024]{1,0:T(8,128)(2,1)}), bf16[2048,1024]{1,0:T(8,128)(2,1)}) %all-gather.31.cloned.1.call-update) | async-done | bytes 4194320 | tf_op jit(solution)/shard_map/all_gather | solution.py:226
  364.5 10.6 fusion.97
  375.1 19.0 all-gather.49.cloned.1.call-done
  394.1 11.7 convolution_convert_fusion.5
  406.6 8.8 all-gather.7
  415.4 7.9 all-gather.8
  423.3 59.0 %reduce-scatter.27.cloned.1.call-done = bf16[512,1024]{1,0:T(8,128)(2,1)} async-done(((bf16[2048,1024]{1,0:T(8,128)(2,1)}), bf16[512,1024]{1,0:T(8,128)(2,1)}) %reduce-scatter.27.cloned.1.call-update) | async-done | bytes 1048592 | tf_op jit(solution)/shard_map/reduce_scatter | solution.py:231
  486.3 13.2 all-gather.10
  499.6 12.3 all-gather.51.cloned.1.call-done
  511.9 82.5 %all-gather.33.cloned.1.call-done = bf16[2048,1024]{1,0:T(8,128)(2,1)} async-done(((bf16[512,1024]{1,0:T(8,128)(2,1)}), bf16[2048,1024]{1,0:T(8,128)(2,1)}) %all-gather.33.cloned.1.call-update) | async-done | bytes 4194320 | tf_op jit(solution)/shard_map/all_gather | solution.py:213
  594.4 6.1 fusion.41
  602.7 6.0 fusion.373
  608.7 5.5 fusion.374
  623.8 5.9 fusion.376
  629.7 5.6 fusion.375
  650.2 74.7 %reduce-scatter.29.cloned.1.call-done = bf16[512,1024]{1,0:T(8,128)(2,1)} async-done(((bf16[2048,1024]{1,0:T(8,128)(2,1)}), bf16[512,1024]{1,0:T(8,128)(2,1)}) %reduce-scatter.29.cloned.1.call-update) | async-done | bytes 1048592 | tf_op jit(solution)/shard_map/reduce_scatter | solution.py:218
  730.5 9.4 all-gather.12
  739.9 16.5 all-gather.53.cloned.1.call-done
  756.4 82.5 %all-gather.35.cloned.1.call-done = bf16[2048,1024]{1,0:T(8,128)(2,1)} async-done(((bf16[512,1024]{1,0:T(8,128)(2,1)}), bf16[2048,1024]{1,0:T(8,128)(2,1)}) %all-gather.35.cloned.1.call-update) | async-done | bytes 4194320 | tf_op jit(solution)/shard_map/all_gather | solution.py:226
  838.8 10.6 fusion.89
  849.5 19.1 all-gather.55.cloned.1.call-done
  868.6 81.9 %all-gather.37.cloned.1.call-done = bf16[2048,1024]{1,0:T(8,128)(2,1)} async-done(((bf16[512,1024]{1,0:T(8,128)(2,1)}), bf16[2048,1024]{1,0:T(8,128)(2,1)}) %all-gather.37.cloned.1.call-update) | async-done | bytes 4194320 | tf_op jit(solution)/shard_map/all_gather | solution.py:285
  950.5 14.4 fusion.377
  966.9 6.3 convolution_convert_fusion.3
  973.7 11.7 convolution_convert_fusion.4
  985.5 63.2 %reduce-scatter.33.cloned.1.call-done = bf16[512,1024]{1,0:T(8,128)(2,1)} async-done(((bf16[2048,1024]{1,0:T(8,128)(2,1)}), bf16[512,1024]{1,0:T(8,128)(2,1)}) %reduce-scatter.33.cloned.1.call-update) | async-done | bytes 1048592 | tf_op jit(solution)/shard_map/reduce_scatter | solution.py:298
  1052.0 76.1 %reduce-scatter.31.cloned.1.call-done = bf16[512,1024]{1,0:T(8,128)(2,1)} async-done(((bf16[2048,1024]{1,0:T(8,128)(2,1)}), bf16[512,1024]{1,0:T(8,128)(2,1)}) %reduce-scatter.31.cloned.1.call-update) | async-done | bytes 1048592 | tf_op jit(solution)/shard_map/reduce_scatter | solution.py:231
  1135.5 81.2 %all-gather.39.cloned.1.call-done = bf16[2048,1024]{1,0:T(8,128)(2,1)} async-done(((bf16[512,1024]{1,0:T(8,128)(2,1)}), bf16[2048,1024]{1,0:T(8,128)(2,1)}) %all-gather.39.cloned.1.call-update) | async-done | bytes 4194320 | tf_op jit(solution)/shard_map/all_gather | solution.py:309
  1246.9 5.6 fusion.164
  1296.3 7.4 bitcast_convert_fusion.1
  1304.2 75.0 %reduce-scatter.35.cloned.1.call-done = bf16[512,1024]{1,0:T(8,128)(2,1)} async-done(((bf16[2048,1024]{1,0:T(8,128)(2,1)}), bf16[512,1024]{1,0:T(8,128)(2,1)}) %reduce-scatter.35.cloned.1.call-update) | async-done | bytes 1048592 | tf_op jit(solution)/shard_map/reduce_scatter | solution.py:322
  1389.2 81.3 %all-gather.41.cloned.1.call-done = bf16[2048,1024]{1,0:T(8,128)(2,1)} async-done(((bf16[512,1024]{1,0:T(8,128)(2,1)}), bf16[2048,1024]{1,0:T(8,128)(2,1)}) %all-gather.41.cloned.1.call-update) | async-done | bytes 4194320 | tf_op jit(solution)/shard_map/all_gather | solution.py:285
  1470.5 14.2 fusion.378
  1486.7 6.3 convolution_convert_fusion.2
  1493.3 75.3 %reduce-scatter.37.cloned.1.call-done = bf16[512,1024]{1,0:T(8,128)(2,1)} async-done(((bf16[2048,1024]{1,0:T(8,128)(2,1)}), bf16[512,1024]{1,0:T(8,128)(2,1)}) %reduce-scatter.37.cloned.1.call-update) | async-done | bytes 1048592 | tf_op jit(solution)/shard_map/reduce_scatter | solution.py:298
  1577.1 10.6 convolution_convert_fusion.8
  1595.4 10.6 convolution_convert_fusion.9
  1608.7 9.4 convolution_convert_fusion.10
  1618.6 9.5 convolution_convert_fusion.11
  1628.2 30.2 %all-gather.43.cloned.1.call-done = bf16[2048,1024]{1,0:T(8,128)(2,1)} async-done(((bf16[512,1024]{1,0:T(8,128)(2,1)}), bf16[2048,1024]{1,0:T(8,128)(2,1)}) %all-gather.43.cloned.1.call-update) | async-done | bytes 4194320 | tf_op jit(solution)/shard_map/all_gather | solution.py:309
  1663.2 7.3 fusion.148
  1738.6 7.2 fusion.145
  1746.2 7.1 bitcast_convert_fusion
  1758.1 12.0 all-reduce.3
  1770.8 13.2 reduce-scatter.53.cloned.1.call-done
  1786.1 42.5 %reduce-scatter.47.cloned.1.call-done = bf16[128,1024]{1,0:T(8,128)(2,1)} async-done(((bf16[1024,1024]{1,0:T(8,128)(2,1)}), bf16[128,1024]{1,0:T(8,128)(2,1)}) %reduce-scatter.47.cloned.1.call-update) | async-done | bytes 262160 | tf_op jit(solution)/shard_map/reduce_scatter | solution.py:340
  1828.5 44.7 %reduce-scatter.45.cloned.1.call-done = bf16[128,1024]{1,0:T(8,128)(2,1)} async-done(((bf16[1024,1024]{1,0:T(8,128)(2,1)}), bf16[128,1024]{1,0:T(8,128)(2,1)}) %reduce-scatter.45.cloned.1.call-update) | async-done | bytes 262160 | tf_op jit(solution)/shard_map/reduce_scatter | solution.py:340
  1875.2 34.7 %reduce-scatter.49.cloned.1.call-done = bf16[128,256]{1,0:T(8,128)(2,1)} async-done(((bf16[1024,256]{1,0:T(8,128)(2,1)}), bf16[128,256]{1,0:T(8,128)(2,1)}) %reduce-scatter.49.cloned.1.call-update) | async-done | bytes 65552
  1911.5 41.0 %reduce-scatter.43.cloned.1.call-done = bf16[128,3,256]{2,0,1:T(8,128)(2,1)} async-done(((bf16[1024,3,256]{2,0,1:T(8,128)(2,1)}), bf16[128,3,256]{2,0,1:T(8,128)(2,1)}) %reduce-scatter.43.cloned.1.call-update) | async-done | bytes 196624 | tf_op jit(solution)/shard_map/reduce_scatter | solution.py:334
  1952.5 42.7 %reduce-scatter.41.cloned.1.call-done = bf16[128,3,256]{2,0,1:T(8,128)(2,1)} async-done(((bf16[1024,3,256]{2,0,1:T(8,128)(2,1)}), bf16[128,3,256]{2,0,1:T(8,128)(2,1)}) %reduce-scatter.41.cloned.1.call-update) | async-done | bytes 196624 | tf_op jit(solution)/shard_map/reduce_scatter | solution.py:334
  2000.3 74.0 %reduce-scatter.39.cloned.1.call-done = bf16[512,1024]{1,0:T(8,128)(2,1)} async-done(((bf16[2048,1024]{1,0:T(8,128)(2,1)}), bf16[512,1024]{1,0:T(8,128)(2,1)}) %reduce-scatter.39.cloned.1.call-update) | async-done | bytes 1048592 | tf_op jit(solution)/shard_map/reduce_scatter | solution.py:322
  2082.4 41.0 %all-reduce.2 = (f32[]{:T(128)}, f32[1,2,1024]{2,1,0:T(2,128)}, f32[1,2,1024]{2,1,0:T(2,128)}, f32[1,3,1024]{2,1,0:T(4,128)}, f32[1,3,1024]{2,1,0:T(4,128)}) all-reduce(f32[]{:T(128)S(6)} %add.439, f32[1,2,1024]{2,1,0:T(2,128)} %maximum_bitcast_fusion.6, ...), channel_id=1, replica_groups=mesh['dp'=8,'mp'=4] {'dp','mp'}, use_global_device_ids=true, to_apply=%region_65.66 | all-reduce | flops 10241 | bytes 81928 | tf_op jit(solution)/shard_map/psum | solution.py:364
  (542 shorter events, 322.6 us)
Async XLA Ops:
  7.2 44.8 %all-gather.45.cloned.1.call-start = ((), (), s32[]{:S(2)}) async-start(), calls=%async_computation.36 | async-start | bytes 1769472 | tf_op jit(solution)/shard_map/all_gather | solution.py:196
  9.5 111.9 %all-gather.29.cloned.1.call-start = ((), (), s32[]{:S(2)}) async-start(), calls=%async_computation.16 | async-start | bytes 5242880 | tf_op jit(solution)/shard_map/all_gather | solution.py:213
  33.6 220.6 %copy-start.81 = (f32[1,1,1024]{2,1,0:T(1,128)}, f32[1,1,1024]{2,1,0:T(1,128)S(1)}, u32[]{:S(2)}) copy-start(f32[1,1,1024]{2,1,0:T(1,128)S(1)} %get-tuple-element.171) | copy-start | bytes 12292
  35.1 215.6 %reduce-scatter.25.cloned.1.call-start = ((), (), s32[]{:S(2)}) async-start(), calls=%async_computation.17 | async-start | bytes 5242880 | tf_op jit(solution)/shard_map/reduce_scatter | solution.py:218
  127.7 28.1 %copy-start.53 = (bf16[512,1,256]{0,2,1:T(8,128)(2,1)}, bf16[512,1,256]{0,2,1:T(8,128)(2,1)S(1)}, u32[]{:S(2)}) copy-start(bf16[512,1,256]{0,2,1:T(8,128)(2,1)S(1)} %get-tuple-element.131) | copy-start | bytes 786436
  127.7 38.3 %copy-start.58 = (bf16[512,1,256]{0,2,1:T(8,128)(2,1)}, bf16[512,1,256]{0,2,1:T(8,128)(2,1)S(1)}, u32[]{:S(2)}) copy-start(bf16[512,1,256]{0,2,1:T(8,128)(2,1)S(1)} %get-tuple-element.134) | copy-start | bytes 786436
  129.0 37.1 %copy-start.19 = (bf16[1024,1,256]{0,2,1:T(8,128)(2,1)}, bf16[1024,1,256]{0,2,1:T(8,128)(2,1)S(1)}, u32[]{:S(2)}) copy-start(bf16[1024,1,256]{0,2,1:T(8,128)(2,1)S(1)} %get-tuple-element.135) | copy-start | bytes 1572868
  175.2 106.8 %all-gather.47.cloned.1.call-start = ((), (), s32[]{:S(2)}) async-start(), calls=%async_computation.37 | async-start | bytes 2359296 | tf_op jit(solution)/shard_map/all_gather | solution.py:198
  177.3 78.4 %copy-start.39 = (f32[2,1024,128]{2,1,0:T(8,128)S(1)}, f32[2,1024,128]{2,1,0:T(8,128)}, u32[]{:S(2)}) copy-start(f32[2,1024,128]{2,1,0:T(8,128)} %param.37) | copy-start | bytes 3145732
  177.4 187.1 %all-gather.31.cloned.1.call-start = ((), (), s32[]{:S(2)}) async-start(), calls=%async_computation.18 | async-start | bytes 5242880 | tf_op jit(solution)/shard_map/all_gather | solution.py:226
  255.7 138.4 %all-gather.49.cloned.1.call-start = ((), (), s32[]{:S(2)}) async-start(), calls=%async_computation.38 | async-start | bytes 2359296 | tf_op jit(solution)/shard_map/all_gather | solution.py:201
  256.7 225.7 %reduce-scatter.27.cloned.1.call-start = ((), (), s32[]{:S(2)}) async-start(), calls=%async_computation.19 | async-start | bytes 5242880 | tf_op jit(solution)/shard_map/reduce_scatter | solution.py:231
  266.2 127.9 %copy-start.131 = (f32[1,1024]{1,0:T(1,128)}, f32[1,1024]{1,0:T(1,128)S(1)}, u32[]{:S(2)}) copy-start(f32[1,1024]{1,0:T(1,128)S(1)} %convert_element_type.519) | copy-start | bytes 12292
  405.8 106.0 %all-gather.51.cloned.1.call-start = ((), (), s32[]{:S(2)}) async-start(), calls=%async_computation.39 | async-start | bytes 1769472 | tf_op jit(solution)/shard_map/all_gather | solution.py:196
  406.6 187.8 %all-gather.33.cloned.1.call-start = ((), (), s32[]{:S(2)}) async-start(), calls=%async_computation.20 | async-start | bytes 5242880 | tf_op jit(solution)/shard_map/all_gather | solution.py:213
  423.3 62.9 %copy-start.86 = (f32[1,1,1024]{2,1,0:T(1,128)}, f32[1,1,1024]{2,1,0:T(1,128)S(1)}, u32[]{:S(2)}) copy-start(f32[1,1,1024]{2,1,0:T(1,128)S(1)} %get-tuple-element.170) | copy-start | bytes 12292
  484.5 116.1 %copy-start.92 = (f32[512]{0:T(512)}, f32[512]{0:T(512)S(1)}, u32[]{:S(2)}) copy-start(f32[512]{0:T(512)S(1)} %broadcast_multiply_fusion.1) | copy-start | bytes 6148
  484.8 109.6 %copy-start.115 = (f32[512]{0:T(512)}, f32[512]{0:T(512)S(1)}, u32[]{:S(2)}) copy-start(f32[512]{0:T(512)S(1)} %multiply_reduce_fusion.9) | copy-start | bytes 6148
  484.9 109.6 %copy-start.102 = (f32[512]{0:T(512)}, f32[512]{0:T(512)S(1)}, u32[]{:S(2)}) copy-start(f32[512]{0:T(512)S(1)} %fusion.241) | copy-start | bytes 6148
  486.3 238.6 %reduce-scatter.29.cloned.1.call-start = ((), (), s32[]{:S(2)}) async-start(), calls=%async_computation.21 | async-start | bytes 5242880 | tf_op jit(solution)/shard_map/reduce_scatter | solution.py:218
  602.7 37.4 %copy-start.28 = (bf16[1024,1,256]{0,2,1:T(8,128)(2,1)}, bf16[1024,1,256]{0,2,1:T(8,128)(2,1)S(1)}, u32[]{:S(2)}) copy-start(bf16[1024,1,256]{0,2,1:T(8,128)(2,1)S(1)} %get-tuple-element.127) | copy-start | bytes 1572868
  649.4 106.9 %all-gather.53.cloned.1.call-start = ((), (), s32[]{:S(2)}) async-start(), calls=%async_computation.40 | async-start | bytes 2359296 | tf_op jit(solution)/shard_map/all_gather | solution.py:198
  650.2 188.7 %all-gather.35.cloned.1.call-start = ((), (), s32[]{:S(2)}) async-start(), calls=%async_computation.22 | async-start | bytes 5242880 | tf_op jit(solution)/shard_map/all_gather | solution.py:226
  729.1 139.5 %all-gather.55.cloned.1.call-start = ((), (), s32[]{:S(2)}) async-start(), calls=%async_computation.41 | async-start | bytes 2359296 | tf_op jit(solution)/shard_map/all_gather | solution.py:201
  729.9 220.6 %all-gather.37.cloned.1.call-start = ((), (), s32[]{:S(2)}) async-start(), calls=%async_computation.24 | async-start | bytes 5242880 | tf_op jit(solution)/shard_map/all_gather | solution.py:285
  730.5 318.2 %reduce-scatter.33.cloned.1.call-start = ((), (), s32[]{:S(2)}) async-start(), calls=%async_computation.25 | async-start | bytes 5242880 | tf_op jit(solution)/shard_map/reduce_scatter | solution.py:298
  973.2 154.9 %reduce-scatter.31.cloned.1.call-start = ((), (), s32[]{:S(2)}) async-start(), calls=%async_computation.23 | async-start | bytes 5242880 | tf_op jit(solution)/shard_map/reduce_scatter | solution.py:231
  985.4 231.3 %all-gather.39.cloned.1.call-start = ((), (), s32[]{:S(2)}) async-start(), calls=%async_computation.26 | async-start | bytes 5242880 | tf_op jit(solution)/shard_map/all_gather | solution.py:309
  1135.3 243.9 %reduce-scatter.35.cloned.1.call-start = ((), (), s32[]{:S(2)}) async-start(), calls=%async_computation.27 | async-start | bytes 5242880 | tf_op jit(solution)/shard_map/reduce_scatter | solution.py:322
  1303.7 75.5 %copy-start.87 = (f32[1,1,1024]{2,1,0:T(1,128)S(1)}, f32[1,1,1024]{2,1,0:T(1,128)}, u32[]{:S(2)}) copy-start(f32[1,1,1024]{2,1,0:T(1,128)} %copy-done.86) | copy-start | bytes 12292
  1303.7 75.5 %copy-start.93 = (f32[512]{0:T(512)S(1)}, f32[512]{0:T(512)}, u32[]{:S(2)}) copy-start(f32[512]{0:T(512)} %copy-done.92) | copy-start | bytes 6148
  1303.7 78.1 %copy-start.116 = (f32[512]{0:T(512)S(1)}, f32[512]{0:T(512)}, u32[]{:S(2)}) copy-start(f32[512]{0:T(512)} %copy-done.115) | copy-start | bytes 6148
  1303.7 78.1 %copy-start.103 = (f32[512]{0:T(512)S(1)}, f32[512]{0:T(512)}, u32[]{:S(2)}) copy-start(f32[512]{0:T(512)} %copy-done.102) | copy-start | bytes 6148
  1303.8 166.8 %all-gather.41.cloned.1.call-start = ((), (), s32[]{:S(2)}) async-start(), calls=%async_computation.28 | async-start | bytes 5242880 | tf_op jit(solution)/shard_map/all_gather | solution.py:285
  1386.6 83.9 %copy-start.132 = (f32[1,1024]{1,0:T(1,128)S(1)}, f32[1,1024]{1,0:T(1,128)}, u32[]{:S(2)}) copy-start(f32[1,1024]{1,0:T(1,128)} %copy-done.131) | copy-start | bytes 12292
  1389.1 97.6 %copy-start.138 = (bf16[1,1024,1024]{2,1,0:T(8,128)(2,1)S(1)}, bf16[1,1024,1024]{2,1,0:T(8,128)(2,1)}, u32[]{:S(2)}) copy-start(bf16[1,1024,1024]{2,1,0:T(8,128)(2,1)} %all-gather.47.cloned.1.call-done) | copy-start | bytes 6291460
  1389.1 179.5 %reduce-scatter.37.cloned.1.call-start = ((), (), s32[]{:S(2)}) async-start(), calls=%async_computation.29 | async-start | bytes 5242880 | tf_op jit(solution)/shard_map/reduce_scatter | solution.py:298
  1493.0 75.6 %copy-start.1 = (bf16[512,1024]{1,0:T(8,128)(2,1)S(1)}, bf16[512,1024]{1,0:T(8,128)(2,1)}, u32[]{:S(2)}) copy-start(bf16[512,1024]{1,0:T(8,128)(2,1)} %param.25) | copy-start | bytes 3145732
  1493.0 75.6 %copy-start.3 = (bf16[512,1024]{1,0:T(8,128)(2,1)S(1)}, bf16[512,1024]{1,0:T(8,128)(2,1)}, u32[]{:S(2)}) copy-start(bf16[512,1024]{1,0:T(8,128)(2,1)} %reduce-scatter.25.cloned.1.call-done) | copy-start | bytes 3145732
  1493.0 75.6 %copy-start.82 = (f32[1,1,1024]{2,1,0:T(1,128)S(1)}, f32[1,1,1024]{2,1,0:T(1,128)}, u32[]{:S(2)}) copy-start(f32[1,1,1024]{2,1,0:T(1,128)} %copy-done.81) | copy-start | bytes 12292
  1493.0 75.6 %copy-start.89 = (f32[512]{0:T(512)S(1)}, f32[512]{0:T(512)}, u32[]{:S(2)}) copy-start(f32[512]{0:T(512)} %copy-done.88) | copy-start | bytes 6148
  1493.0 78.3 %copy-start.114 = (f32[512]{0:T(512)S(1)}, f32[512]{0:T(512)}, u32[]{:S(2)}) copy-start(f32[512]{0:T(512)} %copy-done.113) | copy-start | bytes 6148
  1493.1 78.3 %copy-start.97 = (f32[512]{0:T(512)S(1)}, f32[512]{0:T(512)}, u32[]{:S(2)}) copy-start(f32[512]{0:T(512)} %copy-done.96) | copy-start | bytes 6148
  1493.1 165.3 %all-gather.43.cloned.1.call-start = ((), (), s32[]{:S(2)}) async-start(), calls=%async_computation.30 | async-start | bytes 5242880 | tf_op jit(solution)/shard_map/all_gather | solution.py:309
  1577.0 178.2 %reduce-scatter.55.cloned.1.call-start = ((), (), s32[]{:S(2)}) async-start(), calls=%async_computation.45 | async-start | bytes 2359296
  1590.3 166.1 %reduce-scatter.51.cloned.1.call-start = ((), (), s32[]{:S(2)}) async-start(), calls=%async_computation.43 | async-start | bytes 589824
  1595.1 188.9 %reduce-scatter.53.cloned.1.call-start = ((), (), s32[]{:S(2)}) async-start(), calls=%async_computation.44 | async-start | bytes 2359296
  1608.7 219.9 %reduce-scatter.47.cloned.1.call-start = ((), (), s32[]{:S(2)}) async-start(), calls=%async_computation.35 | async-start | bytes 2359296 | tf_op jit(solution)/shard_map/reduce_scatter | solution.py:340
  1618.2 40.2 %copy-start.141 = (bf16[2,128,512]{2,1,0:T(8,128)(2,1)S(1)}, bf16[2,128,512]{2,1,0:T(8,128)(2,1)}, u32[]{:S(2)}) copy-start(bf16[2,128,512]{2,1,0:T(8,128)(2,1)} %convolution_convert_fusion.18) | copy-start | bytes 786436
  1618.2 255.1 %reduce-scatter.45.cloned.1.call-start = ((), (), s32[]{:S(2)}) async-start(), calls=%async_computation.34 | async-start | bytes 2359296 | tf_op jit(solution)/shard_map/reduce_scatter | solution.py:340
  1628.1 35.1 %copy-start.65 = (bf16[1024,1,256]{2,0,1:T(8,128)(2,1)S(1)}, bf16[1024,1,256]{2,0,1:T(8,128)(2,1)}, u32[]{:S(2)}) copy-start(bf16[1024,1,256]{2,0,1:T(8,128)(2,1)} %copy.194) | copy-start | bytes 1572868
  1628.1 35.1 %copy-start.66 = (bf16[1024,1,256]{2,0,1:T(8,128)(2,1)S(1)}, bf16[1024,1,256]{2,0,1:T(8,128)(2,1)}, u32[]{:S(2)}) copy-start(bf16[1024,1,256]{2,0,1:T(8,128)(2,1)} %copy.186) | copy-start | bytes 1572868
  1628.1 35.1 %copy-start.67 = (bf16[1024,1,256]{2,0,1:T(8,128)(2,1)S(1)}, bf16[1024,1,256]{2,0,1:T(8,128)(2,1)}, u32[]{:S(2)}) copy-start(bf16[1024,1,256]{2,0,1:T(8,128)(2,1)} %copy.185) | copy-start | bytes 1572868
  1628.2 281.8 %reduce-scatter.49.cloned.1.call-start = ((), (), s32[]{:S(2)}) async-start(), calls=%async_computation.42 | async-start | bytes 589824
  1663.1 289.4 %reduce-scatter.43.cloned.1.call-start = ((), (), s32[]{:S(2)}) async-start(), calls=%async_computation.33 | async-start | bytes 1769472 | tf_op jit(solution)/shard_map/reduce_scatter | solution.py:334
  1670.6 324.6 %reduce-scatter.41.cloned.1.call-start = ((), (), s32[]{:S(2)}) async-start(), calls=%async_computation.32 | async-start | bytes 1769472 | tf_op jit(solution)/shard_map/reduce_scatter | solution.py:334
  1745.9 328.4 %reduce-scatter.39.cloned.1.call-start = ((), (), s32[]{:S(2)}) async-start(), calls=%async_computation.31 | async-start | bytes 5242880 | tf_op jit(solution)/shard_map/reduce_scatter | solution.py:322
  1753.4 320.9 %copy-start.85 = (f32[1,1,1024]{2,1,0:T(1,128)S(1)}, f32[1,1,1024]{2,1,0:T(1,128)}, u32[]{:S(2)}) copy-start(f32[1,1,1024]{2,1,0:T(1,128)} %copy-done.84) | copy-start | bytes 12292
  1753.4 320.9 %copy-start.95 = (f32[512]{0:T(512)S(1)}, f32[512]{0:T(512)}, u32[]{:S(2)}) copy-start(f32[512]{0:T(512)} %copy-done.94) | copy-start | bytes 6148
  1753.4 322.8 %copy-start.110 = (f32[512]{0:T(512)S(1)}, f32[512]{0:T(512)}, u32[]{:S(2)}) copy-start(f32[512]{0:T(512)} %copy-done.109) | copy-start | bytes 6148
  1770.1 139.8 %copy-start.136 = (bf16[1,128]{1,0:T(2,128)(2,1)}, bf16[1,128]{1,0:T(2,128)(2,1)S(1)}, u32[]{:S(2)}) copy-start(bf16[1,128]{1,0:T(2,128)(2,1)S(1)} %dynamic-slice_bitcast_fusion) | copy-start | bytes 772
  1770.2 139.7 %copy-start.137 = (bf16[1,128]{1,0:T(2,128)(2,1)}, bf16[1,128]{1,0:T(2,128)(2,1)S(1)}, u32[]{:S(2)}) copy-start(bf16[1,128]{1,0:T(2,128)(2,1)S(1)} %dynamic-slice_bitcast_fusion.1) | copy-start | bytes 772
  1784.0 353.7 %copy-start.43 = (f32[2,128,3,256]{3,1,2,0:T(8,128)S(1)}, f32[2,128,3,256]{3,1,2,0:T(8,128)}, u32[]{:S(2)}) copy-start(f32[2,128,3,256]{3,1,2,0:T(8,128)} %param.28) | copy-start | bytes 2359300
  2076.7 64.3 %copy-start.40 = (f32[2,1024,128]{2,1,0:T(8,128)S(1)}, f32[2,1024,128]{2,1,0:T(8,128)}, u32[]{:S(2)}) copy-start(f32[2,1024,128]{2,1,0:T(8,128)} %param.37) | copy-start | bytes 3145732
  (114 other events, 573.8 us)
Sparse Core Ops, SparseCore 0:
  10.5 28.3 all-gather.44
  41.1 80.3 all-gather.28
  175.3 75.2 reduce-scatter.24
  253.2 28.7 all-gather.46
  284.1 80.3 all-gather.30
  366.9 27.1 all-gather.48
  406.0 76.3 reduce-scatter.26
  484.8 27.0 all-gather.50
  514.0 80.3 all-gather.32
  649.6 75.2 reduce-scatter.28
  727.5 28.7 all-gather.52
  758.5 80.3 all-gather.34
  841.4 27.1 all-gather.54
  870.1 80.3 all-gather.36
  973.3 75.3 reduce-scatter.32
  1050.9 77.2 reduce-scatter.30
  1135.4 81.2 all-gather.38
  1303.9 75.2 reduce-scatter.34
  1389.2 81.2 all-gather.40
  1493.2 75.3 reduce-scatter.36
  1577.1 81.2 all-gather.42
  1662.0 39.7 reduce-scatter.54
  1704.9 33.6 reduce-scatter.50
  1742.1 41.7 reduce-scatter.52
  1787.3 41.2 reduce-scatter.46
  1832.0 41.2 reduce-scatter.44
  1876.2 33.6 reduce-scatter.48
  1913.6 38.9 reduce-scatter.42
  1956.7 38.4 reduce-scatter.40
  1997.5 76.7 reduce-scatter.38
where the time goes:
time: 2170 us; the launch traced here: 2160 us
  waiting for transfers between devices  1470 us (68%)
  matrix products  371 us (17%)
  blocking collectives  131 us (6%)
  other arithmetic  89.1 us (4%)
  local copies, waits for them, and re-layouts  74.8 us (3%)
  between operations  23.5 us (1%)
    all_gather x2, waiting for transfers between devices, shards(): full_two = lax.all_gather(normed_two, 'mp', axis=0, tiled=True)  165 us
    all_gather x2, waiting for transfers between devices, shards(): lax.all_gather(grad_stream.astype(jnp.bfloat16), 'mp', axis=0, tiled=True)  163 us
    all_gather x2, waiting for transfers between devices, shards(): full_normed = lax.all_gather(normed, 'mp', axis=0, tiled=True)  152 us
    reduce_scatter x2, waiting for transfers between devices, shards(): lax.psum_scatter(jnp.einsum('tcf,dcf->td', qkv_rows_grad, qkv_low, prefer...  149 us
    reduce_scatter x2, waiting for transfers between devices, shards(): lax.psum_scatter(jnp.dot(attended, proj_low, preferred_element_type=jnp.f...  148 us
    reduce_scatter x2, waiting for transfers between devices, shards(): lax.psum_scatter(lax.dot_general(hidden_grad, upper_low, contract_cols, p...  139 us
    reduce_scatter x2, waiting for transfers between devices, shards(): lax.psum_scatter(jnp.dot(active, lower_low, preferred_element_type=jnp.fl...  135 us
    all_gather x2, waiting for transfers between devices, shards(): lax.all_gather(middle_grad.astype(jnp.bfloat16), 'mp', axis=0, tiled=True)  111 us
  transfers between devices with their start and end apart: 30, of which 27 were waited for; matrix products, arithmetic and copies ran while one was open for 10% of the time, Pallas kernels for 0%

commit v1 on v0

v1 whole, which is shorter than its diff:
```python
import functools
import math

import jax
import jax.numpy as jnp
import numpy as np
from jax import lax
from jax.experimental import pallas as pl
from jax.experimental.pallas import tpu as pltpu
from jax.sharding import PartitionSpec as P

H = 8
HD = 128
STEP = 5
MAX_DOC = 512

norm_eps = 1e-05
clip_bound = 1.0
beta_first = 0.9
beta_second = 0.95
adam_eps = 1e-08
masked_score = -1e30
group_rates = (0.03, 0.12, 0.03, 0.015, 0.3, 0.7, 0.3)
group_decays = (0.1, 0.1, 0.1, 0.1, 0.0, 0.0, 0.0)
contract_rows = (((0,), (0,)), ((), ()))
contract_cols = (((1,), (1,)), ((), ()))
f32 = jnp.float32
bf16 = jnp.bfloat16
score_scale = 1.0 / math.sqrt(HD)


def adam_update(master, moment, square, gradient, factor, step_rate, decay_rate):
    clipped = gradient * factor
    moment_new = beta_first * moment + (1.0 - beta_first) * clipped
    square_new = beta_second * square + (1.0 - beta_second) * clipped * clipped
    first_hat = moment_new / (1.0 - beta_first**STEP)
    second_hat = square_new / (1.0 - beta_second**STEP)
    master_new = master - step_rate * (
        first_hat / (jnp.sqrt(second_hat) + adam_eps) + decay_rate * master
    )
    return (master_new, moment_new, square_new)


def gelu_tanh(values):
    return jax.nn.gelu(values, approximate=True)


def layer_norm(values, scale_vec, shift_vec):
    center = values - jnp.mean(values, axis=-1, keepdims=True)
    spread = jnp.mean(center * center, axis=-1, keepdims=True)
    return center * lax.rsqrt(spread + norm_eps) * scale_vec + shift_vec


def dot(left, right):
    return jnp.dot(left, right, preferred_element_type=f32)


def dot_rows(left, right):
    return lax.dot_general(left, right, contract_rows, preferred_element_type=f32)


def dot_cols(left, right):
    return lax.dot_general(left, right, contract_cols, preferred_element_type=f32)


def masked_scores(slope, doc_col, doc_row, query, key, first_row, first_col):
    scores = dot_cols(query, key) * score_scale
    rows = first_row + lax.broadcasted_iota(jnp.int32, scores.shape, 0)
    cols = first_col + lax.broadcasted_iota(jnp.int32, scores.shape, 1)
    distance = rows - cols
    allowed = (distance >= 0) & (doc_col == doc_row)
    return jnp.where(allowed, scores - slope * distance.astype(f32), masked_score)


def key_range(first_row, block):
    low = max(0, first_row - (MAX_DOC - 1)) // block * block
    return low, first_row + block


def attend_kernel(heads, block, slope_ref, dcol_ref, drow_ref, qk_ref, v_ref, o_ref):
    length = v_ref.shape[0]
    for head in range(heads):
        slope = slope_ref[pl.program_id(0) * heads + head]
        at = head * HD
        kat = (heads + head) * HD
        for first_row in range(0, length, block):
            low, high = key_range(first_row, block)
            scores = masked_scores(
                slope,
                dcol_ref[first_row : first_row + block, :],
                drow_ref[:, low:high],
                qk_ref[first_row : first_row + block, at : at + HD],
                qk_ref[low:high, kat : kat + HD],
                first_row,
                low,
            )
            shifted = jnp.exp(scores - jnp.max(scores, axis=-1, keepdims=True))
            total = jnp.sum(shifted, axis=-1, keepdims=True)
            prob_low = (shifted * (1.0 / total)).astype(bf16)
            o_ref[first_row : first_row + block, at : at + HD] = dot(
                prob_low, v_ref[low:high, at : at + HD]
            ).astype(bf16)


def attend_back_kernel(
    heads, block, slope_ref, dcol_ref, drow_ref, qk_ref, v_ref, o_ref, do_ref,
    dqk_ref, dv_ref, key_acc, value_acc,
):
    length = v_ref.shape[0]
    for head in range(heads):
        slope = slope_ref[pl.program_id(0) * heads + head]
        at = head * HD
        kat = (heads + head) * HD
        key_acc[...] = jnp.zeros_like(key_acc)
        value_acc[...] = jnp.zeros_like(value_acc)
        for first_row in range(0, length, block):
            low, high = key_range(first_row, block)
            rows = slice(first_row, first_row + block)
            query = qk_ref[rows, at : at + HD]
            key = qk_ref[low:high, kat : kat + HD]
            scores = masked_scores(
                slope, dcol_ref[rows, :], drow_ref[:, low:high], query, key, first_row, low
            )
            shifted = jnp.exp(scores - jnp.max(scores, axis=-1, keepdims=True))
            total = jnp.sum(shifted, axis=-1, keepdims=True)
            probs = shifted * (1.0 / total)
            out_grad = do_ref[rows, at : at + HD]
            value_acc[low:high, :] += dot_rows(probs.astype(bf16), out_grad)
            prob_grad = dot_cols(out_grad, v_ref[low:high, at : at + HD])
            inner = jnp.sum(
                out_grad.astype(f32) * o_ref[rows, at : at + HD].astype(f32),
                axis=-1,
                keepdims=True,
            )
            score_grad = (probs * (prob_grad - inner)).astype(bf16)
            dqk_ref[rows, at : at + HD] = (dot(score_grad, key) * score_scale).astype(bf16)
            key_acc[low:high, :] += dot_rows(score_grad, query)
        dqk_ref[:, kat : kat + HD] = (key_acc[...] * score_scale).astype(bf16)
        dv_ref[:, at : at + HD] = value_acc[...].astype(bf16)


def attend_specs(length, width, slots):
    def columns(each):
        return pl.BlockSpec((length, each), lambda s: (0, s))

    fixed = [
        pl.BlockSpec(memory_space=pltpu.SMEM),
        pl.BlockSpec((length, 1), lambda s: (0, 0)),
        pl.BlockSpec((1, length), lambda s: (0, 0)),
    ]
    return fixed, columns(2 * width), columns(width)


def attend(slopes, docs, qk, v, slots):
    length = v.shape[0]
    width = v.shape[1] // slots
    fixed, wide, narrow = attend_specs(length, width, slots)
    pairs = slots * width // HD * length * length
    return pl.pallas_call(
        functools.partial(attend_kernel, width // HD, min(256, length)),
        grid=(slots,),
        in_specs=fixed + [wide, narrow],
        out_specs=narrow,
        out_shape=jax.ShapeDtypeStruct(v.shape, bf16),
        compiler_params=pltpu.CompilerParams(vmem_limit_bytes=32 * 2**20),
        cost_estimate=pl.CostEstimate(
            flops=4 * pairs * HD, bytes_accessed=8 * v.size, transcendentals=pairs
        ),
    )(slopes, docs.reshape(-1, 1), docs.reshape(1, -1), qk, v)


def attend_back(slopes, docs, qk, v, o, do, slots):
    length = v.shape[0]
    width = v.shape[1] // slots
    fixed, wide, narrow = attend_specs(length, width, slots)
    pairs = slots * width // HD * length * length
    return pl.pallas_call(
        functools.partial(attend_back_kernel, width // HD, min(256, length)),
        grid=(slots,),
        in_specs=fixed + [wide, narrow, narrow, narrow],
        out_specs=[wide, narrow],
        out_shape=[jax.ShapeDtypeStruct(qk.shape, bf16), jax.ShapeDtypeStruct(v.shape, bf16)],
        scratch_shapes=[pltpu.VMEM((length, HD), f32), pltpu.VMEM((length, HD), f32)],
        compiler_params=pltpu.CompilerParams(vmem_limit_bytes=32 * 2**20),
        cost_estimate=pl.CostEstimate(
            flops=10 * pairs * HD, bytes_accessed=20 * v.size, transcendentals=pairs
        ),
    )(slopes, docs.reshape(-1, 1), docs.reshape(1, -1), qk, v, o, do)


def bits_of(size):
    return [1 << at for at in range(size.bit_length() - 1)]


def program(dp_size, mp_size, args):
    (
        inputs, documents, cotangent,
        qkv_weight, qkv_moment, qkv_square,
        proj_weight, proj_moment, proj_square,
        upper_weight, upper_moment, upper_square,
        lower_weight, lower_moment, lower_square,
        hidden_bias, bias_moment, bias_square,
        norm_gains, gains_moment, gains_square,
        shift_params, shifts_moment, shifts_square,
    ) = args
    layers = qkv_weight.shape[0]
    tokens, features = inputs.shape
    length = documents.shape[1]
    pieces = length // tokens
    slots = mp_size // pieces
    wide = features // dp_size
    z_cols = qkv_weight.shape[3]
    heads_slot = z_cols // HD
    me_dp = lax.axis_index("dp")
    me_mp = lax.axis_index("mp")
    core = me_dp & 1
    dp_bits = bits_of(dp_size)
    mp_bits = bits_of(mp_size)
    upper_bits = dp_bits[1:]

    def swap(values, axis, bit):
        size = dp_size if axis == "dp" else mp_size
        return lax.ppermute(values, axis, [(at, at ^ bit) for at in range(size)])

    order = [2 * k + c for c in (0, 1) for k in range(dp_size // 2)]

    def to_relative(values):
        parts = [lax.dynamic_slice_in_dim(values, (me_dp ^ r) * wide, wide, 1) for r in order]
        return jnp.concatenate(parts, axis=1)

    place_of = np.zeros((dp_size,), np.int32)
    for place, r in enumerate(order):
        place_of[r] = place
    place_table = jnp.asarray(place_of)

    def to_absolute(values):
        parts = [
            lax.dynamic_slice_in_dim(values, place_table[me_dp ^ b] * wide, wide, 1)
            for b in range(dp_size)
        ]
        return jnp.concatenate(parts, axis=1)

    def gather(shard, bits):
        for bit in mp_bits:
            shard = jnp.concatenate([shard, swap(shard, "mp", bit)], axis=1)
        parts = {0: shard}
        for bit in list(bits) + [1]:
            for r in sorted(parts):
                parts[r | bit] = swap(parts[r], "dp", bit)
        return [parts[r] for r in order]

    def scatter(kept, sent, bits):
        values = (kept.astype(f32) + swap(sent, "dp", 1).astype(f32)).astype(bf16)
        cols = values.shape[1] // mp_size
        values = values.reshape((2,) * len(upper_bits) + (wide, mp_size * cols))
        left = list(upper_bits)
        for bit in bits:
            axis = len(left) - 1 - left.index(bit)
            left.remove(bit)
            sent = swap(lax.index_in_dim(values, 1, axis, False), "dp", bit)
            kept = lax.index_in_dim(values, 0, axis, False)
            values = (kept.astype(f32) + sent.astype(f32)).astype(bf16)
        for bit in reversed(mp_bits):
            half = values.shape[1] // 2
            sent = swap(values[:, half:], "mp", bit)
            values = values[:, :half].astype(f32) + sent.astype(f32)
            if bit != 1:
                values = values.astype(bf16)
        return values

    def by_core(own, other, axis):
        first = jnp.where(core == 0, own, other)
        second = jnp.where(core == 0, other, own)
        return jnp.concatenate([first, second], axis=axis)

    paired = pieces == 2 and dp_size % 2 == 0 and mp_size % 2 == 0
    if paired:
        moved = core != (me_mp & 1)
        pairs = []
        for d in range(dp_size):
            for m in range(mp_size):
                if (d & 1) != (m & 1):
                    pairs.append((d * mp_size + m, (d ^ 1) * mp_size + (m ^ 1)))

        def trade(values):
            other = lax.ppermute(values, ("dp", "mp"), pairs)
            return jnp.where(moved, other, values)

        doc_rows = jnp.where(moved, swap(documents, "dp", 1), documents)
        docs = lax.dynamic_index_in_dim(doc_rows, me_mp // 2, 0, False)
        first_slot = core * slots

        def share_heads(values):
            half = values.shape[1] // 2
            own = lax.dynamic_slice_in_dim(values, core * half, half, 1)
            sent = lax.dynamic_slice_in_dim(values, (1 - core) * half, half, 1)
            return by_core(own, swap(sent, "dp", 1), 0)

        def return_heads(values):
            own = lax.dynamic_slice_in_dim(values, core * tokens, tokens, 0)
            sent = lax.dynamic_slice_in_dim(values, (1 - core) * tokens, tokens, 0)
            return by_core(own, swap(sent, "dp", 1), 1)

        slot_ids = me_mp ^ (first_slot + jnp.arange(slots))
    else:
        groups = [list(range(g * pieces, (g + 1) * pieces)) for g in range(mp_size // pieces)]

        def trade(values):
            return values

        docs = lax.dynamic_index_in_dim(documents, me_mp // pieces, 0, False)
        flipped = jnp.arange(mp_size) ^ me_mp

        def flip(values):
            parts = values.reshape(values.shape[0], mp_size, -1)
            return jnp.take(parts, flipped, axis=1).reshape(values.shape)

        def share_heads(values):
            return lax.all_to_all(
                flip(values), "mp", 1, 0, axis_index_groups=groups, tiled=True
            )

        def return_heads(values):
            return flip(
                lax.all_to_all(values, "mp", 0, 1, axis_index_groups=groups, tiled=True)
            )

        slot_ids = (me_mp % pieces) * slots + jnp.arange(slots)

    head_ids = (slot_ids[:, None] * heads_slot + jnp.arange(heads_slot)[None, :]).reshape(-1)
    slope_table = jnp.asarray(0.5 ** (np.arange(H) + 1.0), dtype=f32)
    slopes = jnp.take(slope_table, head_ids)

    small = jnp.concatenate(
        [
            norm_gains.reshape(-1, wide),
            shift_params.reshape(-1, wide),
            hidden_bias.reshape(-1, wide),
        ],
        axis=0,
    ).astype(bf16)
    small_all = lax.all_gather(small, ("mp", "dp"), axis=0).astype(f32)
    small_all = small_all.reshape(mp_size, dp_size, small.shape[0], wide)
    rel = jnp.asarray(order, dtype=jnp.int32) ^ me_dp
    gain_rows = norm_gains.shape[1]
    shift_count = shift_params.shape[1]
    vectors = jnp.take(small_all[0], rel, axis=0).transpose(1, 0, 2).reshape(-1, features)
    gains = vectors[: layers * gain_rows].reshape(layers, gain_rows, features)
    shifts = vectors[layers * gain_rows : layers * (gain_rows + shift_count)].reshape(
        layers, shift_count, features
    )
    bias_parts = small_all[:, :, layers * (gain_rows + shift_count) :]
    bias_parts = jnp.take(bias_parts, jnp.arange(mp_size) ^ me_mp, axis=0)
    biases = bias_parts.transpose(2, 0, 1, 3).reshape(layers, -1)

    first_order = upper_bits
    second_order = upper_bits[::-1]
    gathered = []
    for layer in range(layers):
        qk_shard = qkv_weight[layer, :, :2].astype(bf16).reshape(wide, 2 * z_cols)
        vo_shard = jnp.concatenate(
            [qkv_weight[layer, :, 2].astype(bf16), proj_weight[layer].astype(bf16).T], axis=1
        )
        up_shard = upper_weight[layer].astype(bf16)
        down_shard = lower_weight[layer].astype(bf16).T
        qk = jnp.concatenate(gather(qk_shard, first_order), axis=0)
        vo = [
            part.reshape(wide, mp_size, 2, z_cols) for part in gather(vo_shard, second_order)
        ]
        value = jnp.concatenate([part[:, :, 0] for part in vo], axis=0).reshape(features, -1)
        proj = jnp.concatenate([part[:, :, 1] for part in vo], axis=0).reshape(features, -1)
        upper = jnp.concatenate(gather(up_shard, first_order), axis=0)
        lower = jnp.concatenate(gather(down_shard, second_order), axis=0)
        gathered.append((qk, value, proj, upper, lower))

    stream = to_relative(trade(inputs)).astype(f32)
    grad_stream = to_relative(trade(cotangent)).astype(f32)
    stored = []
    for layer in range(layers):
        qk_w, value_w, proj_w, upper_w, lower_w = gathered[layer]
        normed = layer_norm(stream, gains[layer, 0], shifts[layer, 0]).astype(bf16)
        qk = share_heads(dot(normed, qk_w).astype(bf16))
        value = share_heads(dot(normed, value_w).astype(bf16))
        mixed = attend(slopes, docs, qk, value, slots)
        attended = return_heads(mixed)
        middle = stream + dot_cols(attended, proj_w)
        normed_two = layer_norm(middle, gains[layer, 1], shifts[layer, 1]).astype(bf16)
        hidden = dot(normed_two, upper_w) + biases[layer]
        active = gelu_tanh(hidden).astype(bf16)
        stored.append(
            (stream, middle, normed, qk, value, mixed, attended, normed_two, hidden, active)
        )
        stream = middle + dot_cols(active, lower_w) + shifts[layer, 2]
    output_stream = to_absolute(stream)
    if paired:
        other = lax.ppermute(output_stream.astype(bf16), ("dp", "mp"), pairs)
        output_stream = jnp.where(moved, other.astype(f32), output_stream)

    half = features // 2

    def weight_gradient(left, right, bits):
        sent = dot_rows(left[:, half:], right).astype(bf16)
        kept = dot_rows(left[:, :half], right).astype(bf16)
        return scatter(kept, sent, bits)

    weight_grads = [None] * layers
    small_grads = [None] * layers
    for layer in reversed(range(layers)):
        qk_w, value_w, proj_w, upper_w, lower_w = gathered[layer]
        (
            stream_in, middle, normed, qk, value, mixed, attended, normed_two, hidden, active
        ) = stored[layer]
        no_shift = jnp.zeros((features,), f32)
        out_shift_grad = jnp.sum(grad_stream, axis=0)
        grad_low = grad_stream.astype(bf16)
        active_grad = dot(grad_low, lower_w)
        _, pull_gelu = jax.vjp(gelu_tanh, hidden)
        hidden_grad = pull_gelu(active_grad)[0].astype(bf16)
        lower_grad = weight_gradient(grad_low, active, second_order)
        upper_grad = weight_gradient(normed_two, hidden_grad, first_order)
        bias_grad = jnp.sum(hidden_grad, axis=0, dtype=f32)
        normed_two_grad = dot_cols(hidden_grad, upper_w)
        _, pull_two = jax.vjp(layer_norm, middle, gains[layer, 1], no_shift)
        middle_part, gain_two, shift_two = pull_two(normed_two_grad)
        middle_grad = grad_stream + middle_part
        middle_low = middle_grad.astype(bf16)
        attended_grad = dot(middle_low, proj_w).astype(bf16)
        proj_grad = weight_gradient(middle_low, attended, second_order)
        mixed_grad = share_heads(attended_grad)
        qk_grad, value_grad = attend_back(slopes, docs, qk, value, mixed, mixed_grad, slots)
        qk_grad = return_heads(qk_grad)
        value_grad = return_heads(value_grad)
        normed_grad = dot_cols(qk_grad, qk_w) + dot_cols(value_grad, value_w)
        qk_weight_grad = weight_gradient(normed, qk_grad, first_order)
        value_weight_grad = weight_gradient(normed, value_grad, second_order)
        _, pull_one = jax.vjp(layer_norm, stream_in, gains[layer, 0], no_shift)
        stream_part, gain_one, shift_one = pull_one(normed_grad)
        grad_stream = middle_grad + stream_part
        weight_grads[layer] = (
            jnp.concatenate([qk_weight_grad, value_weight_grad], axis=1).reshape(
                wide, 3, z_cols
            ),
            proj_grad.T,
            upper_grad,
            lower_grad.T,
        )
        vectors = to_absolute(
            jnp.stack([gain_one, gain_two, shift_one, shift_two, out_shift_grad])
        )
        bias_grad = jnp.take(
            bias_grad.reshape(mp_size, -1), jnp.arange(mp_size) ^ me_mp, axis=0
        ).reshape(-1, features)
        small_grads[layer] = lax.psum(
            jnp.concatenate([vectors, bias_grad], axis=0), ("dp", "mp")
        )
    input_grad = to_absolute(grad_stream)
    if paired:
        other = lax.ppermute(input_grad.astype(bf16), ("dp", "mp"), pairs)
        input_grad = jnp.where(moved, other.astype(f32), input_grad)

    owned = jnp.float32(0.0)
    for member in range(4):
        for layer in range(layers):
            gradient = weight_grads[layer][member]
            owned = owned + jnp.sum(gradient * gradient)
    stacked = [jnp.stack([weight_grads[at][member] for at in range(layers)]) for member in range(4)]
    small_grad = jnp.stack(small_grads)
    sum_squares = lax.psum(owned, ("dp", "mp")) + jnp.sum(small_grad * small_grad)
    grad_norm = jnp.sqrt(sum_squares)
    factor = jnp.minimum(1.0, clip_bound / grad_norm)
    vector_grads = lax.dynamic_slice_in_dim(small_grad[:, :5], me_dp * wide, wide, 2)
    bias_wide = hidden_bias.shape[1]
    bias_grads = lax.dynamic_slice_in_dim(
        small_grad[:, 5:].reshape(layers, -1),
        (me_mp * dp_size + me_dp) * bias_wide,
        bias_wide,
        1,
    )
    masters = (
        qkv_weight, proj_weight, upper_weight, lower_weight, hidden_bias, norm_gains, shift_params
    )
    moments = (
        qkv_moment, proj_moment, upper_moment, lower_moment, bias_moment, gains_moment,
        shifts_moment,
    )
    squares = (
        qkv_square, proj_square, upper_square, lower_square, bias_square, gains_square,
        shifts_square,
    )
    gradients = (*stacked, bias_grads, vector_grads[:, :2], vector_grads[:, 2:])
    results = [output_stream, input_grad]
    for at in range(7):
        results.extend(
            adam_update(
                masters[at], moments[at], squares[at], gradients[at], factor,
                group_rates[at], group_decays[at],
            )
        )
    results.append(grad_norm)
    return tuple(results)


def solution(mesh):
    dp_size = mesh.shape["dp"]
    mp_size = mesh.shape["mp"]
    rows = P(("dp", "mp"), None)
    split_rows = P(None, "dp", None, "mp")
    split_upper = P(None, "dp", "mp")
    split_lower = P(None, "mp", "dp")
    split_bias = P(None, ("mp", "dp"))
    split_vector = P(None, None, "dp")
    groups = (
        split_rows, split_lower, split_upper, split_lower, split_bias, split_vector, split_vector
    )
    placed = tuple(spec for spec in groups for _ in range(3))

    def shards(*args):
        return program(dp_size, mp_size, args)

    return jax.shard_map(
        shards,
        mesh=mesh,
        in_specs=(rows, P("dp", None), rows) + placed,
        out_specs=(rows, rows) + placed + (P(),),
        check_vma=False,
    )
```

time: 2170 us -> 1270 us (0.59)
  waiting for transfers between devices: 1470 us -> 545 us
  matrix products: 371 us -> 187 us
  starting transfers between devices: 3.43 us -> 123 us
  local copies, waits for them, and re-layouts: 74.8 us -> 144 us
  Pallas kernels: 0 us -> 47.9 us
  blocking collectives: 131 us -> 91.4 us
    reduce_scatter x12 -> x0, waiting for transfers between devices: 742 us -> none  [the longest x2 149 us: shards(): lax.psum_scatter(jnp.einsum('tcf,dcf->td', qkv_rows_grad, qkv_low, prefer...]
    all_gather x14 -> x0, waiting for transfers between devices: 674 us -> none  [the longest x2 165 us: shards(): full_two = lax.all_gather(normed_two, 'mp', axis=0, tiled=True)]
    ppermute x0 -> x139, waiting for transfers between devices: none -> 545 us  [the longest x135 545 us: swap(): return lax.ppermute(values, axis, [(at, at ^ bit) for at in range(size)])]
    dot_general x64 -> x40, matrix products: 325 us -> 187 us  [the longest x10 69 us: dot(): return jnp.dot(left, right, preferred_element_type=f32)]
    ppermute x0 -> x139, starting transfers between devices: none -> 123 us  [the longest x135 112 us: swap(): return lax.ppermute(values, axis, [(at, at ^ bit) for at in range(size)])]
    unnamed x34 -> x0, waiting for transfers between devices: 51 us -> none
    pallas_call x0 -> x4, Pallas kernels: none -> 47.9 us  [the longest x2 29.3 us: attend_back(): pl.pallas_call(functools.partial(attend_back_kernel, width // HD, min(256...]
    sub x8 -> x0, matrix products: 45.7 us -> none  [attend_forward(): shifted = jnp.exp(scores - row_max)]
  transfers between devices with their start and end apart: 30 -> 139, of which waited for: 27 -> 55; matrix products, arithmetic and copies ran while one was open for 10% -> 28% of each run, Pallas kernels for 0% -> 4%
where the time goes in v1:
time: 1270 us; the launch traced here: 1260 us
  waiting for transfers between devices  545 us (43%)
  matrix products  187 us (15%)
  local copies, waits for them, and re-layouts  144 us (11%)
  starting transfers between devices  123 us (10%)
  other arithmetic  105 us (8%)
  blocking collectives  91.4 us (7%)
  Pallas kernels  47.9 us (4%)
  between operations  17.8 us (1%)
    ppermute x135, waiting for transfers between devices, swap(): return lax.ppermute(values, axis, [(at, at ^ bit) for at in range(size)])  545 us
    ppermute x135, starting transfers between devices, swap(): return lax.ppermute(values, axis, [(at, at ^ bit) for at in range(size)])  112 us
    unnamed x463, local copies, waits for them, and re-layouts  78.5 us
    dot_general x10, matrix products, dot(): return jnp.dot(left, right, preferred_element_type=f32)  69 us
    dot_general x20, matrix products, dot_rows(): lax.dot_general(left, right, contract_rows, preferred_element_type=f32)  67.4 us
    all_gather x1, blocking collectives, program(): small_all = lax.all_gather(small, ('mp', 'dp'), axis=0).astype(f32)  51.6 us
    dot_general x10, matrix products, dot_cols(): lax.dot_general(left, right, contract_cols, preferred_element_type=f32)  50.6 us
    psum x1, blocking collectives, program(): lax.psum(owned, ('dp', 'mp')) + jnp.sum(small_grad * small_grad)  39.8 us
  transfers between devices with their start and end apart: 139, of which 55 were waited for; matrix products, arithmetic and copies ran while one was open for 28% of the time, Pallas kernels for 4%

profile of v1, /device:TPU:1, one launch (start us, length us, event | category | flops | bytes accessed | tf_op | source)
XLA Modules:
  0.0 1260.8 jit_solution(2359882955339907822)
XLA Ops:
  8.8 51.6 %all_gather.4 = bf16[32,12,128]{2,1,0:T(8,128)(2,1)S(1)} all-gather(bf16[1,12,128]{2,1,0:T(8,128)(2,1)S(1)} %pad_maximum_fusion.50), channel_id=1, replica_groups=mesh['dp'=8,'mp'=4] {'mp','dp'}, dimensions={0}, use_global_device_ids=true | all-gather | bytes 101376 | tf_op jit(solution)/shard_map/all_gather | solution.py:342
  89.5 4.5 collective-permute-start
  100.7 38.7 %collective-permute-done.52 = bf16[128,1024]{0,1:T(8,128)(2,1)S(1)} collective-permute-done((bf16[128,1024]{0,1:T(8,128)(2,1)S(1)}, bf16[128,1024]{0,1:T(8,128)(2,1)S(1)}, u32[]{:S(2)}, u32[]{:S(2)}) %collective-permute-start.52) | collective-permute-done | bytes 262176 | tf_op jit(solution)/shard_map/ppermute | solution.py:223
  142.8 40.9 %collective-permute-done.42 = bf16[128,1024]{0,1:T(8,128)(2,1)S(1)} collective-permute-done((bf16[128,1024]{0,1:T(8,128)(2,1)S(1)}, bf16[128,1024]{0,1:T(8,128)(2,1)S(1)}, u32[]{:S(2)}, u32[]{:S(2)}) %collective-permute-start.42) | collective-permute-done | bytes 262176 | tf_op jit(solution)/shard_map/ppermute | solution.py:223
  190.1 21.7 %collective-permute-done.24 = bf16[128,2048]{1,0:T(8,128)(2,1)S(1)} collective-permute-done((bf16[128,2048]{1,0:T(8,128)(2,1)S(1)}, bf16[128,2048]{1,0:T(8,128)(2,1)S(1)}, u32[]{:S(2)}, u32[]{:S(2)}) %collective-permute-start.24) | collective-permute-done | bytes 524320 | tf_op jit(solution)/shard_map/ppermute | solution.py:223
  213.8 9.1 collective-permute-done.63
  225.2 8.1 collective-permute-done.33
  236.4 10.5 collective-permute-done.43
  248.6 9.5 collective-permute-done.14
  260.1 10.1 collective-permute-done.54
  273.8 8.1 collective-permute-done.4
  284.6 9.0 collective-permute-done.5
  305.3 7.6 collective-permute-done.45
  318.8 6.3 collective-permute-done.55
  331.6 16.0 %collective-permute-done.6 = bf16[128,2048]{0,1:T(8,128)(2,1)S(1)} collective-permute-done((bf16[128,2048]{0,1:T(8,128)(2,1)S(1)}, bf16[128,2048]{0,1:T(8,128)(2,1)S(1)}, u32[]{:S(2)}, u32[]{:S(2)}) %collective-permute-start.6) | collective-permute-done | bytes 524320 | tf_op jit(solution)/shard_map/ppermute | solution.py:223
  361.1 17.6 %collective-permute-done.64 = bf16[128,4096]{1,0:T(8,128)(2,1)S(1)} collective-permute-done((bf16[128,4096]{1,0:T(8,128)(2,1)S(1)}, bf16[128,4096]{1,0:T(8,128)(2,1)S(1)}, u32[]{:S(2)}, u32[]{:S(2)}) %collective-permute-start.64) | collective-permute-done | bytes 1048608 | tf_op jit(solution)/shard_map/ppermute | solution.py:223
  383.5 17.8 %collective-permute-done.34 = bf16[128,4096]{0,1:T(8,128)(2,1)S(1)} collective-permute-done((bf16[128,4096]{0,1:T(8,128)(2,1)S(1)}, bf16[128,4096]{0,1:T(8,128)(2,1)S(1)}, u32[]{:S(2)}, u32[]{:S(2)}) %collective-permute-start.34) | collective-permute-done | bytes 1048608 | tf_op jit(solution)/shard_map/ppermute | solution.py:223
  408.1 15.6 %collective-permute-done.73 = bf16[128,4096]{0,1:T(8,128)(2,1)S(1)} collective-permute-done((bf16[128,4096]{0,1:T(8,128)(2,1)S(1)}, bf16[128,4096]{0,1:T(8,128)(2,1)S(1)}, u32[]{:S(2)}, u32[]{:S(2)}) %collective-permute-start.73) | collective-permute-done | bytes 1048608 | tf_op jit(solution)/shard_map/ppermute | solution.py:223
  430.7 5.0 convolution_convert_fusion.9
  444.3 8.4 collective-permute-done.27
  460.2 19.6 %collective-permute-done.66 = bf16[128,4096]{1,0:T(8,128)(2,1)S(1)} collective-permute-done((bf16[128,4096]{1,0:T(8,128)(2,1)S(1)}, bf16[128,4096]{1,0:T(8,128)(2,1)S(1)}, u32[]{:S(2)}, u32[]{:S(2)}) %collective-permute-start.66) | collective-permute-done | bytes 1048608 | tf_op jit(solution)/shard_map/ppermute | solution.py:223
  486.6 19.9 %collective-permute-done.36 = bf16[128,4096]{0,1:T(8,128)(2,1)S(1)} collective-permute-done((bf16[128,4096]{0,1:T(8,128)(2,1)S(1)}, bf16[128,4096]{0,1:T(8,128)(2,1)S(1)}, u32[]{:S(2)}, u32[]{:S(2)}) %collective-permute-start.36) | collective-permute-done | bytes 1048608 | tf_op jit(solution)/shard_map/ppermute | solution.py:223
  514.5 9.3 shard_map.442.o_ref
  523.9 9.9 collective-permute-done.75
  541.2 12.0 multiply_convert_fusion.1
  554.4 7.7 fusion.170
  573.1 9.3 shard_map.443.o_ref
  588.5 10.5 fusion.172
  599.0 14.9 %convert_reduce_fusion = (f32[4096]{0:T(1024)S(1)}, bf16[512,4096]{1,0:T(8,128)(2,1)S(1)}, bf16[512,4096]{1,0:T(8,128)(2,1)}) fusion(f32[512,4096]{1,0:T(8,128)} %fusion.172, f32[4096]{0:T(1024)S(1)} %bitcast.422, bf16[512,1024]{1,0:T(8,128)(2,1)S(1)} %get-tuple-element.154, bf16[1024,4096]{0,1:T(8,128)(2,1)} %copy-done.122), kind=kOutput, calls=%fused_computation.23 | convolution fusion | flops 4347392000 | bytes 26247168 | tf_op jit(solution)/shard_map/dot_general | solution.py:55
  613.9 9.4 multiply_reduce_fusion
  629.5 4.5 convolution_convert_fusion.4
  636.4 8.2 add_add_fusion.7
  648.5 4.3 convolution_convert_fusion
  658.4 14.6 %shard_map.444 = (bf16[1024,1024]{1,0:T(8,128)(2,1)S(1)}, bf16[1024,512]{1,0:T(8,128)(2,1)S(1)}) custom-call(f32[4]{0:T(128)S(1)} %and_select_fusion.slope_ref, s32[1024,1]{1,0:T(8,128)S(1)} %copy-done.12, s32[1,1024]{1,0:T(1,128)S(1)} %broadcast_select_fusion.28.drow_ref, bf16[1024,1024]{1,0:T(8,128)(2,1)S(1)} %copy-done.3, ...), custom_call_target="tpu_custom_call" | custom-call | flops 5368709120 | bytes 10485760 | tf_op jit(solution)/shard_map/pallas_call | solution.py:177
  706.6 14.4 %convert_reduce_fusion.1 = (f32[4096]{0:T(1024)S(1)}, bf16[512,4096]{1,0:T(8,128)(2,1)S(1)}) fusion(f32[512,4096]{1,0:T(8,128)} %get-tuple-element.301, f32[4096]{0:T(1024)S(1)} %bitcast.421, bf16[512,1024]{1,0:T(8,128)(2,1)S(1)} %convert_element_type.697, bf16[1024,4096]{0,1:T(8,128)(2,1)} %constant_dynamic-update-slice_fusion.40), kind=kOutput, calls=%fused_computation.24 | convolution fusion | flops 4343197696 | bytes 22052864 | tf_op jit(solution)/shard_map/dot_general | solution.py:55
  721.1 9.9 multiply_reduce_fusion.2
  731.0 4.4 convolution_convert_fusion.6
  735.5 4.5 convolution_convert_fusion.2
  753.1 4.1 collective-permute-done.117
  771.8 14.6 %shard_map.445 = (bf16[1024,1024]{1,0:T(8,128)(2,1)S(1)}, bf16[1024,512]{1,0:T(8,128)(2,1)S(1)}) custom-call(f32[4]{0:T(128)S(1)} %and_select_fusion.slope_ref, s32[1024,1]{1,0:T(8,128)S(1)} %copy-done.13, s32[1,1024]{1,0:T(1,128)S(1)} %broadcast_select_fusion.28.drow_ref, bf16[1024,1024]{1,0:T(8,128)(2,1)S(1)} %copy-done.1, ...), custom_call_target="tpu_custom_call" | custom-call | flops 5368709120 | bytes 10485760 | tf_op jit(solution)/shard_map/pallas_call | solution.py:177
  801.7 3.8 collective-permute-done.106
  807.4 6.6 collective-permute-done.107
  823.0 5.6 fusion.125
  845.4 6.8 collective-permute-done.112
  875.6 5.9 add_convert_fusion
  884.0 4.3 collective-permute-done.95
  890.0 4.6 add_convert_fusion.2
  894.7 23.1 %collective-permute-done.96 = bf16[128,1024]{0,1:T(8,128)(2,1)S(1)} collective-permute-done((bf16[128,1024]{0,1:T(8,128)(2,1)S(1)}, bf16[128,1024]{0,1:T(8,128)(2,1)S(1)}, u32[]{:S(2)}, u32[]{:S(2)}) %collective-permute-start.96) | collective-permute-done | bytes 262176 | tf_op jit(solution)/shard_map/ppermute | solution.py:223
  931.1 4.3 copy.142
  948.3 9.3 collective-permute-done.102
  963.7 5.9 add_convert_fusion.1
  971.1 4.1 copy.140
  978.7 5.9 add_convert_fusion.3
  988.9 19.1 %collective-permute-done.90 = bf16[2,128,2048]{1,2,0:T(8,128)(2,1)} collective-permute-done((bf16[2,128,2048]{1,2,0:T(8,128)(2,1)}, bf16[2,128,2048]{1,2,0:T(8,128)(2,1)}, u32[]{:S(2)}, u32[]{:S(2)}) %collective-permute-start.90) | collective-permute-done | bytes 1048608 | tf_op jit(solution)/shard_map/ppermute | solution.py:223
  1014.6 29.3 %collective-permute-done.91 = bf16[128,2048]{0,1:T(8,128)(2,1)S(1)} collective-permute-done((bf16[128,2048]{0,1:T(8,128)(2,1)S(1)}, bf16[128,2048]{0,1:T(8,128)(2,1)S(1)}, u32[]{:S(2)}, u32[]{:S(2)}) %collective-permute-start.91) | collective-permute-done | bytes 524320 | tf_op jit(solution)/shard_map/ppermute | solution.py:223
  1048.5 9.6 collective-permute-done.92
  1069.0 14.0 %collective-permute-done.136 = bf16[128,4096]{0,1:T(8,128)(2,1)} collective-permute-done((bf16[128,4096]{0,1:T(8,128)(2,1)}, bf16[128,4096]{0,1:T(8,128)(2,1)}, u32[]{:S(2)}, u32[]{:S(2)}) %collective-permute-start.136) | collective-permute-done | bytes 1048608 | tf_op jit(solution)/shard_map/ppermute | solution.py:223
  1087.9 15.5 %collective-permute-done.127 = bf16[128,2048]{1,0:T(8,128)(2,1)S(1)} collective-permute-done((bf16[128,2048]{1,0:T(8,128)(2,1)S(1)}, bf16[128,2048]{1,0:T(8,128)(2,1)S(1)}, u32[]{:S(2)}, u32[]{:S(2)}) %collective-permute-start.127) | collective-permute-done | bytes 524320 | tf_op jit(solution)/shard_map/ppermute | solution.py:223
  1110.3 4.3 collective-permute-done.137
  1115.3 14.7 %collective-permute-done.121 = bf16[128,4096]{1,0:T(8,128)(2,1)S(1)} collective-permute-done((bf16[128,4096]{1,0:T(8,128)(2,1)S(1)}, bf16[128,4096]{1,0:T(8,128)(2,1)S(1)}, u32[]{:S(2)}, u32[]{:S(2)}) %collective-permute-start.121) | collective-permute-done | bytes 1048608 | tf_op jit(solution)/shard_map/ppermute | solution.py:223
  1138.0 30.3 %collective-permute-done.122 = bf16[128,2048]{1,0:T(8,128)(2,1)S(1)} collective-permute-done((bf16[128,2048]{1,0:T(8,128)(2,1)S(1)}, bf16[128,2048]{1,0:T(8,128)(2,1)S(1)}, u32[]{:S(2)}, u32[]{:S(2)}) %collective-permute-start.122) | collective-permute-done | bytes 524320 | tf_op jit(solution)/shard_map/ppermute | solution.py:223
  1168.5 11.0 collective-permute-done.132
  1180.6 4.6 collective-permute-done.123
  1193.9 39.8 %all-reduce.2 = (f32[]{:T(128)}, f32[1,9,1024]{2,1,0:T(8,128)S(1)}, f32[1,9,1024]{2,1,0:T(8,128)S(1)}) all-reduce(f32[]{:T(128)S(6)} %add.844, f32[1,9,1024]{2,1,0:T(8,128)S(1)} %copy-done.120, f32[1,9,1024]{2,1,0:T(8,128)S(1)} %copy-done.121), channel_id=1, replica_groups=mesh['dp'=8,'mp'=4] {'dp','mp'}, use_global_device_ids=true, to_apply=%region_24.25 | all-reduce | flops 18433 | bytes 147464 | tf_op jit(solution)/shard_map/psum | solution.py:468
  (1015 shorter events, 438.5 us)
Async XLA Ops:
  0.7 79.4 %collective-permute-start.1 = (s32[2,1024]{1,0:T(2,128)}, s32[2,1024]{1,0:T(2,128)S(1)}, u32[]{:S(2)}, u32[]{:S(2)}) collective-permute-start(s32[2,1024]{1,0:T(2,128)} %param.30), channel_id=1, source_target_pairs={{0,4},{4,0},{8,12},{12,8},{16,20},{20,16},{24,28},{28,24},{1,5},{5... | collective-permute-start | bytes 24584 | tf_op jit(solution)/shard_map/ppermute | solution.py:223
  2.2 95.7 %collective-permute-start.62 = (bf16[128,1024]{1,0:T(8,128)(2,1)S(1)}, bf16[128,1024]{1,0:T(8,128)(2,1)S(1)}, u32[]{:S(2)}, u32[]{:S(2)}) collective-permute-start(bf16[128,1024]{1,0:T(8,128)(2,1)S(1)} %get-tuple-element.228), channel_id=1, source_target_pairs={{0,1},{1,0},{2,3},{3,2},{4,5},{5,4},{6,7},{7,6},{8,9},{9,8},{10,11... | collective-permute-start | bytes 786440 | tf_op jit(solution)/shard_map/ppermute | solution.py:223
  5.0 89.9 %collective-permute-start.23 = (bf16[128,1024]{1,0:T(8,128)(2,1)S(1)}, bf16[128,1024]{1,0:T(8,128)(2,1)}, u32[]{:S(2)}, u32[]{:S(2)}) collective-permute-start(bf16[128,1024]{1,0:T(8,128)(2,1)S(1)} %get-tuple-element.229), channel_id=1, source_target_pairs={{0,1},{1,0},{2,3},{3,2},{4,5},{5,4},{6,7},{7,6},{8,9},{9,8},{10,11... | collective-permute-start | bytes 786440 | tf_op jit(solution)/shard_map/ppermute | solution.py:223
  5.2 95.3 %collective-permute-start.71 = (bf16[128,1024]{0,1:T(8,128)(2,1)S(1)}, bf16[128,1024]{0,1:T(8,128)(2,1)S(1)}, u32[]{:S(2)}, u32[]{:S(2)}) collective-permute-start(bf16[128,1024]{0,1:T(8,128)(2,1)S(1)} %get-tuple-element.226), channel_id=1, source_target_pairs={{0,1},{1,0},{2,3},{3,2},{4,5},{5,4},{6,7},{7,6},{8,9},{9,8},{10,11... | collective-permute-start | bytes 786440 | tf_op jit(solution)/shard_map/ppermute | solution.py:223
  8.2 72.1 %collective-permute-start.41 = (bf16[128,512]{0,1:T(8,128)(2,1)S(1)}, bf16[128,512]{0,1:T(8,128)(2,1)}, u32[]{:S(2)}, u32[]{:S(2)}) collective-permute-start(bf16[128,512]{0,1:T(8,128)(2,1)S(1)} %bitcast.348), channel_id=1, source_target_pairs={{0,1},{1,0},{2,3},{3,2},{4,5},{5,4},{6,7},{7,6},{8,9},{9,8},{10,11... | collective-permute-start | bytes 393224 | tf_op jit(solution)/shard_map/ppermute | solution.py:223
  89.5 208.3 %collective-permute-start = (bf16[512,1024]{1,0:T(8,128)(2,1)S(1)}, bf16[512,1024]{1,0:T(8,128)(2,1)S(1)}, u32[]{:S(2)}, u32[]{:S(2)}) collective-permute-start(bf16[512,1024]{1,0:T(8,128)(2,1)S(1)} %copy-done.75), channel_id=1, source_target_pairs={{1,4},{3,6},{4,1},{6,3},{9,12},{11,14},{12,9},{14,11},{17,20},{19,... | collective-permute-start | bytes 3145736 | tf_op jit(solution)/shard_map/ppermute | solution.py:286
  94.8 204.7 %collective-permute-start.81 = (bf16[512,1024]{1,0:T(8,128)(2,1)S(1)}, bf16[512,1024]{1,0:T(8,128)(2,1)S(1)}, u32[]{:S(2)}, u32[]{:S(2)}) collective-permute-start(bf16[512,1024]{1,0:T(8,128)(2,1)S(1)} %copy-done.76), channel_id=1, source_target_pairs={{1,4},{3,6},{4,1},{6,3},{9,12},{11,14},{12,9},{14,11},{17,20},{19,... | collective-permute-start | bytes 3145736 | tf_op jit(solution)/shard_map/ppermute | solution.py:286
  98.0 44.6 %collective-permute-start.13 = (bf16[128,1024]{0,1:T(8,128)(2,1)S(1)}, bf16[128,1024]{0,1:T(8,128)(2,1)S(1)}, u32[]{:S(2)}, u32[]{:S(2)}) collective-permute-start(bf16[128,1024]{0,1:T(8,128)(2,1)S(1)} %pad_maximum_fusion.45), channel_id=1, source_target_pairs={{0,2},{1,3},{2,0},{3,1},{4,6},{5,7},{6,4},{7,5},{8,10},{9,11},{10,... | collective-permute-start | bytes 786440 | tf_op jit(solution)/shard_map/ppermute | solution.py:223
  98.1 41.3 %collective-permute-start.52 = (bf16[128,1024]{0,1:T(8,128)(2,1)S(1)}, bf16[128,1024]{0,1:T(8,128)(2,1)S(1)}, u32[]{:S(2)}, u32[]{:S(2)}) collective-permute-start(bf16[128,1024]{0,1:T(8,128)(2,1)S(1)} %pad_maximum_fusion.47), channel_id=1, source_target_pairs={{0,2},{1,3},{2,0},{3,1},{4,6},{5,7},{6,4},{7,5},{8,10},{9,11},{10,... | collective-permute-start | bytes 786440 | tf_op jit(solution)/shard_map/ppermute | solution.py:223
  100.6 84.4 %collective-permute-start.3 = (bf16[128,1024]{0,1:T(8,128)(2,1)S(1)}, bf16[128,1024]{0,1:T(8,128)(2,1)S(1)}, u32[]{:S(2)}, u32[]{:S(2)}) collective-permute-start(bf16[128,1024]{0,1:T(8,128)(2,1)S(1)} %pad_maximum_fusion.44), channel_id=1, source_target_pairs={{0,2},{1,3},{2,0},{3,1},{4,6},{5,7},{6,4},{7,5},{8,10},{9,11},{10,... | collective-permute-start | bytes 786440 | tf_op jit(solution)/shard_map/ppermute | solution.py:223
  139.4 44.3 %collective-permute-start.42 = (bf16[128,1024]{0,1:T(8,128)(2,1)S(1)}, bf16[128,1024]{0,1:T(8,128)(2,1)S(1)}, u32[]{:S(2)}, u32[]{:S(2)}) collective-permute-start(bf16[128,1024]{0,1:T(8,128)(2,1)S(1)} %pad_maximum_fusion.46), channel_id=1, source_target_pairs={{0,2},{1,3},{2,0},{3,1},{4,6},{5,7},{6,4},{7,5},{8,10},{9,11},{10,... | collective-permute-start | bytes 786440 | tf_op jit(solution)/shard_map/ppermute | solution.py:223
  142.6 92.4 %collective-permute-start.72 = (bf16[128,2048]{0,1:T(8,128)(2,1)S(1)}, bf16[128,2048]{0,1:T(8,128)(2,1)S(1)}, u32[]{:S(2)}, u32[]{:S(2)}) collective-permute-start(bf16[128,2048]{0,1:T(8,128)(2,1)S(1)} %pad_maximum_fusion.29), channel_id=1, source_target_pairs={{0,2},{1,3},{2,0},{3,1},{4,6},{5,7},{6,4},{7,5},{8,10},{9,11},{10,... | collective-permute-start | bytes 1572872 | tf_op jit(solution)/shard_map/ppermute | solution.py:223
  183.7 28.1 %collective-permute-start.24 = (bf16[128,2048]{1,0:T(8,128)(2,1)S(1)}, bf16[128,2048]{1,0:T(8,128)(2,1)S(1)}, u32[]{:S(2)}, u32[]{:S(2)}) collective-permute-start(bf16[128,2048]{1,0:T(8,128)(2,1)S(1)} %pad_maximum_fusion.24), channel_id=1, source_target_pairs={{0,2},{1,3},{2,0},{3,1},{4,6},{5,7},{6,4},{7,5},{8,10},{9,11},{10,... | collective-permute-start | bytes 1572872 | tf_op jit(solution)/shard_map/ppermute | solution.py:223
  185.0 38.0 %collective-permute-start.63 = (bf16[128,2048]{1,0:T(8,128)(2,1)S(1)}, bf16[128,2048]{1,0:T(8,128)(2,1)S(1)}, u32[]{:S(2)}, u32[]{:S(2)}) collective-permute-start(bf16[128,2048]{1,0:T(8,128)(2,1)S(1)} %pad_maximum_fusion.28), channel_id=1, source_target_pairs={{0,2},{1,3},{2,0},{3,1},{4,6},{5,7},{6,4},{7,5},{8,10},{9,11},{10,... | collective-permute-start | bytes 1572872 | tf_op jit(solution)/shard_map/ppermute | solution.py:223
  270.2 26.9 %collective-permute-start.56 = (bf16[128,2048]{0,1:T(8,128)(2,1)S(1)}, bf16[128,2048]{0,1:T(8,128)(2,1)S(1)}, u32[]{:S(2)}, u32[]{:S(2)}) collective-permute-start(bf16[128,2048]{0,1:T(8,128)(2,1)S(1)} %pad_maximum_fusion.27), channel_id=1, source_target_pairs={{0,4},{4,0},{8,12},{12,8},{16,20},{20,16},{24,28},{28,24},{1,5},{5... | collective-permute-start | bytes 1572872 | tf_op jit(solution)/shard_map/ppermute | solution.py:223
  297.1 56.0 %collective-permute-start.7 = (bf16[128,2048]{0,1:T(8,128)(2,1)S(1)}, bf16[128,2048]{0,1:T(8,128)(2,1)S(1)}, u32[]{:S(2)}, u32[]{:S(2)}) collective-permute-start(bf16[128,2048]{0,1:T(8,128)(2,1)S(1)} %get-tuple-element.264), channel_id=1, source_target_pairs={{0,4},{4,0},{8,12},{12,8},{16,20},{20,16},{24,28},{28,24},{1,5},{5... | collective-permute-start | bytes 1572872 | tf_op jit(solution)/shard_map/ppermute | solution.py:223
  312.9 46.8 %collective-permute-start.26 = (bf16[128,4096]{1,0:T(8,128)(2,1)S(1)}, bf16[128,4096]{1,0:T(8,128)(2,1)S(1)}, u32[]{:S(2)}, u32[]{:S(2)}) collective-permute-start(bf16[128,4096]{1,0:T(8,128)(2,1)S(1)} %get-tuple-element.220), channel_id=1, source_target_pairs={{0,16},{4,20},{8,24},{12,28},{16,0},{20,4},{24,8},{28,12},{1,17},{... | collective-permute-start | bytes 3145736 | tf_op jit(solution)/shard_map/ppermute | solution.py:223
  329.7 27.8 %collective-permute-start.25 = (bf16[128,4096]{1,0:T(8,128)(2,1)S(1)}, bf16[128,4096]{1,0:T(8,128)(2,1)S(1)}, u32[]{:S(2)}, u32[]{:S(2)}) collective-permute-start(bf16[128,4096]{1,0:T(8,128)(2,1)S(1)} %get-tuple-element.220), channel_id=1, source_target_pairs={{0,8},{4,12},{8,0},{12,4},{16,24},{20,28},{24,16},{28,20},{1,9},{5... | collective-permute-start | bytes 3145736 | tf_op jit(solution)/shard_map/ppermute | solution.py:223
  353.1 101.9 %collective-permute-start.28 = (bf16[128,4096]{1,0:T(8,128)(2,1)S(1)}, bf16[128,4096]{1,0:T(8,128)(2,1)S(1)}, u32[]{:S(2)}, u32[]{:S(2)}) collective-permute-start(bf16[128,4096]{1,0:T(8,128)(2,1)S(1)} %get-tuple-element.220), channel_id=1, source_target_pairs={{0,4},{4,0},{8,12},{12,8},{16,20},{20,16},{24,28},{28,24},{1,5},{5... | collective-permute-start | bytes 3145736 | tf_op jit(solution)/shard_map/ppermute | solution.py:223
  354.0 27.3 %collective-permute-start.65 = (bf16[128,4096]{1,0:T(8,128)(2,1)S(1)}, bf16[128,4096]{1,0:T(8,128)(2,1)S(1)}, u32[]{:S(2)}, u32[]{:S(2)}) collective-permute-start(bf16[128,4096]{1,0:T(8,128)(2,1)S(1)} %get-tuple-element.216), channel_id=1, source_target_pairs={{0,16},{4,20},{8,24},{12,28},{16,0},{20,4},{24,8},{28,12},{1,17},{... | collective-permute-start | bytes 3145736 | tf_op jit(solution)/shard_map/ppermute | solution.py:223
  357.6 124.2 %collective-permute-start.67 = (bf16[128,4096]{1,0:T(8,128)(2,1)S(1)}, bf16[128,4096]{1,0:T(8,128)(2,1)S(1)}, u32[]{:S(2)}, u32[]{:S(2)}) collective-permute-start(bf16[128,4096]{1,0:T(8,128)(2,1)S(1)} %get-tuple-element.216), channel_id=1, source_target_pairs={{0,4},{4,0},{8,12},{12,8},{16,20},{20,16},{24,28},{28,24},{1,5},{5... | collective-permute-start | bytes 3145736 | tf_op jit(solution)/shard_map/ppermute | solution.py:223
  359.7 41.6 %collective-permute-start.34 = (bf16[128,4096]{0,1:T(8,128)(2,1)S(1)}, bf16[128,4096]{0,1:T(8,128)(2,1)S(1)}, u32[]{:S(2)}, u32[]{:S(2)}) collective-permute-start(bf16[128,4096]{0,1:T(8,128)(2,1)S(1)} %get-tuple-element.218), channel_id=1, source_target_pairs={{0,8},{4,12},{8,0},{12,4},{16,24},{20,28},{24,16},{28,20},{1,9},{5... | collective-permute-start | bytes 3145736 | tf_op jit(solution)/shard_map/ppermute | solution.py:223
  378.8 25.0 %collective-permute-start.35 = (bf16[128,4096]{0,1:T(8,128)(2,1)S(1)}, bf16[128,4096]{0,1:T(8,128)(2,1)S(1)}, u32[]{:S(2)}, u32[]{:S(2)}) collective-permute-start(bf16[128,4096]{0,1:T(8,128)(2,1)S(1)} %get-tuple-element.218), channel_id=1, source_target_pairs={{0,16},{4,20},{8,24},{12,28},{16,0},{20,4},{24,8},{28,12},{1,17},{... | collective-permute-start | bytes 3145736 | tf_op jit(solution)/shard_map/ppermute | solution.py:223
  381.3 42.4 %collective-permute-start.73 = (bf16[128,4096]{0,1:T(8,128)(2,1)S(1)}, bf16[128,4096]{0,1:T(8,128)(2,1)S(1)}, u32[]{:S(2)}, u32[]{:S(2)}) collective-permute-start(bf16[128,4096]{0,1:T(8,128)(2,1)S(1)} %get-tuple-element.214), channel_id=1, source_target_pairs={{0,8},{4,12},{8,0},{12,4},{16,24},{20,28},{24,16},{28,20},{1,9},{5... | collective-permute-start | bytes 3145736 | tf_op jit(solution)/shard_map/ppermute | solution.py:223
  403.8 35.7 %collective-permute-start.59 = (bf16[128,2048]{0,1:T(8,128)(2,1)S(1)}, bf16[128,2048]{0,1:T(8,128)(2,1)S(1)}, u32[]{:S(2)}, u32[]{:S(2)}) collective-permute-start(bf16[128,2048]{0,1:T(8,128)(2,1)S(1)} %collective-permute-done.55), channel_id=1, source_target_pairs={{0,4},{4,0},{8,12},{12,8},{16,20},{20,16},{24,28},{28,24},{1,5},{5... | collective-permute-start | bytes 1572872 | tf_op jit(solution)/shard_map/ppermute | solution.py:223
  441.7 66.8 %collective-permute-start.37 = (bf16[128,4096]{0,1:T(8,128)(2,1)S(1)}, bf16[128,4096]{0,1:T(8,128)(2,1)S(1)}, u32[]{:S(2)}, u32[]{:S(2)}) collective-permute-start(bf16[128,4096]{0,1:T(8,128)(2,1)S(1)} %get-tuple-element.218), channel_id=1, source_target_pairs={{0,4},{4,0},{8,12},{12,8},{16,20},{20,16},{24,28},{28,24},{1,5},{5... | collective-permute-start | bytes 3145736 | tf_op jit(solution)/shard_map/ppermute | solution.py:223
  455.0 24.8 %collective-permute-start.66 = (bf16[128,4096]{1,0:T(8,128)(2,1)S(1)}, bf16[128,4096]{1,0:T(8,128)(2,1)S(1)}, u32[]{:S(2)}, u32[]{:S(2)}) collective-permute-start(bf16[128,4096]{1,0:T(8,128)(2,1)S(1)} %collective-permute-done.64), channel_id=1, source_target_pairs={{0,16},{4,20},{8,24},{12,28},{16,0},{20,4},{24,8},{28,12},{1,17},{... | collective-permute-start | bytes 3145736 | tf_op jit(solution)/shard_map/ppermute | solution.py:223
  457.6 78.0 %collective-permute-start.76 = (bf16[128,4096]{0,1:T(8,128)(2,1)S(1)}, bf16[128,4096]{0,1:T(8,128)(2,1)S(1)}, u32[]{:S(2)}, u32[]{:S(2)}) collective-permute-start(bf16[128,4096]{0,1:T(8,128)(2,1)S(1)} %get-tuple-element.214), channel_id=1, source_target_pairs={{0,4},{4,0},{8,12},{12,8},{16,20},{20,16},{24,28},{28,24},{1,5},{5... | collective-permute-start | bytes 3145736 | tf_op jit(solution)/shard_map/ppermute | solution.py:223
  458.9 25.0 %collective-permute-start.68 = (bf16[128,4096]{1,0:T(8,128)(2,1)S(1)}, bf16[128,4096]{1,0:T(8,128)(2,1)S(1)}, u32[]{:S(2)}, u32[]{:S(2)}) collective-permute-start(bf16[128,4096]{1,0:T(8,128)(2,1)S(1)} %collective-permute-done.64), channel_id=1, source_target_pairs={{0,4},{4,0},{8,12},{12,8},{16,20},{20,16},{24,28},{28,24},{1,5},{5... | collective-permute-start | bytes 3145736 | tf_op jit(solution)/shard_map/ppermute | solution.py:223
  484.0 27.8 %collective-permute-start.39 = (bf16[128,4096]{0,1:T(8,128)(2,1)S(1)}, bf16[128,4096]{0,1:T(8,128)(2,1)S(1)}, u32[]{:S(2)}, u32[]{:S(2)}) collective-permute-start(bf16[128,4096]{0,1:T(8,128)(2,1)S(1)} %collective-permute-done.35), channel_id=1, source_target_pairs={{0,4},{4,0},{8,12},{12,8},{16,20},{20,16},{24,28},{28,24},{1,5},{5... | collective-permute-start | bytes 3145736 | tf_op jit(solution)/shard_map/ppermute | solution.py:223
  506.5 63.6 %collective-permute-start.78 = (bf16[128,4096]{0,1:T(8,128)(2,1)S(1)}, bf16[128,4096]{0,1:T(8,128)(2,1)S(1)}, u32[]{:S(2)}, u32[]{:S(2)}) collective-permute-start(bf16[128,4096]{0,1:T(8,128)(2,1)S(1)} %collective-permute-done.74), channel_id=1, source_target_pairs={{0,4},{4,0},{8,12},{12,8},{16,20},{20,16},{24,28},{28,24},{1,5},{5... | collective-permute-start | bytes 3145736 | tf_op jit(solution)/shard_map/ppermute | solution.py:223
  511.8 57.8 %collective-permute-start.77 = (bf16[128,4096]{0,1:T(8,128)(2,1)S(1)}, bf16[128,4096]{0,1:T(8,128)(2,1)S(1)}, u32[]{:S(2)}, u32[]{:S(2)}) collective-permute-start(bf16[128,4096]{0,1:T(8,128)(2,1)S(1)} %collective-permute-done.73), channel_id=1, source_target_pairs={{0,4},{4,0},{8,12},{12,8},{16,20},{20,16},{24,28},{28,24},{1,5},{5... | collective-permute-start | bytes 3145736 | tf_op jit(solution)/shard_map/ppermute | solution.py:223
  513.7 26.2 %collective-permute-start.31 = (bf16[128,4096]{1,0:T(8,128)(2,1)S(1)}, bf16[128,4096]{1,0:T(8,128)(2,1)S(1)}, u32[]{:S(2)}, u32[]{:S(2)}) collective-permute-start(bf16[128,4096]{1,0:T(8,128)(2,1)S(1)} %collective-permute-done.27), channel_id=1, source_target_pairs={{0,4},{4,0},{8,12},{12,8},{16,20},{20,16},{24,28},{28,24},{1,5},{5... | collective-permute-start | bytes 3145736 | tf_op jit(solution)/shard_map/ppermute | solution.py:223
  535.5 47.2 %collective-permute-start.70 = (bf16[128,4096]{1,0:T(8,128)(2,1)S(1)}, bf16[128,4096]{1,0:T(8,128)(2,1)S(1)}, u32[]{:S(2)}, u32[]{:S(2)}) collective-permute-start(bf16[128,4096]{1,0:T(8,128)(2,1)S(1)} %collective-permute-done.66), channel_id=1, source_target_pairs={{0,4},{4,0},{8,12},{12,8},{16,20},{20,16},{24,28},{28,24},{1,5},{5... | collective-permute-start | bytes 3145736 | tf_op jit(solution)/shard_map/ppermute | solution.py:223
  539.9 43.9 %collective-permute-start.79 = (bf16[128,4096]{0,1:T(8,128)(2,1)S(1)}, bf16[128,4096]{0,1:T(8,128)(2,1)S(1)}, u32[]{:S(2)}, u32[]{:S(2)}) collective-permute-start(bf16[128,4096]{0,1:T(8,128)(2,1)S(1)} %collective-permute-done.75), channel_id=1, source_target_pairs={{0,4},{4,0},{8,12},{12,8},{16,20},{20,16},{24,28},{28,24},{1,5},{5... | collective-permute-start | bytes 3145736 | tf_op jit(solution)/shard_map/ppermute | solution.py:223
  636.2 38.1 %collective-permute-start.114 = (bf16[512,1024]{1,0:T(8,128)(2,1)}, bf16[512,1024]{1,0:T(8,128)(2,1)}, u32[]{:S(2)}, u32[]{:S(2)}) collective-permute-start(bf16[512,1024]{1,0:T(8,128)(2,1)} %convolution_convert_fusion.18), channel_id=1, source_target_pairs={{0,4},{4,0},{8,12},{12,8},{16,20},{20,16},{24,28},{28,24},{1,5},{5... | collective-permute-start | bytes 3145736 | tf_op jit(solution)/shard_map/ppermute | solution.py:223
  646.2 44.3 %collective-permute-start.80 = (bf16[512,1024]{1,0:T(8,128)(2,1)}, bf16[512,1024]{1,0:T(8,128)(2,1)}, u32[]{:S(2)}, u32[]{:S(2)}) collective-permute-start(bf16[512,1024]{1,0:T(8,128)(2,1)} %convert_element_type.691), channel_id=1, source_target_pairs={{1,4},{3,6},{4,1},{6,3},{9,12},{11,14},{12,9},{14,11},{17,20},{19,... | collective-permute-start | bytes 3145736 | tf_op jit(solution)/shard_map/ppermute | solution.py:396
  648.3 240.5 %collective-permute-start.124 = (bf16[512,4096]{1,0:T(8,128)(2,1)}, bf16[512,4096]{1,0:T(8,128)(2,1)}, u32[]{:S(2)}, u32[]{:S(2)}) collective-permute-start(bf16[512,4096]{1,0:T(8,128)(2,1)} %convolution_convert_fusion.4), channel_id=1, source_target_pairs={{0,4},{4,0},{8,12},{12,8},{16,20},{20,16},{24,28},{28,24},{1,5},{5... | collective-permute-start | bytes 12582920 | tf_op jit(solution)/shard_map/ppermute | solution.py:223
  652.8 221.8 %collective-permute-start.134 = (bf16[512,4096]{1,0:T(8,128)(2,1)}, bf16[512,4096]{1,0:T(8,128)(2,1)}, u32[]{:S(2)}, u32[]{:S(2)}) collective-permute-start(bf16[512,4096]{1,0:T(8,128)(2,1)} %convolution_convert_fusion), channel_id=1, source_target_pairs={{0,4},{4,0},{8,12},{12,8},{16,20},{20,16},{24,28},{28,24},{1,5},{5... | collective-permute-start | bytes 12582920 | tf_op jit(solution)/shard_map/ppermute | solution.py:223
  678.3 61.7 %collective-permute-start.115 = (bf16[2,128,1024]{1,2,0:T(8,128)(2,1)}, bf16[2,128,1024]{1,2,0:T(8,128)(2,1)}, u32[]{:S(2)}, u32[]{:S(2)}) collective-permute-start(bf16[2,128,1024]{1,2,0:T(8,128)(2,1)} %copy.134), channel_id=1, source_target_pairs={{0,16},{4,20},{8,24},{12,28},{16,0},{20,4},{24,8},{28,12},{1,17},{... | collective-permute-start | bytes 1572872 | tf_op jit(solution)/shard_map/ppermute | solution.py:223
  690.4 74.2 %collective-permute-start.104 = (bf16[512,1024]{1,0:T(8,128)(2,1)}, bf16[512,1024]{1,0:T(8,128)(2,1)}, u32[]{:S(2)}, u32[]{:S(2)}) collective-permute-start(bf16[512,1024]{1,0:T(8,128)(2,1)} %convolution_convert_fusion.22), channel_id=1, source_target_pairs={{0,4},{4,0},{8,12},{12,8},{16,20},{20,16},{24,28},{28,24},{1,5},{5... | collective-permute-start | bytes 3145736 | tf_op jit(solution)/shard_map/ppermute | solution.py:223
  760.4 28.0 %collective-permute-start.109 = (bf16[512,1024]{1,0:T(8,128)(2,1)}, bf16[512,1024]{1,0:T(8,128)(2,1)}, u32[]{:S(2)}, u32[]{:S(2)}) collective-permute-start(bf16[512,1024]{1,0:T(8,128)(2,1)} %convolution_convert_fusion.20), channel_id=1, source_target_pairs={{0,4},{4,0},{8,12},{12,8},{16,20},{20,16},{24,28},{28,24},{1,5},{5... | collective-permute-start | bytes 3145736 | tf_op jit(solution)/shard_map/ppermute | solution.py:223
  768.5 27.4 %collective-permute-start.105 = (bf16[2,128,1024]{1,2,0:T(8,128)(2,1)}, bf16[2,128,1024]{1,2,0:T(8,128)(2,1)}, u32[]{:S(2)}, u32[]{:S(2)}) collective-permute-start(bf16[2,128,1024]{1,2,0:T(8,128)(2,1)} %copy.130), channel_id=1, source_target_pairs={{0,16},{4,20},{8,24},{12,28},{16,0},{20,4},{24,8},{28,12},{1,17},{... | collective-permute-start | bytes 1572872 | tf_op jit(solution)/shard_map/ppermute | solution.py:223
  788.4 31.5 %collective-permute-start.86 = (bf16[512,1024]{1,0:T(8,128)(2,1)}, bf16[512,1024]{1,0:T(8,128)(2,1)}, u32[]{:S(2)}, u32[]{:S(2)}) collective-permute-start(bf16[512,1024]{1,0:T(8,128)(2,1)} %constant_dynamic-slice_fusion.21), channel_id=1, source_target_pairs={{0,4},{4,0},{8,12},{12,8},{16,20},{20,16},{24,28},{28,24},{1,5},{5... | collective-permute-start | bytes 3145736 | tf_op jit(solution)/shard_map/ppermute | solution.py:223
  817.2 46.3 %collective-permute-start.99 = (bf16[512,2048]{1,0:T(8,128)(2,1)}, bf16[512,2048]{1,0:T(8,128)(2,1)}, u32[]{:S(2)}, u32[]{:S(2)}) collective-permute-start(bf16[512,2048]{1,0:T(8,128)(2,1)} %convolution_convert_fusion.10), channel_id=1, source_target_pairs={{0,4},{4,0},{8,12},{12,8},{16,20},{20,16},{24,28},{28,24},{1,5},{5... | collective-permute-start | bytes 6291464 | tf_op jit(solution)/shard_map/ppermute | solution.py:223
  819.7 39.0 %collective-permute-start.94 = (bf16[512,1024]{1,0:T(8,128)(2,1)}, bf16[512,1024]{1,0:T(8,128)(2,1)}, u32[]{:S(2)}, u32[]{:S(2)}) collective-permute-start(bf16[512,1024]{1,0:T(8,128)(2,1)} %convolution_convert_fusion.24), channel_id=1, source_target_pairs={{0,4},{4,0},{8,12},{12,8},{16,20},{20,16},{24,28},{28,24},{1,5},{5... | collective-permute-start | bytes 3145736 | tf_op jit(solution)/shard_map/ppermute | solution.py:223
  855.4 108.3 %collective-permute-start.129 = (bf16[512,4096]{1,0:T(8,128)(2,1)}, bf16[512,4096]{1,0:T(8,128)(2,1)}, u32[]{:S(2)}, u32[]{:S(2)}) collective-permute-start(bf16[512,4096]{1,0:T(8,128)(2,1)} %convolution_convert_fusion.2), channel_id=1, source_target_pairs={{0,4},{4,0},{8,12},{12,8},{16,20},{20,16},{24,28},{28,24},{1,5},{5... | collective-permute-start | bytes 12582920 | tf_op jit(solution)/shard_map/ppermute | solution.py:223
  858.7 119.9 %collective-permute-start.119 = (bf16[512,4096]{1,0:T(8,128)(2,1)}, bf16[512,4096]{1,0:T(8,128)(2,1)}, u32[]{:S(2)}, u32[]{:S(2)}) collective-permute-start(bf16[512,4096]{1,0:T(8,128)(2,1)} %convolution_convert_fusion.6), channel_id=1, source_target_pairs={{0,4},{4,0},{8,12},{12,8},{16,20},{20,16},{24,28},{28,24},{1,5},{5... | collective-permute-start | bytes 12582920 | tf_op jit(solution)/shard_map/ppermute | solution.py:223
  863.5 63.7 %collective-permute-start.88 = (bf16[512,1024]{1,0:T(8,128)(2,1)}, bf16[512,1024]{1,0:T(8,128)(2,1)}, u32[]{:S(2)}, u32[]{:S(2)}) collective-permute-start(bf16[512,1024]{1,0:T(8,128)(2,1)} %convert_element_type.701), channel_id=1, source_target_pairs={{1,4},{3,6},{4,1},{6,3},{9,12},{11,14},{12,9},{14,11},{17,20},{19,... | collective-permute-start | bytes 3145736 | tf_op jit(solution)/shard_map/ppermute | solution.py:458
  888.3 37.7 %collective-permute-start.100 = (bf16[2,128,2048]{1,2,0:T(8,128)(2,1)S(1)}, bf16[2,128,2048]{1,2,0:T(8,128)(2,1)S(1)}, u32[]{:S(2)}, u32[]{:S(2)}) collective-permute-start(bf16[2,128,2048]{1,2,0:T(8,128)(2,1)S(1)} %bitcast.351), channel_id=1, source_target_pairs={{0,8},{4,12},{8,0},{12,4},{16,24},{20,28},{24,16},{28,20},{1,9},{5... | collective-permute-start | bytes 3145736 | tf_op jit(solution)/shard_map/ppermute | solution.py:223
  888.8 28.9 %collective-permute-start.96 = (bf16[128,1024]{0,1:T(8,128)(2,1)S(1)}, bf16[128,1024]{0,1:T(8,128)(2,1)S(1)}, u32[]{:S(2)}, u32[]{:S(2)}) collective-permute-start(bf16[128,1024]{0,1:T(8,128)(2,1)S(1)} %slice_bitcast_fusion.22), channel_id=1, source_target_pairs={{0,8},{4,12},{8,0},{12,4},{16,24},{20,28},{24,16},{28,20},{1,9},{5... | collective-permute-start | bytes 786440 | tf_op jit(solution)/shard_map/ppermute | solution.py:223
  938.2 71.8 %collective-permute-start.125 = (bf16[2,128,4096]{2,1,0:T(8,128)(2,1)}, bf16[2,128,4096]{2,1,0:T(8,128)(2,1)}, u32[]{:S(2)}, u32[]{:S(2)}) collective-permute-start(bf16[2,128,4096]{2,1,0:T(8,128)(2,1)} %slice_bitcast_fusion), channel_id=1, source_target_pairs={{0,8},{4,12},{8,0},{12,4},{16,24},{20,28},{24,16},{28,20},{1,9},{5... | collective-permute-start | bytes 6291464 | tf_op jit(solution)/shard_map/ppermute | solution.py:223
  941.0 105.3 %collective-permute-start.135 = (bf16[2,128,4096]{1,2,0:T(8,128)(2,1)}, bf16[2,128,4096]{1,2,0:T(8,128)(2,1)}, u32[]{:S(2)}, u32[]{:S(2)}) collective-permute-start(bf16[2,128,4096]{1,2,0:T(8,128)(2,1)} %copy.142), channel_id=1, source_target_pairs={{0,16},{4,20},{8,24},{12,28},{16,0},{20,4},{24,8},{28,12},{1,17},{... | collective-permute-start | bytes 6291464 | tf_op jit(solution)/shard_map/ppermute | solution.py:223
  961.9 46.0 %collective-permute-start.90 = (bf16[2,128,2048]{1,2,0:T(8,128)(2,1)}, bf16[2,128,2048]{1,2,0:T(8,128)(2,1)}, u32[]{:S(2)}, u32[]{:S(2)}) collective-permute-start(bf16[2,128,2048]{1,2,0:T(8,128)(2,1)} %bitcast.96), channel_id=1, source_target_pairs={{0,8},{4,12},{8,0},{12,4},{16,24},{20,28},{24,16},{28,20},{1,9},{5... | collective-permute-start | bytes 3145736 | tf_op jit(solution)/shard_map/ppermute | solution.py:223
  978.2 129.6 %collective-permute-start.130 = (bf16[2,128,4096]{1,2,0:T(8,128)(2,1)}, bf16[2,128,4096]{1,2,0:T(8,128)(2,1)}, u32[]{:S(2)}, u32[]{:S(2)}) collective-permute-start(bf16[2,128,4096]{1,2,0:T(8,128)(2,1)} %copy.140), channel_id=1, source_target_pairs={{0,16},{4,20},{8,24},{12,28},{16,0},{20,4},{24,8},{28,12},{1,17},{... | collective-permute-start | bytes 6291464 | tf_op jit(solution)/shard_map/ppermute | solution.py:223
  987.7 116.3 %collective-permute-start.120 = (bf16[2,128,4096]{2,1,0:T(8,128)(2,1)}, bf16[2,128,4096]{2,1,0:T(8,128)(2,1)}, u32[]{:S(2)}, u32[]{:S(2)}) collective-permute-start(bf16[2,128,4096]{2,1,0:T(8,128)(2,1)} %slice_bitcast_fusion.2), channel_id=1, source_target_pairs={{0,8},{4,12},{8,0},{12,4},{16,24},{20,28},{24,16},{28,20},{1,9},{5... | collective-permute-start | bytes 6291464 | tf_op jit(solution)/shard_map/ppermute | solution.py:223
  1009.5 34.4 %collective-permute-start.91 = (bf16[128,2048]{0,1:T(8,128)(2,1)S(1)}, bf16[128,2048]{0,1:T(8,128)(2,1)S(1)}, u32[]{:S(2)}, u32[]{:S(2)}) collective-permute-start(bf16[128,2048]{0,1:T(8,128)(2,1)S(1)} %slice_bitcast_fusion.14), channel_id=1, source_target_pairs={{0,16},{4,20},{8,24},{12,28},{16,0},{20,4},{24,8},{28,12},{1,17},{... | collective-permute-start | bytes 1572872 | tf_op jit(solution)/shard_map/ppermute | solution.py:223
  1013.6 52.8 %collective-permute-start.126 = (bf16[128,4096]{1,0:T(8,128)(2,1)}, bf16[128,4096]{1,0:T(8,128)(2,1)S(1)}, u32[]{:S(2)}, u32[]{:S(2)}) collective-permute-start(bf16[128,4096]{1,0:T(8,128)(2,1)} %slice_bitcast_fusion.8), channel_id=1, source_target_pairs={{0,16},{4,20},{8,24},{12,28},{16,0},{20,4},{24,8},{28,12},{1,17},{... | collective-permute-start | bytes 3145736 | tf_op jit(solution)/shard_map/ppermute | solution.py:223
  1066.7 36.7 %collective-permute-start.127 = (bf16[128,2048]{1,0:T(8,128)(2,1)S(1)}, bf16[128,2048]{1,0:T(8,128)(2,1)S(1)}, u32[]{:S(2)}, u32[]{:S(2)}) collective-permute-start(bf16[128,2048]{1,0:T(8,128)(2,1)S(1)} %slice.804), channel_id=1, source_target_pairs={{0,2},{1,3},{2,0},{3,1},{4,6},{5,7},{6,4},{7,5},{8,10},{9,11},{10,... | collective-permute-start | bytes 1572872 | tf_op jit(solution)/shard_map/ppermute | solution.py:223
  1084.7 29.9 %collective-permute-start.137 = (bf16[128,2048]{0,1:T(8,128)(2,1)S(1)}, bf16[128,2048]{0,1:T(8,128)(2,1)S(1)}, u32[]{:S(2)}, u32[]{:S(2)}) collective-permute-start(bf16[128,2048]{0,1:T(8,128)(2,1)S(1)} %slice.822), channel_id=1, source_target_pairs={{0,2},{1,3},{2,0},{3,1},{4,6},{5,7},{6,4},{7,5},{8,10},{9,11},{10,... | collective-permute-start | bytes 1572872 | tf_op jit(solution)/shard_map/ppermute | solution.py:223
  1103.5 33.0 %collective-permute-start.128 = (bf16[128,1024]{1,0:T(8,128)(2,1)S(1)}, bf16[128,1024]{1,0:T(8,128)(2,1)S(1)}, u32[]{:S(2)}, u32[]{:S(2)}) collective-permute-start(bf16[128,1024]{1,0:T(8,128)(2,1)S(1)} %slice.806), channel_id=1, source_target_pairs={{0,1},{1,0},{2,3},{3,2},{4,5},{5,4},{6,7},{7,6},{8,9},{9,8},{10,11... | collective-permute-start | bytes 786440 | tf_op jit(solution)/shard_map/ppermute | solution.py:223
  1114.8 65.1 %collective-permute-start.138 = (bf16[128,1024]{0,1:T(8,128)(2,1)S(1)}, bf16[128,1024]{0,1:T(8,128)(2,1)S(1)}, u32[]{:S(2)}, u32[]{:S(2)}) collective-permute-start(bf16[128,1024]{0,1:T(8,128)(2,1)S(1)} %slice.824), channel_id=1, source_target_pairs={{0,1},{1,0},{2,3},{3,2},{4,5},{5,4},{6,7},{7,6},{8,9},{9,8},{10,11... | collective-permute-start | bytes 786440 | tf_op jit(solution)/shard_map/ppermute | solution.py:223
  1130.3 38.0 %collective-permute-start.122 = (bf16[128,2048]{1,0:T(8,128)(2,1)S(1)}, bf16[128,2048]{1,0:T(8,128)(2,1)S(1)}, u32[]{:S(2)}, u32[]{:S(2)}) collective-permute-start(bf16[128,2048]{1,0:T(8,128)(2,1)S(1)} %slice.794), channel_id=1, source_target_pairs={{0,2},{1,3},{2,0},{3,1},{4,6},{5,7},{6,4},{7,5},{8,10},{9,11},{10,... | collective-permute-start | bytes 1572872 | tf_op jit(solution)/shard_map/ppermute | solution.py:223
  1133.8 45.8 %collective-permute-start.132 = (bf16[128,2048]{0,1:T(8,128)(2,1)S(1)}, bf16[128,2048]{0,1:T(8,128)(2,1)S(1)}, u32[]{:S(2)}, u32[]{:S(2)}) collective-permute-start(bf16[128,2048]{0,1:T(8,128)(2,1)S(1)} %slice.814), channel_id=1, source_target_pairs={{0,2},{1,3},{2,0},{3,1},{4,6},{5,7},{6,4},{7,5},{8,10},{9,11},{10,... | collective-permute-start | bytes 1572872 | tf_op jit(solution)/shard_map/ppermute | solution.py:223
  (246 other events, 4826.1 us)

commit v2 on v1

v2 whole, which is shorter than its diff:
```python
import functools
import math

import jax
import jax.numpy as jnp
import numpy as np
from jax import lax
from jax.experimental import pallas as pl
from jax.experimental.pallas import tpu as pltpu
from jax.sharding import PartitionSpec as P

H = 8
HD = 128
STEP = 5
MAX_DOC = 512

norm_eps = 1e-05
clip_bound = 1.0
beta_first = 0.9
beta_second = 0.95
adam_eps = 1e-08
masked_score = -1e30
group_rates = (0.03, 0.12, 0.03, 0.015, 0.3, 0.7, 0.3)
group_decays = (0.1, 0.1, 0.1, 0.1, 0.0, 0.0, 0.0)
contract_rows = (((0,), (0,)), ((), ()))
contract_cols = (((1,), (1,)), ((), ()))
f32 = jnp.float32
bf16 = jnp.bfloat16
score_scale = 1.0 / math.sqrt(HD)
MESH = pl.DeviceIdType.MESH


def adam_update(master, moment, square, gradient, factor, step_rate, decay_rate):
    clipped = gradient * factor
    moment_new = beta_first * moment + (1.0 - beta_first) * clipped
    square_new = beta_second * square + (1.0 - beta_second) * clipped * clipped
    first_hat = moment_new / (1.0 - beta_first**STEP)
    second_hat = square_new / (1.0 - beta_second**STEP)
    master_new = master - step_rate * (
        first_hat / (jnp.sqrt(second_hat) + adam_eps) + decay_rate * master
    )
    return (master_new, moment_new, square_new)


def gelu_tanh(values):
    return jax.nn.gelu(values, approximate=True)


def layer_norm(values, scale_vec, shift_vec):
    center = values - jnp.mean(values, axis=-1, keepdims=True)
    spread = jnp.mean(center * center, axis=-1, keepdims=True)
    return center * lax.rsqrt(spread + norm_eps) * scale_vec + shift_vec


def dot(left, right):
    return jnp.dot(left, right, preferred_element_type=f32)


def dot_rows(left, right):
    return lax.dot_general(left, right, contract_rows, preferred_element_type=f32)


def dot_cols(left, right):
    return lax.dot_general(left, right, contract_cols, preferred_element_type=f32)


def masked_scores(slope, doc_col, doc_row, query, key, first_row, first_col):
    scores = dot_cols(query, key) * score_scale
    rows = first_row + lax.broadcasted_iota(jnp.int32, scores.shape, 0)
    cols = first_col + lax.broadcasted_iota(jnp.int32, scores.shape, 1)
    distance = rows - cols
    allowed = (distance >= 0) & (doc_col == doc_row)
    return jnp.where(allowed, scores - slope * distance.astype(f32), masked_score)


def key_range(first_row, block):
    low = max(0, first_row - (MAX_DOC - 1)) // block * block
    return low, first_row + block


def attend_kernel(heads, block, slope_ref, dcol_ref, drow_ref, qkv_ref, o_ref):
    length = o_ref.shape[0]
    for head in range(heads):
        slope = slope_ref[pl.program_id(0) * heads + head]
        at = head * HD
        kat = (heads + head) * HD
        vat = (2 * heads + head) * HD
        for first_row in range(0, length, block):
            low, high = key_range(first_row, block)
            scores = masked_scores(
                slope,
                dcol_ref[first_row : first_row + block, :],
                drow_ref[:, low:high],
                qkv_ref[first_row : first_row + block, at : at + HD],
                qkv_ref[low:high, kat : kat + HD],
                first_row,
                low,
            )
            shifted = jnp.exp(scores - jnp.max(scores, axis=-1, keepdims=True))
            total = jnp.sum(shifted, axis=-1, keepdims=True)
            prob_low = (shifted * (1.0 / total)).astype(bf16)
            o_ref[first_row : first_row + block, at : at + HD] = dot(
                prob_low, qkv_ref[low:high, vat : vat + HD]
            ).astype(bf16)


def attend_back_kernel(
    heads, block, slope_ref, dcol_ref, drow_ref, qkv_ref, o_ref, do_ref,
    grad_ref, key_acc, value_acc,
):
    length = o_ref.shape[0]
    for head in range(heads):
        slope = slope_ref[pl.program_id(0) * heads + head]
        at = head * HD
        kat = (heads + head) * HD
        vat = (2 * heads + head) * HD
        key_acc[...] = jnp.zeros_like(key_acc)
        value_acc[...] = jnp.zeros_like(value_acc)
        for first_row in range(0, length, block):
            low, high = key_range(first_row, block)
            rows = slice(first_row, first_row + block)
            query = qkv_ref[rows, at : at + HD]
            key = qkv_ref[low:high, kat : kat + HD]
            scores = masked_scores(
                slope, dcol_ref[rows, :], drow_ref[:, low:high], query, key, first_row, low
            )
            shifted = jnp.exp(scores - jnp.max(scores, axis=-1, keepdims=True))
            total = jnp.sum(shifted, axis=-1, keepdims=True)
            probs = shifted * (1.0 / total)
            out_grad = do_ref[rows, at : at + HD]
            value_acc[low:high, :] += dot_rows(probs.astype(bf16), out_grad)
            prob_grad = dot_cols(out_grad, qkv_ref[low:high, vat : vat + HD])
            inner = jnp.sum(
                out_grad.astype(f32) * o_ref[rows, at : at + HD].astype(f32),
                axis=-1,
                keepdims=True,
            )
            score_grad = (probs * (prob_grad - inner)).astype(bf16)
            grad_ref[rows, at : at + HD] = (dot(score_grad, key) * score_scale).astype(bf16)
            key_acc[low:high, :] += dot_rows(score_grad, query)
        grad_ref[:, kat : kat + HD] = (key_acc[...] * score_scale).astype(bf16)
        grad_ref[:, vat : vat + HD] = value_acc[...].astype(bf16)


def attend_specs(length, width):
    def columns(each):
        return pl.BlockSpec((length, each), lambda s: (0, s))

    fixed = [
        pl.BlockSpec(memory_space=pltpu.SMEM),
        pl.BlockSpec((length, 1), lambda s: (0, 0)),
        pl.BlockSpec((1, length), lambda s: (0, 0)),
    ]
    return fixed, columns(3 * width), columns(width)


def attend(slopes, docs, qkv, slots):
    length = qkv.shape[0]
    width = qkv.shape[1] // (3 * slots)
    fixed, wide, narrow = attend_specs(length, width)
    pairs = slots * width // HD * length * length
    return pl.pallas_call(
        functools.partial(attend_kernel, width // HD, min(256, length)),
        grid=(slots,),
        in_specs=fixed + [wide],
        out_specs=narrow,
        out_shape=jax.ShapeDtypeStruct((length, slots * width), bf16),
        compiler_params=pltpu.CompilerParams(vmem_limit_bytes=32 * 2**20),
        cost_estimate=pl.CostEstimate(
            flops=4 * pairs * HD, bytes_accessed=3 * qkv.size, transcendentals=pairs
        ),
    )(slopes, docs.reshape(-1, 1), docs.reshape(1, -1), qkv)


def attend_back(slopes, docs, qkv, o, do, slots):
    length = qkv.shape[0]
    width = qkv.shape[1] // (3 * slots)
    fixed, wide, narrow = attend_specs(length, width)
    pairs = slots * width // HD * length * length
    return pl.pallas_call(
        functools.partial(attend_back_kernel, width // HD, min(256, length)),
        grid=(slots,),
        in_specs=fixed + [wide, narrow, narrow],
        out_specs=wide,
        out_shape=jax.ShapeDtypeStruct(qkv.shape, bf16),
        scratch_shapes=[pltpu.VMEM((length, HD), f32), pltpu.VMEM((length, HD), f32)],
        compiler_params=pltpu.CompilerParams(vmem_limit_bytes=32 * 2**20),
        cost_estimate=pl.CostEstimate(
            flops=10 * pairs * HD, bytes_accessed=6 * qkv.size, transcendentals=pairs
        ),
    )(slopes, docs.reshape(-1, 1), docs.reshape(1, -1), qkv, o, do)


def flip(value, mask):
    bit = 1
    while bit <= mask:
        if mask & bit:
            value = value + bit * (1 - 2 * ((value // bit) % 2))
        bit *= 2
    return value


def place(at, size):
    return pl.multiple_of(at * size, size)


class Spread:
    def __init__(self, dims, mp_size):
        self.dims = tuple(dims)
        self.events = []
        masks, spread = [0], False
        for stage, dim in enumerate(self.dims):
            for mask in masks:
                if dim == "mp":
                    for hops in range(1, mp_size):
                        self.events += [(stage, mask, way, hops) for way in (1, -1)]
                else:
                    places = range(mp_size) if spread else (0,)
                    self.events += [(stage, mask | dim, 0, at) for at in places]
            if dim == "mp":
                spread = True
            else:
                masks = masks + [mask | dim for mask in masks]
        self.events += [(len(self.dims), mask | 1, 0, 0) for mask in masks]

    def full(self, stage):
        return "mp" in self.dims[:stage]


class Fold:
    def __init__(self, dims, mp_size):
        self.dims = tuple(dims)
        masks = [0]
        for dim in self.dims:
            if dim != "mp":
                masks = masks + [mask | dim for mask in masks]
        self.masks = masks
        self.kept = {}
        self.events = [(0, mask, 0, 0) for mask in sorted(masks, key=self.leaves)]
        rows = list(masks)
        for stage, dim in enumerate(self.dims, 1):
            if dim != "mp":
                rows = [mask for mask in rows if not mask & dim]
            self.kept[stage] = list(rows)
            if dim == "mp":
                for hops in reversed(range(mp_size - 1)):
                    for mask in rows:
                        self.events += [(stage, mask, way, hops) for way in (1, -1)]
            else:
                places = reversed(range(mp_size)) if self.full(stage) else (0,)
                places = list(places)
                for mask in rows:
                    self.events += [(stage, mask, 0, at) for at in places]

    def leaves(self, mask):
        for at, dim in enumerate(self.dims):
            if dim != "mp" and mask & dim:
                return at
        return len(self.dims)

    def full(self, stage):
        return "mp" not in self.dims[: stage - 1]


def number(plans, mp_size, single):
    index, total = {}, 0
    for t, plan in enumerate(plans):
        for event in plan.events:
            stage, mask, way, at = event
            if way or single(plan, stage):
                index[(t,) + event] = total
                total += 1
            elif (t, stage, mask) not in index:
                index[t, stage, mask] = total
                total += mp_size
    return index, total


def spread_single(plan, stage):
    return stage == len(plan.dims)


def fold_single(plan, stage):
    return stage == 0


def merge_small(order, plans):
    t = len(plans) - 1
    small = [(t, event) for event in plans[t].events]
    out, used = [], 0
    for at, step in enumerate(order):
        out.append(step)
        while used < len(small) and (used + 1) * len(order) <= (at + 1) * (len(small) + 1):
            out.append(small[used])
            used += 1
    return out + small[used:]


def step_order(plans, table, by_stage):
    steps = [(t, event) for t, plan in enumerate(plans[:-1]) for event in plan.events]
    if len(table) == len(steps):
        return merge_small([steps[at] for at in table], plans)
    ranked = sorted(range(len(steps)), key=lambda at: (by_stage(steps[at][0], steps[at][1][0]), at))
    return merge_small([steps[at] for at in ranked], plans)


def greet(z, d, upper, mp_size):
    barrier = pltpu.get_barrier_semaphore()
    for bit in [1] + upper:
        pl.semaphore_signal(
            barrier, inc=1, device_id={"dp": flip(d, bit)}, device_id_type=MESH
        )
    for way in (1, -1):

        @pl.when((z + way >= 0) & (z + way < mp_size))
        def _(way=way):
            pl.semaphore_signal(
                barrier, inc=1, device_id={"mp": z + way}, device_id_type=MESH
            )

    around = jnp.where(z > 0, 1, 0) + jnp.where(z < mp_size - 1, 1, 0)
    pl.semaphore_wait(barrier, 1 + len(upper) + around)


def spread_kernel(plans, order, mp_size, *refs):
    n = len(plans)
    shards, outs = refs[:n], refs[n : 2 * n]
    send_sems, recv_sems, own_sems = refs[2 * n :]
    z = lax.axis_index("mp")
    d = lax.axis_index("dp")
    upper = [dim for dim in plans[0].dims if dim != "mp"]
    index, _ = number(plans, mp_size, spread_single)

    def inside(at):
        return (at >= 0) & (at < mp_size)

    def region(t, mask, block):
        wide, cols = shards[t].shape
        rows = pl.ds(place(flip(d, mask), wide), wide)
        if block is None:
            return outs[t].at[rows, :]
        return outs[t].at[rows, pl.ds(place(block, cols), cols)]

    def remote(t, event, block, src, dst, to):
        stage, mask, way, at = event
        if way or stage == len(plans[t].dims):
            sem = index[(t,) + event]
        else:
            sem = index[t, stage, mask] + block
        return pltpu.make_async_remote_copy(
            src_ref=src,
            dst_ref=dst,
            send_sem=send_sems.at[sem],
            recv_sem=recv_sems.at[sem],
            device_id=to,
            device_id_type=MESH,
        )

    def sending(t, event, block, to, own=False):
        stage, mask, way, at = event
        dims = plans[t].dims
        bit = 0 if way else 1 if stage == len(dims) else dims[stage]
        dst = region(t, mask ^ bit, block)
        return remote(t, event, block, shards[t] if own else dst, dst, to)

    def arrival(t, event, block):
        dst = region(t, event[1], block)
        return remote(t, event, block, dst, dst, {"dp": d, "mp": z})

    def on_line(t, stage, mask, block, way, hops, own):
        @pl.when(inside(z + way))
        def _():
            sending(t, (stage, mask, way, hops), block, {"mp": z + way}, own).start()

    def onward(t, stage, mask, block, own=False):
        dims = plans[t].dims
        for later in range(stage, len(dims)):
            if dims[later] == "mp":
                for way in (1, -1):
                    on_line(t, later, mask, block, way, 1, own)
            else:
                to = {"dp": flip(d, dims[later])}
                sending(t, (later, mask | dims[later], 0, None), block, to, own).start()

    greet(z, d, upper, mp_size)
    owns = []
    for t in range(n):
        onward(t, 0, 0, z, True)
        owns.append(pltpu.make_async_copy(shards[t], region(t, 0, z), own_sems.at[t]))
        owns[t].start()

    left = {}
    for t, event in order:
        if event[0] < len(plans[t].dims):
            left[t, event[1]] = left.get((t, event[1]), 0) + 1

    def place_of(t, event):
        stage, mask, way, at = event
        return flip(z, at) if plans[t].full(stage) else z

    for t, event in order:
        stage, mask, way, at = event
        last = len(plans[t].dims)
        if stage == last:
            arrival(t, event, None).wait_recv()
            continue
        if way:
            block = z - way * at

            @pl.when(inside(block))
            def _():
                arrival(t, event, block).wait_recv()
                if at + 1 < mp_size:
                    on_line(t, stage, mask, block, way, at + 1, False)
                onward(t, stage + 1, mask, block)

        else:
            block = place_of(t, event)
            arrival(t, event, block).wait_recv()
            onward(t, stage + 1, mask, block)
        left[t, mask] -= 1
        if left[t, mask] == 0:
            if mask == 0:
                owns[t].wait()
            sending(t, (last, mask | 1, 0, 0), None, {"dp": flip(d, 1)}).start()

    for t, event in order:
        stage, mask, way, at = event
        if stage == len(plans[t].dims):
            sending(t, event, None, {"dp": flip(d, 1)}).wait_send()
        elif way:

            @pl.when(inside(z - way * (at - 1)) & inside(z + way))
            def _():
                sending(t, event, z - way * (at - 1), {"mp": z + way}).wait_send()

        else:
            to = {"dp": flip(d, plans[t].dims[stage])}
            sending(t, event, place_of(t, event), to).wait_send()


def spread_all(shards, plans, order, dp_size, mp_size):
    _, total = number(plans, mp_size, spread_single)
    return pl.pallas_call(
        functools.partial(spread_kernel, plans, order, mp_size),
        out_shape=[
            jax.ShapeDtypeStruct((s.shape[0] * dp_size, s.shape[1] * mp_size), s.dtype)
            for s in shards
        ],
        in_specs=[pl.BlockSpec(memory_space=pl.ANY)] * len(shards),
        out_specs=[pl.BlockSpec(memory_space=pl.ANY)] * len(shards),
        scratch_shapes=[
            pltpu.SemaphoreType.DMA((total,)),
            pltpu.SemaphoreType.DMA((total,)),
            pltpu.SemaphoreType.DMA((len(shards),)),
        ],
        compiler_params=pltpu.CompilerParams(collective_id=0, has_side_effects=True),
    )(*shards)


def fold_kernel(plans, order, mp_size, *refs):
    n = len(plans)
    grads, outs, landed, sums = (refs[at * n : (at + 1) * n] for at in range(4))
    at = 4 * n
    recv = {}
    for t, plan in enumerate(plans):
        for stage in range(1, len(plan.dims) + 1):
            recv[t, stage] = refs[at]
            at += 1
    staging, load_sems, own_sems, send_sems, recv_sems = refs[at:]
    z = lax.axis_index("mp")
    d = lax.axis_index("dp")
    upper = [dim for dim in plans[0].dims if dim != "mp"]
    index, _ = number(plans, mp_size, fold_single)
    wides = [out.shape[0] for out in outs]
    cols = [out.shape[1] for out in outs]

    def inside(at):
        return (at >= 0) & (at < mp_size)

    def rows_of(t, mask):
        return pl.ds(plans[t].masks.index(mask) * wides[t], wides[t])

    def sum_at(t, mask, block):
        return sums[t].at[rows_of(t, mask), pl.ds(place(block, cols[t]), cols[t])]

    def landing(t, event, block):
        stage, mask, way, at = event
        kept = plans[t].kept[stage].index(mask)
        if way:
            return recv[t, stage].at[kept, (0 if way == 1 else mp_size - 1) + at]
        return recv[t, stage].at[kept, block if plans[t].full(stage) else 0]

    def remote(t, event, block, src, dst, to):
        stage, mask, way, at = event
        if way or stage == 0:
            sem = index[(t,) + event]
        else:
            sem = index[t, stage, mask] + block
        return pltpu.make_async_remote_copy(
            src_ref=src,
            dst_ref=dst,
            send_sem=send_sems.at[sem],
            recv_sem=recv_sems.at[sem],
            device_id=to,
            device_id_type=MESH,
        )

    def core_copy(t, mask):
        rows = pl.ds(place(flip(d, mask | 1), wides[t]), wides[t])
        dst = landed[t].at[rows_of(t, mask), :]
        return remote(t, (0, mask, 0, 0), 0, grads[t].at[rows, :], dst, {"dp": flip(d, 1)})

    def own_copy(t, mask):
        rows = pl.ds(place(flip(d, mask), wides[t]), wides[t])
        return pltpu.make_async_copy(
            grads[t].at[rows, :],
            sums[t].at[rows_of(t, mask), :],
            own_sems.at[t, plans[t].masks.index(mask)],
        )

    def bit_copy(t, stage, mask, block):
        dim = plans[t].dims[stage - 1]
        event = (stage, mask & ~dim, 0, None)
        dst = landing(t, event, block)
        return remote(t, event, block, sum_at(t, mask, block), dst, {"dp": flip(d, dim)})

    def line_copy(t, stage, mask, way, hops):
        event = (stage, mask, way, hops - 1)
        src = sum_at(t, mask, z + way * hops)
        return remote(t, event, None, src, landing(t, event, None), {"mp": z + way})

    def arrival(t, event, block):
        dst = landing(t, event, block)
        return remote(t, event, block, dst, dst, {"dp": d, "mp": z})

    def add(dst, src, wide):
        step = 16

        def some_rows(at, carry):
            rows = pl.ds(pl.multiple_of(at * step, step), step)
            total = dst[rows, :].astype(f32) + src[rows, :].astype(f32)
            dst[rows, :] = total.astype(bf16)
            return carry

        lax.fori_loop(0, wide // step, some_rows, 0)

    def advance(t, stage, mask, block, other):
        if stage > len(plans[t].dims):
            return
        dim = plans[t].dims[stage - 1]
        if dim == "mp":
            if other:
                for way, end in ((1, 0), (-1, mp_size - 1)):

                    @pl.when(z == end)
                    def _(way=way):
                        line_copy(t, stage, mask, way, other).start()

        elif mask & dim:
            bit_copy(t, stage, mask, block).start()

    greet(z, d, upper, mp_size)
    cores = [(t, event[1]) for t, event in order if event[0] == 0]
    for t, mask in cores:
        core_copy(t, mask).start()
        own_copy(t, mask).start()

    def load(at):
        t, mask = cores[at]
        return pltpu.make_async_copy(
            landed[t].at[rows_of(t, mask), :],
            staging.at[at % 2, pl.ds(0, wides[t]), pl.ds(0, cols[t] * mp_size)],
            load_sems.at[at % 2],
        )

    seen = 0
    brought = {}
    for t, event in order:
        stage, mask, way, at = event
        plan = plans[t]
        if stage == 0:
            for ahead in (0, 1) if seen == 0 else (seen + 1,):
                if ahead < len(cores):
                    core_copy(*cores[ahead]).wait_recv()
                    load(ahead).start()
            load(seen).wait()
            own_copy(t, mask).wait()
            part = staging.at[seen % 2, pl.ds(0, wides[t]), pl.ds(0, cols[t] * mp_size)]
            add(sums[t].at[rows_of(t, mask), :], part, wides[t])
            seen += 1
            for other in reversed(range(mp_size)):
                advance(t, 1, mask, flip(z, other), other)
        elif way:
            block = z + way * at

            @pl.when(inside(block) & inside(z - way))
            def _():
                arrival(t, event, None).wait_recv()
                add(sum_at(t, mask, block), landing(t, event, None), wides[t])
                if at > 0:
                    line_copy(t, stage, mask, way, at).start()

            if at == 0:
                brought[t, mask] = brought.get((t, mask), 0) + 1
                if brought[t, mask] == 2:
                    advance(t, stage + 1, mask, z, 0)
        else:
            block = flip(z, at) if plan.full(stage) else z
            arrival(t, event, block).wait_recv()
            add(sum_at(t, mask, block), landing(t, event, block), wides[t])
            advance(t, stage + 1, mask, block, at)

    for t in range(n):
        outs[t][...] = sum_at(t, 0, z)[...].astype(f32)

    for t, event in order:
        stage, mask, way, at = event
        if stage == 0:
            core_copy(t, mask).wait_send()
        elif way:

            @pl.when(inside(z + way) & inside(z + way * (at + 1)))
            def _():
                line_copy(t, stage, mask, way, at + 1).wait_send()

        else:
            block = flip(z, at) if plans[t].full(stage) else z
            bit_copy(t, stage, mask | plans[t].dims[stage - 1], block).wait_send()


def fold_all(grads, plans, order, dp_size, mp_size):
    n = len(grads)
    _, total = number(plans, mp_size, fold_single)
    wides = [g.shape[0] // dp_size for g in grads]
    cols = [g.shape[1] // mp_size for g in grads]
    halves = [(dp_size // 2 * wide, mp_size * each) for wide, each in zip(wides, cols)]
    scratch = [pltpu.VMEM(half, bf16) for half in halves]
    for plan, wide, each in zip(plans, wides, cols):
        for stage, dim in enumerate(plan.dims, 1):
            blocks = 2 * (mp_size - 1) if dim == "mp" else mp_size if plan.full(stage) else 1
            scratch.append(pltpu.VMEM((len(plan.kept[stage]), blocks, wide, each), bf16))
    scratch += [
        pltpu.VMEM((2, max(wides), mp_size * max(cols)), bf16),
        pltpu.SemaphoreType.DMA((2,)),
        pltpu.SemaphoreType.DMA((n, dp_size // 2)),
        pltpu.SemaphoreType.DMA((total,)),
        pltpu.SemaphoreType.DMA((total,)),
    ]
    out = pl.pallas_call(
        functools.partial(fold_kernel, plans, order, mp_size),
        out_shape=[jax.ShapeDtypeStruct((wide, each), f32) for wide, each in zip(wides, cols)]
        + [jax.ShapeDtypeStruct(half, bf16) for half in halves],
        in_specs=[pl.BlockSpec(memory_space=pl.ANY)] * n,
        out_specs=[pl.BlockSpec(memory_space=pltpu.VMEM)] * n
        + [pl.BlockSpec(memory_space=pl.ANY)] * n,
        scratch_shapes=scratch,
        compiler_params=pltpu.CompilerParams(
            collective_id=1, has_side_effects=True, vmem_limit_bytes=63 * 2**20
        ),
    )(*grads)
    return list(out[:n])


spread_table = (
    45, 0, 46, 22, 23, 94, 116, 1, 95, 117, 2, 3, 25, 119, 118, 24, 97, 120, 26, 4, 96, 47, 71, 5,
    27, 69, 140, 165, 28, 7, 44, 6, 121, 99, 98, 125, 48, 30, 51, 8, 70, 122, 76, 72, 53, 128, 77,
    33, 34, 78, 50, 9, 112, 35, 129, 15, 123, 107, 29, 104, 73, 124, 79, 103, 101, 102, 52, 31,
    54, 80, 127, 49, 81, 139, 56, 19, 75, 106, 57, 74, 164, 60, 126, 141, 142, 40, 55, 100, 88,
    87, 105, 166, 167, 138, 12, 144, 136, 83, 111, 38, 113, 168, 82, 134, 13, 59, 169, 66, 184,
    64, 143, 163, 86, 32, 146, 16, 159, 18, 89, 176, 85, 41, 110, 58, 10, 151, 42, 145, 84, 61,
    148, 93, 11, 63, 39, 37, 131, 65, 130, 36, 17, 170, 154, 114, 147, 171, 62, 132, 152, 108,
    109, 20, 177, 91, 150, 172, 153, 135, 149, 14, 179, 68, 178, 90, 173, 175, 174, 180, 161, 43,
    160, 182, 156, 181, 133, 92, 155, 67, 157, 158, 115, 21, 186, 185, 137, 183, 162, 187,
)
fold_table = (
    50, 25, 1, 28, 29, 122, 169, 2, 8, 30, 9, 0, 145, 119, 31, 95, 53, 51, 55, 3, 74, 11, 10, 26,
    15, 4, 6, 96, 146, 75, 123, 32, 72, 97, 19, 147, 7, 27, 102, 124, 14, 38, 125, 73, 5, 52, 94,
    126, 37, 12, 103, 131, 54, 132, 136, 104, 105, 76, 109, 42, 18, 33, 57, 36, 168, 135, 166,
    113, 34, 35, 108, 144, 39, 98, 16, 40, 46, 120, 80, 112, 58, 81, 13, 170, 140, 99, 20, 101,
    172, 79, 56, 78, 83, 41, 60, 77, 148, 100, 82, 167, 44, 106, 107, 17, 121, 150, 43, 59, 110,
    127, 111, 84, 173, 129, 128, 47, 153, 61, 130, 85, 87, 174, 133, 62, 134, 114, 149, 86, 171,
    45, 89, 175, 88, 65, 178, 137, 138, 63, 152, 151, 177, 154, 156, 48, 176, 179, 21, 64, 91,
    157, 67, 90, 115, 116, 22, 181, 66, 155, 180, 117, 142, 182, 159, 183, 69, 158, 161, 141, 93,
    23, 160, 68, 92, 185, 184, 162, 71, 70, 163, 139, 24, 49, 118, 187, 143, 186, 164, 165,
)


def bits_of(size):
    return [1 << at for at in range(size.bit_length() - 1)]


def program(dp_size, mp_size, args):
    (
        inputs, documents, cotangent,
        qkv_weight, qkv_moment, qkv_square,
        proj_weight, proj_moment, proj_square,
        upper_weight, upper_moment, upper_square,
        lower_weight, lower_moment, lower_square,
        hidden_bias, bias_moment, bias_square,
        norm_gains, gains_moment, gains_square,
        shift_params, shifts_moment, shifts_square,
    ) = args
    layers = qkv_weight.shape[0]
    tokens, features = inputs.shape
    length = documents.shape[1]
    pieces = length // tokens
    slots = mp_size // pieces
    wide = features // dp_size
    z_cols = qkv_weight.shape[3]
    heads_slot = z_cols // HD
    me_dp = lax.axis_index("dp")
    me_mp = lax.axis_index("mp")
    core = me_dp % 2

    def swap(values):
        return lax.ppermute(values, "dp", [(at, at ^ 1) for at in range(dp_size)])

    def by_core(own, other, axis):
        first = jnp.where(core == 0, own, other)
        second = jnp.where(core == 0, other, own)
        return jnp.concatenate([first, second], axis=axis)

    paired = pieces == 2 and dp_size % 2 == 0 and mp_size % 2 == 0
    if paired:
        moved = core != me_mp % 2
        pairs = []
        for d in range(dp_size):
            for m in range(mp_size):
                if d % 2 != m % 2:
                    pairs.append((d * mp_size + m, (d ^ 1) * mp_size + (m ^ 1)))

        def trade(values):
            other = lax.ppermute(values, ("dp", "mp"), pairs)
            return jnp.where(moved, other, values)

        doc_rows = jnp.where(moved, swap(documents), documents)
        docs = lax.dynamic_index_in_dim(doc_rows, me_mp // 2, 0, False)

        def share_heads(values):
            half = values.shape[1] // 2
            own = lax.dynamic_slice_in_dim(values, core * half, half, 1)
            sent = lax.dynamic_slice_in_dim(values, (1 - core) * half, half, 1)
            return by_core(own, swap(sent), 0)

        def return_heads(values):
            own = lax.dynamic_slice_in_dim(values, core * tokens, tokens, 0)
            sent = lax.dynamic_slice_in_dim(values, (1 - core) * tokens, tokens, 0)
            return by_core(own, swap(sent), 1)

        first_slot = core * slots
    else:
        groups = [list(range(g * pieces, (g + 1) * pieces)) for g in range(mp_size // pieces)]

        def trade(values):
            return values

        docs = lax.dynamic_index_in_dim(documents, me_mp // pieces, 0, False)

        def share_heads(values):
            return lax.all_to_all(values, "mp", 1, 0, axis_index_groups=groups, tiled=True)

        def return_heads(values):
            return lax.all_to_all(values, "mp", 0, 1, axis_index_groups=groups, tiled=True)

        first_slot = (me_mp % pieces) * slots
    slope_table = jnp.asarray(0.5 ** (np.arange(H) + 1.0), dtype=f32)
    slopes = lax.dynamic_slice_in_dim(
        slope_table, first_slot * heads_slot, slots * heads_slot
    )

    bits = bits_of(dp_size)[1:]
    line_first = [("mp", *bits), ("mp", *bits[::-1])]
    line_second = [(bits[0], "mp", *bits[1:]), (bits[-1], "mp", *bits[:-1][::-1])]

    gain_rows = norm_gains.shape[1]
    shift_rows = shift_params.shape[1]
    vector_count = layers * (gain_rows + shift_rows)
    bias_wide = hidden_bias.shape[1]
    lanes = max(wide, HD)
    small_rows = -(-(vector_count + layers) // 16) * 16

    def padded(values):
        return jnp.pad(values, [(0, 0)] * (values.ndim - 1) + [(0, lanes - values.shape[-1])])

    small = jnp.concatenate(
        [
            padded(norm_gains.reshape(-1, wide)),
            padded(shift_params.reshape(-1, wide)),
            padded(hidden_bias),
            jnp.zeros((small_rows - vector_count - layers, lanes), f32),
        ],
        axis=0,
    ).astype(bf16)

    shards = []
    spreads = []
    for layer in range(layers):
        shards += [
            qkv_weight[layer].astype(bf16).reshape(wide, 3 * z_cols),
            proj_weight[layer].astype(bf16).T,
            upper_weight[layer].astype(bf16),
            lower_weight[layer].astype(bf16).T,
        ]
        spreads += line_first[:: 1 if layer % 2 == 0 else -1] + line_second
    shards.append(small)
    spreads.append(line_first[0])
    spreads = [Spread(dims, mp_size) for dims in spreads]
    tabled = dp_size == 8 and mp_size == 4 and layers == 2
    spread_order = step_order(
        spreads, spread_table if tabled else (), lambda t, stage: t // 2 + stage
    )
    full = spread_all(shards, spreads, spread_order, dp_size, mp_size)
    small_all = full[-1].reshape(dp_size, small_rows, mp_size, lanes).astype(f32)
    vectors = small_all[:, :vector_count, 0, :wide].transpose(1, 0, 2)
    vectors = vectors.reshape(vector_count, features)
    gains = vectors[: layers * gain_rows].reshape(layers, gain_rows, features)
    shifts = vectors[layers * gain_rows :].reshape(layers, shift_rows, features)
    biases = small_all[:, vector_count : vector_count + layers, :, :bias_wide]
    biases = biases.transpose(1, 2, 0, 3).reshape(layers, -1)

    stream = trade(inputs).astype(f32)
    grad_stream = trade(cotangent).astype(f32)
    stored = []
    for layer in range(layers):
        qkv_w, proj_w, upper_w, lower_w = full[4 * layer : 4 * layer + 4]
        normed = layer_norm(stream, gains[layer, 0], shifts[layer, 0]).astype(bf16)
        qkv = share_heads(dot(normed, qkv_w).astype(bf16))
        mixed = attend(slopes, docs, qkv, slots)
        attended = return_heads(mixed)
        middle = stream + dot_cols(attended, proj_w)
        normed_two = layer_norm(middle, gains[layer, 1], shifts[layer, 1]).astype(bf16)
        hidden = dot(normed_two, upper_w) + biases[layer]
        active = gelu_tanh(hidden).astype(bf16)
        stored.append((stream, middle, normed, qkv, mixed, attended, normed_two, hidden, active))
        stream = middle + dot_cols(active, lower_w) + shifts[layer, 2]
    output_stream = stream
    if paired:
        other = lax.ppermute(output_stream.astype(bf16), ("dp", "mp"), pairs)
        output_stream = jnp.where(moved, other.astype(f32), output_stream)

    weight_grads = [None] * layers
    vector_grads = [None] * layers
    bias_grads = [None] * layers
    no_shift = jnp.zeros((features,), f32)
    for layer in reversed(range(layers)):
        qkv_w, proj_w, upper_w, lower_w = full[4 * layer : 4 * layer + 4]
        stream_in, middle, normed, qkv, mixed, attended, normed_two, hidden, active = stored[layer]
        out_shift_grad = jnp.sum(grad_stream, axis=0)
        grad_low = grad_stream.astype(bf16)
        active_grad = dot(grad_low, lower_w)
        _, pull_gelu = jax.vjp(gelu_tanh, hidden)
        hidden_grad = pull_gelu(active_grad)[0].astype(bf16)
        lower_grad = dot_rows(grad_low, active).astype(bf16)
        upper_grad = dot_rows(normed_two, hidden_grad).astype(bf16)
        bias_grads[layer] = jnp.sum(hidden_grad, axis=0, dtype=f32)
        normed_two_grad = dot_cols(hidden_grad, upper_w)
        _, pull_two = jax.vjp(layer_norm, middle, gains[layer, 1], no_shift)
        middle_part, gain_two, shift_two = pull_two(normed_two_grad)
        middle_grad = grad_stream + middle_part
        middle_low = middle_grad.astype(bf16)
        mixed_grad = share_heads(dot(middle_low, proj_w).astype(bf16))
        proj_grad = dot_rows(middle_low, attended).astype(bf16)
        qkv_grad = return_heads(attend_back(slopes, docs, qkv, mixed, mixed_grad, slots))
        normed_grad = dot_cols(qkv_grad, qkv_w)
        qkv_weight_grad = dot_rows(normed, qkv_grad).astype(bf16)
        _, pull_one = jax.vjp(layer_norm, stream_in, gains[layer, 0], no_shift)
        stream_part, gain_one, shift_one = pull_one(normed_grad)
        grad_stream = middle_grad + stream_part
        weight_grads[layer] = (lower_grad, upper_grad, proj_grad, qkv_weight_grad)
        vector_grads[layer] = (
            jnp.stack([gain_one, gain_two]),
            jnp.stack([shift_one, shift_two, out_shift_grad]),
        )
    input_grad = grad_stream
    if paired:
        other = lax.ppermute(input_grad.astype(bf16), ("dp", "mp"), pairs)
        input_grad = jnp.where(moved, other.astype(f32), input_grad)

    vector_sums = jnp.concatenate(
        [jnp.concatenate([vector_grads[at][kind] for at in range(layers)]) for kind in (0, 1)]
    )
    vector_sums = padded(vector_sums.reshape(vector_count, dp_size, wide)).transpose(1, 0, 2)
    vector_sums = jnp.broadcast_to(
        vector_sums[:, :, None], (dp_size, vector_count, mp_size, lanes)
    )
    bias_sums = padded(jnp.stack(bias_grads).reshape(layers, mp_size, dp_size, bias_wide))
    bias_sums = bias_sums.transpose(2, 0, 1, 3)
    rest = jnp.zeros((dp_size, small_rows - vector_count - layers, mp_size, lanes), f32)
    small_grad = jnp.concatenate([vector_sums, bias_sums, rest], axis=1)
    small_grad = small_grad.reshape(dp_size * small_rows, mp_size * lanes).astype(bf16)

    folds = []
    local = []
    for layer in reversed(range(layers)):
        local += weight_grads[layer]
        folds += fold_dims(line_first, line_second, layer)
    local.append(small_grad)
    folds.append(line_first[0][::-1])
    folds = [Fold(dims, mp_size) for dims in folds]
    fold_order = step_order(
        folds, fold_table if tabled else (), lambda t, stage: t // 2 + stage
    )
    owned = fold_all(local, folds, fold_order, dp_size, mp_size)
    small_owned = owned.pop()

    squares_sum = jnp.float32(0.0)
    for gradient in owned:
        squares_sum = squares_sum + jnp.sum(gradient * gradient)
    vector_owned = small_owned[:vector_count, :wide]
    bias_owned = small_owned[vector_count : vector_count + layers, :bias_wide]
    squares_sum = squares_sum + jnp.sum(vector_owned * vector_owned) / mp_size
    squares_sum = squares_sum + jnp.sum(bias_owned * bias_owned)
    grad_norm = jnp.sqrt(lax.psum(squares_sum, ("dp", "mp")))
    factor = jnp.minimum(1.0, clip_bound / grad_norm)

    by_layer = [owned[4 * at : 4 * at + 4] for at in reversed(range(layers))]
    gradients = (
        jnp.stack([each[3].reshape(wide, 3, z_cols) for each in by_layer]),
        jnp.stack([each[2].T for each in by_layer]),
        jnp.stack([each[1] for each in by_layer]),
        jnp.stack([each[0].T for each in by_layer]),
        bias_owned,
        vector_owned[: layers * gain_rows].reshape(layers, gain_rows, wide),
        vector_owned[layers * gain_rows :].reshape(layers, shift_rows, wide),
    )
    masters = (
        qkv_weight, proj_weight, upper_weight, lower_weight, hidden_bias, norm_gains, shift_params
    )
    moments = (
        qkv_moment, proj_moment, upper_moment, lower_moment, bias_moment, gains_moment,
        shifts_moment,
    )
    squares = (
        qkv_square, proj_square, upper_square, lower_square, bias_square, gains_square,
        shifts_square,
    )
    results = [output_stream, input_grad]
    for at in range(7):
        results.extend(
            adam_update(
                masters[at], moments[at], squares[at], gradients[at], factor,
                group_rates[at], group_decays[at],
            )
        )
    results.append(grad_norm)
    return tuple(results)


def fold_dims(line_first, line_second, layer):
    first = [dims[::-1] for dims in line_first]
    second = [dims[::-1] for dims in line_second]
    return second + (first if layer % 2 else first[::-1])


def solution(mesh):
    dp_size = mesh.shape["dp"]
    mp_size = mesh.shape["mp"]
    rows = P(("dp", "mp"), None)
    split_rows = P(None, "dp", None, "mp")
    split_upper = P(None, "dp", "mp")
    split_lower = P(None, "mp", "dp")
    split_bias = P(None, ("mp", "dp"))
    split_vector = P(None, None, "dp")
    groups = (
        split_rows, split_lower, split_upper, split_lower, split_bias, split_vector, split_vector
    )
    placed = tuple(spec for spec in groups for _ in range(3))

    def shards(*args):
        return program(dp_size, mp_size, args)

    return jax.shard_map(
        shards,
        mesh=mesh,
        in_specs=(rows, P("dp", None), rows) + placed,
        out_specs=(rows, rows) + placed + (P(),),
        check_vma=False,
    )
```

time: 1270 us -> 814 us (0.64)
  waiting for transfers between devices: 545 us -> 7.94 us
  Pallas kernels: 47.9 us -> 439 us
  starting transfers between devices: 123 us -> 17.4 us
  local copies, waits for them, and re-layouts: 144 us -> 58.7 us
  blocking collectives: 91.4 us -> 37.1 us
  other arithmetic: 105 us -> 50.8 us
    ppermute x135 -> x9, waiting for transfers between devices: 545 us -> 7.93 us  [swap(): return lax.ppermute(values, 'dp', [(at, at ^ 1) for at in range(dp_size)])]
    pallas_call x0 -> x2, Pallas kernels: none -> 391 us  [the longest x1 198 us: spread_all(): pl.pallas_call(functools.partial(spread_kernel, plans, order, mp_size), o...]
    ppermute x135 -> x9, starting transfers between devices: 112 us -> 2.22 us  [swap(): return lax.ppermute(values, 'dp', [(at, at ^ 1) for at in range(dp_size)])]
    all_gather x1 -> x0, blocking collectives: 51.6 us -> none  [program(): small_all = lax.all_gather(small, ('mp', 'dp'), axis=0).astype(f32)]
    convert_element_type x43 -> x0, other arithmetic: 34.4 us -> none  [the longest x20 18.1 us: scatter(): values = (kept.astype(f32) + sent.astype(f32)).astype(bf16)]
    unnamed x463 -> x196, local copies, waits for them, and re-layouts: 78.5 us -> 47.4 us
    squeeze x18 -> x0, local copies, waits for them, and re-layouts: 19.6 us -> none  [scatter(): sent = swap(lax.index_in_dim(values, 1, axis, False), 'dp', bit)]
    concatenate x22 -> x2, other arithmetic: 16.6 us -> 0.79 us  [the longest x1 0.67 us: program(): jnp.concatenate([padded(norm_gains.reshape(-1, wide)), padded(shift_param...]
  transfers between devices with their start and end apart: 139 -> 13, of which waited for: 55 -> 4; matrix products, arithmetic and copies ran while one was open for 28% -> 13% of each run, Pallas kernels for 4% -> 26%
where the time goes in v2:
time: 814 us; the launch traced here: 805 us
  Pallas kernels  439 us (54%)
  matrix products  183 us (22%)
  local copies, waits for them, and re-layouts  58.7 us (7%)
  other arithmetic  50.8 us (6%)
  blocking collectives  37.1 us (5%)
  starting transfers between devices  17.4 us (2%)
  between operations  10.6 us (1%)
    pallas_call x1, Pallas kernels, spread_all(): pl.pallas_call(functools.partial(spread_kernel, plans, order, mp_size), o...  198 us
    pallas_call x1, Pallas kernels, fold_all(): pl.pallas_call(functools.partial(fold_kernel, plans, order, mp_size), out...  193 us
    dot_general x8, matrix products, dot(): return jnp.dot(left, right, preferred_element_type=f32)  63.2 us
    dot_general x8, matrix products, dot_cols(): lax.dot_general(left, right, contract_cols, preferred_element_type=f32)  61 us
    dot_general x8, matrix products, dot_rows(): lax.dot_general(left, right, contract_rows, preferred_element_type=f32)  59.2 us
    unnamed x196, local copies, waits for them, and re-layouts  47.4 us
    psum x1, blocking collectives, program(): grad_norm = jnp.sqrt(lax.psum(squares_sum, ('dp', 'mp')))  37.1 us
    pallas_call x2, Pallas kernels, attend_back(): pl.pallas_call(functools.partial(attend_back_kernel, width // HD, min(256...  29 us
  transfers between devices with their start and end apart: 13, of which 4 were waited for; matrix products, arithmetic and copies ran while one was open for 13% of the time, Pallas kernels for 26%

profile of v2, /device:TPU:1, one launch (start us, length us, event | category | flops | bytes accessed | tf_op | source)
XLA Modules:
  0.0 805.0 jit_solution(7166136163870336789)
XLA Ops:
  0.7 4.7 collective-permute-start
  5.4 1.9 collective-permute-start.7
  11.5 1.6 copy.75
  15.7 198.0 %shard_map.424 = (bf16[1024,3072]{1,0:T(8,128)(2,1)}, bf16[1024,1024]{1,0:T(8,128)(2,1)}, bf16[1024,4096]{1,0:T(8,128)(2,1)}, bf16[1024,4096]{1,0:T(8,128)(2,1)}...) custom-call(bf16[128,768]{1,0:T(8,128)(2,1)} %copy.77.refs_0_, ...), custom_call_target="tpu_custom_call" | custom-call | tf_op jit(solution)/shard_map/pallas_call | solution.py:444
  215.0 4.0 convert_reduce_fusion
  219.5 4.2 convolution_convert_fusion.7
  223.7 1.6 copy-done.28
  227.2 2.5 collective-permute-done.1
  230.4 2.4 broadcast_select_fusion.7
  233.0 9.4 %shard_map.425.o_ref = bf16[1024,512]{1,0:T(8,128)(2,1)S(1)} custom-call(f32[4]{0:T(128)S(1)} %dynamic_slice.55.slope_ref, s32[1024,1]{1,0:T(8,128)S(1)} %copy.80.dcol_ref, s32[1,1024]{1,0:T(1,128)S(1)} %broadcast_select_fusion.18.drow_ref, bf16[1024,1536]{1,0:T(8,128)(2,1)S(1)} %pad_maximum_fusion.qkv_ref), custom_call_target="tpu_custom_call" | custom-call | flops 2147483648 | bytes 4718592 | tf_op jit(solution)/shard_map/pallas_call | solution.py:162
  242.7 1.7 collective-permute-done.3
  246.5 10.6 %fusion.60 = f32[512,4096]{1,0:T(8,128)} fusion(bf16[1024,4096]{1,0:T(8,128)(2,1)} %get-tuple-element.45, f32[512,1024]{1,0:T(8,128)S(1)} %get-tuple-element.194, f32[1024]{0:T(1024)S(1)} %bitcast.151, f32[1024]{0:T(1024)S(1)} %bitcast.136, f32[512]{0:T(512)S(1)} %fusion.46, f32[512]{0:T(512)S(1)} %broadcast_multiply_fusion.2), kind=kOutput, calls=%fused_computation.210 | convolution fusion | flops 4297588736 | bytes 18886656 | tf_op jit(solution)/shard_map/dot_general | solution.py:56
  257.2 10.8 %fusion.81 = (f32[512]{0:T(512)S(1)}, f32[512,1024]{1,0:T(8,128)S(1)}) fusion(f32[1024]{0:T(1024)S(1)} %bitcast.158, f32[512,1024]{1,0:T(8,128)S(1)} %get-tuple-element.194, bf16[1024,4096]{1,0:T(8,128)(2,1)} %get-tuple-element.46, f32[512,4096]{1,0:T(8,128)} %fusion.60, f32[4096]{0:T(1024)S(1)} %get-tuple-element.182), kind=kOutput, calls=%fused_computation.222 | convolution fusion | flops 4317511168 | bytes 20994048 | tf_op jit(solution)/shard_map/dot_general | solution.py:64
  268.4 7.0 convolution_convert_fusion.6
  275.7 3.3 collective-permute-done.4
  280.7 9.8 %shard_map.426.o_ref = bf16[1024,512]{1,0:T(8,128)(2,1)S(1)} custom-call(f32[4]{0:T(128)S(1)} %dynamic_slice.55.slope_ref, s32[1024,1]{1,0:T(8,128)S(1)} %copy-done.7, s32[1,1024]{1,0:T(1,128)S(1)} %broadcast_select_fusion.18.drow_ref, bf16[1024,1536]{1,0:T(8,128)(2,1)S(1)} %pad_maximum_fusion.1.qkv_ref), custom_call_target="tpu_custom_call" | custom-call | flops 2147483648 | bytes 4718592 | tf_op jit(solution)/shard_map/pallas_call | solution.py:162
  292.4 2.3 copy.85
  294.7 2.3 copy.89
  297.8 1.8 copy.93
  299.6 2.5 copy.96
  302.1 2.6 copy.97
  304.7 1.5 broadcast_select_fusion.15
  306.6 3.0 fusion.82
  309.9 10.3 %fusion.61 = f32[512,4096]{1,0:T(8,128)} fusion(bf16[1024,4096]{1,0:T(8,128)(2,1)} %get-tuple-element.49, f32[512,1024]{1,0:T(8,128)S(1)} %get-tuple-element.198, f32[1024]{0:T(1024)S(1)} %bitcast.153, f32[1024]{0:T(1024)S(1)} %bitcast.140, f32[512]{0:T(512)S(1)} %fusion.48, f32[512]{0:T(512)S(1)} %broadcast_multiply_fusion), kind=kOutput, calls=%fused_computation.211 | convolution fusion | flops 4297588736 | bytes 18886656 | tf_op jit(solution)/shard_map/dot_general | solution.py:56
  320.2 13.0 %fusion.83 = (bf16[512,1024]{1,0:T(8,128)(2,1)}, f32[512,1024]{1,0:T(8,128)}) fusion(f32[1024]{0:T(1024)S(1)} %bitcast.155, f32[512,1024]{1,0:T(8,128)S(1)} %get-tuple-element.198, bf16[1024,4096]{1,0:T(8,128)(2,1)} %get-tuple-element.50, f32[512,4096]{1,0:T(8,128)} %fusion.61, f32[4096]{0:T(1024)S(1)} %get-tuple-element.181), kind=kOutput, calls=%fused_computation.224 | convolution fusion | flops 4317511680 | bytes 22040576 | tf_op jit(solution)/shard_map/dot_general | solution.py:64
  333.2 13.2 %fusion.71 = (bf16[4096]{0:T(1024)(128)(2,1)S(1)}, bf16[512,4096]{1,0:T(8,128)(2,1)S(1)}) fusion(f32[512,4096]{1,0:T(8,128)} %fusion.61, f32[4096]{0:T(1024)S(1)} %get-tuple-element.181, bf16[512,1024]{1,0:T(8,128)(2,1)S(1)} %copy-done.18, bf16[1024,4096]{1,0:T(8,128)(2,1)} %get-tuple-element.50), kind=kOutput, calls=%fused_computation.213 | convolution fusion | flops 4341100544 | bytes 22044672 | tf_op jit(solution)/shard_map/dot_general | solution.py:56
  346.4 9.6 %multiply_reduce_fusion = (f32[1024]{0:T(1024)S(1)}, f32[512]{0:T(512)S(1)}, f32[1024]{0:T(1024)S(1)}, f32[512,1024]{1,0:T(8,128)S(1)}) fusion(f32[512,1024]{1,0:T(8,128)S(1)} %get-tuple-element.198, f32[512]{0:T(512)S(1)} %fusion.48, f32[512]{0:T(512)S(1)} %broadcast_multiply_fusion, f32[1024]{0:T(1024)S(1)} %bitcast.141, ...), kind=kOutput, calls=%fused_computation.52 | convolution fusion | flops 4299159040 | bytes 16795648 | tf_op jit(solution)/shard_map/dot_general | solution.py:64
  360.2 11.4 %convolution_convert_fusion.3.refs_0_ = bf16[1024,4096]{1,0:T(8,128)(2,1)} fusion(bf16[512,1024]{1,0:T(8,128)(2,1)S(1)} %copy-done.18, f32[512,4096]{1,0:T(8,128)} %fusion.61, f32[4096]{0:T(1024)S(1)} %get-tuple-element.181), kind=kOutput, calls=%fused_computation.23 | convolution fusion | flops 4320133120 | bytes 17842176 | tf_op jit(solution)/shard_map/dot_general | solution.py:60
  371.6 1.9 collective-permute-start.6
  373.5 2.6 convolution_convert_fusion.9.refs_2_
  377.5 14.6 %shard_map.427 = bf16[1024,1536]{1,0:T(8,128)(2,1)S(1)} custom-call(f32[4]{0:T(128)S(1)} %dynamic_slice.55.slope_ref, s32[1024,1]{1,0:T(8,128)S(1)} %copy-done.8, s32[1,1024]{1,0:T(1,128)S(1)} %broadcast_select_fusion.18.drow_ref, bf16[1024,1536]{1,0:T(8,128)(2,1)S(1)} %pad_maximum_fusion.1.qkv_ref, bf16[1024,512]{1,0:T(8,128)(2,1)S(1)} %copy-done.5, ...), custom_call_target="tpu_custom_call" | custom-call | flops 5368709120 | bytes 9437184 | tf_op jit(solution)/shard_map/pallas_call | solution.py:180
  392.4 9.4 %convolution_convert_fusion.2.refs_1_ = bf16[1024,4096]{1,0:T(8,128)(2,1)} fusion(bf16[512,4096]{1,0:T(8,128)(2,1)} %copy-done.85, f32[512,1024]{1,0:T(8,128)S(1)} %get-tuple-element.198, f32[1024]{0:T(1024)S(1)} %bitcast.154, f32[1024]{0:T(1024)S(1)} %bitcast.143, f32[512]{0:T(512)S(1)} %fusion.48, f32[512]{0:T(512)S(1)} %broadcast_multiply_fusion), kind=kOutput, calls=%fused_computation.22 | convolution fusion | flops 4301783040 | bytes 14692352 | tf_op jit(solution)/shard_map/dot_general | solution.py:60
  401.8 1.7 convert_select_fusion.1
  404.2 6.6 multiply_reduce_fusion.1
  412.0 15.4 %fusion.84 = (bf16[4096]{0:T(1024)(128)(2,1)S(1)}, bf16[512,4096]{1,0:T(8,128)(2,1)}) fusion(f32[512,4096]{1,0:T(8,128)} %fusion.60, f32[4096]{0:T(1024)S(1)} %get-tuple-element.182, bf16[1024,4096]{1,0:T(8,128)(2,1)} %get-tuple-element.46, f32[512,1024]{1,0:T(8,128)S(1)} %get-tuple-element.144), kind=kOutput, calls=%fused_computation.225 | convolution fusion | flops 4341624832 | bytes 23093248 | tf_op jit(solution)/shard_map/dot_general | solution.py:56
  427.4 8.7 %multiply_reduce_fusion.2 = (f32[1024]{0:T(1024)S(1)}, f32[512]{0:T(512)S(1)}, f32[1024]{0:T(1024)S(1)}, f32[512,1024]{1,0:T(8,128)S(1)}) fusion(f32[512,1024]{1,0:T(8,128)S(1)} %copy-done.22, f32[512]{0:T(512)S(1)} %fusion.46, f32[512]{0:T(512)S(1)} %broadcast_multiply_fusion.2, f32[1024]{0:T(1024)S(1)} %bitcast.137, ...), kind=kOutput, calls=%fused_computation.54 | convolution fusion | flops 4299159040 | bytes 16795648 | tf_op jit(solution)/shard_map/dot_general | solution.py:64
  436.1 9.6 %convolution_convert_fusion.refs_5_ = bf16[1024,4096]{1,0:T(8,128)(2,1)} fusion(bf16[512,4096]{1,0:T(8,128)(2,1)} %get-tuple-element.206, f32[512,1024]{1,0:T(8,128)S(1)} %copy-done.22, f32[1024]{0:T(1024)S(1)} %bitcast.152, f32[1024]{0:T(1024)S(1)} %bitcast.138, f32[512]{0:T(512)S(1)} %fusion.46, f32[512]{0:T(512)S(1)} %broadcast_multiply_fusion.2), kind=kOutput, calls=%fused_computation.20 | convolution fusion | flops 4301783040 | bytes 14692352 | tf_op jit(solution)/shard_map/dot_general | solution.py:60
  450.1 2.6 convolution_convert_fusion.8.refs_6_
  453.2 6.1 convolution_convert_fusion.5.refs_3_
  459.6 1.6 copy-done.1
  461.4 14.4 %shard_map.428 = bf16[1024,1536]{1,0:T(8,128)(2,1)S(1)} custom-call(f32[4]{0:T(128)S(1)} %dynamic_slice.55.slope_ref, s32[1024,1]{1,0:T(8,128)S(1)} %copy-done.8, s32[1,1024]{1,0:T(1,128)S(1)} %broadcast_select_fusion.18.drow_ref, bf16[1024,1536]{1,0:T(8,128)(2,1)S(1)} %copy-done.1, bf16[1024,512]{1,0:T(8,128)(2,1)S(1)} %copy-done.3, ...), custom_call_target="tpu_custom_call" | custom-call | flops 5368709120 | bytes 9437184 | tf_op jit(solution)/shard_map/pallas_call | solution.py:180
  476.2 11.4 %convolution_convert_fusion.1.refs_4_ = bf16[1024,4096]{1,0:T(8,128)(2,1)} fusion(f32[512,1024]{1,0:T(8,128)S(1)} %get-tuple-element.144, f32[512,4096]{1,0:T(8,128)} %fusion.60, f32[4096]{0:T(1024)S(1)} %get-tuple-element.182), kind=kOutput, calls=%fused_computation.21 | convolution fusion | flops 4320657408 | bytes 18890752 | tf_op jit(solution)/shard_map/dot_general | solution.py:60
  488.8 8.0 fusion.22
  496.8 5.9 convolution_convert_fusion.4.refs_7_
  503.7 192.9 %shard_map.429 = (f32[128,1024]{1,0:T(8,128)}, f32[128,1024]{1,0:T(8,128)}, f32[128,256]{1,0:T(8,128)}, f32[128,768]{1,0:T(8,128)}, f32[128,1024]{1,0:T(8,128)},...) custom-call(bf16[1024,4096]{1,0:T(8,128)(2,1)} %convolution_convert_, ...), custom_call_target="tpu_custom_call" | custom-call | tf_op jit(solution)/shard_map/pallas_call | solution.py:650
  699.2 1.7 multiply_reduce_fusion.14
  702.1 1.7 multiply_reduce_fusion.13
  703.8 1.9 copy.87
  705.8 2.5 fusion.73
  720.2 6.6 collective-permute-start.12
  726.9 37.1 %psum.7 = f32[]{:T(128)} all-reduce(f32[]{:T(128)S(6)} %add.395), channel_id=1, replica_groups=mesh['dp'=8,'mp'=4] {'dp','mp'}, use_global_device_ids=true, to_apply=%region_38.39 | all-reduce | flops 1 | bytes 8 | tf_op jit(solution)/shard_map/psum | solution.py:914
  764.7 3.3 multiply_subtract_fusion.2
  768.0 2.4 copy.104
  770.4 2.3 copy.105
  773.8 2.2 multiply_subtract_fusion.3
  776.0 1.8 copy.107
  777.8 1.8 copy.108
  779.6 1.8 copy.109
  781.3 4.2 multiply_subtract_fusion
  785.5 2.5 copy.110
  788.1 2.6 copy.111
  790.8 2.5 copy.112
  796.3 4.3 multiply_subtract_fusion.1
  800.7 2.9 convert_select_fusion
  (298 shorter events, 47.9 us)
Async XLA Ops:
  0.7 8.2 %copy-start.45 = (f32[2,256,128]{2,1,0:T(8,128)S(1)}, f32[2,256,128]{2,1,0:T(8,128)}, u32[]{:S(2)}) copy-start(f32[2,256,128]{2,1,0:T(8,128)} %param.31) | copy-start | bytes 786436
  0.7 9.1 %copy-start.76 = (f32[2,128]{1,0:T(2,128)S(1)}, f32[2,128]{1,0:T(2,128)}, u32[]{:S(2)}) copy-start(f32[2,128]{1,0:T(2,128)} %param.40) | copy-start | bytes 3076
  0.7 9.1 %copy-start.57 = (f32[2,3,128]{2,0,1:T(2,128)S(1)}, f32[2,3,128]{2,0,1:T(2,128)}, u32[]{:S(2)}) copy-start(f32[2,3,128]{2,0,1:T(2,128)} %param.46) | copy-start | bytes 9220
  0.7 9.1 %copy-start.61 = (f32[2,2,128]{2,1,0:T(2,128)S(1)}, f32[2,2,128]{2,1,0:T(2,128)}, u32[]{:S(2)}) copy-start(f32[2,2,128]{2,1,0:T(2,128)} %param.43) | copy-start | bytes 6148
  0.7 214.3 %collective-permute-start = (bf16[512,1024]{1,0:T(8,128)(2,1)}, bf16[512,1024]{1,0:T(8,128)(2,1)}, u32[]{:S(2)}, u32[]{:S(2)}) collective-permute-start(bf16[512,1024]{1,0:T(8,128)(2,1)} %param.25), channel_id=1, source_target_pairs={{1,4},{3,6},{4,1},{6,3},{9,12},{11,14},{12,9},{14,11},{17,20},{19,... | collective-permute-start | bytes 3145736 | tf_op jit(solution)/shard_map/ppermute | solution.py:734
  5.4 209.6 %collective-permute-start.7 = (bf16[512,1024]{1,0:T(8,128)(2,1)}, bf16[512,1024]{1,0:T(8,128)(2,1)}, u32[]{:S(2)}, u32[]{:S(2)}) collective-permute-start(bf16[512,1024]{1,0:T(8,128)(2,1)} %param.27), channel_id=1, source_target_pairs={{1,4},{3,6},{4,1},{6,3},{9,12},{11,14},{12,9},{14,11},{17,20},{19,... | collective-permute-start | bytes 3145736 | tf_op jit(solution)/shard_map/ppermute | solution.py:734
  13.0 200.7 %copy-start.16 = (f32[2,1024,128]{1,2,0:T(8,128)}, f32[2,1024,128]{1,2,0:T(8,128)S(1)}, u32[]{:S(2)}) copy-start(f32[2,1024,128]{1,2,0:T(8,128)S(1)} %copy.75) | copy-start | bytes 3145732
  14.9 200.1 %copy-start.36 = (bf16[512,1024]{1,0:T(8,128)(2,1)S(1)}, bf16[512,1024]{1,0:T(8,128)(2,1)}, u32[]{:S(2)}) copy-start(bf16[512,1024]{1,0:T(8,128)(2,1)} %param.25) | copy-start | bytes 3145732
  214.9 4.5 copy-start.55
  214.9 4.5 copy-start.63
  214.9 31.6 %copy-start.67 = (f32[1,1,1024]{2,1,0:T(1,128)}, f32[1,1,1024]{2,1,0:T(1,128)S(1)}, u32[]{:S(2)}) copy-start(f32[1,1,1024]{2,1,0:T(1,128)S(1)} %get-tuple-element.187) | copy-start | bytes 12292
  215.0 53.4 %copy-start.65 = (f32[1,1,1024]{2,1,0:T(1,128)}, f32[1,1,1024]{2,1,0:T(1,128)S(1)}, u32[]{:S(2)}) copy-start(f32[1,1,1024]{2,1,0:T(1,128)S(1)} %get-tuple-element.185) | copy-start | bytes 12292
  215.0 4.5 copy-start.80
  219.0 25.7 %copy-start.13 = (bf16[512,1024]{1,0:T(8,128)(2,1)}, bf16[512,1024]{1,0:T(8,128)(2,1)S(1)}, u32[]{:S(2)}) copy-start(bf16[512,1024]{1,0:T(8,128)(2,1)S(1)} %get-tuple-element.156) | copy-start | bytes 3145732
  219.0 4.7 copy-start.48
  219.4 4.3 copy-start.50
  219.4 4.3 copy-start.59
  226.6 3.8 collective-permute-start.2
  226.6 3.0 collective-permute-start.1
  233.0 9.4 %copy-start = (bf16[1024,1536]{1,0:T(8,128)(2,1)}, bf16[1024,1536]{1,0:T(8,128)(2,1)S(1)}, u32[]{:S(2)}) copy-start(bf16[1024,1536]{1,0:T(8,128)(2,1)S(1)} %pad_maximum_fusion.qkv_ref) | copy-start | bytes 9437188
  242.5 2.0 collective-permute-start.3
  246.1 11.0 %copy-start.21 = (f32[512,1024]{1,0:T(8,128)}, f32[512,1024]{1,0:T(8,128)S(1)}, u32[]{:S(2)}) copy-start(f32[512,1024]{1,0:T(8,128)S(1)} %get-tuple-element.194) | copy-start | bytes 6291460
  246.5 10.7 %copy-start.52 = (f32[512]{0:T(512)}, f32[512]{0:T(512)S(1)}, u32[]{:S(2)}) copy-start(f32[512]{0:T(512)S(1)} %multiply_reduce_fusion.8) | copy-start | bytes 6148
  268.0 7.4 copy-start.19
  275.5 3.5 collective-permute-start.4
  291.4 5.5 copy-start.46
  292.3 12.4 %collective-permute-start.5 = (bf16[512,512]{1,0:T(8,128)(2,1)}, bf16[512,512]{1,0:T(8,128)(2,1)}, u32[]{:S(2)}, u32[]{:S(2)}) collective-permute-start(bf16[512,512]{1,0:T(8,128)(2,1)} %constant_dynamic-slice_fusion.5), channel_id=1, source_target_pairs={{0,4},{4,0},{8,12},{12,8},{16,20},{20,16},{24,28},{28,24},{1,5},{5... | collective-permute-start | bytes 1572872 | tf_op jit(solution)/shard_map/ppermute | solution.py:717
  320.2 13.0 %copy-start.18 = (bf16[512,1024]{1,0:T(8,128)(2,1)S(1)}, bf16[512,1024]{1,0:T(8,128)(2,1)}, u32[]{:S(2)}) copy-start(bf16[512,1024]{1,0:T(8,128)(2,1)} %get-tuple-element.208) | copy-start | bytes 3145732
  346.4 9.7 %copy-start.85 = (bf16[512,4096]{1,0:T(8,128)(2,1)}, bf16[512,4096]{1,0:T(8,128)(2,1)S(1)}, u32[]{:S(2)}) copy-start(bf16[512,4096]{1,0:T(8,128)(2,1)S(1)} %get-tuple-element.146) | copy-start | bytes 12582916
  359.7 13.8 %copy-start.42 = (bf16[512,512]{1,0:T(8,128)(2,1)S(1)}, bf16[512,512]{1,0:T(8,128)(2,1)}, u32[]{:S(2)}) copy-start(bf16[512,512]{1,0:T(8,128)(2,1)} %copy-done.41) | copy-start | bytes 1572868
  359.7 16.5 %collective-permute-start.8 = (bf16[512,512]{1,0:T(8,128)(2,1)S(1)}, bf16[512,512]{1,0:T(8,128)(2,1)S(1)}, u32[]{:S(2)}, u32[]{:S(2)}) collective-permute-start(bf16[512,512]{1,0:T(8,128)(2,1)S(1)} %constant_dynamic-slice_fusion.4), channel_id=1, source_target_pairs={{0,4},{4,0},{8,12},{12,8},{16,20},{20,16},{24,28},{28,24},{1,5},{5... | collective-permute-start | bytes 1572872 | tf_op jit(solution)/shard_map/ppermute | solution.py:717
  371.6 30.2 %collective-permute-start.6 = (bf16[512,1024]{1,0:T(8,128)(2,1)}, bf16[512,1024]{1,0:T(8,128)(2,1)S(1)}, u32[]{:S(2)}, u32[]{:S(2)}) collective-permute-start(bf16[512,1024]{1,0:T(8,128)(2,1)} %get-tuple-element.199), channel_id=1, source_target_pairs={{1,4},{3,6},{4,1},{6,3},{9,12},{11,14},{12,9},{14,11},{17,20},{19,... | collective-permute-start | bytes 3145736 | tf_op jit(solution)/shard_map/ppermute | solution.py:839
  392.3 9.6 %copy-start.31 = (f32[512,1024]{1,0:T(8,128)S(1)}, f32[512,1024]{1,0:T(8,128)}, u32[]{:S(2)}) copy-start(f32[512,1024]{1,0:T(8,128)} %get-tuple-element.200) | copy-start | bytes 6291460
  392.3 11.2 %collective-permute-start.9 = (bf16[512,1536]{1,0:T(8,128)(2,1)S(1)}, bf16[512,1536]{1,0:T(8,128)(2,1)S(1)}, u32[]{:S(2)}, u32[]{:S(2)}) collective-permute-start(bf16[512,1536]{1,0:T(8,128)(2,1)S(1)} %constant_dynamic-slice_fusion.3), channel_id=1, source_target_pairs={{0,4},{4,0},{8,12},{12,8},{16,20},{20,16},{24,28},{28,24},{1,5},{5... | collective-permute-start | bytes 4718600 | tf_op jit(solution)/shard_map/ppermute | solution.py:717
  412.0 15.4 %copy-start.22 = (f32[512,1024]{1,0:T(8,128)S(1)}, f32[512,1024]{1,0:T(8,128)}, u32[]{:S(2)}) copy-start(f32[512,1024]{1,0:T(8,128)} %copy-done.21) | copy-start | bytes 6291460
  427.4 8.7 %copy-start.68 = (f32[1,1,1024]{2,1,0:T(1,128)S(1)}, f32[1,1,1024]{2,1,0:T(1,128)}, u32[]{:S(2)}) copy-start(f32[1,1,1024]{2,1,0:T(1,128)} %copy-done.67) | copy-start | bytes 12292
  436.1 9.6 %copy-start.53 = (f32[512]{0:T(512)S(1)}, f32[512]{0:T(512)}, u32[]{:S(2)}) copy-start(f32[512]{0:T(512)} %copy-done.52) | copy-start | bytes 6148
  452.7 6.5 collective-permute-start.10
  475.9 11.7 %collective-permute-start.11 = (bf16[512,1536]{1,0:T(8,128)(2,1)S(1)}, bf16[512,1536]{1,0:T(8,128)(2,1)S(1)}, u32[]{:S(2)}, u32[]{:S(2)}) collective-permute-start(bf16[512,1536]{1,0:T(8,128)(2,1)S(1)} %constant_dynamic-slice_fusion.1), channel_id=1, source_target_pairs={{0,4},{4,0},{8,12},{12,8},{16,20},{20,16},{24,28},{28,24},{1,5},{5... | collective-permute-start | bytes 4718600 | tf_op jit(solution)/shard_map/ppermute | solution.py:717
  488.8 8.0 copy-start.64
  496.8 5.9 copy-start.54
  496.8 6.1 copy-start.72
  696.5 9.2 %copy-start.51 = (f32[512]{0:T(512)S(1)}, f32[512]{0:T(512)}, u32[]{:S(2)}) copy-start(f32[512]{0:T(512)} %copy-done.50) | copy-start | bytes 6148
  696.6 9.2 %copy-start.15 = (bf16[512,1024]{1,0:T(8,128)(2,1)S(1)}, bf16[512,1024]{1,0:T(8,128)(2,1)}, u32[]{:S(2)}) copy-start(bf16[512,1024]{1,0:T(8,128)(2,1)} %copy-done.13) | copy-start | bytes 3145732
  705.8 4.6 copy-start.35
  705.8 5.4 copy-start.33
  708.3 4.3 copy-start.11
  712.5 52.2 %copy-start.47 = (f32[16,128]{1,0:T(8,128)S(1)}, f32[16,128]{1,0:T(8,128)}, u32[]{:S(2)}) copy-start(f32[16,128]{1,0:T(8,128)} %get-tuple-element.59) | copy-start | bytes 24580
  712.5 52.2 %copy-start.24 = (f32[2,128,3,256]{1,3,2,0:T(8,128)S(1)}, f32[2,128,3,256]{1,3,2,0:T(8,128)}, u32[]{:S(2)}) copy-start(f32[2,128,3,256]{1,3,2,0:T(8,128)} %copy-done.23) | copy-start | bytes 2359300
  720.2 80.4 %collective-permute-start.12 = (bf16[512,1024]{1,0:T(8,128)(2,1)}, bf16[512,1024]{1,0:T(8,128)(2,1)}, u32[]{:S(2)}, u32[]{:S(2)}) collective-permute-start(bf16[512,1024]{1,0:T(8,128)(2,1)} %fusion.38), channel_id=1, source_target_pairs={{1,4},{3,6},{4,1},{6,3},{9,12},{11,14},{12,9},{14,11},{17,20},{19,... | collective-permute-start | bytes 3145736 | tf_op jit(solution)/shard_map/ppermute | solution.py:877
  768.0 4.7 copy-start.27
  768.0 5.8 copy-start.30
  773.8 7.5 copy-start.17
  788.1 5.2 copy-start.58
  788.1 5.2 copy-start.69
  788.1 5.2 copy-start.70
  788.1 7.0 copy-start.77
  788.1 7.0 copy-start.78
  788.1 7.0 copy-start.79
  788.1 7.6 copy-start.62
  788.1 7.6 copy-start.73
  788.1 7.6 copy-start.74
  788.1 8.2 %copy-start.26 = (f32[2,128,1024]{2,1,0:T(8,128)S(1)}, f32[2,128,1024]{2,1,0:T(8,128)}, u32[]{:S(2)}) copy-start(f32[2,128,1024]{2,1,0:T(8,128)} %param.34) | copy-start | bytes 3145732
  796.3 4.3 copy-start.12
  (35 other events, 73.7 us)

commit v3 on v2

--- a/solution.py
+++ b/solution.py
@@ -191,6 +191,10 @@
     )(slopes, docs.reshape(-1, 1), docs.reshape(1, -1), qkv, o, do)
 
 
+def bits_of(size):
+    return [1 << at for at in range(size.bit_length() - 1)]
+
+
 def flip(value, mask):
     bit = 1
     while bit <= mask:
@@ -304,12 +308,33 @@
     return merge_small([steps[at] for at in ranked], plans)
 
 
-def greet(z, d, upper, mp_size):
+def forward_order(plans, layers, table):
+    steps = [(t, event) for t, plan in enumerate(plans) for event in plan.events]
+    compute = [(layer, name) for layer in range(layers) for name in FORWARD_STEPS]
+    if len(table) == len(steps) + len(compute):
+        steps += compute
+        return [steps[at] for at in table]
+    return steps + compute
+
+
+def greet(z, d, upper, mp_size, mp_bits=(), across=None, moved=None):
     barrier = pltpu.get_barrier_semaphore()
+    for bit in mp_bits:
+        pl.semaphore_signal(
+            barrier, inc=1, device_id={"mp": flip(z, bit)}, device_id_type=MESH
+        )
     for bit in [1] + upper:
         pl.semaphore_signal(
             barrier, inc=1, device_id={"dp": flip(d, bit)}, device_id_type=MESH
         )
+    also = 0
+    if across is not None:
+
+        @pl.when(moved)
+        def _():
+            pl.semaphore_signal(barrier, inc=1, device_id=across, device_id_type=MESH)
+
+        also = jnp.where(moved, 1, 0)
     for way in (1, -1):
 
         @pl.when((z + way >= 0) & (z + way < mp_size))
@@ -319,124 +344,142 @@
             )
 
     around = jnp.where(z > 0, 1, 0) + jnp.where(z < mp_size - 1, 1, 0)
-    pl.semaphore_wait(barrier, 1 + len(upper) + around)
-
-
-def spread_kernel(plans, order, mp_size, *refs):
-    n = len(plans)
-    shards, outs = refs[:n], refs[n : 2 * n]
-    send_sems, recv_sems, own_sems = refs[2 * n :]
-    z = lax.axis_index("mp")
-    d = lax.axis_index("dp")
-    upper = [dim for dim in plans[0].dims if dim != "mp"]
-    index, _ = number(plans, mp_size, spread_single)
-
-    def inside(at):
-        return (at >= 0) & (at < mp_size)
-
-    def region(t, mask, block):
-        wide, cols = shards[t].shape
-        rows = pl.ds(place(flip(d, mask), wide), wide)
+    pl.semaphore_wait(barrier, 1 + len(upper) + len(mp_bits) + around + also)
+
+
+class SpreadWork:
+    def __init__(self, plans, order, mp_size, shards, outs, send_sems, recv_sems, own_sems):
+        self.plans, self.mp_size = plans, mp_size
+        self.order = [step for step in order if not isinstance(step[1], str)]
+        self.shards, self.outs = shards, outs
+        self.sems = send_sems, recv_sems
+        self.own_sems = own_sems
+        self.z = lax.axis_index("mp")
+        self.d = lax.axis_index("dp")
+        self.upper = [dim for dim in plans[0].dims if dim != "mp"]
+        self.index, _ = number(plans, mp_size, spread_single)
+        self.owns = []
+        self.left = {}
+        for t, event in self.order:
+            if event[0] < len(plans[t].dims):
+                self.left[t, event[1]] = self.left.get((t, event[1]), 0) + 1
+
+    def inside(self, at):
+        return (at >= 0) & (at < self.mp_size)
+
+    def region(self, t, mask, block):
+        wide, cols = self.shards[t].shape
+        rows = pl.ds(place(flip(self.d, mask), wide), wide)
         if block is None:
-            return outs[t].at[rows, :]
-        return outs[t].at[rows, pl.ds(place(block, cols), cols)]
-
-    def remote(t, event, block, src, dst, to):
+            return self.outs[t].at[rows, :]
+        return self.outs[t].at[rows, pl.ds(place(block, cols), cols)]
+
+    def remote(self, t, event, block, src, dst, to):
         stage, mask, way, at = event
-        if way or stage == len(plans[t].dims):
-            sem = index[(t,) + event]
+        if way or stage == len(self.plans[t].dims):
+            sem = self.index[(t,) + event]
         else:
-            sem = index[t, stage, mask] + block
+            sem = self.index[t, stage, mask] + block
         return pltpu.make_async_remote_copy(
             src_ref=src,
             dst_ref=dst,
-            send_sem=send_sems.at[sem],
-            recv_sem=recv_sems.at[sem],
+            send_sem=self.sems[0].at[sem],
+            recv_sem=self.sems[1].at[sem],
             device_id=to,
             device_id_type=MESH,
         )
 
-    def sending(t, event, block, to, own=False):
+    def sending(self, t, event, block, to, own=False):
         stage, mask, way, at = event
-        dims = plans[t].dims
+        dims = self.plans[t].dims
         bit = 0 if way else 1 if stage == len(dims) else dims[stage]
-        dst = region(t, mask ^ bit, block)
-        return remote(t, event, block, shards[t] if own else dst, dst, to)
-
-    def arrival(t, event, block):
-        dst = region(t, event[1], block)
-        return remote(t, event, block, dst, dst, {"dp": d, "mp": z})
-
-    def on_line(t, stage, mask, block, way, hops, own):
-        @pl.when(inside(z + way))
+        dst = self.region(t, mask ^ bit, block)
+        return self.remote(t, event, block, self.shards[t] if own else dst, dst, to)
+
+    def arrival(self, t, event, block):
+        dst = self.region(t, event[1], block)
+        return self.remote(t, event, block, dst, dst, {"dp": self.d, "mp": self.z})
+
+    def on_line(self, t, stage, mask, block, way, hops, own):
+        @pl.when(self.inside(self.z + way))
         def _():
-            sending(t, (stage, mask, way, hops), block, {"mp": z + way}, own).start()
-
-    def onward(t, stage, mask, block, own=False):
-        dims = plans[t].dims
+            to = {"mp": self.z + way}
+            self.sending(t, (stage, mask, way, hops), block, to, own).start()
+
+    def onward(self, t, stage, mask, block, own=False):
+        dims = self.plans[t].dims
         for later in range(stage, len(dims)):
             if dims[later] == "mp":
                 for way in (1, -1):
-                    on_line(t, later, mask, block, way, 1, own)
+                    self.on_line(t, later, mask, block, way, 1, own)
             else:
-                to = {"dp": flip(d, dims[later])}
-                sending(t, (later, mask | dims[later], 0, None), block, to, own).start()
-
-    greet(z, d, upper, mp_size)
-    owns = []
-    for t in range(n):
-        onward(t, 0, 0, z, True)
-        owns.append(pltpu.make_async_copy(shards[t], region(t, 0, z), own_sems.at[t]))
-        owns[t].start()
-
-    left = {}
+                to = {"dp": flip(self.d, dims[later])}
+                self.sending(t, (later, mask | dims[later], 0, None), block, to, own).start()
+
+    def place_of(self, t, event):
+        return flip(self.z, event[3]) if self.plans[t].full(event[0]) else self.z
+
+    def begin(self):
+        for t in range(len(self.plans)):
+            self.onward(t, 0, 0, self.z, True)
+            own = pltpu.make_async_copy(
+                self.shards[t], self.region(t, 0, self.z), self.own_sems.at[t]
+            )
+            own.start()
+            self.owns.append(own)
+
+    def step(self, t, event):
+        stage, mask, way, at = event
+        last = len(self.plans[t].dims)
+        if stage == last:
+            self.arrival(t, event, None).wait_recv()
+            return
+        if way:
+            block = self.z - way * at
+
+            @pl.when(self.inside(block))
+            def _():
+                self.arrival(t, event, block).wait_recv()
+                if at + 1 < self.mp_size:
+                    self.on_line(t, stage, mask, block, way, at + 1, False)
+                self.onward(t, stage + 1, mask, block)
+
+        else:
+            block = self.place_of(t, event)
+            self.arrival(t, event, block).wait_recv()
+            self.onward(t, stage + 1, mask, block)
+        self.left[t, mask] -= 1
+        if self.left[t, mask] == 0:
+            if mask == 0:
+                self.owns[t].wait()
+            to = {"dp": flip(self.d, 1)}
+            self.sending(t, (last, mask | 1, 0, 0), None, to).start()
+
+    def finish(self):
+        for t, event in self.order:
+            stage, mask, way, at = event
+            if stage == len(self.plans[t].dims):
+                self.sending(t, event, None, {"dp": flip(self.d, 1)}).wait_send()
+            elif way:
+
+                @pl.when(self.inside(self.z - way * (at - 1)) & self.inside(self.z + way))
+                def _():
+                    to = {"mp": self.z + way}
+                    self.sending(t, event, self.z - way * (at - 1), to).wait_send()
+
+            else:
+                to = {"dp": flip(self.d, self.plans[t].dims[stage])}
+                self.sending(t, event, self.place_of(t, event), to).wait_send()
+
+
+def spread_kernel(plans, order, mp_size, *refs):
+    n = len(plans)
+    work = SpreadWork(plans, order, mp_size, refs[:n], refs[n : 2 * n], *refs[2 * n :])
+    greet(work.z, work.d, work.upper, mp_size)
+    work.begin()
     for t, event in order:
-        if event[0] < len(plans[t].dims):
-            left[t, event[1]] = left.get((t, event[1]), 0) + 1
-
-    def place_of(t, event):
-        stage, mask, way, at = event
-        return flip(z, at) if plans[t].full(stage) else z
-
-    for t, event in order:
-        stage, mask, way, at = event
-        last = len(plans[t].dims)
-        if stage == last:
-            arrival(t, event, None).wait_recv()
-            continue
-        if way:
-            block = z - way * at
-
-            @pl.when(inside(block))
-            def _():
-                arrival(t, event, block).wait_recv()
-                if at + 1 < mp_size:
-                    on_line(t, stage, mask, block, way, at + 1, False)
-                onward(t, stage + 1, mask, block)
-
-        else:
-            block = place_of(t, event)
-            arrival(t, event, block).wait_recv()
-            onward(t, stage + 1, mask, block)
-        left[t, mask] -= 1
-        if left[t, mask] == 0:
-            if mask == 0:
-                owns[t].wait()
-            sending(t, (last, mask | 1, 0, 0), None, {"dp": flip(d, 1)}).start()
-
-    for t, event in order:
-        stage, mask, way, at = event
-        if stage == len(plans[t].dims):
-            sending(t, event, None, {"dp": flip(d, 1)}).wait_send()
-        elif way:
-
-            @pl.when(inside(z - way * (at - 1)) & inside(z + way))
-            def _():
-                sending(t, event, z - way * (at - 1), {"mp": z + way}).wait_send()
-
-        else:
-            to = {"dp": flip(d, plans[t].dims[stage])}
-            sending(t, event, place_of(t, event), to).wait_send()
+        work.step(t, event)
+    work.finish()
 
 
 def spread_all(shards, plans, order, dp_size, mp_size):
@@ -458,16 +501,18 @@
     )(*shards)
 
 
-def fold_kernel(plans, order, mp_size, *refs):
+def fold_kernel(plans, order, mp_size, vector_count, *refs):
     n = len(plans)
-    grads, outs, landed, sums = (refs[at * n : (at + 1) * n] for at in range(4))
-    at = 4 * n
+    grads, outs = refs[:n], refs[n : 2 * n]
+    norm_ref = refs[2 * n]
+    landed, sums = refs[2 * n + 1 : 3 * n + 1], refs[3 * n + 1 : 4 * n + 1]
+    at = 4 * n + 1
     recv = {}
     for t, plan in enumerate(plans):
         for stage in range(1, len(plan.dims) + 1):
             recv[t, stage] = refs[at]
             at += 1
-    staging, load_sems, own_sems, send_sems, recv_sems = refs[at:]
+    staging, tiles, load_sems, own_sems, tile_sems, send_sems, recv_sems = refs[at:]
     z = lax.axis_index("mp")
     d = lax.axis_index("dp")
     upper = [dim for dim in plans[0].dims if dim != "mp"]
@@ -560,7 +605,8 @@
         elif mask & dim:
             bit_copy(t, stage, mask, block).start()
 
-    greet(z, d, upper, mp_size)
+    mp_bits = bits_of(mp_size)
+    greet(z, d, upper, mp_size, mp_bits)
     cores = [(t, event[1]) for t, event in order if event[0] == 0]
     for t, mask in cores:
         core_copy(t, mask).start()
@@ -611,8 +657,47 @@
             add(sum_at(t, mask, block), landing(t, event, block), wides[t])
             advance(t, stage + 1, mask, block, at)
 
+    tiles[0] = jnp.zeros(tiles.shape[1:], f32)
     for t in range(n):
-        outs[t][...] = sum_at(t, 0, z)[...].astype(f32)
+        step = 16
+
+        def some_rows(at, carry, t=t):
+            rows = pl.ds(pl.multiple_of(at * step, step), step)
+            part = sums[t][rows, pl.ds(place(z, cols[t]), cols[t])].astype(f32)
+            outs[t][rows, :] = part
+            part = part * part
+            total = carry
+            for low in range(0, step, 8):
+                for left in range(0, cols[t], HD):
+                    total = total + part[low : low + 8, left : left + HD]
+            return total
+
+        if t == n - 1:
+            whole = sums[t][pl.ds(0, wides[t]), pl.ds(place(z, cols[t]), cols[t])].astype(f32)
+            outs[t][...] = whole
+            row = lax.broadcasted_iota(jnp.int32, whole.shape, 0)
+            whole = whole * whole
+            whole = jnp.where(row < vector_count, whole * (1.0 / mp_size), whole)
+            for low in range(0, wides[t], 8):
+                tiles[0] += whole[low : low + 8, :HD]
+        else:
+            zero = jnp.zeros((8, HD), f32)
+            tiles[0] += lax.fori_loop(0, wides[t] // step, some_rows, zero)
+    pairs = [{"dp": flip(d, bit)} for bit in [1] + upper]
+    pairs += [{"mp": flip(z, bit)} for bit in mp_bits]
+    for at, to in enumerate(pairs):
+        exchange = pltpu.make_async_remote_copy(
+            src_ref=tiles.at[2 * at],
+            dst_ref=tiles.at[2 * at + 1],
+            send_sem=tile_sems.at[2 * at],
+            recv_sem=tile_sems.at[2 * at + 1],
+            device_id=to,
+            device_id_type=MESH,
+        )
+        exchange.start()
+        exchange.wait()
+        tiles[2 * at + 2] = tiles[2 * at] + tiles[2 * at + 1]
+    norm_ref[...] = tiles[2 * len(pairs)]
 
     for t, event in order:
         stage, mask, way, at = event
@@ -629,11 +714,12 @@
             bit_copy(t, stage, mask | plans[t].dims[stage - 1], block).wait_send()
 
 
-def fold_all(grads, plans, order, dp_size, mp_size):
+def fold_all(grads, plans, order, dp_size, mp_size, vector_count):
     n = len(grads)
     _, total = number(plans, mp_size, fold_single)
     wides = [g.shape[0] // dp_size for g in grads]
     cols = [g.shape[1] // mp_size for g in grads]
+    rounds = len(bits_of(dp_size)) + len(bits_of(mp_size))
     halves = [(dp_size // 2 * wide, mp_size * each) for wide, each in zip(wides, cols)]
     scratch = [pltpu.VMEM(half, bf16) for half in halves]
     for plan, wide, each in zip(plans, wides, cols):
@@ -642,36 +728,477 @@
             scratch.append(pltpu.VMEM((len(plan.kept[stage]), blocks, wide, each), bf16))
     scratch += [
         pltpu.VMEM((2, max(wides), mp_size * max(cols)), bf16),
+        pltpu.VMEM((2 * rounds + 1, 8, HD), f32),
         pltpu.SemaphoreType.DMA((2,)),
         pltpu.SemaphoreType.DMA((n, dp_size // 2)),
+        pltpu.SemaphoreType.DMA((2 * rounds,)),
         pltpu.SemaphoreType.DMA((total,)),
         pltpu.SemaphoreType.DMA((total,)),
     ]
     out = pl.pallas_call(
-        functools.partial(fold_kernel, plans, order, mp_size),
+        functools.partial(fold_kernel, plans, order, mp_size, vector_count),
         out_shape=[jax.ShapeDtypeStruct((wide, each), f32) for wide, each in zip(wides, cols)]
+        + [jax.ShapeDtypeStruct((8, HD), f32)]
         + [jax.ShapeDtypeStruct(half, bf16) for half in halves],
         in_specs=[pl.BlockSpec(memory_space=pl.ANY)] * n,
-        out_specs=[pl.BlockSpec(memory_space=pltpu.VMEM)] * n
+        out_specs=[pl.BlockSpec(memory_space=pltpu.VMEM)] * (n + 1)
         + [pl.BlockSpec(memory_space=pl.ANY)] * n,
         scratch_shapes=scratch,
         compiler_params=pltpu.CompilerParams(
             collective_id=1, has_side_effects=True, vmem_limit_bytes=63 * 2**20
         ),
     )(*grads)
-    return list(out[:n])
-
-
-spread_table = (
-    45, 0, 46, 22, 23, 94, 116, 1, 95, 117, 2, 3, 25, 119, 118, 24, 97, 120, 26, 4, 96, 47, 71, 5,
-    27, 69, 140, 165, 28, 7, 44, 6, 121, 99, 98, 125, 48, 30, 51, 8, 70, 122, 76, 72, 53, 128, 77,
-    33, 34, 78, 50, 9, 112, 35, 129, 15, 123, 107, 29, 104, 73, 124, 79, 103, 101, 102, 52, 31,
-    54, 80, 127, 49, 81, 139, 56, 19, 75, 106, 57, 74, 164, 60, 126, 141, 142, 40, 55, 100, 88,
-    87, 105, 166, 167, 138, 12, 144, 136, 83, 111, 38, 113, 168, 82, 134, 13, 59, 169, 66, 184,
-    64, 143, 163, 86, 32, 146, 16, 159, 18, 89, 176, 85, 41, 110, 58, 10, 151, 42, 145, 84, 61,
-    148, 93, 11, 63, 39, 37, 131, 65, 130, 36, 17, 170, 154, 114, 147, 171, 62, 132, 152, 108,
-    109, 20, 177, 91, 150, 172, 153, 135, 149, 14, 179, 68, 178, 90, 173, 175, 174, 180, 161, 43,
-    160, 182, 156, 181, 133, 92, 155, 67, 157, 158, 115, 21, 186, 185, 137, 183, 162, 187,
+    return list(out[:n]), out[n]
+
+
+def adam_kernel(
+    factor_ref, qkv_1, qkv_0, proj_1, proj_0, upper_1, upper_0, lower_1, lower_0, *refs
+):
+    factor = factor_ref[0, 0]
+    ins, outs = refs[:12], refs[12:]
+
+    def update(group, at, gradient):
+        found = [ins[3 * group + which][at] for which in range(3)]
+        new = adam_update(
+            *found, gradient, factor, group_rates[group], group_decays[group]
+        )
+        for which in range(3):
+            outs[3 * group + which][at] = new[which]
+
+    for layer, gradient in enumerate((qkv_0, qkv_1)):
+        wide, cols = gradient.shape[0], gradient.shape[1] // 3
+        for part in range(3):
+            for low in range(0, wide, 64):
+                update(
+                    0,
+                    (layer, part, slice(low, low + 64)),
+                    gradient[low : low + 64, part * cols : (part + 1) * cols],
+                )
+    for layer, gradient in enumerate((proj_0, proj_1)):
+        for low in range(0, gradient.shape[1], HD):
+            update(1, (layer, slice(low, low + HD)), gradient[:, low : low + HD].T)
+    for layer, gradient in enumerate((upper_0, upper_1)):
+        for low in range(0, gradient.shape[0], 16):
+            update(2, (layer, slice(low, low + 16)), gradient[low : low + 16, :])
+    for layer, gradient in enumerate((lower_0, lower_1)):
+        for low in range(0, gradient.shape[1], HD):
+            update(3, (layer, slice(low, low + HD)), gradient[:, low : low + HD].T)
+
+
+def adam_all(factor, gradients, states):
+    vmem = pl.BlockSpec(memory_space=pltpu.VMEM)
+    return pl.pallas_call(
+        adam_kernel,
+        out_shape=[jax.ShapeDtypeStruct(state.shape, f32) for state in states],
+        in_specs=[pl.BlockSpec(memory_space=pltpu.SMEM)] + [vmem] * (8 + len(states)),
+        out_specs=[vmem] * len(states),
+        compiler_params=pltpu.CompilerParams(vmem_limit_bytes=60 * 2**20),
+    )(factor.reshape(1, 1), *gradients, *states)
+
+
+ROWS = 64
+TILE = 256
+
+
+def norm_rows(src, dst, gain, shift):
+    def some_rows(at, carry):
+        rows = pl.ds(pl.multiple_of(at * ROWS, ROWS), ROWS)
+        dst[rows, :] = layer_norm(src[rows, :], gain, shift).astype(bf16)
+        return carry
+
+    lax.fori_loop(0, src.shape[0] // ROWS, some_rows, 0)
+
+
+def tiles_of(width, body):
+    def one(at, carry):
+        body(pl.multiple_of(at * TILE, TILE))
+        return carry
+
+    lax.fori_loop(0, width // TILE, one, 0)
+
+
+def attend_head(qkv, out, at, width, out_at, slope, doc_cols, doc_rows):
+    length = qkv.shape[0]
+    block = min(256, length)
+    for first_row in range(0, length, block):
+        low, high = key_range(first_row, block)
+        scores = masked_scores(
+            slope,
+            doc_cols[first_row : first_row + block, :],
+            doc_rows[:, low:high],
+            qkv[first_row : first_row + block, at : at + HD],
+            qkv[low:high, at + width : at + width + HD],
+            first_row,
+            low,
+        )
+        shifted = jnp.exp(scores - jnp.max(scores, axis=-1, keepdims=True))
+        total = jnp.sum(shifted, axis=-1, keepdims=True)
+        prob_low = (shifted * (1.0 / total)).astype(bf16)
+        value = qkv[low:high, at + 2 * width : at + 2 * width + HD]
+        out[first_row : first_row + block, out_at : out_at + HD] = dot(prob_low, value).astype(bf16)
+
+
+FORWARD_STEPS = (
+    ("norm_one", "other_0", "other_1", "own_0", "own_1", "share")
+    + tuple(f"head_{at}" for at in range(4))
+    + ("back", "proj", "norm_two")
+    + tuple(f"up_{at}" for at in range(8))
+    + tuple(f"down_{at}" for at in range(4))
+)
+
+
+def forward_kernel(plans, order, mp_size, layers, vector_count, gain_rows, shift_rows, *refs):
+    n = len(plans)
+    shards = refs[:n]
+    inputs, doc_cols, doc_rows = refs[n : n + 3]
+    outs = refs[n + 3 : 2 * n + 3]
+    at = 2 * n + 3
+    saved = [refs[at + 9 * layer : at + 9 * layer + 9] for layer in range(layers)]
+    at += 9 * layers
+    last_stream = refs[at]
+    (
+        streams, middles, normed_one, normed_two, send_buf, qkv_full, mixed, attended,
+        hidden, active, w_qkv, w_proj, w_up, w_down, small_buf, vectors, biases, traded,
+        load_sems, save_sems, trade_sems, head_sems, send_sems, recv_sems, own_sems,
+    ) = refs[at + 1 :]
+    work = SpreadWork(plans, order, mp_size, shards, outs, send_sems, recv_sems, own_sems)
+    z, d = work.z, work.d
+    core = d % 2
+    moved = core != z % 2
+    partner = {"dp": flip(d, 1)}
+    across = {"dp": flip(d, 1), "mp": flip(z, 1)}
+    tokens = inputs.shape[0]
+    features = inputs.shape[1]
+    half = attended.shape[2] // 2
+    wide_small = shards[-1].shape[0]
+    lanes = shards[-1].shape[1]
+    third = w_qkv.shape[2] // 3
+    slots = qkv_full.shape[2] // w_qkv.shape[2]
+    heads_slot = third // HD
+
+    greet(z, d, work.upper, mp_size, (), across, moved)
+    trade = pltpu.make_async_remote_copy(
+        src_ref=inputs, dst_ref=traded, send_sem=trade_sems.at[0], recv_sem=trade_sems.at[1],
+        device_id=across, device_id_type=MESH,
+    )
+    keep = pltpu.make_async_copy(inputs, traded, trade_sems.at[2])
+
+    @pl.when(moved)
+    def _():
+        trade.start()
+
+    @pl.when(jnp.logical_not(moved))
+    def _():
+        keep.start()
+
+    work.begin()
+
+    saves = []
+
+    def save(src, dst):
+        copy = pltpu.make_async_copy(src, dst, save_sems.at[len(saves)])
+        copy.start()
+        saves.append(copy)
+        return copy
+
+    loads = {}
+
+    def load(key, src, dst, slot):
+        copy = pltpu.make_async_copy(src, dst, load_sems.at[slot])
+        copy.start()
+        loads[key] = copy
+
+    def load_tile(layer, kind, at):
+        full = outs[4 * layer : 4 * layer + 4]
+        if kind == "qkv":
+            cols = w_qkv.shape[2]
+            first = (1 - core) * slots if at < slots else core * slots
+            where = pl.ds(place(first + at % slots, cols), cols)
+            load((layer, kind, at), full[0].at[:, where], w_qkv.at[at % 2], at % 2)
+        elif kind == "proj":
+            load((layer, kind, at), full[1], w_proj, 2)
+        elif kind == "up":
+            cols = w_up.shape[2]
+            where = pl.ds(at * cols, cols)
+            load((layer, kind, at), full[2].at[:, where], w_up.at[at % 2], 3 + at % 2)
+        else:
+            rows = w_down.shape[1]
+            where = pl.ds(at * rows, rows)
+            load((layer, kind, at), full[3].at[where, :], w_down.at[at % 2], 5 + at % 2)
+
+    def tile(layer, kind, at, count):
+        if (layer, kind, at) not in loads:
+            load_tile(layer, kind, at)
+        loads[layer, kind, at].wait()
+        if at + 1 < count:
+            load_tile(layer, kind, at + 1)
+
+    def share_copy(layer):
+        rows = pl.ds(place(core, tokens), tokens)
+        return pltpu.make_async_remote_copy(
+            src_ref=send_buf.at[layer], dst_ref=qkv_full.at[layer, rows, :],
+            send_sem=head_sems.at[4 * layer], recv_sem=head_sems.at[4 * layer + 1],
+            device_id=partner, device_id_type=MESH,
+        )
+
+    def back_copy(layer):
+        rows = pl.ds(place(1 - core, tokens), tokens)
+        return pltpu.make_async_remote_copy(
+            src_ref=mixed.at[layer, rows, :],
+            dst_ref=attended.at[layer, :, pl.ds(place(core, half), half)],
+            send_sem=head_sems.at[4 * layer + 2], recv_sem=head_sems.at[4 * layer + 3],
+            device_id=partner, device_id_type=MESH,
+        )
+
+    def vector(at):
+        return vectors[at : at + 1, :]
+
+    ahead = {
+        "norm_one": ("qkv", 0), "head_0": ("proj", 1), "proj": ("up", 2), "up_6": ("down", 3)
+    }
+
+    def compute(layer, name):
+        kind, _, at = name.partition("_")
+        if name in ahead and 4 * layer + ahead[name][1] not in missing:
+            load_tile(layer, ahead[name][0], 0)
+        gain = layer * gain_rows
+        shift = layers * gain_rows + layer * shift_rows
+        keeps = saved[layer]
+        if name == "norm_one":
+            if layer == 0:
+                small = pltpu.make_async_copy(outs[-1], small_buf, load_sems.at[7])
+                small.start()
+
+                @pl.when(moved)
+                def _():
+                    trade.wait_recv()
+
+                @pl.when(jnp.logical_not(moved))
+                def _():
+                    keep.wait()
+
+                streams[0] = traded[...].astype(f32)
+                small.wait()
+                for b in range(outs[-1].shape[0] // wide_small):
+                    rows = small_buf[b * wide_small : (b + 1) * wide_small, :].astype(f32)
+                    vectors[:, b * lanes : (b + 1) * lanes] = rows[:, :lanes]
+                    for m in range(mp_size):
+                        first = m * (biases.shape[1] // mp_size) + b * lanes
+                        biases[:, first : first + lanes] = rows[:, m * lanes : (m + 1) * lanes]
+            norm_rows(streams.at[layer], normed_one.at[layer], vector(gain), vector(shift))
+            save(streams.at[layer], keeps[0])
+            save(normed_one.at[layer], keeps[2])
+        elif kind in ("other", "own"):
+            at = int(at)
+            tile(layer, "qkv", at + (slots if kind == "own" else 0), 2 * slots)
+            weight = w_qkv.at[at % 2]
+            cols = w_qkv.shape[2]
+
+            def piece(first):
+                values = dot(normed_one[layer], weight[:, pl.ds(first, TILE)]).astype(bf16)
+                to = pl.ds(pl.multiple_of(at * cols + first, TILE), TILE)
+                if kind == "own":
+                    qkv_full[layer, pl.ds(place(core, tokens), tokens), to] = values
+                else:
+                    send_buf[layer, :, to] = values
+
+            tiles_of(cols, piece)
+            if kind == "other" and at == slots - 1:
+                share_copy(layer).start()
+        elif kind == "share":
+            arrived = pltpu.make_async_remote_copy(
+                src_ref=send_buf.at[layer],
+                dst_ref=qkv_full.at[layer, pl.ds(place(1 - core, tokens), tokens), :],
+                send_sem=head_sems.at[4 * layer], recv_sem=head_sems.at[4 * layer + 1],
+                device_id=partner, device_id_type=MESH,
+            )
+            arrived.wait_recv()
+            save(qkv_full.at[layer], keeps[3])
+        elif kind == "head":
+            head = int(at)
+            slot, place_in = head // heads_slot, head % heads_slot
+            slope = 0.5 ** (head + 1.0) * jnp.where(core == 0, 1.0, 0.5 ** (slots * heads_slot))
+            attend_head(
+                qkv_full.at[layer], mixed.at[layer], slot * 3 * third + place_in * HD, third,
+                head * HD, slope, doc_cols, doc_rows,
+            )
+            if head == slots * heads_slot - 1:
+                back_copy(layer).start()
+                rows = pl.ds(place(core, tokens), tokens)
+                attended[layer, :, pl.ds(place(core, half), half)] = mixed[layer, rows, :]
+                save(mixed.at[layer], keeps[4])
+        elif kind == "back":
+            arrived = pltpu.make_async_remote_copy(
+                src_ref=mixed.at[layer, pl.ds(0, tokens), :],
+                dst_ref=attended.at[layer, :, pl.ds(place(1 - core, half), half)],
+                send_sem=head_sems.at[4 * layer + 2], recv_sem=head_sems.at[4 * layer + 3],
+                device_id=partner, device_id_type=MESH,
+            )
+            arrived.wait_recv()
+            save(attended.at[layer], keeps[5])
+        elif kind == "proj":
+            tile(layer, "proj", 0, 1)
+
+            def piece(first):
+                cols = pl.ds(first, TILE)
+                values = dot_cols(attended[layer], w_proj[cols, :])
+                middles[layer, :, cols] = streams[layer, :, cols] + values
+
+            tiles_of(features, piece)
+        elif name == "norm_two":
+            norm_rows(
+                middles.at[layer], normed_two.at[layer], vector(gain + 1), vector(shift + 1)
+            )
+            save(middles.at[layer], keeps[1])
+            save(normed_two.at[layer], keeps[6])
+        elif kind == "up":
+            at = int(at)
+            if at == 0 and layer > 0:
+                for copy in big_saves[layer - 1]:
+                    copy.wait()
+            cols = w_up.shape[2]
+            tile(layer, "up", at, hidden.shape[1] // cols)
+            weight = w_up.at[at % 2]
+
+            def piece(first):
+                to = pl.ds(pl.multiple_of(at * cols + first, TILE), TILE)
+                bias = biases[vector_count + layer : vector_count + layer + 1, to]
+                values = dot(normed_two[layer], weight[:, pl.ds(first, TILE)]) + bias
+                hidden[:, to] = values.astype(bf16)
+                active[:, to] = gelu_tanh(values).astype(bf16)
+
+            tiles_of(cols, piece)
+            if (at + 1) * cols == hidden.shape[1]:
+                big_saves[layer] = [save(hidden, keeps[7]), save(active, keeps[8])]
+        elif kind == "down":
+            at = int(at)
+            rows = w_down.shape[1]
+            tile(layer, "down", at, features // rows)
+            weight = w_down.at[at % 2]
+            out = streams.at[layer + 1]
+            cols = pl.ds(at * rows, rows)
+            out[:, cols] = middles[layer, :, cols] + vector(shift + 2)[:, at * rows : (at + 1) * rows]
+
+            def piece(step, carry):
+                inner = pl.ds(pl.multiple_of(step * 1024, 1024), 1024)
+                out[:, cols] += dot_cols(active[:, inner], weight[:, inner])
+                return carry
+
+            lax.fori_loop(0, hidden.shape[1] // 1024, piece, 0)
+
+    big_saves = {}
+    missing = {}
+    for t, _ in work.order:
+        missing[t] = missing.get(t, 0) + 1
+    for step in order:
+        if isinstance(step[1], str):
+            compute(*step)
+        else:
+            work.step(*step)
+            missing[step[0]] -= 1
+            if missing[step[0]] == 0:
+                del missing[step[0]]
+    save(streams.at[layers], last_stream)
+    done_already = [id(copy) for layer in range(layers - 1) for copy in big_saves[layer]]
+    for copy in saves:
+        if id(copy) not in done_already:
+            copy.wait()
+    for layer in range(layers):
+        share_copy(layer).wait_send()
+        back_copy(layer).wait_send()
+
+    @pl.when(moved)
+    def _():
+        trade.wait_send()
+
+    work.finish()
+
+
+def forward_all(
+    shards, inputs, docs, plans, order, dp_size, mp_size, layers, vector_count, gain_rows, shift_rows
+):
+    _, total = number(plans, mp_size, spread_single)
+    tokens, features = inputs.shape
+    length = docs.shape[0]
+    half = features // 2
+    units = shards[2].shape[1] * mp_size
+    cols = shards[0].shape[1]
+    slots = mp_size // 2
+    any_place = pl.BlockSpec(memory_space=pl.ANY)
+    vmem = pl.BlockSpec(memory_space=pltpu.VMEM)
+    saved = [
+        jax.ShapeDtypeStruct((tokens, features), f32),
+        jax.ShapeDtypeStruct((tokens, features), f32),
+        jax.ShapeDtypeStruct((tokens, features), bf16),
+        jax.ShapeDtypeStruct((length, slots * cols), bf16),
+        jax.ShapeDtypeStruct((length, half), bf16),
+        jax.ShapeDtypeStruct((tokens, features), bf16),
+        jax.ShapeDtypeStruct((tokens, features), bf16),
+        jax.ShapeDtypeStruct((tokens, units), bf16),
+        jax.ShapeDtypeStruct((tokens, units), bf16),
+    ]
+    small_shape = (shards[-1].shape[0] * dp_size, shards[-1].shape[1] * mp_size)
+    out_shape = [
+        jax.ShapeDtypeStruct((s.shape[0] * dp_size, s.shape[1] * mp_size), s.dtype)
+        for s in shards
+    ]
+    out_shape += saved * layers + [jax.ShapeDtypeStruct((tokens, features), f32)]
+    out = pl.pallas_call(
+        functools.partial(
+            forward_kernel, plans, order, mp_size, layers, vector_count, gain_rows, shift_rows
+        ),
+        out_shape=out_shape,
+        in_specs=[any_place] * (len(shards) + 1) + [vmem] * 2,
+        out_specs=[any_place] * len(out_shape),
+        scratch_shapes=[
+            pltpu.VMEM((layers + 1, tokens, features), f32),
+            pltpu.VMEM((layers, tokens, features), f32),
+            pltpu.VMEM((layers, tokens, features), bf16),
+            pltpu.VMEM((layers, tokens, features), bf16),
+            pltpu.VMEM((layers, tokens, slots * cols), bf16),
+            pltpu.VMEM((layers, length, slots * cols), bf16),
+            pltpu.VMEM((layers, length, half), bf16),
+            pltpu.VMEM((layers, tokens, features), bf16),
+            pltpu.VMEM((tokens, units), bf16),
+            pltpu.VMEM((tokens, units), bf16),
+            pltpu.VMEM((2, features, cols), bf16),
+            pltpu.VMEM((features, features), bf16),
+            pltpu.VMEM((2, features, units // 8), bf16),
+            pltpu.VMEM((2, features // 4, units), bf16),
+            pltpu.VMEM(small_shape, bf16),
+            pltpu.VMEM((shards[-1].shape[0], features), f32),
+            pltpu.VMEM((shards[-1].shape[0], units), f32),
+            pltpu.VMEM((tokens, features), bf16),
+            pltpu.SemaphoreType.DMA((8,)),
+            pltpu.SemaphoreType.DMA((9 * layers + 1,)),
+            pltpu.SemaphoreType.DMA((3,)),
+            pltpu.SemaphoreType.DMA((4 * layers,)),
+            pltpu.SemaphoreType.DMA((total,)),
+            pltpu.SemaphoreType.DMA((total,)),
+            pltpu.SemaphoreType.DMA((len(shards),)),
+        ],
+        compiler_params=pltpu.CompilerParams(
+            collective_id=2, has_side_effects=True, vmem_limit_bytes=62 * 2**20
+        ),
+    )(*shards, inputs, docs.reshape(-1, 1), docs.reshape(1, -1))
+    n = len(shards)
+    return out[:n], [out[n + 9 * at : n + 9 * at + 9] for at in range(layers)], out[-1]
+
+
+forward_table = (
+    23, 22, 117, 25, 95, 0, 189, 27, 94, 119, 1, 116, 188, 2, 191, 96, 190, 3, 24, 4, 45, 121,
+    118, 26, 97, 46, 98, 193, 70, 192, 47, 69, 5, 71, 194, 48, 197, 13, 196, 195, 28, 120, 49, 18,
+    200, 99, 30, 124, 34, 31, 29, 76, 10, 9, 123, 50, 72, 12, 198, 199, 129, 126, 41, 207, 11, 58,
+    8, 6, 32, 73, 77, 7, 201, 101, 112, 78, 33, 125, 122, 105, 44, 208, 205, 203, 127, 74, 75,
+    134, 128, 59, 107, 36, 35, 103, 106, 60, 204, 104, 39, 83, 135, 37, 40, 79, 17, 102, 202, 57,
+    65, 80, 131, 52, 42, 90, 82, 38, 209, 114, 206, 136, 81, 86, 100, 67, 51, 16, 165, 210, 20,
+    84, 132, 164, 14, 43, 91, 19, 54, 113, 15, 53, 140, 163, 87, 133, 130, 21, 211, 212, 167, 137,
+    213, 109, 85, 214, 55, 56, 138, 215, 216, 88, 142, 217, 218, 219, 166, 171, 62, 111, 139, 145,
+    89, 61, 170, 63, 66, 110, 92, 220, 169, 64, 221, 222, 68, 108, 223, 224, 225, 226, 227, 93,
+    228, 141, 229, 230, 147, 146, 231, 115, 232, 233, 234, 148, 144, 143, 153, 168, 172, 235, 236,
+    237, 150, 184, 238, 173, 239, 149, 177, 176, 157, 240, 241, 178, 174, 175, 242, 179, 154, 180,
+    243, 244, 156, 151, 152, 159, 160, 181, 158, 155, 182, 183, 186, 245, 246, 161, 247, 162, 248,
+    249, 250, 251, 185, 187, 252, 253, 254, 255, 256, 257, 258, 259,
 )
 fold_table = (
     50, 25, 1, 28, 29, 122, 169, 2, 8, 30, 9, 0, 145, 119, 31, 95, 53, 51, 55, 3, 74, 11, 10, 26,
@@ -684,10 +1211,6 @@
     157, 67, 90, 115, 116, 22, 181, 66, 155, 180, 117, 142, 182, 159, 183, 69, 158, 161, 141, 93,
     23, 160, 68, 92, 185, 184, 162, 71, 70, 163, 139, 24, 49, 118, 187, 143, 186, 164, 165,
 )
-
-
-def bits_of(size):
-    return [1 << at for at in range(size.bit_length() - 1)]
 
 
 def program(dp_size, mp_size, args):
@@ -807,10 +1330,15 @@
     spreads.append(line_first[0])
     spreads = [Spread(dims, mp_size) for dims in spreads]
     tabled = dp_size == 8 and mp_size == 4 and layers == 2
-    spread_order = step_order(
-        spreads, spread_table if tabled else (), lambda t, stage: t // 2 + stage
-    )
-    full = spread_all(shards, spreads, spread_order, dp_size, mp_size)
+    if paired:
+        spread_order = forward_order(spreads, layers, forward_table if tabled else ())
+        full, stored, stream = forward_all(
+            shards, inputs, docs, spreads, spread_order, dp_size, mp_size, layers,
+            vector_count, gain_rows, shift_rows,
+        )
+    else:
+        spread_order = step_order(spreads, (), lambda t, stage: t // 2 + stage)
+        full = spread_all(shards, spreads, spread_order, dp_size, mp_size)
     small_all = full[-1].reshape(dp_size, small_rows, mp_size, lanes).astype(f32)
     vectors = small_all[:, :vector_count, 0, :wide].transpose(1, 0, 2)
     vectors = vectors.reshape(vector_count, features)
@@ -819,21 +1347,24 @@
     biases = small_all[:, vector_count : vector_count + layers, :, :bias_wide]
     biases = biases.transpose(1, 2, 0, 3).reshape(layers, -1)
 
-    stream = trade(inputs).astype(f32)
     grad_stream = trade(cotangent).astype(f32)
-    stored = []
-    for layer in range(layers):
-        qkv_w, proj_w, upper_w, lower_w = full[4 * layer : 4 * layer + 4]
-        normed = layer_norm(stream, gains[layer, 0], shifts[layer, 0]).astype(bf16)
-        qkv = share_heads(dot(normed, qkv_w).astype(bf16))
-        mixed = attend(slopes, docs, qkv, slots)
-        attended = return_heads(mixed)
-        middle = stream + dot_cols(attended, proj_w)
-        normed_two = layer_norm(middle, gains[layer, 1], shifts[layer, 1]).astype(bf16)
-        hidden = dot(normed_two, upper_w) + biases[layer]
-        active = gelu_tanh(hidden).astype(bf16)
-        stored.append((stream, middle, normed, qkv, mixed, attended, normed_two, hidden, active))
-        stream = middle + dot_cols(active, lower_w) + shifts[layer, 2]
+    if not paired:
+        stream = inputs.astype(f32)
+        stored = []
+        for layer in range(layers):
+            qkv_w, proj_w, upper_w, lower_w = full[4 * layer : 4 * layer + 4]
+            normed = layer_norm(stream, gains[layer, 0], shifts[layer, 0]).astype(bf16)
+            qkv = share_heads(dot(normed, qkv_w).astype(bf16))
+            mixed = attend(slopes, docs, qkv, slots)
+            attended = return_heads(mixed)
+            middle = stream + dot_cols(attended, proj_w)
+            normed_two = layer_norm(middle, gains[layer, 1], shifts[layer, 1]).astype(bf16)
+            hidden = dot(normed_two, upper_w) + biases[layer]
+            active = gelu_tanh(hidden).astype(bf16)
+            stored.append(
+                (stream, middle, normed, qkv, mixed, attended, normed_two, hidden, active)
+            )
+            stream = middle + dot_cols(active, lower_w) + shifts[layer, 2]
     output_stream = stream
     if paired:
         other = lax.ppermute(output_stream.astype(bf16), ("dp", "mp"), pairs)
@@ -849,7 +1380,7 @@
         out_shift_grad = jnp.sum(grad_stream, axis=0)
         grad_low = grad_stream.astype(bf16)
         active_grad = dot(grad_low, lower_w)
-        _, pull_gelu = jax.vjp(gelu_tanh, hidden)
+        _, pull_gelu = jax.vjp(gelu_tanh, hidden.astype(f32))
         hidden_grad = pull_gelu(active_grad)[0].astype(bf16)
         lower_grad = dot_rows(grad_low, active).astype(bf16)
         upper_grad = dot_rows(normed_two, hidden_grad).astype(bf16)
@@ -901,48 +1432,37 @@
     fold_order = step_order(
         folds, fold_table if tabled else (), lambda t, stage: t // 2 + stage
     )
-    owned = fold_all(local, folds, fold_order, dp_size, mp_size)
+    owned, norm_tile = fold_all(local, folds, fold_order, dp_size, mp_size, vector_count)
     small_owned = owned.pop()
-
-    squares_sum = jnp.float32(0.0)
-    for gradient in owned:
-        squares_sum = squares_sum + jnp.sum(gradient * gradient)
     vector_owned = small_owned[:vector_count, :wide]
     bias_owned = small_owned[vector_count : vector_count + layers, :bias_wide]
-    squares_sum = squares_sum + jnp.sum(vector_owned * vector_owned) / mp_size
-    squares_sum = squares_sum + jnp.sum(bias_owned * bias_owned)
-    grad_norm = jnp.sqrt(lax.psum(squares_sum, ("dp", "mp")))
+    grad_norm = jnp.sqrt(jnp.sum(norm_tile))
     factor = jnp.minimum(1.0, clip_bound / grad_norm)
 
-    by_layer = [owned[4 * at : 4 * at + 4] for at in reversed(range(layers))]
-    gradients = (
-        jnp.stack([each[3].reshape(wide, 3, z_cols) for each in by_layer]),
-        jnp.stack([each[2].T for each in by_layer]),
-        jnp.stack([each[1] for each in by_layer]),
-        jnp.stack([each[0].T for each in by_layer]),
-        bias_owned,
-        vector_owned[: layers * gain_rows].reshape(layers, gain_rows, wide),
-        vector_owned[layers * gain_rows :].reshape(layers, shift_rows, wide),
+    states = []
+    for each in (qkv_weight, qkv_moment, qkv_square):
+        states.append(each.transpose(0, 2, 1, 3))
+    states += [
+        proj_weight, proj_moment, proj_square, upper_weight, upper_moment, upper_square,
+        lower_weight, lower_moment, lower_square,
+    ]
+    ordered = [owned[4 * layer + kind] for kind in (3, 2, 1, 0) for layer in range(layers)]
+    matrices = list(adam_all(factor, ordered, states))
+    matrices[:3] = [each.transpose(0, 2, 1, 3) for each in matrices[:3]]
+    results = [output_stream, input_grad] + matrices
+    rest = (
+        (hidden_bias, bias_moment, bias_square, bias_owned),
+        (
+            norm_gains, gains_moment, gains_square,
+            vector_owned[: layers * gain_rows].reshape(layers, gain_rows, wide),
+        ),
+        (
+            shift_params, shifts_moment, shifts_square,
+            vector_owned[layers * gain_rows :].reshape(layers, shift_rows, wide),
+        ),
     )
-    masters = (
-        qkv_weight, proj_weight, upper_weight, lower_weight, hidden_bias, norm_gains, shift_params
-    )
-    moments = (
-        qkv_moment, proj_moment, upper_moment, lower_moment, bias_moment, gains_moment,
-        shifts_moment,
-    )
-    squares = (
-        qkv_square, proj_square, upper_square, lower_square, bias_square, gains_square,
-        shifts_square,
-    )
-    results = [output_stream, input_grad]
-    for at in range(7):
-        results.extend(
-            adam_update(
-                masters[at], moments[at], squares[at], gradients[at], factor,
-                group_rates[at], group_decays[at],
-            )
-        )
+    for at, group in enumerate(rest, 4):
+        results.extend(adam_update(*group, factor, group_rates[at], group_decays[at]))
     results.append(grad_norm)
     return tuple(results)
 

time: 814 us -> 674 us (0.83)
  matrix products: 183 us -> 105 us
  Pallas kernels: 439 us -> 481 us
  blocking collectives: 37.1 us -> 0 us
  local copies, waits for them, and re-layouts: 58.7 us -> 25.1 us
  other arithmetic: 50.8 us -> 38.1 us
    pallas_call x4 -> x3, Pallas kernels: 410 us -> 452 us  [the longest x1 237 us: forward_all(): pl.pallas_call(functools.partial(forward_kernel, plans, order, mp_size, l...]
    psum x1 -> x0, blocking collectives: 37.1 us -> none  [program(): grad_norm = jnp.sqrt(lax.psum(squares_sum, ('dp', 'mp')))]
    dot_general x8 -> x4, matrix products: 61 us -> 26.7 us  [dot_cols(): lax.dot_general(left, right, contract_cols, preferred_element_type=f32)]
    dot_general x8 -> x4, matrix products: 63.2 us -> 29.1 us  [dot(): return jnp.dot(left, right, preferred_element_type=f32)]
    unnamed x196 -> x126, local copies, waits for them, and re-layouts: 47.4 us -> 18.8 us
    sub x7 -> x3, other arithmetic: 15.2 us -> 1.9 us  [adam_update(): master - step_rate * (first_hat / (jnp.sqrt(second_hat) + adam_eps) + dec...]
    dot_general x8, matrix products: 59.2 us -> 48.7 us  [dot_rows(): lax.dot_general(left, right, contract_rows, preferred_element_type=f32)]
    reduce_sum x10 -> x1, other arithmetic: 10.3 us -> 1.28 us  [program(): grad_norm = jnp.sqrt(jnp.sum(norm_tile))]
  transfers between devices with their start and end apart: 13 -> 8, of which waited for: 4 -> 0; matrix products, arithmetic and copies ran while one was open for 13% -> 16% of each run, Pallas kernels for 26% -> 70%
where the time goes in v3:
time: 674 us; the launch traced here: 663 us
  Pallas kernels  481 us (71%)
  matrix products  105 us (16%)
  other arithmetic  38.1 us (6%)
  local copies, waits for them, and re-layouts  25.1 us (4%)
  starting transfers between devices  10.6 us (2%)
    pallas_call x1, Pallas kernels, forward_all(): pl.pallas_call(functools.partial(forward_kernel, plans, order, mp_size, l...  237 us
    pallas_call x1, Pallas kernels, fold_all(): pl.pallas_call(functools.partial(fold_kernel, plans, order, mp_size, vect...  205 us
    dot_general x8, matrix products, dot_rows(): lax.dot_general(left, right, contract_rows, preferred_element_type=f32)  48.7 us
    dot_general x4, matrix products, dot(): return jnp.dot(left, right, preferred_element_type=f32)  29.1 us
    pallas_call x2, Pallas kernels, attend_back(): pl.pallas_call(functools.partial(attend_back_kernel, width // HD, min(256...  28.9 us
    dot_general x4, matrix products, dot_cols(): lax.dot_general(left, right, contract_cols, preferred_element_type=f32)  26.7 us
    unnamed x126, local copies, waits for them, and re-layouts  18.8 us
  transfers between devices with their start and end apart: 8, of which 0 were waited for; matrix products, arithmetic and copies ran while one was open for 16% of the time, Pallas kernels for 70%

profile of v3, /device:TPU:1, one launch (start us, length us, event | category | flops | bytes accessed | tf_op | source)
XLA Modules:
  0.0 662.6 jit_solution(12894396341350236236)
XLA Ops:
  0.8 4.7 collective-permute-start.2
  5.5 1.4 copy.57
  7.8 0.8 slice_bitcast_fusion.1
  8.9 0.8 slice_bitcast_fusion
  10.5 0.8 copy.61.refs_0_
  11.3 0.8 copy.62.refs_4_
  12.3 1.0 copy.63.refs_10_.dcol_ref
  13.3 237.0 %shard_map.424 = (bf16[1024,3072]{1,0:T(8,128)(2,1)}, bf16[1024,1024]{1,0:T(8,128)(2,1)}, bf16[1024,4096]{1,0:T(8,128)(2,1)}, bf16[1024,4096]{1,0:T(8,128)(2,1)}...) custom-call(bf16[128,768]{1,0:T(8,128)(2,1)} %copy.61.refs_0_, ...), custom_call_target="tpu_custom_call" | custom-call | tf_op jit(solution)/shard_map/pallas_call | solution.py:1146
  250.3 1.7 convert_element_type.121
  252.0 1.9 collective-permute-start.1
  254.0 1.8 reduce_sum.267
  255.7 1.8 reduce_sum.260
  257.5 2.8 multiply_reduce_fusion.7
  260.5 1.8 reduce_sum.253
  262.3 1.9 multiply_reduce_fusion.11
  264.2 1.9 reduce_sum.274
  266.1 2.1 multiply_reduce_fusion.5
  269.4 2.5 convert_reduce_fusion
  271.9 13.3 %fusion.48 = (bf16[4096]{0:T(1024)(128)(2,1)S(1)}, bf16[512,4096]{1,0:T(8,128)(2,1)}) fusion(bf16[512,4096]{1,0:T(8,128)(2,1)S(1)} %copy-done.44, bf16[512,1024]{1,0:T(8,128)(2,1)S(1)} %get-tuple-element.170, bf16[1024,4096]{1,0:T(8,128)(2,1)} %get-tuple-element.75), kind=kOutput, calls=%fused_computation.145 | convolution fusion | flops 4341100544 | bytes 17833984 | tf_op jit(solution)/shard_map/dot_general | solution.py:56
  285.2 7.0 %multiply_reduce_fusion = (f32[1024]{0:T(1024)S(1)}, f32[512]{0:T(512)S(1)}, f32[1024]{0:T(1024)S(1)}, f32[512,1024]{1,0:T(8,128)S(1)}) fusion(f32[512,1024]{1,0:T(8,128)S(1)} %copy-done.13, f32[512]{0:T(512)S(1)} %fusion.32, f32[512]{0:T(512)S(1)} %broadcast_multiply_fusion.3, f32[1024]{0:T(1024)S(1)} %bitcast.105, ...), kind=kOutput, calls=%fused_computation.40 | convolution fusion | flops 4299159040 | bytes 16795648 | tf_op jit(solution)/shard_map/dot_general | solution.py:64
  292.3 0.7 fusion.53
  293.4 1.3 copy-done.46
  294.6 1.3 convolution_convert_fusion.9
  296.0 0.8 copy-done.43
  296.8 6.9 %convolution_convert_fusion.3.refs_0_ = bf16[1024,4096]{1,0:T(8,128)(2,1)} fusion(bf16[512,1024]{1,0:T(8,128)(2,1)S(1)} %get-tuple-element.170, bf16[512,4096]{1,0:T(8,128)(2,1)S(1)} %copy-done.43), kind=kOutput, calls=%fused_computation.29 | convolution fusion | flops 4299161600 | bytes 13631488 | tf_op jit(solution)/shard_map/dot_general | solution.py:60
  304.8 1.0 copy-done.4
  305.8 14.7 %shard_map.425 = bf16[1024,1536]{1,0:T(8,128)(2,1)S(1)} custom-call(f32[4]{0:T(128)S(1)} %dynamic_slice.32.slope_ref, s32[1024,1]{1,0:T(8,128)S(1)} %copy-done, s32[1,1024]{1,0:T(1,128)S(1)} %copy-done.2, bf16[1024,1536]{1,0:T(8,128)(2,1)S(1)} %copy-done.4, bf16[1024,512]{1,0:T(8,128)(2,1)S(1)} %copy-done.6, bf16[1024,512]{1,0:T(8,128)(2,1)S(1)} %pad_maximum_fusion.6.do_ref), custom_call_target="tpu_custom_call" | custom-call | flops 5368709120 | bytes 9437184 | tf_op jit(solution)/shard_map/pallas_call | solution.py:180
  320.7 1.0 copy-done.52
  321.7 2.6 convolution_convert_fusion.7.refs_2_
  324.3 9.2 %convolution_convert_fusion.2.refs_1_ = bf16[1024,4096]{1,0:T(8,128)(2,1)} fusion(bf16[512,1024]{1,0:T(8,128)(2,1)S(1)} %copy-done.51, bf16[512,4096]{1,0:T(8,128)(2,1)} %get-tuple-element.176), kind=kOutput, calls=%fused_computation.28 | convolution fusion | flops 4299161600 | bytes 13631488 | tf_op jit(solution)/shard_map/dot_general | solution.py:60
  333.5 2.8 convert_select_fusion.1
  336.4 0.7 broadcast_select_fusion.3
  337.1 0.9 copy-done.11
  338.0 6.7 %multiply_reduce_fusion.1 = (f32[1024]{0:T(1024)S(1)}, f32[512]{0:T(512)S(1)}, f32[1024]{0:T(1024)S(1)}, f32[512,1024]{1,0:T(8,128)S(1)}) fusion(f32[512,1024]{1,0:T(8,128)S(1)} %copy-done.11, f32[512]{0:T(512)S(1)} %fusion.33, f32[512]{0:T(512)S(1)} %broadcast_multiply_fusion.2, f32[1024]{0:T(1024)S(1)} %bitcast.103, ...), kind=kOutput, calls=%fused_computation.41 | convolution fusion | flops 3231708672 | bytes 13649920 | tf_op jit(solution)/shard_map/dot_general | solution.py:64
  344.6 0.7 fusion.52
  345.9 1.7 copy-done.42
  347.6 13.3 %fusion.46 = (bf16[4096]{0:T(1024)(128)(2,1)S(1)}, bf16[512,4096]{1,0:T(8,128)(2,1)}) fusion(bf16[512,4096]{1,0:T(8,128)(2,1)S(1)} %copy-done.42, bf16[1024,4096]{1,0:T(8,128)(2,1)} %get-tuple-element.85, f32[512,1024]{1,0:T(8,128)S(1)} %get-tuple-element.172), kind=kOutput, calls=%fused_computation.144 | convolution fusion | flops 4341624832 | bytes 18882560 | tf_op jit(solution)/shard_map/dot_general | solution.py:56
  360.8 9.2 %multiply_reduce_fusion.2 = (f32[1024]{0:T(1024)S(1)}, f32[512]{0:T(512)S(1)}, f32[1024]{0:T(1024)S(1)}, f32[512,1024]{1,0:T(8,128)S(1)}) fusion(f32[512,1024]{1,0:T(8,128)S(1)} %copy-done.10, f32[512]{0:T(512)S(1)} %fusion.34, f32[512]{0:T(512)S(1)} %broadcast_multiply_fusion.1, f32[1024]{0:T(1024)S(1)} %bitcast.101, ...), kind=kOutput, calls=%fused_computation.42 | convolution fusion | flops 4299159040 | bytes 16795648 | tf_op jit(solution)/shard_map/dot_general | solution.py:64
  370.0 0.7 fusion.51
  371.0 2.1 copy-done.45
  373.1 1.3 convolution_convert_fusion.8
  374.5 1.1 copy-done.54
  375.6 6.9 %convolution_convert_fusion.refs_5_ = bf16[1024,4096]{1,0:T(8,128)(2,1)} fusion(bf16[512,1024]{1,0:T(8,128)(2,1)S(1)} %copy-done.50, bf16[512,4096]{1,0:T(8,128)(2,1)S(1)} %copy-done.54), kind=kOutput, calls=%fused_computation.26 | convolution fusion | flops 4299161600 | bytes 13631488 | tf_op jit(solution)/shard_map/dot_general | solution.py:60
  382.6 5.6 convolution_convert_fusion.5.refs_3_
  388.5 1.5 copy-done.3
  390.3 14.3 %shard_map.426 = bf16[1024,1536]{1,0:T(8,128)(2,1)S(1)} custom-call(f32[4]{0:T(128)S(1)} %dynamic_slice.32.slope_ref, s32[1024,1]{1,0:T(8,128)S(1)} %copy-done, s32[1,1024]{1,0:T(1,128)S(1)} %copy-done.2, bf16[1024,1536]{1,0:T(8,128)(2,1)S(1)} %copy-done.3, bf16[1024,512]{1,0:T(8,128)(2,1)S(1)} %copy-done.5, bf16[1024,512]{1,0:T(8,128)(2,1)S(1)} %pad_maximum_fusion.7.do_ref), custom_call_target="tpu_custom_call" | custom-call | flops 5368709120 | bytes 9437184 | tf_op jit(solution)/shard_map/pallas_call | solution.py:180
  404.8 1.0 copy-done.48
  405.8 2.6 convolution_convert_fusion.6.refs_6_
  408.5 9.2 %convolution_convert_fusion.1.refs_4_ = bf16[1024,4096]{1,0:T(8,128)(2,1)} fusion(bf16[512,4096]{1,0:T(8,128)(2,1)} %get-tuple-element.98, f32[512,1024]{1,0:T(8,128)S(1)} %get-tuple-element.172), kind=kOutput, calls=%fused_computation.27 | convolution fusion | flops 4299685888 | bytes 14680064 | tf_op jit(solution)/shard_map/dot_general | solution.py:60
  417.7 0.7 broadcast_select_fusion.1
  418.5 0.8 copy-done.7
  419.3 3.9 multiply_reduce_fusion.3
  423.2 0.7 fusion.50
  423.9 1.3 fusion.26
  425.6 3.6 collective-permute-start.7
  429.3 5.6 convolution_convert_fusion.4.refs_7_
  435.1 0.7 copy.95
  435.8 205.0 %shard_map.427 = (f32[128,1024]{1,0:T(8,128)}, f32[128,1024]{1,0:T(8,128)}, f32[128,256]{1,0:T(8,128)}, f32[128,768]{1,0:T(8,128)}, f32[128,1024]{1,0:T(8,128)},...) custom-call(bf16[1024,4096]{1,0:T(8,128)(2,1)} %convolution_convert_, ...), custom_call_target="tpu_custom_call" | custom-call | tf_op jit(solution)/shard_map/pallas_call | solution.py:738
  640.8 1.3 reduce_sum.302
  642.8 0.7 slice_multiply_fusion
  645.3 9.8 %shard_map.428 = (f32[2,3,128,256]{3,2,1,0:T(8,128)}, f32[2,3,128,256]{3,2,1,0:T(8,128)}, f32[2,3,128,256]{3,2,1,0:T(8,128)}, f32[2,256,128]{2,1,0:T(8,128)}, f3...) custom-call(f32[1,1]{1,0:T(1,128)} %bitcast.34.factor_ref, ...), custom_call_target="tpu_custom_call" | custom-call | tf_op jit(solution)/shard_map/pallas_call | solution.py:790
  655.1 0.7 slice_multiply_fusion.1
  655.8 1.3 multiply_subtract_fusion.1
  657.7 3.6 convert_select_fusion
  (181 shorter events, 10.0 us)
Async XLA Ops:
  0.7 6.3 copy-start.17
  0.7 7.0 %copy-start.15 = (f32[2,128,1024]{2,1,0:T(8,128)S(1)}, f32[2,128,1024]{2,1,0:T(8,128)}, u32[]{:S(2)}) copy-start(f32[2,128,1024]{2,1,0:T(8,128)} %refs_6_.1) | copy-start | bytes 3145732
  0.7 11.6 %collective-permute-start = (s32[2,1024]{1,0:T(2,128)}, s32[2,1024]{1,0:T(2,128)S(1)}, u32[]{:S(2)}, u32[]{:S(2)}) collective-permute-start(s32[2,1024]{1,0:T(2,128)} %param.26), channel_id=1, source_target_pairs={{0,4},{4,0},{8,12},{12,8},{16,20},{20,16},{24,28},{28,24},{1,5},{5... | collective-permute-start | bytes 24584 | tf_op jit(solution)/shard_map/ppermute | solution.py:1240
  0.8 268.6 %collective-permute-start.2 = (bf16[512,1024]{1,0:T(8,128)(2,1)}, bf16[512,1024]{1,0:T(8,128)(2,1)}, u32[]{:S(2)}, u32[]{:S(2)}) collective-permute-start(bf16[512,1024]{1,0:T(8,128)(2,1)} %param.27), channel_id=1, source_target_pairs={{1,4},{3,6},{4,1},{6,3},{9,12},{11,14},{12,9},{14,11},{17,20},{19,... | collective-permute-start | bytes 3145736 | tf_op jit(solution)/shard_map/ppermute | solution.py:1257
  6.9 1.8 copy-start.16
  7.8 1.9 copy-start.38
  7.8 1.9 copy-start.26
  7.8 2.0 copy-start.29
  7.8 4.4 copy-start.53
  7.8 4.4 copy-start.37
  9.8 2.4 copy-start.33
  252.0 81.5 %collective-permute-start.1 = (bf16[512,1024]{1,0:T(8,128)(2,1)S(1)}, bf16[512,1024]{1,0:T(8,128)(2,1)}, u32[]{:S(2)}, u32[]{:S(2)}) collective-permute-start(bf16[512,1024]{1,0:T(8,128)(2,1)S(1)} %convert_element_type.121), channel_id=1, source_target_pairs={{1,4},{3,6},{4,1},{6,3},{9,12},{11,14},{12,9},{14,11},{17,20},{19,... | collective-permute-start | bytes 3145736 | tf_op jit(solution)/shard_map/ppermute | solution.py:1370
  257.5 2.8 copy-start.19
  264.2 5.2 copy-start.18
  266.1 5.8 copy-start.20
  266.1 5.8 copy-start.44
  268.2 17.0 %copy-start.22 = (f32[512]{0:T(512)}, f32[512]{0:T(512)S(1)}, u32[]{:S(2)}) copy-start(f32[512]{0:T(512)S(1)} %multiply_reduce_fusion.5) | copy-start | bytes 6148
  269.4 15.8 %slice-start = ((s8[8388608]{0:T(1024)(128)(4,1)}), s8[4194304]{0:T(1024)(128)(4,1)S(1)}, s32[]{:S(2)}) async-start(s8[8388608]{0:T(1024)(128)(4,1)} %bitcast.119), calls=%async_computation | async-start | bytes 8388608
  271.9 13.3 %copy-start.13 = (f32[512,1024]{1,0:T(8,128)S(1)}, f32[512,1024]{1,0:T(8,128)}, u32[]{:S(2)}) copy-start(f32[512,1024]{1,0:T(8,128)} %get-tuple-element.79) | copy-start | bytes 6291460
  271.9 13.3 %slice-start.1 = ((s8[8388608]{0:T(1024)(128)(4,1)}), s8[4194304]{0:T(1024)(128)(4,1)S(1)}, s32[]{:S(2)}) async-start(s8[8388608]{0:T(1024)(128)(4,1)} %bitcast.119), calls=%async_computation.1 | async-start | bytes 8388608
  293.0 1.6 copy-start.46
  294.6 2.2 copy-start.43
  295.9 7.8 %collective-permute-start.3 = (bf16[512,512]{1,0:T(8,128)(2,1)S(1)}, bf16[512,512]{1,0:T(8,128)(2,1)S(1)}, u32[]{:S(2)}, u32[]{:S(2)}) collective-permute-start(bf16[512,512]{1,0:T(8,128)(2,1)S(1)} %constant_dynamic-slice_fusion.3), channel_id=1, source_target_pairs={{0,4},{4,0},{8,12},{12,8},{16,20},{20,16},{24,28},{28,24},{1,5},{5... | collective-permute-start | bytes 1572872 | tf_op jit(solution)/shard_map/ppermute | solution.py:1240
  296.8 7.3 %copy-start.6 = (bf16[1024,512]{1,0:T(8,128)(2,1)S(1)}, bf16[1024,512]{1,0:T(8,128)(2,1)}, u32[]{:S(2)}) copy-start(bf16[1024,512]{1,0:T(8,128)(2,1)} %get-tuple-element.81.o_ref) | copy-start | bytes 3145732
  303.7 2.1 copy-start.4
  320.5 1.2 copy-start.52
  320.6 15.8 %collective-permute-start.4 = (bf16[512,1536]{1,0:T(8,128)(2,1)S(1)}, bf16[512,1536]{1,0:T(8,128)(2,1)S(1)}, u32[]{:S(2)}, u32[]{:S(2)}) collective-permute-start(bf16[512,1536]{1,0:T(8,128)(2,1)S(1)} %constant_dynamic-slice_fusion.2), channel_id=1, source_target_pairs={{0,4},{4,0},{8,12},{12,8},{16,20},{20,16},{24,28},{28,24},{1,5},{5... | collective-permute-start | bytes 4718600 | tf_op jit(solution)/shard_map/ppermute | solution.py:1240
  321.7 2.6 copy-start.51
  324.3 9.2 %copy-start.14 = (f32[512,1024]{1,0:T(8,128)S(1)}, f32[512,1024]{1,0:T(8,128)}, u32[]{:S(2)}) copy-start(f32[512,1024]{1,0:T(8,128)} %get-tuple-element.74) | copy-start | bytes 6291460
  336.4 1.6 copy-start.11
  345.4 2.2 copy-start.42
  347.6 13.3 %copy-start.10 = (f32[512,1024]{1,0:T(8,128)S(1)}, f32[512,1024]{1,0:T(8,128)}, u32[]{:S(2)}) copy-start(f32[512,1024]{1,0:T(8,128)} %get-tuple-element.88) | copy-start | bytes 6291460
  370.7 2.4 copy-start.45
  371.0 52.9 %copy-start.8 = (f32[512,1024]{1,0:T(8,128)}, f32[512,1024]{1,0:T(8,128)S(1)}, u32[]{:S(2)}) copy-start(f32[512,1024]{1,0:T(8,128)S(1)} %add_add_fusion.5) | copy-start | bytes 6291460
  373.1 1.4 copy-start.50
  373.1 2.5 copy-start.54
  374.4 13.7 %collective-permute-start.5 = (bf16[512,512]{1,0:T(8,128)(2,1)S(1)}, bf16[512,512]{1,0:T(8,128)(2,1)S(1)}, u32[]{:S(2)}, u32[]{:S(2)}) collective-permute-start(bf16[512,512]{1,0:T(8,128)(2,1)S(1)} %constant_dynamic-slice_fusion.1), channel_id=1, source_target_pairs={{0,4},{4,0},{8,12},{12,8},{16,20},{20,16},{24,28},{28,24},{1,5},{5... | collective-permute-start | bytes 1572872 | tf_op jit(solution)/shard_map/ppermute | solution.py:1240
  375.6 7.0 %copy-start.49 = (bf16[512,1024]{1,0:T(8,128)(2,1)S(1)}, bf16[512,1024]{1,0:T(8,128)(2,1)}, u32[]{:S(2)}) copy-start(bf16[512,1024]{1,0:T(8,128)(2,1)} %get-tuple-element.97) | copy-start | bytes 3145732
  388.1 1.9 copy-start.3
  388.1 2.2 copy-start.5
  404.6 1.2 copy-start.48
  404.7 13.0 %collective-permute-start.6 = (bf16[512,1536]{1,0:T(8,128)(2,1)S(1)}, bf16[512,1536]{1,0:T(8,128)(2,1)S(1)}, u32[]{:S(2)}, u32[]{:S(2)}) collective-permute-start(bf16[512,1536]{1,0:T(8,128)(2,1)S(1)} %constant_dynamic-slice_fusion), channel_id=1, source_target_pairs={{0,4},{4,0},{8,12},{12,8},{16,20},{20,16},{24,28},{28,24},{1,5},{5... | collective-permute-start | bytes 4718600 | tf_op jit(solution)/shard_map/ppermute | solution.py:1240
  405.8 12.6 %slice-start.2 = ((s8[6291456]{0:T(1024)(128)(4,1)}), s8[4194304]{0:T(1024)(128)(4,1)S(1)}, s32[]{:S(2)}) async-start(s8[6291456]{0:T(1024)(128)(4,1)} %bitcast.121), calls=%async_computation.2 | async-start | bytes 8388608
  408.5 10.0 %slice-start.3 = ((s8[6291456]{0:T(1024)(128)(4,1)}), s8[2097152]{0:T(1024)(128)(4,1)S(1)}, s32[]{:S(2)}) async-start(s8[6291456]{0:T(1024)(128)(4,1)} %bitcast.121), calls=%async_computation.3 | async-start | bytes 4194304
  417.7 1.6 copy-start.7
  417.7 1.6 copy-start.21
  417.7 1.6 copy-start.25
  417.7 1.6 copy-start.28
  419.3 3.9 copy-start.23
  423.9 1.7 copy-start.12
  423.9 5.3 copy-start.47
  425.6 232.1 %collective-permute-start.7 = (bf16[512,1024]{1,0:T(8,128)(2,1)}, bf16[512,1024]{1,0:T(8,128)(2,1)}, u32[]{:S(2)}, u32[]{:S(2)}) collective-permute-start(bf16[512,1024]{1,0:T(8,128)(2,1)} %fusion.26), channel_id=1, source_target_pairs={{1,4},{3,6},{4,1},{6,3},{9,12},{11,14},{12,9},{14,11},{17,20},{19,... | collective-permute-start | bytes 3145736 | tf_op jit(solution)/shard_map/ppermute | solution.py:1408
  429.3 5.6 copy-start.24
  429.3 5.7 copy-start.34
  435.8 207.7 %copy-start.27 = (f32[2,3,128]{2,0,1:T(2,128)S(1)}, f32[2,3,128]{2,0,1:T(2,128)}, u32[]{:S(2)}) copy-start(f32[2,3,128]{2,0,1:T(2,128)} %param.46) | copy-start | bytes 9220
  435.8 207.7 %copy-start.31 = (f32[2,3,128]{2,0,1:T(2,128)S(1)}, f32[2,3,128]{2,0,1:T(2,128)}, u32[]{:S(2)}) copy-start(f32[2,3,128]{2,0,1:T(2,128)} %param.47) | copy-start | bytes 9220
  435.8 207.7 %copy-start.32 = (f32[2,3,128]{2,0,1:T(2,128)S(1)}, f32[2,3,128]{2,0,1:T(2,128)}, u32[]{:S(2)}) copy-start(f32[2,3,128]{2,0,1:T(2,128)} %param.48) | copy-start | bytes 9220
  645.3 10.5 %copy-start.39 = (f32[2,128]{1,0:T(2,128)S(1)}, f32[2,128]{1,0:T(2,128)}, u32[]{:S(2)}) copy-start(f32[2,128]{1,0:T(2,128)} %param.40) | copy-start | bytes 3076
  645.3 10.5 %copy-start.40 = (f32[2,128]{1,0:T(2,128)S(1)}, f32[2,128]{1,0:T(2,128)}, u32[]{:S(2)}) copy-start(f32[2,128]{1,0:T(2,128)} %param.41) | copy-start | bytes 3076
  645.3 10.5 %copy-start.41 = (f32[2,128]{1,0:T(2,128)S(1)}, f32[2,128]{1,0:T(2,128)}, u32[]{:S(2)}) copy-start(f32[2,128]{1,0:T(2,128)} %param.42) | copy-start | bytes 3076
  645.3 11.8 %copy-start.30 = (f32[2,2,128]{2,1,0:T(2,128)S(1)}, f32[2,2,128]{2,1,0:T(2,128)}, u32[]{:S(2)}) copy-start(f32[2,2,128]{2,1,0:T(2,128)} %param.43) | copy-start | bytes 6148
  645.3 11.8 %copy-start.35 = (f32[2,2,128]{2,1,0:T(2,128)S(1)}, f32[2,2,128]{2,1,0:T(2,128)}, u32[]{:S(2)}) copy-start(f32[2,2,128]{2,1,0:T(2,128)} %param.44) | copy-start | bytes 6148
  645.3 11.8 %copy-start.36 = (f32[2,2,128]{2,1,0:T(2,128)S(1)}, f32[2,2,128]{2,1,0:T(2,128)}, u32[]{:S(2)}) copy-start(f32[2,2,128]{2,1,0:T(2,128)} %param.45) | copy-start | bytes 6148
  645.3 12.4 %copy-start.9 = (f32[512,1024]{1,0:T(8,128)S(1)}, f32[512,1024]{1,0:T(8,128)}, u32[]{:S(2)}) copy-start(f32[512,1024]{1,0:T(8,128)} %copy-done.8) | copy-start | bytes 6291460
  (3 other events, 3.1 us)

commit v4 on v3

--- a/solution.py
+++ b/solution.py
@@ -9,6 +9,8 @@
 from jax.experimental.pallas import tpu as pltpu
 from jax.sharding import PartitionSpec as P
 
+DP = "dp"
+MP = "mp"
 H = 8
 HD = 128
 STEP = 5
@@ -205,6 +207,8 @@
 
 
 def place(at, size):
+    if isinstance(at, int):
+        return at * size
     return pl.multiple_of(at * size, size)
 
 
@@ -215,38 +219,39 @@
         masks, spread = [0], False
         for stage, dim in enumerate(self.dims):
             for mask in masks:
-                if dim == "mp":
+                if dim == MP:
                     for hops in range(1, mp_size):
                         self.events += [(stage, mask, way, hops) for way in (1, -1)]
                 else:
                     places = range(mp_size) if spread else (0,)
                     self.events += [(stage, mask | dim, 0, at) for at in places]
-            if dim == "mp":
+            if dim == MP:
                 spread = True
             else:
                 masks = masks + [mask | dim for mask in masks]
         self.events += [(len(self.dims), mask | 1, 0, 0) for mask in masks]
 
     def full(self, stage):
-        return "mp" in self.dims[:stage]
+        return MP in self.dims[:stage]
 
 
 class Fold:
-    def __init__(self, dims, mp_size):
+    def __init__(self, dims, mp_size, halves=1):
         self.dims = tuple(dims)
         masks = [0]
         for dim in self.dims:
-            if dim != "mp":
+            if dim != MP:
                 masks = masks + [mask | dim for mask in masks]
         self.masks = masks
         self.kept = {}
-        self.events = [(0, mask, 0, 0) for mask in sorted(masks, key=self.leaves)]
+        sent_first = sorted(masks, key=self.leaves)
+        self.events = [(0, mask, 0, half) for mask in sent_first for half in range(halves)]
         rows = list(masks)
         for stage, dim in enumerate(self.dims, 1):
-            if dim != "mp":
+            if dim != MP:
                 rows = [mask for mask in rows if not mask & dim]
             self.kept[stage] = list(rows)
-            if dim == "mp":
+            if dim == MP:
                 for hops in reversed(range(mp_size - 1)):
                     for mask in rows:
                         self.events += [(stage, mask, way, hops) for way in (1, -1)]
@@ -258,12 +263,12 @@
 
     def leaves(self, mask):
         for at, dim in enumerate(self.dims):
-            if dim != "mp" and mask & dim:
+            if dim != MP and mask & dim:
                 return at
         return len(self.dims)
 
     def full(self, stage):
-        return "mp" not in self.dims[: stage - 1]
+        return MP not in self.dims[: stage - 1]
 
 
 def number(plans, mp_size, single):
@@ -321,11 +326,11 @@
     barrier = pltpu.get_barrier_semaphore()
     for bit in mp_bits:
         pl.semaphore_signal(
-            barrier, inc=1, device_id={"mp": flip(z, bit)}, device_id_type=MESH
+            barrier, inc=1, device_id={MP: flip(z, bit)}, device_id_type=MESH
         )
     for bit in [1] + upper:
         pl.semaphore_signal(
-            barrier, inc=1, device_id={"dp": flip(d, bit)}, device_id_type=MESH
+            barrier, inc=1, device_id={DP: flip(d, bit)}, device_id_type=MESH
         )
     also = 0
     if across is not None:
@@ -340,7 +345,7 @@
         @pl.when((z + way >= 0) & (z + way < mp_size))
         def _(way=way):
             pl.semaphore_signal(
-                barrier, inc=1, device_id={"mp": z + way}, device_id_type=MESH
+                barrier, inc=1, device_id={MP: z + way}, device_id_type=MESH
             )
 
     around = jnp.where(z > 0, 1, 0) + jnp.where(z < mp_size - 1, 1, 0)
@@ -354,9 +359,9 @@
         self.shards, self.outs = shards, outs
         self.sems = send_sems, recv_sems
         self.own_sems = own_sems
-        self.z = lax.axis_index("mp")
-        self.d = lax.axis_index("dp")
-        self.upper = [dim for dim in plans[0].dims if dim != "mp"]
+        self.z = lax.axis_index(MP)
+        self.d = lax.axis_index(DP)
+        self.upper = [dim for dim in plans[0].dims if dim != MP]
         self.index, _ = number(plans, mp_size, spread_single)
         self.owns = []
         self.left = {}
@@ -398,22 +403,22 @@
 
     def arrival(self, t, event, block):
         dst = self.region(t, event[1], block)
-        return self.remote(t, event, block, dst, dst, {"dp": self.d, "mp": self.z})
+        return self.remote(t, event, block, dst, dst, {DP: self.d, MP: self.z})
 
     def on_line(self, t, stage, mask, block, way, hops, own):
         @pl.when(self.inside(self.z + way))
         def _():
-            to = {"mp": self.z + way}
+            to = {MP: self.z + way}
             self.sending(t, (stage, mask, way, hops), block, to, own).start()
 
     def onward(self, t, stage, mask, block, own=False):
         dims = self.plans[t].dims
         for later in range(stage, len(dims)):
-            if dims[later] == "mp":
+            if dims[later] == MP:
                 for way in (1, -1):
                     self.on_line(t, later, mask, block, way, 1, own)
             else:
-                to = {"dp": flip(self.d, dims[later])}
+                to = {DP: flip(self.d, dims[later])}
                 self.sending(t, (later, mask | dims[later], 0, None), block, to, own).start()
 
     def place_of(self, t, event):
@@ -452,23 +457,23 @@
         if self.left[t, mask] == 0:
             if mask == 0:
                 self.owns[t].wait()
-            to = {"dp": flip(self.d, 1)}
+            to = {DP: flip(self.d, 1)}
             self.sending(t, (last, mask | 1, 0, 0), None, to).start()
 
     def finish(self):
         for t, event in self.order:
             stage, mask, way, at = event
             if stage == len(self.plans[t].dims):
-                self.sending(t, event, None, {"dp": flip(self.d, 1)}).wait_send()
+                self.sending(t, event, None, {DP: flip(self.d, 1)}).wait_send()
             elif way:
 
                 @pl.when(self.inside(self.z - way * (at - 1)) & self.inside(self.z + way))
                 def _():
-                    to = {"mp": self.z + way}
+                    to = {MP: self.z + way}
                     self.sending(t, event, self.z - way * (at - 1), to).wait_send()
 
             else:
-                to = {"dp": flip(self.d, self.plans[t].dims[stage])}
+                to = {DP: flip(self.d, self.plans[t].dims[stage])}
                 self.sending(t, event, self.place_of(t, event), to).wait_send()
 
 
@@ -513,9 +518,9 @@
             recv[t, stage] = refs[at]
             at += 1
     staging, tiles, load_sems, own_sems, tile_sems, send_sems, recv_sems = refs[at:]
-    z = lax.axis_index("mp")
-    d = lax.axis_index("dp")
-    upper = [dim for dim in plans[0].dims if dim != "mp"]
+    z = lax.axis_index(MP)
+    d = lax.axis_index(DP)
+    upper = [dim for dim in plans[0].dims if dim != MP]
     index, _ = number(plans, mp_size, fold_single)
     wides = [out.shape[0] for out in outs]
     cols = [out.shape[1] for out in outs]
@@ -554,7 +559,7 @@
     def core_copy(t, mask):
         rows = pl.ds(place(flip(d, mask | 1), wides[t]), wides[t])
         dst = landed[t].at[rows_of(t, mask), :]
-        return remote(t, (0, mask, 0, 0), 0, grads[t].at[rows, :], dst, {"dp": flip(d, 1)})
+        return remote(t, (0, mask, 0, 0), 0, grads[t].at[rows, :], dst, {DP: flip(d, 1)})
 
     def own_copy(t, mask):
         rows = pl.ds(place(flip(d, mask), wides[t]), wides[t])
@@ -568,16 +573,16 @@
         dim = plans[t].dims[stage - 1]
         event = (stage, mask & ~dim, 0, None)
         dst = landing(t, event, block)
-        return remote(t, event, block, sum_at(t, mask, block), dst, {"dp": flip(d, dim)})
+        return remote(t, event, block, sum_at(t, mask, block), dst, {DP: flip(d, dim)})
 
     def line_copy(t, stage, mask, way, hops):
         event = (stage, mask, way, hops - 1)
         src = sum_at(t, mask, z + way * hops)
-        return remote(t, event, None, src, landing(t, event, None), {"mp": z + way})
+        return remote(t, event, None, src, landing(t, event, None), {MP: z + way})
 
     def arrival(t, event, block):
         dst = landing(t, event, block)
-        return remote(t, event, block, dst, dst, {"dp": d, "mp": z})
+        return remote(t, event, block, dst, dst, {DP: d, MP: z})
 
     def add(dst, src, wide):
         step = 16
@@ -594,7 +599,7 @@
         if stage > len(plans[t].dims):
             return
         dim = plans[t].dims[stage - 1]
-        if dim == "mp":
+        if dim == MP:
             if other:
                 for way, end in ((1, 0), (-1, mp_size - 1)):
 
@@ -683,8 +688,8 @@
         else:
             zero = jnp.zeros((8, HD), f32)
             tiles[0] += lax.fori_loop(0, wides[t] // step, some_rows, zero)
-    pairs = [{"dp": flip(d, bit)} for bit in [1] + upper]
-    pairs += [{"mp": flip(z, bit)} for bit in mp_bits]
+    pairs = [{DP: flip(d, bit)} for bit in [1] + upper]
+    pairs += [{MP: flip(z, bit)} for bit in mp_bits]
     for at, to in enumerate(pairs):
         exchange = pltpu.make_async_remote_copy(
             src_ref=tiles.at[2 * at],
@@ -724,7 +729,7 @@
     scratch = [pltpu.VMEM(half, bf16) for half in halves]
     for plan, wide, each in zip(plans, wides, cols):
         for stage, dim in enumerate(plan.dims, 1):
-            blocks = 2 * (mp_size - 1) if dim == "mp" else mp_size if plan.full(stage) else 1
+            blocks = 2 * (mp_size - 1) if dim == MP else mp_size if plan.full(stage) else 1
             scratch.append(pltpu.VMEM((len(plan.kept[stage]), blocks, wide, each), bf16))
     scratch += [
         pltpu.VMEM((2, max(wides), mp_size * max(cols)), bf16),
@@ -751,59 +756,153 @@
     return list(out[:n]), out[n]
 
 
-def adam_kernel(
-    factor_ref, qkv_1, qkv_0, proj_1, proj_0, upper_1, upper_0, lower_1, lower_0, *refs
-):
-    factor = factor_ref[0, 0]
-    ins, outs = refs[:12], refs[12:]
+def prepare_kernel(layers, *refs):
+    count = 4 * layers + 1
+    states, outs = refs[:7], refs[7 : 7 + count]
+    held, made = refs[7 + count : 14 + count], refs[14 + count : 14 + 2 * count]
+    in_sems, out_sems = refs[14 + 2 * count :]
+    loads = [pltpu.make_async_copy(a, b, in_sems.at[at]) for at, (a, b) in enumerate(zip(states, held))]
+    for copy in loads:
+        copy.start()
+    qkv, proj, upper, lower, gains, shifts, bias = held
+    stores = [pltpu.make_async_copy(a, b, out_sems.at[at]) for at, (a, b) in enumerate(zip(made, outs))]
+    for kind in range(4):
+        loads[kind].wait()
+        for layer in range(layers):
+            out = made[4 * layer + kind]
+            if kind == 0:
+                cols = qkv.shape[3]
+                for part in range(3):
+                    out[:, part * cols : (part + 1) * cols] = qkv[layer, part].astype(bf16)
+            elif kind == 2:
+                for low in range(0, upper.shape[2], 256):
+                    out[:, low : low + 256] = upper[layer, :, low : low + 256].astype(bf16)
+            else:
+                from_ref = proj if kind == 1 else lower
+                for low in range(0, from_ref.shape[1], HD):
+                    out[:, low : low + HD] = from_ref[layer, low : low + HD, :].T.astype(bf16)
+            stores[4 * layer + kind].start()
+    for copy in loads[4:]:
+        copy.wait()
+    small = made[-1]
+    rows = [each[layer] for each in (gains, shifts) for layer in range(layers)] + [bias[...]]
+    used = sum(each.shape[0] for each in rows)
+    rows.append(jnp.zeros((small.shape[0] - used, small.shape[1]), f32))
+    small[...] = jnp.concatenate(rows, axis=0).astype(bf16)
+    stores[-1].start()
+    for copy in stores:
+        copy.wait()
+
+
+def prepare_all(states, small_rows):
+    qkv, proj, upper, lower = states[:4]
+    layers = qkv.shape[0]
+    wide = upper.shape[1]
+    each = [3 * qkv.shape[3], proj.shape[1], upper.shape[2], lower.shape[1]] * layers
+    shapes = [(wide, cols) for cols in each] + [(small_rows, wide)]
+    any_place = pl.BlockSpec(memory_space=pl.ANY)
+    return pl.pallas_call(
+        functools.partial(prepare_kernel, layers),
+        out_shape=[jax.ShapeDtypeStruct(shape, bf16) for shape in shapes],
+        in_specs=[any_place] * 7,
+        out_specs=[any_place] * len(shapes),
+        scratch_shapes=[pltpu.VMEM(state.shape, f32) for state in states]
+        + [pltpu.VMEM(shape, bf16) for shape in shapes]
+        + [pltpu.SemaphoreType.DMA((7,)), pltpu.SemaphoreType.DMA((len(shapes),))],
+        compiler_params=pltpu.CompilerParams(vmem_limit_bytes=56 * 2**20),
+    )(*states)
+
+
+def adam_kernel(streams, scalars, *refs):
+    ins = 20 + 2 * streams
+    news = 12 + streams
+    sources, outs = refs[:ins], refs[ins : ins + news]
+    held, made = refs[ins + news : 2 * ins + news], refs[2 * ins + news : 2 * (ins + news)]
+    in_sems, out_sems = refs[2 * (ins + news) :]
+    loads = [
+        pltpu.make_async_copy(a, b, in_sems.at[at]) for at, (a, b) in enumerate(zip(sources, held))
+    ]
+    stores = [pltpu.make_async_copy(a, b, out_sems.at[at]) for at, (a, b) in enumerate(zip(made, outs))]
+    order = []
+    for group in range(4):
+        order += [2 * group, 2 * group + 1] + [8 + 3 * group + which for which in range(3)]
+    for at in order + list(range(20, ins)):
+        loads[at].start()
+    factor = scalars[0, 0]
 
     def update(group, at, gradient):
-        found = [ins[3 * group + which][at] for which in range(3)]
+        found = [held[8 + 3 * group + which][at] for which in range(3)]
         new = adam_update(
-            *found, gradient, factor, group_rates[group], group_decays[group]
+            *found, gradient.astype(f32), factor, group_rates[group], group_decays[group]
         )
         for which in range(3):
-            outs[3 * group + which][at] = new[which]
-
-    for layer, gradient in enumerate((qkv_0, qkv_1)):
-        wide, cols = gradient.shape[0], gradient.shape[1] // 3
-        for part in range(3):
-            for low in range(0, wide, 64):
-                update(
-                    0,
-                    (layer, part, slice(low, low + 64)),
-                    gradient[low : low + 64, part * cols : (part + 1) * cols],
-                )
-    for layer, gradient in enumerate((proj_0, proj_1)):
-        for low in range(0, gradient.shape[1], HD):
-            update(1, (layer, slice(low, low + HD)), gradient[:, low : low + HD].T)
-    for layer, gradient in enumerate((upper_0, upper_1)):
-        for low in range(0, gradient.shape[0], 16):
-            update(2, (layer, slice(low, low + 16)), gradient[low : low + 16, :])
-    for layer, gradient in enumerate((lower_0, lower_1)):
-        for low in range(0, gradient.shape[1], HD):
-            update(3, (layer, slice(low, low + HD)), gradient[:, low : low + HD].T)
-
-
-def adam_all(factor, gradients, states):
-    vmem = pl.BlockSpec(memory_space=pltpu.VMEM)
+            made[3 * group + which][at] = new[which]
+
+    for group in range(4):
+        for at in order[5 * group : 5 * group + 5]:
+            loads[at].wait()
+        for layer, gradient in enumerate((held[2 * group + 1], held[2 * group])):
+            if group == 0:
+                wide, cols = gradient.shape[0], gradient.shape[1] // 3
+                for part in range(3):
+                    for low in range(0, wide, 64):
+                        update(
+                            0,
+                            (layer, part, slice(low, low + 64)),
+                            gradient[low : low + 64, part * cols : (part + 1) * cols],
+                        )
+            elif group == 2:
+                for low in range(0, gradient.shape[0], 16):
+                    update(2, (layer, slice(low, low + 16)), gradient[low : low + 16, :])
+            else:
+                for low in range(0, gradient.shape[1], HD):
+                    part = gradient[:, low : low + HD].astype(f32).T
+                    update(group, (layer, slice(low, low + HD)), part)
+        for which in range(3):
+            stores[3 * group + which].start()
+    for at in range(streams):
+        for which in range(2):
+            loads[20 + 2 * at + which].wait()
+        ours, others = held[20 + 2 * at : 22 + 2 * at]
+        for low in range(0, ours.shape[0], 64):
+            rows = slice(low, low + 64)
+            values = jnp.where(scalars[0, 1] > 0.5, others[rows, :].astype(f32), ours[rows, :])
+            made[12 + at][rows, :] = values
+        stores[12 + at].start()
+    for copy in stores:
+        copy.wait()
+
+
+def adam_all(factor, moved, gradients, states, streams):
+    scalars = jnp.stack([factor, jnp.where(moved, 1.0, 0.0).astype(f32)]).reshape(1, 2)
+    any_place = pl.BlockSpec(memory_space=pl.ANY)
+    operands = list(gradients) + list(states) + list(streams)
+    news = [jax.ShapeDtypeStruct(each.shape, f32) for each in list(states) + list(streams[::2])]
     return pl.pallas_call(
-        adam_kernel,
-        out_shape=[jax.ShapeDtypeStruct(state.shape, f32) for state in states],
-        in_specs=[pl.BlockSpec(memory_space=pltpu.SMEM)] + [vmem] * (8 + len(states)),
-        out_specs=[vmem] * len(states),
+        functools.partial(adam_kernel, len(streams) // 2),
+        out_shape=news,
+        in_specs=[pl.BlockSpec(memory_space=pltpu.SMEM)] + [any_place] * len(operands),
+        out_specs=[any_place] * len(news),
+        scratch_shapes=[pltpu.VMEM(each.shape, each.dtype) for each in operands + news]
+        + [
+            pltpu.SemaphoreType.DMA((len(operands),)),
+            pltpu.SemaphoreType.DMA((len(news),)),
+        ],
         compiler_params=pltpu.CompilerParams(vmem_limit_bytes=60 * 2**20),
-    )(factor.reshape(1, 1), *gradients, *states)
+    )(scalars, *operands)
 
 
 ROWS = 64
+SAVED = 9
 TILE = 256
 
 
-def norm_rows(src, dst, gain, shift):
+def norm_rows(src, dst, low, gain, shift):
     def some_rows(at, carry):
         rows = pl.ds(pl.multiple_of(at * ROWS, ROWS), ROWS)
-        dst[rows, :] = layer_norm(src[rows, :], gain, shift).astype(bf16)
+        values = src[rows, :]
+        low[rows, :] = values.astype(bf16)
+        dst[rows, :] = layer_norm(values, gain, shift).astype(bf16)
         return carry
 
     lax.fori_loop(0, src.shape[0] // ROWS, some_rows, 0)
@@ -817,30 +916,63 @@
     lax.fori_loop(0, width // TILE, one, 0)
 
 
-def attend_head(qkv, out, at, width, out_at, slope, doc_cols, doc_rows):
+def block_scores(query, key, slope, doc_col, doc_row, first_col, diagonal):
+    cols = first_col + lax.broadcasted_iota(jnp.int32, (1, key.shape[0]), 1)
+    scores = dot_cols(query, key) * score_scale + slope * cols.astype(f32)
+    allowed = doc_col == doc_row
+    if diagonal:
+        row = lax.broadcasted_iota(jnp.int32, scores.shape, 0)
+        col = lax.broadcasted_iota(jnp.int32, scores.shape, 1)
+        allowed = allowed & (row >= col)
+    return jnp.where(allowed, scores, masked_score)
+
+
+def lane_of(values, lane):
+    return lax.broadcasted_iota(jnp.int32, values.shape, 1) == lane
+
+
+def head_slope(slot, inner, slots, heads_slot, core):
+    slope = 0.5 ** (slot * heads_slot + 1.0)
+    for later in range(1, heads_slot):
+        slope = jnp.where(inner == later, 0.5 ** (slot * heads_slot + later + 1.0), slope)
+    return slope * jnp.where(core == 0, 1.0, 0.5 ** (slots * heads_slot))
+
+
+def attend_head(qkv, out, logs, head, at, width, slope, doc_cols, doc_rows):
+    query_cols, key_cols, value_cols = (
+        pl.ds(pl.multiple_of(at + part * width, HD), HD) for part in range(3)
+    )
     length = qkv.shape[0]
     block = min(256, length)
     for first_row in range(0, length, block):
+        rows = slice(first_row, first_row + block)
         low, high = key_range(first_row, block)
-        scores = masked_scores(
-            slope,
-            doc_cols[first_row : first_row + block, :],
-            doc_rows[:, low:high],
-            qkv[first_row : first_row + block, at : at + HD],
-            qkv[low:high, at + width : at + width + HD],
-            first_row,
-            low,
-        )
-        shifted = jnp.exp(scores - jnp.max(scores, axis=-1, keepdims=True))
-        total = jnp.sum(shifted, axis=-1, keepdims=True)
-        prob_low = (shifted * (1.0 / total)).astype(bf16)
-        value = qkv[low:high, at + 2 * width : at + 2 * width + HD]
-        out[first_row : first_row + block, out_at : out_at + HD] = dot(prob_low, value).astype(bf16)
+        blocks = [slice(first, first + block) for first in range(low, high, block)]
+        query = qkv[rows, query_cols]
+        scores = [
+            block_scores(
+                query, qkv[cols, key_cols], slope, doc_cols[rows, :],
+                doc_rows[:, cols], cols.start, cols == rows,
+            )
+            for cols in blocks
+        ]
+        top = scores[0]
+        for each in scores[1:]:
+            top = jnp.maximum(top, each)
+        top = jnp.max(top, axis=-1, keepdims=True)
+        total, mixed = 0.0, 0.0
+        for cols, each in zip(blocks, scores):
+            shifted = jnp.exp(each - top)
+            total = total + jnp.sum(shifted, axis=-1, keepdims=True)
+            mixed = mixed + dot(shifted.astype(bf16), qkv[cols, value_cols])
+        to = pl.ds(pl.multiple_of(head * HD, HD), HD)
+        out[rows, to] = (mixed * (1.0 / total)).astype(bf16)
+        logs[rows, :] = jnp.where(lane_of(logs[rows, :], head), top + jnp.log(total), logs[rows, :])
 
 
 FORWARD_STEPS = (
     ("norm_one", "other_0", "other_1", "own_0", "own_1", "share")
-    + tuple(f"head_{at}" for at in range(4))
+    + ("head_0", "head_1")
     + ("back", "proj", "norm_two")
     + tuple(f"up_{at}" for at in range(8))
     + tuple(f"down_{at}" for at in range(4))
@@ -853,20 +985,20 @@
     inputs, doc_cols, doc_rows = refs[n : n + 3]
     outs = refs[n + 3 : 2 * n + 3]
     at = 2 * n + 3
-    saved = [refs[at + 9 * layer : at + 9 * layer + 9] for layer in range(layers)]
-    at += 9 * layers
-    last_stream = refs[at]
+    saved = [refs[at + SAVED * layer : at + SAVED * (layer + 1)] for layer in range(layers)]
+    at += SAVED * layers
+    last_stream, last_low, vectors = refs[at : at + 3]
     (
-        streams, middles, normed_one, normed_two, send_buf, qkv_full, mixed, attended,
-        hidden, active, w_qkv, w_proj, w_up, w_down, small_buf, vectors, biases, traded,
+        streams, middles, lows, normed_one, normed_two, send_buf, qkv_full, mixed, logs, attended,
+        hidden, active, w_qkv, w_proj, w_up, w_down, small_buf, biases, traded,
         load_sems, save_sems, trade_sems, head_sems, send_sems, recv_sems, own_sems,
-    ) = refs[at + 1 :]
+    ) = refs[at + 3 :]
     work = SpreadWork(plans, order, mp_size, shards, outs, send_sems, recv_sems, own_sems)
     z, d = work.z, work.d
     core = d % 2
     moved = core != z % 2
-    partner = {"dp": flip(d, 1)}
-    across = {"dp": flip(d, 1), "mp": flip(z, 1)}
+    partner = {DP: flip(d, 1)}
+    across = {DP: flip(d, 1), MP: flip(z, 1)}
     tokens = inputs.shape[0]
     features = inputs.shape[1]
     half = attended.shape[2] // 2
@@ -950,6 +1082,15 @@
             device_id=partner, device_id_type=MESH,
         )
 
+    def active_copy(layer):
+        rows = pl.ds(place(core, tokens), tokens)
+        return pltpu.make_async_remote_copy(
+            src_ref=active, dst_ref=saved[layer][7].at[rows, :],
+            send_sem=head_sems.at[4 * layers + 2 * layer],
+            recv_sem=head_sems.at[4 * layers + 2 * layer + 1],
+            device_id=partner, device_id_type=MESH,
+        )
+
     def vector(at):
         return vectors[at : at + 1, :]
 
@@ -985,8 +1126,11 @@
                     for m in range(mp_size):
                         first = m * (biases.shape[1] // mp_size) + b * lanes
                         biases[:, first : first + lanes] = rows[:, m * lanes : (m + 1) * lanes]
-            norm_rows(streams.at[layer], normed_one.at[layer], vector(gain), vector(shift))
-            save(streams.at[layer], keeps[0])
+            norm_rows(
+                streams.at[layer], normed_one.at[layer], lows.at[2 * layer],
+                vector(gain), vector(shift),
+            )
+            save(lows.at[2 * layer], keeps[0])
             save(normed_one.at[layer], keeps[2])
         elif kind in ("other", "own"):
             at = int(at)
@@ -1015,18 +1159,25 @@
             arrived.wait_recv()
             save(qkv_full.at[layer], keeps[3])
         elif kind == "head":
-            head = int(at)
-            slot, place_in = head // heads_slot, head % heads_slot
-            slope = 0.5 ** (head + 1.0) * jnp.where(core == 0, 1.0, 0.5 ** (slots * heads_slot))
-            attend_head(
-                qkv_full.at[layer], mixed.at[layer], slot * 3 * third + place_in * HD, third,
-                head * HD, slope, doc_cols, doc_rows,
-            )
-            if head == slots * heads_slot - 1:
+            slot = int(at)
+            if slot == 0:
+                logs[layer] = jnp.zeros(logs.shape[1:], f32)
+
+            def one_head(inner, carry):
+                attend_head(
+                    qkv_full.at[layer], mixed.at[layer], logs.at[layer], slot * heads_slot + inner,
+                    slot * 3 * third + inner * HD, third,
+                    head_slope(slot, inner, slots, heads_slot, core), doc_cols, doc_rows,
+                )
+                return carry
+
+            lax.fori_loop(0, heads_slot, one_head, 0)
+            if slot == slots - 1:
                 back_copy(layer).start()
                 rows = pl.ds(place(core, tokens), tokens)
                 attended[layer, :, pl.ds(place(core, half), half)] = mixed[layer, rows, :]
                 save(mixed.at[layer], keeps[4])
+                save(logs.at[layer], keeps[8])
         elif kind == "back":
             arrived = pltpu.make_async_remote_copy(
                 src_ref=mixed.at[layer, pl.ds(0, tokens), :],
@@ -1035,7 +1186,6 @@
                 device_id=partner, device_id_type=MESH,
             )
             arrived.wait_recv()
-            save(attended.at[layer], keeps[5])
         elif kind == "proj":
             tile(layer, "proj", 0, 1)
 
@@ -1047,15 +1197,17 @@
             tiles_of(features, piece)
         elif name == "norm_two":
             norm_rows(
-                middles.at[layer], normed_two.at[layer], vector(gain + 1), vector(shift + 1)
+                middles.at[layer], normed_two.at[layer], lows.at[2 * layer + 1],
+                vector(gain + 1), vector(shift + 1),
             )
-            save(middles.at[layer], keeps[1])
-            save(normed_two.at[layer], keeps[6])
+            save(lows.at[2 * layer + 1], keeps[1])
+            save(normed_two.at[layer], keeps[5])
         elif kind == "up":
             at = int(at)
             if at == 0 and layer > 0:
                 for copy in big_saves[layer - 1]:
                     copy.wait()
+                active_copy(layer - 1).wait_send()
             cols = w_up.shape[2]
             tile(layer, "up", at, hidden.shape[1] // cols)
             weight = w_up.at[at % 2]
@@ -1069,7 +1221,9 @@
 
             tiles_of(cols, piece)
             if (at + 1) * cols == hidden.shape[1]:
-                big_saves[layer] = [save(hidden, keeps[7]), save(active, keeps[8])]
+                rows = pl.ds(place(core, tokens), tokens)
+                big_saves[layer] = [save(hidden, keeps[6]), save(active, keeps[7].at[rows, :])]
+                active_copy(layer).start()
         elif kind == "down":
             at = int(at)
             rows = w_down.shape[1]
@@ -1099,6 +1253,8 @@
             if missing[step[0]] == 0:
                 del missing[step[0]]
     save(streams.at[layers], last_stream)
+    traded[...] = streams[layers].astype(bf16)
+    save(traded, last_low)
     done_already = [id(copy) for layer in range(layers - 1) for copy in big_saves[layer]]
     for copy in saves:
         if id(copy) not in done_already:
@@ -1106,6 +1262,14 @@
     for layer in range(layers):
         share_copy(layer).wait_send()
         back_copy(layer).wait_send()
+        rows = pl.ds(place(1 - core, tokens), tokens)
+        pltpu.make_async_remote_copy(
+            src_ref=active, dst_ref=saved[layer][7].at[rows, :],
+            send_sem=head_sems.at[4 * layers + 2 * layer],
+            recv_sem=head_sems.at[4 * layers + 2 * layer + 1],
+            device_id=partner, device_id_type=MESH,
+        ).wait_recv()
+    active_copy(layers - 1).wait_send()
 
     @pl.when(moved)
     def _():
@@ -1127,37 +1291,43 @@
     any_place = pl.BlockSpec(memory_space=pl.ANY)
     vmem = pl.BlockSpec(memory_space=pltpu.VMEM)
     saved = [
-        jax.ShapeDtypeStruct((tokens, features), f32),
-        jax.ShapeDtypeStruct((tokens, features), f32),
+        jax.ShapeDtypeStruct((tokens, features), bf16),
+        jax.ShapeDtypeStruct((tokens, features), bf16),
         jax.ShapeDtypeStruct((tokens, features), bf16),
         jax.ShapeDtypeStruct((length, slots * cols), bf16),
         jax.ShapeDtypeStruct((length, half), bf16),
         jax.ShapeDtypeStruct((tokens, features), bf16),
-        jax.ShapeDtypeStruct((tokens, features), bf16),
         jax.ShapeDtypeStruct((tokens, units), bf16),
-        jax.ShapeDtypeStruct((tokens, units), bf16),
+        jax.ShapeDtypeStruct((length, units), bf16),
+        jax.ShapeDtypeStruct((length, HD), f32),
     ]
     small_shape = (shards[-1].shape[0] * dp_size, shards[-1].shape[1] * mp_size)
     out_shape = [
         jax.ShapeDtypeStruct((s.shape[0] * dp_size, s.shape[1] * mp_size), s.dtype)
         for s in shards
     ]
-    out_shape += saved * layers + [jax.ShapeDtypeStruct((tokens, features), f32)]
+    out_shape += saved * layers + [
+        jax.ShapeDtypeStruct((tokens, features), f32),
+        jax.ShapeDtypeStruct((tokens, features), bf16),
+    ]
+    out_shape.append(jax.ShapeDtypeStruct((shards[-1].shape[0], features), f32))
     out = pl.pallas_call(
         functools.partial(
             forward_kernel, plans, order, mp_size, layers, vector_count, gain_rows, shift_rows
         ),
         out_shape=out_shape,
         in_specs=[any_place] * (len(shards) + 1) + [vmem] * 2,
-        out_specs=[any_place] * len(out_shape),
+        out_specs=[any_place] * (len(out_shape) - 1) + [vmem],
         scratch_shapes=[
             pltpu.VMEM((layers + 1, tokens, features), f32),
             pltpu.VMEM((layers, tokens, features), f32),
+            pltpu.VMEM((2 * layers, tokens, features), bf16),
             pltpu.VMEM((layers, tokens, features), bf16),
             pltpu.VMEM((layers, tokens, features), bf16),
             pltpu.VMEM((layers, tokens, slots * cols), bf16),
             pltpu.VMEM((layers, length, slots * cols), bf16),
             pltpu.VMEM((layers, length, half), bf16),
+            pltpu.VMEM((layers, length, HD), f32),
             pltpu.VMEM((layers, tokens, features), bf16),
             pltpu.VMEM((tokens, units), bf16),
             pltpu.VMEM((tokens, units), bf16),
@@ -1166,13 +1336,12 @@
             pltpu.VMEM((2, features, units // 8), bf16),
             pltpu.VMEM((2, features // 4, units), bf16),
             pltpu.VMEM(small_shape, bf16),
-            pltpu.VMEM((shards[-1].shape[0], features), f32),
             pltpu.VMEM((shards[-1].shape[0], units), f32),
             pltpu.VMEM((tokens, features), bf16),
             pltpu.SemaphoreType.DMA((8,)),
-            pltpu.SemaphoreType.DMA((9 * layers + 1,)),
+            pltpu.SemaphoreType.DMA((SAVED * layers + 2,)),
             pltpu.SemaphoreType.DMA((3,)),
-            pltpu.SemaphoreType.DMA((4 * layers,)),
+            pltpu.SemaphoreType.DMA((6 * layers,)),
             pltpu.SemaphoreType.DMA((total,)),
             pltpu.SemaphoreType.DMA((total,)),
             pltpu.SemaphoreType.DMA((len(shards),)),
@@ -1182,34 +1351,862 @@
         ),
     )(*shards, inputs, docs.reshape(-1, 1), docs.reshape(1, -1))
     n = len(shards)
-    return out[:n], [out[n + 9 * at : n + 9 * at + 9] for at in range(layers)], out[-1]
+    stored = [out[n + SAVED * at : n + SAVED * (at + 1)] for at in range(layers)]
+    return out[:n], stored, out[-3], out[-2], out[-1]
+
+
+KINDS = ("down", "up", "proj", "qkv")
+BACKWARD_STEPS = (
+    "turn_down", "W0", "W1", "W2", "W3",
+    "turn_up", "hidden_0", "hidden_1", "hidden_2", "hidden_3", "W0",
+    "hidden_4", "hidden_5", "W1", "hidden_6", "hidden_7", "norm_two", "mixed_0", "mixed_1",
+    "W2", "W3", "turn_proj", "W0", "W1", "W2", "W3", "turn_qkv",
+    "share", "head_0", "head_1", "rows_0", "rows_1", "rows_2",
+    "back", "W0", "W1", "W2", "W3", "rows_3", "rows_4", "rows_5", "norm_one",
+)
+
+
+def gelu_slope(v):
+    root = math.sqrt(2.0 / math.pi)
+    t = jnp.tanh(root * (v + 0.044715 * v * v * v))
+    return 0.5 * (1.0 + t) + 0.5 * v * (1.0 - t * t) * root * (1.0 + 3 * 0.044715 * v * v)
+
+
+def norm_back(src, upstream, total, low, gain):
+    features = src.shape[1]
+
+    def some_rows(at, carry):
+        rows = pl.ds(pl.multiple_of(at * ROWS, ROWS), ROWS)
+        value = src[rows, :].astype(f32)
+        center = value - jnp.mean(value, axis=-1, keepdims=True)
+        scale = lax.rsqrt(jnp.mean(center * center, axis=-1, keepdims=True) + norm_eps)
+        normal = center * scale
+        grad = upstream[rows, :]
+        inner = grad * gain
+        mean_inner = jnp.mean(inner, axis=-1, keepdims=True)
+        mean_both = jnp.mean(inner * normal, axis=-1, keepdims=True)
+        new = total[rows, :] + scale * (inner - mean_inner - normal * mean_both)
+        total[rows, :] = new
+        low[rows, :] = new.astype(bf16)
+        return (
+            carry[0] + jnp.sum(grad * normal, axis=0, keepdims=True),
+            carry[1] + jnp.sum(grad, axis=0, keepdims=True),
+            carry[2] + jnp.sum(new, axis=0, keepdims=True),
+        )
+
+    zero = jnp.zeros((1, features), f32)
+    return lax.fori_loop(0, src.shape[0] // ROWS, some_rows, (zero, zero, zero))
+
+
+def attend_back_head(
+    qkv, mixed, mixed_grad, logs, key_acc, value_acc, head, at, width, slope, doc_cols, doc_rows
+):
+    length = qkv.shape[0]
+    block = min(256, length)
+    key_acc[...] = jnp.zeros_like(key_acc)
+    value_acc[...] = jnp.zeros_like(value_acc)
+    query_cols, key_cols, value_cols = (
+        pl.ds(pl.multiple_of(at + part * width, HD), HD) for part in range(3)
+    )
+    mine = pl.ds(pl.multiple_of(head * HD, HD), HD)
+    for first_row in range(0, length, block):
+        rows = slice(first_row, first_row + block)
+        low, high = key_range(first_row, block)
+        query = qkv[rows, query_cols]
+        out_grad = mixed_grad[rows, mine]
+        values = mixed[rows, mine]
+        inner = jnp.sum(out_grad.astype(f32) * values.astype(f32), axis=-1, keepdims=True)
+        log = logs[rows, :]
+        log = jnp.sum(jnp.where(lane_of(log, head), log, 0.0), axis=-1, keepdims=True)
+        query_grad = 0.0
+        for first in range(low, high, block):
+            cols = slice(first, first + block)
+            key = qkv[cols, key_cols]
+            scores = block_scores(
+                query, key, slope, doc_cols[rows, :], doc_rows[:, cols], first, first == first_row
+            )
+            probs = jnp.exp(scores - log)
+            value_acc[cols, :] += dot_rows(probs.astype(bf16), out_grad)
+            prob_grad = dot_cols(out_grad, qkv[cols, value_cols])
+            score_grad = (probs * (prob_grad - inner)).astype(bf16)
+            query_grad = query_grad + dot(score_grad, key)
+            key_acc[cols, :] += dot_rows(score_grad, query)
+        qkv[rows, query_cols] = (query_grad * score_scale).astype(bf16)
+    qkv[:, key_cols] = (key_acc[...] * score_scale).astype(bf16)
+    qkv[:, value_cols] = value_acc[...].astype(bf16)
+
+
+class Rows:
+    def __init__(self, dims, mp_size, merged=False):
+        self.dims = tuple(dims)
+        self.merged = merged
+        self.masks = [0]
+        for dim in reversed([dim for dim in self.dims if dim != MP]):
+            self.masks = self.masks + [mask | dim for mask in self.masks]
+        self.kept = {0: len(self.masks)}
+        self.events = []
+        for stage, dim in enumerate(self.dims, 1):
+            self.kept[stage] = self.kept[stage - 1] // (1 if dim == MP else 2)
+            if dim == MP:
+                for hops in reversed(range(mp_size - 1)):
+                    self.events += [(stage, way, hops) for way in (1, -1)]
+            else:
+                count = mp_size if self.full(stage) and not merged else 1
+                self.events += [(stage, 0, at) for at in range(count)]
+
+    def full(self, stage):
+        return MP not in self.dims[: stage - 1]
+
+
+def number_rows(plans, mp_size):
+    index, total = {}, 0
+    for t, plan in enumerate(plans):
+        for stage, way, at in plan.events:
+            if way:
+                index[t, stage, way, at] = total
+                total += 1
+            elif (t, stage) not in index:
+                index[t, stage] = total
+                total += mp_size
+    return index, total
+
+
+class RowsWork:
+    def __init__(self, plans, mp_size, wides, cols, sums, recv, sems):
+        self.plans, self.mp_size = plans, mp_size
+        self.wides, self.cols = wides, cols
+        self.sums, self.recv = sums, recv
+        self.send_sems, self.recv_sems, self.credit_sems = sems
+        self.z = lax.axis_index(MP)
+        self.d = lax.axis_index(DP)
+        self.index, _ = number_rows(plans, mp_size)
+        self.brought = {}
+        self.credited = set()
+        self.outgoing = {}
+        self.left, self.left_stage = {}, {}
+        for t, plan in enumerate(plans):
+            self.left[t] = len(plan.events)
+            for event in plan.events:
+                key = t, event[0]
+                self.left_stage[key] = self.left_stage.get(key, 0) + 1
+
+    def inside(self, at):
+        return (at >= 0) & (at < self.mp_size)
+
+    def slab(self, t):
+        return t % 4 if t < 8 else 4
+
+    def part(self, t, low, high, block):
+        wide, cols = self.wides[t], self.cols[t]
+        where = pl.ds(0, cols * self.mp_size) if block is None else pl.ds(place(block, cols), cols)
+        return self.sums[self.slab(t)].at[pl.ds(low * wide, (high - low) * wide), where]
+
+    def landing(self, t, event, block):
+        stage, way, at = event
+        ref = self.recv[self.slab(t), stage]
+        if way:
+            return ref.at[block if way == 1 or at > 0 else self.mp_size]
+        if block is None:
+            return ref.at[0]
+        return ref.at[block if self.plans[t].full(stage) else 0]
+
+    def remote(self, t, event, block, src, dst, to):
+        stage, way, at = event
+        if way:
+            sem = self.index[(t,) + event]
+        else:
+            sem = self.index[t, stage] + (0 if block is None else block)
+        return pltpu.make_async_remote_copy(
+            src_ref=src,
+            dst_ref=dst,
+            send_sem=self.send_sems.at[sem],
+            recv_sem=self.recv_sems.at[sem],
+            device_id=to,
+            device_id_type=MESH,
+        )
+
+    def launch(self, t, copy, when=None):
+        if when is None:
+            copy.start()
+        else:
+            pl.when(when)(copy.start)
+        self.outgoing.setdefault(t, []).append((copy, when))
+
+    def settle(self, t):
+        for copy, when in self.outgoing.pop(t, []):
+            if when is None:
+                copy.wait_send()
+            else:
+                pl.when(when)(copy.wait_send)
+
+    def take_credit(self, t, stage, way=0):
+        if not 4 <= t < 8 or (t, stage, way) in self.credited:
+            return
+        self.credited.add((t, stage, way))
+        sem = self.credit_sems.at[t - 4, stage, 1 if way == -1 else 0]
+        if way:
+            pl.when(self.inside(self.z + way))(lambda: pl.semaphore_wait(sem, 1))
+        else:
+            pl.semaphore_wait(sem, 1)
+
+    def give_credit(self, t, stage):
+        dim = self.plans[t + 4].dims[stage - 1]
+        if dim != MP:
+            pl.semaphore_signal(
+                self.credit_sems.at[t, stage, 0], inc=1,
+                device_id={DP: flip(self.d, dim)}, device_id_type=MESH,
+            )
+            return
+        for way in (1, -1):
+
+            @pl.when(self.inside(self.z - way))
+            def _(way=way):
+                pl.semaphore_signal(
+                    self.credit_sems.at[t, stage, 1 if way == -1 else 0], inc=1,
+                    device_id={MP: self.z - way}, device_id_type=MESH,
+                )
+
+    def line_copy(self, t, stage, way, hops):
+        event = (stage, way, hops - 1)
+        block = self.z + way * hops
+        dst = self.landing(t, event, block)
+        src = self.part(t, 0, self.plans[t].kept[stage], block)
+        return self.remote(t, event, block, src, dst, {MP: self.z + way})
+
+    def arrival(self, t, event, block):
+        dst = self.landing(t, event, block)
+        return self.remote(t, event, block, dst, dst, {DP: self.d, MP: self.z})
+
+    def add(self, dst, src, rows_count):
+        step = 16
+
+        def some_rows(at, carry):
+            rows = pl.ds(pl.multiple_of(at * step, step), step)
+            dst[rows, :] += src[rows, :]
+            return carry
+
+        lax.fori_loop(0, rows_count // step, some_rows, 0)
+
+    def advance(self, t, stage, block, other):
+        plan = self.plans[t]
+        if stage > len(plan.dims):
+            return
+        dim = plan.dims[stage - 1]
+        if dim == MP:
+            for way, end in ((1, 0), (-1, self.mp_size - 1)):
+                self.take_credit(t, stage, way)
+                for hops in range(1, self.mp_size) if block is None else (other,) * (other > 0):
+                    copy = self.line_copy(t, stage, way, hops)
+                    self.launch(t, copy, self.z == end)
+            return
+        self.take_credit(t, stage)
+        event = (stage, 0, None)
+        src = self.part(t, plan.kept[stage], plan.kept[stage - 1], block)
+        dst = self.landing(t, event, block)
+        self.launch(t, self.remote(t, event, block, src, dst, {DP: flip(self.d, dim)}))
+
+    def step(self, t, event, finish):
+        stage, way, at = event
+        plan = self.plans[t]
+        kept = plan.kept[stage]
+        if way:
+            block = self.z + way * at
+            here = self.inside(block) & self.inside(self.z - way)
+            if at > 0:
+                self.take_credit(t, stage, way)
+
+            @pl.when(here)
+            def _():
+                self.arrival(t, event, block).wait_recv()
+                self.add(
+                    self.part(t, 0, kept, block), self.landing(t, event, block),
+                    kept * self.wides[t],
+                )
+
+            if at > 0:
+                self.launch(t, self.line_copy(t, stage, way, at), here)
+            else:
+                self.brought[t] = self.brought.get(t, 0) + 1
+                if self.brought[t] == 2:
+                    self.advance(t, stage + 1, self.z, 0)
+        else:
+            if plan.full(stage):
+                block = None if plan.merged else flip(self.z, at)
+            else:
+                block = self.z
+            self.arrival(t, event, block).wait_recv()
+            self.add(
+                self.part(t, 0, kept, block), self.landing(t, event, block), kept * self.wides[t]
+            )
+            self.advance(t, stage + 1, block, at)
+        self.left[t] -= 1
+        self.left_stage[t, stage] -= 1
+        if t < 4 and self.left_stage[t, stage] == 0:
+            self.give_credit(t, stage)
+        if self.left[t] == 0:
+            finish(t)
+
+
+def backward_kernel(
+    plans, order, mp_size, layers, vector_count, gain_rows, shift_rows, *refs
+):
+    n = len(plans)
+    full = [refs[4 * layer : 4 * layer + 4] for layer in range(layers)]
+    at = 4 * layers
+    cotangent, vectors, doc_cols, doc_rows = refs[at : at + 4]
+    at += 4
+    saved = [refs[at + SAVED * layer : at + SAVED * (layer + 1)] for layer in range(layers)]
+    at += SAVED * layers
+    outs, (norm_ref, input_grad, input_low) = refs[at : at + n], refs[at + n : at + n + 3]
+    at += n + 3
+    sums = refs[at : at + 5]
+    at += 5
+    recv = {}
+    for slab, plan in zip((0, 1, 2, 3, 4), plans[:4] + plans[8:]):
+        for stage in range(1, len(plan.dims) + 1):
+            recv[slab, stage] = refs[at]
+            at += 1
+    (
+        blocks, left_t, turn_send, grad, acc, low, hidden_buf, w_a, w_b, normed,
+        source, qkv, mixed, mixed_other, logs, mixed_grad, mixed_send, row_other, key_acc,
+        value_acc, vector_sums, bias_sums, tiles,
+        load_sems, core_sems, out_sems, tile_sems, send_sems, recv_sems, credit_sems,
+        block_credit, left_credit,
+    ) = refs[at:]
+    cols = [out.shape[1] for out in outs]
+    wides = [out.shape[0] for out in outs]
+    work = RowsWork(plans, mp_size, wides, cols, sums, recv, (send_sems, recv_sems, credit_sems))
+    z, d = work.z, work.d
+    core = d % 2
+    partner = {DP: flip(d, 1)}
+    upper = [dim for dim in plans[0].dims if dim != MP]
+    mp_bits = bits_of(mp_size)
+    tokens, features = low.shape
+    half = features // 2
+    own_rows = pl.ds(place(core, tokens), tokens)
+    other_rows = pl.ds(place(1 - core, tokens), tokens)
+    half_qkv = qkv.shape[1]
+    slots = mp_size // 2
+    third = half_qkv // slots // 3
+    heads_slot = third // HD
+    wide = w_a.shape[2]
+    per_block = cols[0] // wide
+
+    greet(z, d, upper, mp_size, mp_bits)
+
+    loads = {}
+
+    def fetch(key, src, dst):
+        copy = pltpu.make_async_copy(src, dst, load_sems.at[len(loads)])
+        copy.start()
+        loads[key] = copy
+
+    pushes = {}
+
+    def push(key, src, dst):
+        at = 2 * len(pushes)
+        copy = pltpu.make_async_remote_copy(
+            src_ref=src, dst_ref=dst, send_sem=core_sems.at[at], recv_sem=core_sems.at[at + 1],
+            device_id=partner, device_id_type=MESH,
+        )
+        copy.start()
+        pushes[key] = at, copy
+
+    def pushed(key):
+        pushes[key][1].wait_send()
+
+    def arrived(key, dst):
+        at = pushes[key][0]
+        pltpu.make_async_remote_copy(
+            src_ref=dst, dst_ref=dst, send_sem=core_sems.at[at], recv_sem=core_sems.at[at + 1],
+            device_id=partner, device_id_type=MESH,
+        ).wait_recv()
+
+    def give(sem):
+        pl.semaphore_signal(sem, inc=1, device_id=partner, device_id_type=MESH)
+
+    fetch("cotangent", cotangent, low)
+    vector_sums[...] = jnp.zeros_like(vector_sums)
+    bias_sums[...] = jnp.zeros_like(bias_sums)
+
+    def block_cols(at):
+        block = flip(z, at // per_block)
+        return pl.ds(pl.multiple_of(block * cols[0] + (at % per_block) * wide, wide), wide)
+
+    def row_cols(at):
+        count = half_qkv // wide
+        part = core if at < count else 1 - core
+        return pl.ds(pl.multiple_of(part * half_qkv + (at % count) * wide, wide), wide)
+
+    def fetch_tile(layer, name, at):
+        qkv_w, proj, up, down = full[layer]
+        slot = at % 2
+        if name == "hidden":
+            where = block_cols(at)
+            fetch((layer, "w_a", name, at), down.at[:, where], w_a.at[slot])
+            fetch((layer, "w_b", name, at), up.at[:, where], w_b.at[slot])
+            fetch((layer, "z", name, at), saved[layer][6].at[:, where], hidden_buf.at[slot])
+        elif name == "mixed":
+            first = place(1 - core if at == 0 else core, half)
+            fetch((layer, "w_a", name, at), proj.at[:, pl.ds(first, half)], w_a.at[slot])
+        else:
+            fetch((layer, "w_b", name, at), qkv_w.at[:, row_cols(at)], w_b.at[slot])
+
+    counts = {"hidden": mp_size * per_block, "mixed": 2, "rows": 2 * half_qkv // wide}
+
+    def use_tile(layer, name, at):
+        for which in ("w_a", "w_b", "z"):
+            if (layer, which, name, at) in loads:
+                loads[layer, which, name, at].wait()
+        if at + 1 < counts[name]:
+            fetch_tile(layer, name, at + 1)
+
+    def fetch_block(layer, s):
+        where = pl.ds(place(flip(z, s), cols[0]), cols[0])
+        fetch((layer, "block", s), saved[layer][7].at[:, where], blocks.at[s % 2])
+
+    def accumulate(left, weight, first):
+        def piece(at, carry):
+            rows = pl.ds(pl.multiple_of(at * TILE, TILE), TILE)
+            values = dot_cols(left[...], weight[rows, :])
+            if first:
+                acc[:, rows] = values
+            else:
+                acc[:, rows] += values
+            return carry
+
+        lax.fori_loop(0, features // TILE, piece, 0)
+
+    def put_vector(row, values):
+        vector_sums[row : row + 1, :] = values
+
+    def turn(use, src):
+        slot = use % 2
+        masks = plans[use].masks
+        if use >= 2:
+            pushed(("left", use - 2))
+            pl.semaphore_wait(left_credit.at[slot], 1)
+        for row, mask in enumerate(masks):
+            there = pl.ds(row * wides[use], wides[use])
+            theirs = pl.ds(place(flip(d, mask | 1), wides[use]), wides[use])
+            mine = pl.ds(place(flip(d, mask), wides[use]), wides[use])
+            turn_send[slot, there, :] = src[:, theirs].astype(f32).T.astype(bf16)
+            left_t[slot, there, own_rows] = src[:, mine].astype(f32).T.astype(bf16)
+        push(("left", use), turn_send.at[slot], left_t.at[slot, :, own_rows])
+
+    def compute(layer, name):
+        kind, _, at = name.partition("_")
+        keeps = saved[layer]
+        gain = layer * gain_rows
+        shift = layers * gain_rows + layer * shift_rows
+        last = layer == layers - 1
+        use = 4 * (layers - 1 - layer)
+        if name == "turn_down":
+            if last:
+                fetch_block(layer, 0)
+                fetch_block(layer, 1)
+                loads["cotangent"].wait()
+
+                def some_rows(at, carry):
+                    rows = pl.ds(pl.multiple_of(at * ROWS, ROWS), ROWS)
+                    values = low[rows, :].astype(f32)
+                    grad[rows, :] = values
+                    return carry + jnp.sum(values, axis=0, keepdims=True)
+
+                total = lax.fori_loop(
+                    0, tokens // ROWS, some_rows, jnp.zeros((1, features), f32)
+                )
+                put_vector(shift + 2, total)
+            else:
+                pushed((layer + 1, "back"))
+                pushed((layer + 1, "mixed"))
+            fetch_tile(layer, "hidden", 0)
+            fetch((layer, "normed_two"), keeps[5], normed)
+            fetch((layer, "middle"), keeps[1], source)
+            fetch((layer, "qkv"), keeps[3], qkv)
+            fetch((layer, "mixed"), keeps[4], mixed)
+            fetch((layer, "logs"), keeps[8], logs)
+            push((layer, "mixed"), keeps[4], mixed_other)
+            turn(use, low)
+        elif name == "turn_up":
+            loads[layer, "normed_two"].wait()
+            turn(use + 1, normed)
+            fetch((layer, "normed_one"), keeps[2], normed)
+        elif name == "turn_proj":
+            turn(use + 2, low)
+        elif name == "turn_qkv":
+            loads[layer, "normed_one"].wait()
+            turn(use + 3, normed)
+        elif kind == "hidden":
+            at = int(at)
+            use_tile(layer, "hidden", at)
+            slot = at % 2
+            s, inner = at // per_block, at % per_block
+            to_block = s % 2
+            if inner == 0 and s >= 2:
+                pushed((layer, "grads", s - 2))
+
+            def piece(first):
+                here = pl.ds(first, TILE)
+                values = dot(low[...], w_a[slot, :, here])
+                values = values * gelu_slope(hidden_buf[slot, :, here].astype(f32))
+                to = pl.multiple_of(flip(z, s) * cols[0] + inner * wide + first, TILE)
+                bias_sums[vector_count + layer : vector_count + layer + 1, pl.ds(to, TILE)] = (
+                    jnp.sum(values, axis=0, keepdims=True)
+                )
+                to = pl.ds(pl.multiple_of(inner * wide + first, TILE), TILE)
+                blocks[to_block, own_rows, to] = values.astype(bf16)
+
+            tiles_of(wide, piece)
+            left = blocks.at[to_block, own_rows, pl.ds(inner * wide, wide)]
+            accumulate(left, w_b.at[slot], at == 0)
+            if inner == per_block - 1:
+                pl.semaphore_wait(block_credit.at[s], 1)
+                part = blocks.at[to_block, own_rows, :]
+                push((layer, "grads", s), part, part)
+        elif name == "norm_two":
+            loads[layer, "middle"].wait()
+            sums_of = norm_back(source, acc, grad, low, vectors[gain + 1 : gain + 2, :])
+            put_vector(gain + 1, sums_of[0])
+            put_vector(shift + 1, sums_of[1])
+            fetch((layer, "stream"), keeps[0], source)
+            fetch_tile(layer, "mixed", 0)
+        elif kind == "mixed":
+            at = int(at)
+            use_tile(layer, "mixed", at)
+            if at == 0 and not last:
+                pushed((layer + 1, "share"))
+
+            def piece(first):
+                here = pl.ds(first, TILE)
+                values = dot(low[...], w_a[at % 2, :, here]).astype(bf16)
+                if at == 0:
+                    mixed_send[:, here] = values
+                else:
+                    mixed_grad[own_rows, here] = values
+
+            tiles_of(half, piece)
+            if at == 0:
+                push((layer, "share"), mixed_send, mixed_grad.at[own_rows, :])
+        elif name == "share":
+            arrived((layer, "share"), mixed_grad.at[other_rows, :])
+            loads[layer, "qkv"].wait()
+            loads[layer, "logs"].wait()
+            fetch_tile(layer, "rows", 0)
+        elif kind == "head":
+            slot = int(at)
+            if slot == 0 and layer > 0:
+                pushed((layer, "grads", 2))
+                pushed((layer, "grads", 3))
+                fetch_block(layer - 1, 0)
+                fetch_block(layer - 1, 1)
+
+            def one_head(inner, carry):
+                attend_back_head(
+                    qkv, mixed, mixed_grad, logs, key_acc, value_acc, slot * heads_slot + inner,
+                    slot * 3 * third + inner * HD, third,
+                    head_slope(slot, inner, slots, heads_slot, core), doc_cols, doc_rows,
+                )
+                return carry
+
+            lax.fori_loop(0, heads_slot, one_head, 0)
+            if slot == slots - 1:
+                push((layer, "back"), qkv, row_other)
+        elif name == "back":
+            arrived((layer, "back"), row_other)
+        elif kind == "rows":
+            at = int(at)
+            use_tile(layer, "rows", at)
+            count = half_qkv // wide
+            here = pl.ds(at % count * wide, wide)
+            left = (qkv if at < count else row_other).at[own_rows, here]
+            accumulate(left, w_b.at[at % 2], at == 0)
+        elif name == "norm_one":
+            loads[layer, "stream"].wait()
+            sums_of = norm_back(source, acc, grad, low, vectors[gain : gain + 1, :])
+            put_vector(gain, sums_of[0])
+            put_vector(shift, sums_of[1])
+            if layer > 0:
+                put_vector(shift - shift_rows + 2, sums_of[2])
+            else:
+                copy = pltpu.make_async_copy(grad, input_grad, out_sems.at[n])
+                copy.start()
+                loads["input_grad"] = copy
+                copy = pltpu.make_async_copy(low, input_low, out_sems.at[n + 1])
+                copy.start()
+                loads["input_low"] = copy
+
+    def weight(t, s):
+        slab = work.slab(t)
+        out = sums[slab]
+        if t == 8:
+            for row, mask in enumerate(plans[t].masks):
+                block = flip(d, mask)
+                part = vector_sums[:, pl.ds(place(block, cols[t]), cols[t])]
+                for m in range(mp_size):
+                    first = pl.multiple_of(m * (bias_sums.shape[1] // mp_size) + block * cols[t], cols[t])
+                    values = part + bias_sums[:, pl.ds(first, cols[t])]
+                    rows = slice(row * wides[t], (row + 1) * wides[t])
+                    out[rows, m * cols[t] : (m + 1) * cols[t]] = values.astype(bf16)
+            work.advance(t, 1, None, 0)
+            return
+        layer = layers - 1 - t // 4
+        if s == 0:
+            if t >= 4:
+                work.settle(t - 4)
+                loads["out", t - 4].wait()
+            arrived(("left", t), left_t.at[t % 2, :, other_rows])
+        block = flip(z, s)
+        left = left_t.at[t % 2]
+
+        def multiply(right, first, step):
+            def piece(at, carry):
+                here = pl.multiple_of(at * step, step)
+                there = pl.ds(pl.multiple_of(block * cols[t] + here, step), step)
+                values = dot(left[...], right[:, pl.ds(pl.multiple_of(first + here, step), step)])
+                out[:, there] = values.astype(bf16)
+                return carry
+
+            lax.fori_loop(0, cols[t] // step, piece, 0)
+
+        if slab < 2:
+            if slab == 0:
+                loads[layer, "block", s].wait()
+            else:
+                arrived((layer, "grads", s), blocks.at[s % 2, other_rows, :])
+            multiply(blocks.at[s % 2], 0, TILE)
+            if slab == 0 and s < 2:
+                fetch_block(layer, s + 2)
+            elif slab == 0:
+                give(block_credit.at[s - 2])
+            elif s < 2:
+                give(block_credit.at[s + 2])
+        else:
+            if slab == 2 and s == 0:
+                loads[layer, "mixed"].wait()
+                arrived((layer, "mixed"), mixed_other)
+            ours = block // slots == core
+            within = pl.multiple_of((block % slots) * cols[t], cols[t])
+            near, far = ((mixed, mixed_other), (qkv, row_other))[slab - 2]
+            pl.when(ours)(lambda: multiply(near, within, TILE))
+            pl.when(jnp.logical_not(ours))(lambda: multiply(far, within, TILE))
+        if s == mp_size - 1 and t < 6:
+            give(left_credit.at[t % 2])
+        work.advance(t, 1, block, s)
+
+    def finish(t):
+        final = work.part(t, 0, 1, z)
+        copy = pltpu.make_async_copy(final, outs[t], out_sems.at[t])
+        copy.start()
+        loads["out", t] = copy
+        step = 16
+
+        def some_rows(at, carry):
+            rows = pl.ds(pl.multiple_of(at * step, step), step)
+            part = final[rows, :].astype(f32)
+            part = part * part
+            if t == 8:
+                row = at * step + lax.broadcasted_iota(jnp.int32, part.shape, 0)
+                part = jnp.where(row < vector_count, part * (1.0 / mp_size), part)
+            total = carry
+            for top in range(0, step, 8):
+                for side in range(0, cols[t], HD):
+                    total = total + part[top : top + 8, side : side + HD]
+            return total
+
+        tiles[0] += lax.fori_loop(0, wides[t] // step, some_rows, jnp.zeros((8, HD), f32))
+
+    tiles[0] = jnp.zeros(tiles.shape[1:], f32)
+    for step in order:
+        if step[0] == "weight":
+            weight(*step[1:])
+        elif isinstance(step[1], str):
+            compute(*step)
+        else:
+            work.step(*step, finish)
+
+    pairs = [{DP: flip(d, bit)} for bit in [1] + upper]
+    pairs += [{MP: flip(z, bit)} for bit in mp_bits]
+    for at, to in enumerate(pairs):
+        exchange = pltpu.make_async_remote_copy(
+            src_ref=tiles.at[2 * at],
+            dst_ref=tiles.at[2 * at + 1],
+            send_sem=tile_sems.at[2 * at],
+            recv_sem=tile_sems.at[2 * at + 1],
+            device_id=to,
+            device_id_type=MESH,
+        )
+        exchange.start()
+        exchange.wait()
+        tiles[2 * at + 2] = tiles[2 * at] + tiles[2 * at + 1]
+    norm_ref[...] = tiles[2 * len(pairs)]
+
+    for s in (2, 3):
+        pushed((0, "grads", s))
+    for key in ((0, "mixed"), (0, "share"), (0, "back"), ("left", 6), ("left", 7)):
+        pushed(key)
+    for t in range(n):
+        work.settle(t)
+        if t >= 4:
+            loads["out", t].wait()
+    loads["input_grad"].wait()
+    loads["input_low"].wait()
+
+
+def backward_chain(plans, layers):
+    chain = []
+    for done, layer in enumerate(reversed(range(layers))):
+        turns = {"turn_down": 0, "turn_up": 1, "turn_proj": 2, "back": 3}
+        t = None
+        for name in BACKWARD_STEPS:
+            if name.startswith("W"):
+                chain.append(("weight", t, int(name[1:])))
+                continue
+            chain.append((layer, name))
+            if name in turns:
+                t = 4 * done + turns[name]
+            if name == "norm_one" and layer == 0:
+                chain.append(("weight", len(plans) - 1, 0))
+    return chain
+
+
+def backward_order(plans, layers, table):
+    chain = backward_chain(plans, layers)
+    if not table:
+        out = []
+        for at, step in enumerate(chain):
+            out.append(step)
+            if step[0] == "weight" and (step[1] == 8 or step[2] == 3):
+                out += [(step[1], event) for event in plans[step[1]].events]
+        return out
+    steps = chain + [(t, event) for t, plan in enumerate(plans) for event in plan.events]
+    return [steps[at] for at in table]
+
+
+def backward_all(
+    full, cotangent, vectors, docs, stored, plans, order, dp_size, mp_size, layers, vector_count,
+    gain_rows, shift_rows,
+):
+    n = len(plans)
+    _, total = number_rows(plans, mp_size)
+    tokens, features = cotangent.shape
+    length = docs.shape[0]
+    units = full[2].shape[1]
+    wides = [features // dp_size] * 8 + [vectors.shape[0]]
+    cols = [
+        full[4 * layer + kind].shape[1] // mp_size
+        for layer in reversed(range(layers))
+        for kind in (3, 2, 1, 0)
+    ] + [max(HD, features // dp_size)]
+    rounds = len(bits_of(dp_size)) + len(bits_of(mp_size))
+    half_qkv = full[0].shape[1] // 2
+    any_place = pl.BlockSpec(memory_space=pl.ANY)
+    vmem = pl.BlockSpec(memory_space=pltpu.VMEM)
+    out_shape = [jax.ShapeDtypeStruct((wide, each), bf16) for wide, each in zip(wides, cols)]
+    out_shape += [
+        jax.ShapeDtypeStruct((8, HD), f32),
+        jax.ShapeDtypeStruct((tokens, features), f32),
+        jax.ShapeDtypeStruct((tokens, features), bf16),
+    ]
+    slabs = (0, 1, 2, 3, 8)
+    scratch = [
+        pltpu.VMEM((plans[t].kept[0] * wides[t], mp_size * cols[t]), bf16) for t in slabs
+    ]
+    for t in slabs:
+        plan = plans[t]
+        for stage, dim in enumerate(plan.dims, 1):
+            rows = plan.kept[stage] * wides[t]
+            if dim == MP:
+                shape = (mp_size + 1, rows, cols[t])
+            elif not plan.full(stage):
+                shape = (1, rows, cols[t])
+            elif plan.merged:
+                shape = (1, rows, mp_size * cols[t])
+            else:
+                shape = (mp_size, rows, cols[t])
+            scratch.append(pltpu.VMEM(shape, bf16))
+    wide = 512
+    scratch += [
+        pltpu.VMEM((2, length, cols[0]), bf16),
+        pltpu.VMEM((2, features // 2, length), bf16),
+        pltpu.VMEM((2, features // 2, tokens), bf16),
+        pltpu.VMEM((tokens, features), f32),
+        pltpu.VMEM((tokens, features), f32),
+        pltpu.VMEM((tokens, features), bf16),
+        pltpu.VMEM((2, tokens, wide), bf16),
+        pltpu.VMEM((2, features, wide), bf16),
+        pltpu.VMEM((2, features, wide), bf16),
+        pltpu.VMEM((tokens, features), bf16),
+        pltpu.VMEM((tokens, features), bf16),
+        pltpu.VMEM((length, half_qkv), bf16),
+        pltpu.VMEM((length, features // 2), bf16),
+        pltpu.VMEM((length, features // 2), bf16),
+        pltpu.VMEM((length, HD), f32),
+        pltpu.VMEM((length, features // 2), bf16),
+        pltpu.VMEM((tokens, features // 2), bf16),
+        pltpu.VMEM((length, half_qkv), bf16),
+        pltpu.VMEM((length, HD), f32),
+        pltpu.VMEM((length, HD), f32),
+        pltpu.VMEM((wides[8], features), f32),
+        pltpu.VMEM((wides[8], units), f32),
+        pltpu.VMEM((2 * rounds + 1, 8, HD), f32),
+        pltpu.SemaphoreType.DMA((110,)),
+        pltpu.SemaphoreType.DMA((2 * 11 * layers,)),
+        pltpu.SemaphoreType.DMA((n + 2,)),
+        pltpu.SemaphoreType.DMA((2 * rounds,)),
+        pltpu.SemaphoreType.DMA((total,)),
+        pltpu.SemaphoreType.DMA((total,)),
+        pltpu.SemaphoreType.REGULAR((4, len(plans[0].dims) + 1, 2)),
+        pltpu.SemaphoreType.REGULAR((mp_size,)),
+        pltpu.SemaphoreType.REGULAR((2,)),
+    ]
+    operands = list(full[: 4 * layers]) + [cotangent, vectors]
+    operands += [docs.reshape(-1, 1), docs.reshape(1, -1)]
+    specs = [any_place] * (4 * layers + 1) + [vmem] * 3
+    for each in stored:
+        operands += each
+        specs += [any_place] * SAVED
+    out = pl.pallas_call(
+        functools.partial(
+            backward_kernel, plans, order, mp_size, layers, vector_count, gain_rows, shift_rows
+        ),
+        out_shape=out_shape,
+        in_specs=specs,
+        out_specs=[any_place] * n + [vmem, any_place, any_place],
+        scratch_shapes=scratch,
+        compiler_params=pltpu.CompilerParams(
+            collective_id=1, has_side_effects=True, vmem_limit_bytes=63 * 2**20
+        ),
+    )(*operands)
+    return list(out[:n]), out[n], out[n + 1], out[n + 2]
 
 
 forward_table = (
-    23, 22, 117, 25, 95, 0, 189, 27, 94, 119, 1, 116, 188, 2, 191, 96, 190, 3, 24, 4, 45, 121,
-    118, 26, 97, 46, 98, 193, 70, 192, 47, 69, 5, 71, 194, 48, 197, 13, 196, 195, 28, 120, 49, 18,
-    200, 99, 30, 124, 34, 31, 29, 76, 10, 9, 123, 50, 72, 12, 198, 199, 129, 126, 41, 207, 11, 58,
-    8, 6, 32, 73, 77, 7, 201, 101, 112, 78, 33, 125, 122, 105, 44, 208, 205, 203, 127, 74, 75,
-    134, 128, 59, 107, 36, 35, 103, 106, 60, 204, 104, 39, 83, 135, 37, 40, 79, 17, 102, 202, 57,
-    65, 80, 131, 52, 42, 90, 82, 38, 209, 114, 206, 136, 81, 86, 100, 67, 51, 16, 165, 210, 20,
-    84, 132, 164, 14, 43, 91, 19, 54, 113, 15, 53, 140, 163, 87, 133, 130, 21, 211, 212, 167, 137,
-    213, 109, 85, 214, 55, 56, 138, 215, 216, 88, 142, 217, 218, 219, 166, 171, 62, 111, 139, 145,
-    89, 61, 170, 63, 66, 110, 92, 220, 169, 64, 221, 222, 68, 108, 223, 224, 225, 226, 227, 93,
-    228, 141, 229, 230, 147, 146, 231, 115, 232, 233, 234, 148, 144, 143, 153, 168, 172, 235, 236,
-    237, 150, 184, 238, 173, 239, 149, 177, 176, 157, 240, 241, 178, 174, 175, 242, 179, 154, 180,
-    243, 244, 156, 151, 152, 159, 160, 181, 158, 155, 182, 183, 186, 245, 246, 161, 247, 162, 248,
-    249, 250, 251, 185, 187, 252, 253, 254, 255, 256, 257, 258, 259,
+    116, 1, 22, 23, 188, 0, 189, 95, 118, 117, 97, 191, 119, 24, 190, 25, 3, 121, 94, 193, 5, 192,
+    194, 26, 27, 206, 2, 71, 99, 4, 195, 120, 29, 69, 11, 199, 123, 196, 96, 28, 30, 197, 122, 13,
+    70, 128, 31, 127, 73, 6, 7, 8, 98, 33, 34, 9, 129, 44, 203, 72, 10, 32, 77, 202, 14, 45, 134,
+    19, 125, 124, 207, 76, 18, 12, 100, 75, 204, 41, 205, 37, 126, 46, 35, 103, 74, 198, 79, 105,
+    20, 200, 107, 201, 16, 208, 47, 136, 102, 36, 209, 106, 104, 42, 78, 17, 15, 210, 39, 48, 112,
+    52, 38, 21, 211, 101, 51, 49, 82, 43, 83, 81, 212, 80, 135, 213, 50, 57, 54, 113, 214, 165,
+    53, 132, 85, 164, 163, 131, 215, 108, 65, 55, 40, 56, 216, 138, 133, 217, 87, 60, 58, 111, 84,
+    130, 91, 66, 218, 140, 61, 59, 114, 167, 90, 219, 86, 139, 171, 110, 166, 62, 88, 137, 92, 67,
+    170, 146, 63, 64, 145, 89, 109, 220, 68, 221, 222, 223, 141, 142, 224, 115, 169, 225, 226, 93,
+    168, 227, 228, 173, 229, 230, 172, 231, 232, 233, 143, 147, 144, 234, 148, 235, 152, 176, 236,
+    237, 153, 174, 175, 180, 151, 181, 238, 177, 149, 150, 239, 157, 154, 240, 179, 182, 158, 155,
+    156, 178, 184, 183, 159, 241, 242, 161, 160, 185, 243, 162, 244, 245, 246, 247, 187, 248, 249,
+    250, 186, 251, 252, 253, 254, 255,
 )
-fold_table = (
-    50, 25, 1, 28, 29, 122, 169, 2, 8, 30, 9, 0, 145, 119, 31, 95, 53, 51, 55, 3, 74, 11, 10, 26,
-    15, 4, 6, 96, 146, 75, 123, 32, 72, 97, 19, 147, 7, 27, 102, 124, 14, 38, 125, 73, 5, 52, 94,
-    126, 37, 12, 103, 131, 54, 132, 136, 104, 105, 76, 109, 42, 18, 33, 57, 36, 168, 135, 166,
-    113, 34, 35, 108, 144, 39, 98, 16, 40, 46, 120, 80, 112, 58, 81, 13, 170, 140, 99, 20, 101,
-    172, 79, 56, 78, 83, 41, 60, 77, 148, 100, 82, 167, 44, 106, 107, 17, 121, 150, 43, 59, 110,
-    127, 111, 84, 173, 129, 128, 47, 153, 61, 130, 85, 87, 174, 133, 62, 134, 114, 149, 86, 171,
-    45, 89, 175, 88, 65, 178, 137, 138, 63, 152, 151, 177, 154, 156, 48, 176, 179, 21, 64, 91,
-    157, 67, 90, 115, 116, 22, 181, 66, 155, 180, 117, 142, 182, 159, 183, 69, 158, 161, 141, 93,
-    23, 160, 68, 92, 185, 184, 162, 71, 70, 163, 139, 24, 49, 118, 187, 143, 186, 164, 165,
+backward_table = (
+    0, 1, 2, 3, 4, 5, 6, 7, 8, 9, 10, 11, 12, 13, 14, 15, 16, 17, 87, 18, 19, 20, 21, 85, 96, 22,
+    23, 88, 24, 25, 26, 27, 28, 29, 86, 90, 108, 30, 89, 109, 31, 32, 99, 110, 107, 33, 34, 35,
+    111, 98, 92, 91, 36, 97, 37, 113, 38, 100, 114, 101, 122, 93, 121, 112, 103, 102, 125, 39,
+    123, 40, 126, 94, 41, 124, 127, 42, 104, 105, 95, 43, 115, 44, 45, 46, 47, 116, 106, 48, 49,
+    50, 51, 52, 128, 53, 54, 55, 136, 56, 117, 129, 57, 118, 58, 130, 59, 60, 61, 62, 131, 63,
+    120, 132, 119, 137, 64, 65, 66, 67, 68, 69, 138, 70, 71, 135, 146, 72, 133, 73, 74, 134, 140,
+    149, 139, 157, 75, 76, 77, 148, 147, 151, 141, 171, 150, 142, 78, 79, 159, 172, 80, 175, 158,
+    81, 82, 153, 83, 173, 160, 84, 161, 152, 185, 177, 174, 163, 144, 162, 164, 186, 178, 165,
+    154, 187, 143, 176, 166, 167, 180, 189, 179, 168, 155, 188, 181, 182, 170, 190, 145, 191, 169,
+    156, 183, 192, 184, 193,
 )
 
 
@@ -1232,12 +2229,12 @@
     wide = features // dp_size
     z_cols = qkv_weight.shape[3]
     heads_slot = z_cols // HD
-    me_dp = lax.axis_index("dp")
-    me_mp = lax.axis_index("mp")
+    me_dp = lax.axis_index(DP)
+    me_mp = lax.axis_index(MP)
     core = me_dp % 2
 
     def swap(values):
-        return lax.ppermute(values, "dp", [(at, at ^ 1) for at in range(dp_size)])
+        return lax.ppermute(values, DP, [(at, at ^ 1) for at in range(dp_size)])
 
     def by_core(own, other, axis):
         first = jnp.where(core == 0, own, other)
@@ -1254,7 +2251,7 @@
                     pairs.append((d * mp_size + m, (d ^ 1) * mp_size + (m ^ 1)))
 
         def trade(values):
-            other = lax.ppermute(values, ("dp", "mp"), pairs)
+            other = lax.ppermute(values, (DP, MP), pairs)
             return jnp.where(moved, other, values)
 
         doc_rows = jnp.where(moved, swap(documents), documents)
@@ -1281,11 +2278,12 @@
         docs = lax.dynamic_index_in_dim(documents, me_mp // pieces, 0, False)
 
         def share_heads(values):
-            return lax.all_to_all(values, "mp", 1, 0, axis_index_groups=groups, tiled=True)
+            return lax.all_to_all(values, MP, 1, 0, axis_index_groups=groups, tiled=True)
 
         def return_heads(values):
-            return lax.all_to_all(values, "mp", 0, 1, axis_index_groups=groups, tiled=True)
-
+            return lax.all_to_all(values, MP, 0, 1, axis_index_groups=groups, tiled=True)
+
+        moved = False
         first_slot = (me_mp % pieces) * slots
     slope_table = jnp.asarray(0.5 ** (np.arange(H) + 1.0), dtype=f32)
     slopes = lax.dynamic_slice_in_dim(
@@ -1293,8 +2291,8 @@
     )
 
     bits = bits_of(dp_size)[1:]
-    line_first = [("mp", *bits), ("mp", *bits[::-1])]
-    line_second = [(bits[0], "mp", *bits[1:]), (bits[-1], "mp", *bits[:-1][::-1])]
+    line_first = [(MP, *bits), (MP, *bits[::-1])]
+    line_second = [(bits[0], MP, *bits[1:]), (bits[-1], MP, *bits[:-1][::-1])]
 
     gain_rows = norm_gains.shape[1]
     shift_rows = shift_params.shape[1]
@@ -1306,49 +2304,58 @@
     def padded(values):
         return jnp.pad(values, [(0, 0)] * (values.ndim - 1) + [(0, lanes - values.shape[-1])])
 
-    small = jnp.concatenate(
-        [
-            padded(norm_gains.reshape(-1, wide)),
-            padded(shift_params.reshape(-1, wide)),
-            padded(hidden_bias),
-            jnp.zeros((small_rows - vector_count - layers, lanes), f32),
-        ],
-        axis=0,
-    ).astype(bf16)
-
-    shards = []
     spreads = []
     for layer in range(layers):
-        shards += [
-            qkv_weight[layer].astype(bf16).reshape(wide, 3 * z_cols),
-            proj_weight[layer].astype(bf16).T,
-            upper_weight[layer].astype(bf16),
-            lower_weight[layer].astype(bf16).T,
-        ]
         spreads += line_first[:: 1 if layer % 2 == 0 else -1] + line_second
-    shards.append(small)
     spreads.append(line_first[0])
+    qkv_by_part = qkv_weight.transpose(0, 2, 1, 3)
+    if paired and wide == lanes and bias_wide == lanes:
+        shards = prepare_all(
+            [
+                qkv_by_part, proj_weight, upper_weight, lower_weight, norm_gains, shift_params,
+                hidden_bias,
+            ],
+            small_rows,
+        )
+    else:
+        small = jnp.concatenate(
+            [
+                padded(norm_gains.reshape(-1, wide)),
+                padded(shift_params.reshape(-1, wide)),
+                padded(hidden_bias),
+                jnp.zeros((small_rows - vector_count - layers, lanes), f32),
+            ],
+            axis=0,
+        ).astype(bf16)
+        shards = []
+        for layer in range(layers):
+            shards += [
+                qkv_weight[layer].astype(bf16).reshape(wide, 3 * z_cols),
+                proj_weight[layer].astype(bf16).T,
+                upper_weight[layer].astype(bf16),
+                lower_weight[layer].astype(bf16).T,
+            ]
+        shards.append(small)
     spreads = [Spread(dims, mp_size) for dims in spreads]
     tabled = dp_size == 8 and mp_size == 4 and layers == 2
     if paired:
         spread_order = forward_order(spreads, layers, forward_table if tabled else ())
-        full, stored, stream = forward_all(
+        full, stored, stream, stream_low, vectors = forward_all(
             shards, inputs, docs, spreads, spread_order, dp_size, mp_size, layers,
             vector_count, gain_rows, shift_rows,
         )
     else:
         spread_order = step_order(spreads, (), lambda t, stage: t // 2 + stage)
         full = spread_all(shards, spreads, spread_order, dp_size, mp_size)
-    small_all = full[-1].reshape(dp_size, small_rows, mp_size, lanes).astype(f32)
-    vectors = small_all[:, :vector_count, 0, :wide].transpose(1, 0, 2)
-    vectors = vectors.reshape(vector_count, features)
-    gains = vectors[: layers * gain_rows].reshape(layers, gain_rows, features)
-    shifts = vectors[layers * gain_rows :].reshape(layers, shift_rows, features)
-    biases = small_all[:, vector_count : vector_count + layers, :, :bias_wide]
-    biases = biases.transpose(1, 2, 0, 3).reshape(layers, -1)
-
-    grad_stream = trade(cotangent).astype(f32)
+    cotangent = trade(cotangent)
     if not paired:
+        small_all = full[-1].reshape(dp_size, small_rows, mp_size, lanes).astype(f32)
+        vectors = small_all[:, :vector_count, 0, :wide].transpose(1, 0, 2)
+        vectors = vectors.reshape(vector_count, features)
+        gains = vectors[: layers * gain_rows].reshape(layers, gain_rows, features)
+        shifts = vectors[layers * gain_rows :].reshape(layers, shift_rows, features)
+        biases = small_all[:, vector_count : vector_count + layers, :, :bias_wide]
+        biases = biases.transpose(1, 2, 0, 3).reshape(layers, -1)
         stream = inputs.astype(f32)
         stored = []
         for layer in range(layers):
@@ -1367,87 +2374,95 @@
             stream = middle + dot_cols(active, lower_w) + shifts[layer, 2]
     output_stream = stream
     if paired:
-        other = lax.ppermute(output_stream.astype(bf16), ("dp", "mp"), pairs)
-        output_stream = jnp.where(moved, other.astype(f32), output_stream)
-
-    weight_grads = [None] * layers
-    vector_grads = [None] * layers
-    bias_grads = [None] * layers
-    no_shift = jnp.zeros((features,), f32)
+        stream_other = lax.ppermute(stream_low, (DP, MP), pairs)
+
+    ways = []
     for layer in reversed(range(layers)):
-        qkv_w, proj_w, upper_w, lower_w = full[4 * layer : 4 * layer + 4]
-        stream_in, middle, normed, qkv, mixed, attended, normed_two, hidden, active = stored[layer]
-        out_shift_grad = jnp.sum(grad_stream, axis=0)
-        grad_low = grad_stream.astype(bf16)
-        active_grad = dot(grad_low, lower_w)
-        _, pull_gelu = jax.vjp(gelu_tanh, hidden.astype(f32))
-        hidden_grad = pull_gelu(active_grad)[0].astype(bf16)
-        lower_grad = dot_rows(grad_low, active).astype(bf16)
-        upper_grad = dot_rows(normed_two, hidden_grad).astype(bf16)
-        bias_grads[layer] = jnp.sum(hidden_grad, axis=0, dtype=f32)
-        normed_two_grad = dot_cols(hidden_grad, upper_w)
-        _, pull_two = jax.vjp(layer_norm, middle, gains[layer, 1], no_shift)
-        middle_part, gain_two, shift_two = pull_two(normed_two_grad)
-        middle_grad = grad_stream + middle_part
-        middle_low = middle_grad.astype(bf16)
-        mixed_grad = share_heads(dot(middle_low, proj_w).astype(bf16))
-        proj_grad = dot_rows(middle_low, attended).astype(bf16)
-        qkv_grad = return_heads(attend_back(slopes, docs, qkv, mixed, mixed_grad, slots))
-        normed_grad = dot_cols(qkv_grad, qkv_w)
-        qkv_weight_grad = dot_rows(normed, qkv_grad).astype(bf16)
-        _, pull_one = jax.vjp(layer_norm, stream_in, gains[layer, 0], no_shift)
-        stream_part, gain_one, shift_one = pull_one(normed_grad)
-        grad_stream = middle_grad + stream_part
-        weight_grads[layer] = (lower_grad, upper_grad, proj_grad, qkv_weight_grad)
-        vector_grads[layer] = (
-            jnp.stack([gain_one, gain_two]),
-            jnp.stack([shift_one, shift_two, out_shift_grad]),
+        ways += fold_dims(line_first, line_second, layer)
+    ways.append(line_first[0][::-1])
+    if paired:
+        ways[-1] = (1,) + ways[-1]
+        folds = [Rows(dims, mp_size, at == 8) for at, dims in enumerate(ways)]
+        fold_order = backward_order(folds, layers, backward_table if tabled else ())
+        owned, norm_tile, input_grad, grad_low = backward_all(
+            full, cotangent, vectors, docs, stored, folds, fold_order, dp_size, mp_size, layers,
+            vector_count, gain_rows, shift_rows,
         )
-    input_grad = grad_stream
-    if paired:
-        other = lax.ppermute(input_grad.astype(bf16), ("dp", "mp"), pairs)
-        input_grad = jnp.where(moved, other.astype(f32), input_grad)
-
-    vector_sums = jnp.concatenate(
-        [jnp.concatenate([vector_grads[at][kind] for at in range(layers)]) for kind in (0, 1)]
-    )
-    vector_sums = padded(vector_sums.reshape(vector_count, dp_size, wide)).transpose(1, 0, 2)
-    vector_sums = jnp.broadcast_to(
-        vector_sums[:, :, None], (dp_size, vector_count, mp_size, lanes)
-    )
-    bias_sums = padded(jnp.stack(bias_grads).reshape(layers, mp_size, dp_size, bias_wide))
-    bias_sums = bias_sums.transpose(2, 0, 1, 3)
-    rest = jnp.zeros((dp_size, small_rows - vector_count - layers, mp_size, lanes), f32)
-    small_grad = jnp.concatenate([vector_sums, bias_sums, rest], axis=1)
-    small_grad = small_grad.reshape(dp_size * small_rows, mp_size * lanes).astype(bf16)
-
-    folds = []
-    local = []
-    for layer in reversed(range(layers)):
-        local += weight_grads[layer]
-        folds += fold_dims(line_first, line_second, layer)
-    local.append(small_grad)
-    folds.append(line_first[0][::-1])
-    folds = [Fold(dims, mp_size) for dims in folds]
-    fold_order = step_order(
-        folds, fold_table if tabled else (), lambda t, stage: t // 2 + stage
-    )
-    owned, norm_tile = fold_all(local, folds, fold_order, dp_size, mp_size, vector_count)
-    small_owned = owned.pop()
+        grad_other = lax.ppermute(grad_low, (DP, MP), pairs)
+    else:
+        grad_stream = cotangent.astype(f32)
+        weight_grads = [None] * layers
+        vector_grads = [None] * layers
+        bias_grads = [None] * layers
+        no_shift = jnp.zeros((features,), f32)
+        for layer in reversed(range(layers)):
+            qkv_w, proj_w, upper_w, lower_w = full[4 * layer : 4 * layer + 4]
+            stream_in, middle, normed, qkv, mixed, attended, normed_two, hidden, active = stored[layer]
+            out_shift_grad = jnp.sum(grad_stream, axis=0)
+            grad_low = grad_stream.astype(bf16)
+            active_grad = dot(grad_low, lower_w)
+            _, pull_gelu = jax.vjp(gelu_tanh, hidden.astype(f32))
+            hidden_grad = pull_gelu(active_grad)[0].astype(bf16)
+            lower_grad = dot_rows(grad_low, active).astype(bf16)
+            upper_grad = dot_rows(normed_two, hidden_grad).astype(bf16)
+            bias_grads[layer] = jnp.sum(hidden_grad, axis=0, dtype=f32)
+            normed_two_grad = dot_cols(hidden_grad, upper_w)
+            _, pull_two = jax.vjp(layer_norm, middle, gains[layer, 1], no_shift)
+            middle_part, gain_two, shift_two = pull_two(normed_two_grad)
+            middle_grad = grad_stream + middle_part
+            middle_low = middle_grad.astype(bf16)
+            mixed_grad = share_heads(dot(middle_low, proj_w).astype(bf16))
+            proj_grad = dot_rows(middle_low, attended).astype(bf16)
+            qkv_grad = return_heads(attend_back(slopes, docs, qkv, mixed, mixed_grad, slots))
+            normed_grad = dot_cols(qkv_grad, qkv_w)
+            qkv_weight_grad = dot_rows(normed, qkv_grad).astype(bf16)
+            _, pull_one = jax.vjp(layer_norm, stream_in, gains[layer, 0], no_shift)
+            stream_part, gain_one, shift_one = pull_one(normed_grad)
+            grad_stream = middle_grad + stream_part
+            weight_grads[layer] = (lower_grad, upper_grad, proj_grad, qkv_weight_grad)
+            vector_grads[layer] = (
+                jnp.stack([gain_one, gain_two]),
+                jnp.stack([shift_one, shift_two, out_shift_grad]),
+            )
+        input_grad = grad_stream
+
+        vector_sums = jnp.concatenate(
+            [jnp.concatenate([vector_grads[at][kind] for at in range(layers)]) for kind in (0, 1)]
+        )
+        vector_sums = padded(vector_sums.reshape(vector_count, dp_size, wide)).transpose(1, 0, 2)
+        vector_sums = jnp.broadcast_to(
+            vector_sums[:, :, None], (dp_size, vector_count, mp_size, lanes)
+        )
+        bias_sums = padded(jnp.stack(bias_grads).reshape(layers, mp_size, dp_size, bias_wide))
+        bias_sums = bias_sums.transpose(2, 0, 1, 3)
+        rest = jnp.zeros((dp_size, small_rows - vector_count - layers, mp_size, lanes), f32)
+        small_grad = jnp.concatenate([vector_sums, bias_sums, rest], axis=1)
+        small_grad = small_grad.reshape(dp_size * small_rows, mp_size * lanes).astype(bf16)
+
+        local = []
+        for layer in reversed(range(layers)):
+            local += weight_grads[layer]
+        local.append(small_grad)
+        folds = [Fold(dims, mp_size) for dims in ways]
+        fold_order = step_order(folds, (), lambda t, stage: t // 2 + stage)
+        owned, norm_tile = fold_all(local, folds, fold_order, dp_size, mp_size, vector_count)
+    small_owned = owned.pop().astype(f32)
     vector_owned = small_owned[:vector_count, :wide]
     bias_owned = small_owned[vector_count : vector_count + layers, :bias_wide]
     grad_norm = jnp.sqrt(jnp.sum(norm_tile))
     factor = jnp.minimum(1.0, clip_bound / grad_norm)
 
-    states = []
-    for each in (qkv_weight, qkv_moment, qkv_square):
-        states.append(each.transpose(0, 2, 1, 3))
+    states = [qkv_by_part, qkv_moment.transpose(0, 2, 1, 3), qkv_square.transpose(0, 2, 1, 3)]
     states += [
         proj_weight, proj_moment, proj_square, upper_weight, upper_moment, upper_square,
         lower_weight, lower_moment, lower_square,
     ]
     ordered = [owned[4 * layer + kind] for kind in (3, 2, 1, 0) for layer in range(layers)]
-    matrices = list(adam_all(factor, ordered, states))
+    streams = [output_stream, stream_other, input_grad, grad_other] if paired else []
+    matrices = list(adam_all(factor, moved, ordered, states, streams))
+    if paired:
+        output_stream, input_grad = matrices[12:]
+        matrices = matrices[:12]
     matrices[:3] = [each.transpose(0, 2, 1, 3) for each in matrices[:3]]
     results = [output_stream, input_grad] + matrices
     rest = (
@@ -1474,14 +2489,14 @@
 
 
 def solution(mesh):
-    dp_size = mesh.shape["dp"]
-    mp_size = mesh.shape["mp"]
-    rows = P(("dp", "mp"), None)
-    split_rows = P(None, "dp", None, "mp")
-    split_upper = P(None, "dp", "mp")
-    split_lower = P(None, "mp", "dp")
-    split_bias = P(None, ("mp", "dp"))
-    split_vector = P(None, None, "dp")
+    dp_size = mesh.shape[DP]
+    mp_size = mesh.shape[MP]
+    rows = P((DP, MP), None)
+    split_rows = P(None, DP, None, MP)
+    split_upper = P(None, DP, MP)
+    split_lower = P(None, MP, DP)
+    split_bias = P(None, (MP, DP))
+    split_vector = P(None, None, DP)
     groups = (
         split_rows, split_lower, split_upper, split_lower, split_bias, split_vector, split_vector
     )
@@ -1493,7 +2508,7 @@
     return jax.shard_map(
         shards,
         mesh=mesh,
-        in_specs=(rows, P("dp", None), rows) + placed,
+        in_specs=(rows, P(DP, None), rows) + placed,
         out_specs=(rows, rows) + placed + (P(),),
         check_vma=False,
     )

time: 674 us -> 558 us (0.83)
  matrix products: 105 us -> 0 us
  other arithmetic: 38.1 us -> 6.8 us
  Pallas kernels: 481 us -> 511 us
  local copies, waits for them, and re-layouts: 25.1 us -> 5.19 us
  waiting for transfers between devices: 0.02 us -> 9.04 us
    dot_general x16 -> x0, matrix products: 105 us -> none  [the longest x8 48.7 us: dot_rows(): lax.dot_general(left, right, contract_rows, preferred_element_type=f32)]
    pallas_call x4 -> x3, Pallas kernels: 244 us -> 279 us  [the longest x1 265 us: backward_all(): pl.pallas_call(functools.partial(backward_kernel, plans, order, mp_size,...]
    reduce_sum x13 -> x0, other arithmetic: 19.8 us -> none  [the longest x8 10 us: layer_norm(): center = values - jnp.mean(values, axis=-1, keepdims=True)]
    unnamed x126 -> x28, local copies, waits for them, and re-layouts: 18.8 us -> 4.16 us
    ppermute x8 -> x4, waiting for transfers between devices: 0.02 us -> 9.04 us  [the longest x1 9.03 us: program(): grad_other = lax.ppermute(grad_low, (DP, MP), pairs)]
    ppermute x8 -> x4, starting transfers between devices: 10.6 us -> 13.8 us  [the longest x1 7.07 us: program(): grad_other = lax.ppermute(grad_low, (DP, MP), pairs)]
  transfers between devices with their start and end apart: 8 -> 4, of which waited for: 0 -> 1; matrix products, arithmetic and copies ran while one was open for 16% -> 2% of each run, Pallas kernels for 70% -> 91%
where the time goes in v4:
time: 558 us; the launch traced here: 549 us
  Pallas kernels  511 us (92%)
  starting transfers between devices  13.8 us (2%)
  waiting for transfers between devices  9.04 us (2%)
  other arithmetic  6.8 us (1%)
    pallas_call x1, Pallas kernels, backward_all(): pl.pallas_call(functools.partial(backward_kernel, plans, order, mp_size,...  265 us
    pallas_call x1, Pallas kernels, forward_all(): pl.pallas_call(functools.partial(forward_kernel, plans, order, mp_size, l...  232 us
    pallas_call x1, Pallas kernels, adam_all(): pl.pallas_call(functools.partial(adam_kernel, len(streams) // 2), out_sha...  11.2 us
  transfers between devices with their start and end apart: 4, of which 1 were waited for; matrix products, arithmetic and copies ran while one was open for 2% of the time, Pallas kernels for 91%

profile of v4, /device:TPU:1, one launch (start us, length us, event | category | flops | bytes accessed | tf_op | source)
XLA Modules:
  0.0 549.0 jit_solution(16098376820744899621)
XLA Ops:
  0.7 0.0 copy-start.1
  0.7 4.7 collective-permute-start.1
  5.4 0.1 collective-permute-start
  5.5 1.3 copy.52.refs_5_
  6.8 2.9 shard_map.415
  9.7 0.0 collective-permute-done
  9.7 0.7 broadcast_select_fusion.1.refs_11_
  10.5 0.0 copy-start.2
  10.5 1.0 copy.53.refs_10_
  11.5 0.0 copy-done.2
  11.5 232.0 %shard_map.416 = (bf16[1024,3072]{1,0:T(8,128)(2,1)}, bf16[1024,1024]{1,0:T(8,128)(2,1)}, bf16[1024,4096]{1,0:T(8,128)(2,1)}, bf16[1024,4096]{1,0:T(8,128)(2,1)}...) custom-call(bf16[128,768]{1,0:T(8,128)(2,1)} %get-tuple-element.88.r, ...), custom_call_target="tpu_custom_call" | custom-call | tf_op jit(solution)/shard_map/pallas_call | solution.py:1314
  243.5 1.9 collective-permute-start.2
  245.5 0.0 collective-permute-done.1
  245.5 0.0 copy-done.1
  245.5 2.3 broadcast_select_fusion.refs_8_
  247.8 0.0 copy-start.3
  247.8 0.0 copy-start.6
  247.8 0.0 copy-start.7
  247.8 0.0 copy-start.5
  247.8 0.0 copy-start.10
  247.8 0.0 copy-start.11
  247.8 0.0 copy-start.4
  247.9 0.0 copy-start.8
  247.9 0.0 copy-start.9
  247.9 265.0 %shard_map.417 = (bf16[128,1024]{1,0:T(8,128)(2,1)}, bf16[128,1024]{1,0:T(8,128)(2,1)}, bf16[128,256]{1,0:T(8,128)(2,1)}, bf16[128,768]{1,0:T(8,128)(2,1)}, bf16...) custom-call(bf16[1024,3072]{1,0:T(8,128)(2,1)} %get-tuple-element.97, ...), custom_call_target="tpu_custom_call" | custom-call | tf_op jit(solution)/shard_map/pallas_call | solution.py:2169
  512.9 1.3 reduce_sum.9
  514.9 0.7 convert_element_type.3
  515.6 7.1 %collective-permute-start.3 = (bf16[512,1024]{1,0:T(8,128)(2,1)}, bf16[512,1024]{1,0:T(8,128)(2,1)S(1)}, u32[]{:S(2)}, u32[]{:S(2)}) collective-permute-start(bf16[512,1024]{1,0:T(8,128)(2,1)} %get-tuple-element.136), channel_id=1, source_target_pairs={{1,4},{3,6},{4,1},{6,3},{9,12},{11,14},{12,9},{14,11},{17,20},{19,... | collective-permute-start | bytes 3145736 | tf_op jit(solution)/shard_map/ppermute | solution.py:2391
  522.7 0.0 copy-done.3
  522.7 0.0 copy-done.6
  522.7 0.0 copy-done.7
  522.8 0.6 copy.59
  523.3 0.6 copy.60
  523.9 0.6 copy.61
  524.5 0.6 maximum_bitcast_fusion.scalars
  525.1 0.0 copy-done.5
  525.1 0.0 copy-done.10
  525.1 0.0 copy-done.11
  525.1 0.6 multiply_subtract_fusion.2
  525.7 0.0 copy-done.4
  525.7 0.0 copy-done.8
  525.7 0.0 copy-done.9
  525.7 0.6 multiply_subtract_fusion.1
  526.3 0.0 collective-permute-done.2.refs_21_
  526.3 9.0 %collective-permute-done.3.refs_23_ = bf16[512,1024]{1,0:T(8,128)(2,1)S(1)} collective-permute-done((bf16[512,1024]{1,0:T(8,128)(2,1)}, bf16[512,1024]{1,0:T(8,128)(2,1)S(1)}, u32[]{:S(2)}, u32[]{:S(2)}) %collective-permute-start.3) | collective-permute-done | bytes 1048608 | tf_op jit(solution)/shard_map/ppermute | solution.py:2391
  535.4 0.0 copy-start
  535.4 1.1 copy-done
  536.4 11.2 %shard_map.418 = (f32[2,3,128,256]{3,2,1,0:T(8,128)}, f32[2,3,128,256]{3,2,1,0:T(8,128)}, f32[2,3,128,256]{3,2,1,0:T(8,128)}, f32[2,256,128]{2,1,0:T(8,128)}, f3...) custom-call(f32[1,2]{1,0:T(1,128)} %maximum_bitcast_fusion.scalars, ...), custom_call_target="tpu_custom_call" | custom-call | tf_op jit(solution)/shard_map/pallas_call | solution.py:881
  (4 shorter events, 0.0 us)
Async XLA Ops:
  0.7 244.8 %copy-start.1 = (bf16[512,1024]{1,0:T(8,128)(2,1)S(1)}, bf16[512,1024]{1,0:T(8,128)(2,1)}, u32[]{:S(2)}) copy-start(bf16[512,1024]{1,0:T(8,128)(2,1)} %param.26) | copy-start | bytes 3145732
  0.7 244.8 %collective-permute-start.1 = (bf16[512,1024]{1,0:T(8,128)(2,1)}, bf16[512,1024]{1,0:T(8,128)(2,1)}, u32[]{:S(2)}, u32[]{:S(2)}) collective-permute-start(bf16[512,1024]{1,0:T(8,128)(2,1)} %param.26), channel_id=1, source_target_pairs={{1,4},{3,6},{4,1},{6,3},{9,12},{11,14},{12,9},{14,11},{17,20},{19,... | collective-permute-start | bytes 3145736 | tf_op jit(solution)/shard_map/ppermute | solution.py:2254
  5.4 4.3 collective-permute-start
  10.5 1.0 copy-start.2
  243.5 282.8 %collective-permute-start.2 = (bf16[512,1024]{1,0:T(8,128)(2,1)}, bf16[512,1024]{1,0:T(8,128)(2,1)}, u32[]{:S(2)}, u32[]{:S(2)}) collective-permute-start(bf16[512,1024]{1,0:T(8,128)(2,1)} %get-tuple-element.134), channel_id=1, source_target_pairs={{1,4},{3,6},{4,1},{6,3},{9,12},{11,14},{12,9},{14,11},{17,20},{19,... | collective-permute-start | bytes 3145736 | tf_op jit(solution)/shard_map/ppermute | solution.py:2377
  247.8 274.9 %copy-start.3 = (f32[2,3,128]{2,0,1:T(2,128)S(1)}, f32[2,3,128]{2,0,1:T(2,128)}, u32[]{:S(2)}) copy-start(f32[2,3,128]{2,0,1:T(2,128)} %param.45) | copy-start | bytes 9220
  247.8 274.9 %copy-start.6 = (f32[2,3,128]{2,0,1:T(2,128)S(1)}, f32[2,3,128]{2,0,1:T(2,128)}, u32[]{:S(2)}) copy-start(f32[2,3,128]{2,0,1:T(2,128)} %param.46) | copy-start | bytes 9220
  247.8 274.9 %copy-start.7 = (f32[2,3,128]{2,0,1:T(2,128)S(1)}, f32[2,3,128]{2,0,1:T(2,128)}, u32[]{:S(2)}) copy-start(f32[2,3,128]{2,0,1:T(2,128)} %param.47) | copy-start | bytes 9220
  247.8 277.3 %copy-start.5 = (f32[2,128]{1,0:T(2,128)S(1)}, f32[2,128]{1,0:T(2,128)}, u32[]{:S(2)}) copy-start(f32[2,128]{1,0:T(2,128)} %refs_6_.1) | copy-start | bytes 3076
  247.8 277.3 %copy-start.10 = (f32[2,128]{1,0:T(2,128)S(1)}, f32[2,128]{1,0:T(2,128)}, u32[]{:S(2)}) copy-start(f32[2,128]{1,0:T(2,128)} %param.40) | copy-start | bytes 3076
  247.8 277.3 %copy-start.11 = (f32[2,128]{1,0:T(2,128)S(1)}, f32[2,128]{1,0:T(2,128)}, u32[]{:S(2)}) copy-start(f32[2,128]{1,0:T(2,128)} %param.41) | copy-start | bytes 3076
  247.8 277.9 %copy-start.4 = (f32[2,2,128]{2,1,0:T(2,128)S(1)}, f32[2,2,128]{2,1,0:T(2,128)}, u32[]{:S(2)}) copy-start(f32[2,2,128]{2,1,0:T(2,128)} %refs_4_.1) | copy-start | bytes 6148
  247.9 277.8 %copy-start.8 = (f32[2,2,128]{2,1,0:T(2,128)S(1)}, f32[2,2,128]{2,1,0:T(2,128)}, u32[]{:S(2)}) copy-start(f32[2,2,128]{2,1,0:T(2,128)} %param.43) | copy-start | bytes 6148
  247.9 277.8 %copy-start.9 = (f32[2,2,128]{2,1,0:T(2,128)S(1)}, f32[2,2,128]{2,1,0:T(2,128)}, u32[]{:S(2)}) copy-start(f32[2,2,128]{2,1,0:T(2,128)} %param.44) | copy-start | bytes 6148
  515.6 19.8 %collective-permute-start.3 = (bf16[512,1024]{1,0:T(8,128)(2,1)}, bf16[512,1024]{1,0:T(8,128)(2,1)S(1)}, u32[]{:S(2)}, u32[]{:S(2)}) collective-permute-start(bf16[512,1024]{1,0:T(8,128)(2,1)} %get-tuple-element.136), channel_id=1, source_target_pairs={{1,4},{3,6},{4,1},{6,3},{9,12},{11,14},{12,9},{14,11},{17,20},{19,... | collective-permute-start | bytes 3145736 | tf_op jit(solution)/shard_map/ppermute | solution.py:2391
  535.4 1.1 copy-start

commit v5 on v4

--- a/solution.py
+++ b/solution.py
@@ -352,6 +352,24 @@
     pl.semaphore_wait(barrier, 1 + len(upper) + len(mp_bits) + around + also)
 
 
+def greet_all(z, d, dp_size, mp_size, across, moved):
+    barrier = pltpu.get_barrier_semaphore()
+    for mask in range(1, dp_size):
+        pl.semaphore_signal(
+            barrier, inc=1, device_id={DP: flip(d, mask)}, device_id_type=MESH
+        )
+    for mask in range(1, mp_size):
+        pl.semaphore_signal(
+            barrier, inc=1, device_id={MP: flip(z, mask)}, device_id_type=MESH
+        )
+
+    @pl.when(moved)
+    def _():
+        pl.semaphore_signal(barrier, inc=1, device_id=across, device_id_type=MESH)
+
+    pl.semaphore_wait(barrier, dp_size + mp_size - 2 + jnp.where(moved, 1, 0))
+
+
 class SpreadWork:
     def __init__(self, plans, order, mp_size, shards, outs, send_sems, recv_sems, own_sems):
         self.plans, self.mp_size = plans, mp_size
@@ -785,7 +803,8 @@
     for copy in loads[4:]:
         copy.wait()
     small = made[-1]
-    rows = [each[layer] for each in (gains, shifts) for layer in range(layers)] + [bias[...]]
+    rows = [gains[layer] for layer in range(layers)]
+    rows += [shifts[:, layer] for layer in range(layers)] + [bias[...]]
     used = sum(each.shape[0] for each in rows)
     rows.append(jnp.zeros((small.shape[0] - used, small.shape[1]), f32))
     small[...] = jnp.concatenate(rows, axis=0).astype(bf16)
@@ -813,9 +832,9 @@
     )(*states)
 
 
-def adam_kernel(streams, scalars, *refs):
-    ins = 20 + 2 * streams
-    news = 12 + streams
+def adam_kernel(streams, vector_count, gain_rows, *refs):
+    ins = 31 + 2 * streams
+    news = 22 + streams
     sources, outs = refs[:ins], refs[ins : ins + news]
     held, made = refs[ins + news : 2 * ins + news], refs[2 * ins + news : 2 * (ins + news)]
     in_sems, out_sems = refs[2 * (ins + news) :]
@@ -826,9 +845,13 @@
     order = []
     for group in range(4):
         order += [2 * group, 2 * group + 1] + [8 + 3 * group + which for which in range(3)]
-    for at in order + list(range(20, ins)):
+    for at in [21, 20] + order + list(range(22, ins)):
         loads[at].start()
-    factor = scalars[0, 0]
+    loads[21].wait()
+    norm = jnp.sqrt(jnp.sum(held[21][...], keepdims=True))
+    made[21][...] = jnp.broadcast_to(norm, made[21].shape)
+    stores[21].start()
+    factor = jnp.minimum(1.0, clip_bound / norm)
 
     def update(group, at, gradient):
         found = [held[8 + 3 * group + which][at] for which in range(3)]
@@ -860,28 +883,53 @@
                     update(group, (layer, slice(low, low + HD)), part)
         for which in range(3):
             stores[3 * group + which].start()
+    loads[20].wait()
+    small = held[20][...].astype(f32)
+    for group in range(3):
+        for which in range(3):
+            loads[22 + 3 * group + which].wait()
+        for layer in range(2):
+            if group == 0:
+                at = (slice(layer, layer + 1),)
+                first = vector_count + layer
+            elif group == 1:
+                at = (layer,)
+                first = layer * gain_rows
+            else:
+                at = (slice(None), layer)
+                first = 2 * gain_rows + layer * held[28].shape[0]
+            found = [held[22 + 3 * group + which][at] for which in range(3)]
+            part = small[first : first + found[0].shape[0]]
+            new = adam_update(*found, part, factor, group_rates[4 + group], group_decays[4 + group])
+            for which in range(3):
+                made[12 + 3 * group + which][at] = new[which]
+        for which in range(3):
+            stores[12 + 3 * group + which].start()
+    moved = lax.axis_index(DP) % 2 != lax.axis_index(MP) % 2
     for at in range(streams):
         for which in range(2):
-            loads[20 + 2 * at + which].wait()
-        ours, others = held[20 + 2 * at : 22 + 2 * at]
+            loads[31 + 2 * at + which].wait()
+        ours, others = held[31 + 2 * at : 33 + 2 * at]
         for low in range(0, ours.shape[0], 64):
             rows = slice(low, low + 64)
-            values = jnp.where(scalars[0, 1] > 0.5, others[rows, :].astype(f32), ours[rows, :])
-            made[12 + at][rows, :] = values
-        stores[12 + at].start()
+            values = jnp.where(moved, others[rows, :].astype(f32), ours[rows, :])
+            made[22 + at][rows, :] = values
+        stores[22 + at].start()
     for copy in stores:
         copy.wait()
 
 
-def adam_all(factor, moved, gradients, states, streams):
-    scalars = jnp.stack([factor, jnp.where(moved, 1.0, 0.0).astype(f32)]).reshape(1, 2)
+def adam_all(gradients, states, small, norm_tile, small_states, streams, vector_count, gain_rows):
     any_place = pl.BlockSpec(memory_space=pl.ANY)
-    operands = list(gradients) + list(states) + list(streams)
-    news = [jax.ShapeDtypeStruct(each.shape, f32) for each in list(states) + list(streams[::2])]
+    operands = list(gradients) + list(states) + [small, norm_tile] + list(small_states)
+    operands += streams
+    shapes = [each.shape for each in list(states) + list(small_states)] + [(8, HD)]
+    shapes += [each.shape for each in streams[::2]]
+    news = [jax.ShapeDtypeStruct(shape, f32) for shape in shapes]
     return pl.pallas_call(
-        functools.partial(adam_kernel, len(streams) // 2),
+        functools.partial(adam_kernel, len(streams) // 2, vector_count, gain_rows),
         out_shape=news,
-        in_specs=[pl.BlockSpec(memory_space=pltpu.SMEM)] + [any_place] * len(operands),
+        in_specs=[any_place] * len(operands),
         out_specs=[any_place] * len(news),
         scratch_shapes=[pltpu.VMEM(each.shape, each.dtype) for each in operands + news]
         + [
@@ -889,7 +937,7 @@
             pltpu.SemaphoreType.DMA((len(news),)),
         ],
         compiler_params=pltpu.CompilerParams(vmem_limit_bytes=60 * 2**20),
-    )(scalars, *operands)
+    )(*operands)
 
 
 ROWS = 64
@@ -982,17 +1030,17 @@
 def forward_kernel(plans, order, mp_size, layers, vector_count, gain_rows, shift_rows, *refs):
     n = len(plans)
     shards = refs[:n]
-    inputs, doc_cols, doc_rows = refs[n : n + 3]
-    outs = refs[n + 3 : 2 * n + 3]
-    at = 2 * n + 3
+    inputs, cotangent, doc_cols, doc_rows = refs[n : n + 4]
+    outs = refs[n + 4 : 2 * n + 4]
+    at = 2 * n + 4
     saved = [refs[at + SAVED * layer : at + SAVED * (layer + 1)] for layer in range(layers)]
     at += SAVED * layers
-    last_stream, last_low, vectors = refs[at : at + 3]
+    last_stream, last_low, cotangent_out, vectors = refs[at : at + 4]
     (
         streams, middles, lows, normed_one, normed_two, send_buf, qkv_full, mixed, logs, attended,
         hidden, active, w_qkv, w_proj, w_up, w_down, small_buf, biases, traded,
         load_sems, save_sems, trade_sems, head_sems, send_sems, recv_sems, own_sems,
-    ) = refs[at + 3 :]
+    ) = refs[at + 4 :]
     work = SpreadWork(plans, order, mp_size, shards, outs, send_sems, recv_sems, own_sems)
     z, d = work.z, work.d
     core = d % 2
@@ -1014,6 +1062,11 @@
         device_id=across, device_id_type=MESH,
     )
     keep = pltpu.make_async_copy(inputs, traded, trade_sems.at[2])
+    trade_back = pltpu.make_async_remote_copy(
+        src_ref=cotangent, dst_ref=cotangent_out, send_sem=trade_sems.at[3],
+        recv_sem=trade_sems.at[4], device_id=across, device_id_type=MESH,
+    )
+    keep_back = pltpu.make_async_copy(cotangent, cotangent_out, trade_sems.at[5])
 
     @pl.when(moved)
     def _():
@@ -1054,15 +1107,18 @@
             where = pl.ds(at * cols, cols)
             load((layer, kind, at), full[2].at[:, where], w_up.at[at % 2], 3 + at % 2)
         else:
-            rows = w_down.shape[1]
-            where = pl.ds(at * rows, rows)
-            load((layer, kind, at), full[3].at[where, :], w_down.at[at % 2], 5 + at % 2)
+            load((layer, kind, at), full[3].at[pair_of(at), :], w_down.at[at % 2], 5 + at % 2)
+
+    def pair_of(at):
+        rows = w_down.shape[1]
+        return pl.ds(place(flip(d // 2, at), rows), rows)
 
     def tile(layer, kind, at, count):
         if (layer, kind, at) not in loads:
             load_tile(layer, kind, at)
         loads[layer, kind, at].wait()
-        if at + 1 < count:
+        ready = kind != "down" or (4 * layer + 3, 2 * at + 2) in complete
+        if at + 1 < count and ready:
             load_tile(layer, kind, at + 1)
 
     def share_copy(layer):
@@ -1204,6 +1260,9 @@
             save(normed_two.at[layer], keeps[5])
         elif kind == "up":
             at = int(at)
+            if at == 0 and layer == layers - 1:
+                pl.when(moved)(trade_back.start)
+                pl.when(jnp.logical_not(moved))(keep_back.start)
             if at == 0 and layer > 0:
                 for copy in big_saves[layer - 1]:
                     copy.wait()
@@ -1226,12 +1285,11 @@
                 active_copy(layer).start()
         elif kind == "down":
             at = int(at)
-            rows = w_down.shape[1]
-            tile(layer, "down", at, features // rows)
+            tile(layer, "down", at, features // w_down.shape[1])
             weight = w_down.at[at % 2]
             out = streams.at[layer + 1]
-            cols = pl.ds(at * rows, rows)
-            out[:, cols] = middles[layer, :, cols] + vector(shift + 2)[:, at * rows : (at + 1) * rows]
+            cols = pair_of(at)
+            out[:, cols] = middles[layer, :, cols] + vectors[shift + 2 : shift + 3, cols]
 
             def piece(step, carry):
                 inner = pl.ds(pl.multiple_of(step * 1024, 1024), 1024)
@@ -1242,6 +1300,7 @@
 
     big_saves = {}
     missing = {}
+    complete = set()
     for t, _ in work.order:
         missing[t] = missing.get(t, 0) + 1
     for step in order:
@@ -1249,6 +1308,8 @@
             compute(*step)
         else:
             work.step(*step)
+            if step[1][0] == len(plans[step[0]].dims):
+                complete.add((step[0], step[1][1] - 1))
             missing[step[0]] -= 1
             if missing[step[0]] == 0:
                 del missing[step[0]]
@@ -1274,12 +1335,17 @@
     @pl.when(moved)
     def _():
         trade.wait_send()
+        trade_back.wait()
+
+    @pl.when(jnp.logical_not(moved))
+    def _():
+        keep_back.wait()
 
     work.finish()
 
 
 def forward_all(
-    shards, inputs, docs, plans, order, dp_size, mp_size, layers, vector_count, gain_rows, shift_rows
+    shards, inputs, cotangent, docs, plans, order, dp_size, mp_size, layers, vector_count, gain_rows, shift_rows
 ):
     _, total = number(plans, mp_size, spread_single)
     tokens, features = inputs.shape
@@ -1309,6 +1375,7 @@
     out_shape += saved * layers + [
         jax.ShapeDtypeStruct((tokens, features), f32),
         jax.ShapeDtypeStruct((tokens, features), bf16),
+        jax.ShapeDtypeStruct((tokens, features), bf16),
     ]
     out_shape.append(jax.ShapeDtypeStruct((shards[-1].shape[0], features), f32))
     out = pl.pallas_call(
@@ -1316,7 +1383,7 @@
             forward_kernel, plans, order, mp_size, layers, vector_count, gain_rows, shift_rows
         ),
         out_shape=out_shape,
-        in_specs=[any_place] * (len(shards) + 1) + [vmem] * 2,
+        in_specs=[any_place] * (len(shards) + 2) + [vmem] * 2,
         out_specs=[any_place] * (len(out_shape) - 1) + [vmem],
         scratch_shapes=[
             pltpu.VMEM((layers + 1, tokens, features), f32),
@@ -1340,7 +1407,7 @@
             pltpu.VMEM((tokens, features), bf16),
             pltpu.SemaphoreType.DMA((8,)),
             pltpu.SemaphoreType.DMA((SAVED * layers + 2,)),
-            pltpu.SemaphoreType.DMA((3,)),
+            pltpu.SemaphoreType.DMA((6,)),
             pltpu.SemaphoreType.DMA((6 * layers,)),
             pltpu.SemaphoreType.DMA((total,)),
             pltpu.SemaphoreType.DMA((total,)),
@@ -1349,10 +1416,10 @@
         compiler_params=pltpu.CompilerParams(
             collective_id=2, has_side_effects=True, vmem_limit_bytes=62 * 2**20
         ),
-    )(*shards, inputs, docs.reshape(-1, 1), docs.reshape(1, -1))
+    )(*shards, inputs, cotangent, docs.reshape(-1, 1), docs.reshape(1, -1))
     n = len(shards)
     stored = [out[n + SAVED * at : n + SAVED * (at + 1)] for at in range(layers)]
-    return out[:n], stored, out[-3], out[-2], out[-1]
+    return out[:n], stored, *out[-4:]
 
 
 KINDS = ("down", "up", "proj", "qkv")
@@ -1436,6 +1503,14 @@
     qkv[:, value_cols] = value_acc[...].astype(bf16)
 
 
+def flip_by(value, at, size):
+    out = 0
+    for bit in bits_of(size):
+        one = (value // bit) % 2
+        out = out + bit * (1 - one if at & bit else one)
+    return out
+
+
 class Rows:
     def __init__(self, dims, mp_size, merged=False):
         self.dims = tuple(dims)
@@ -1653,12 +1728,13 @@
     n = len(plans)
     full = [refs[4 * layer : 4 * layer + 4] for layer in range(layers)]
     at = 4 * layers
-    cotangent, vectors, doc_cols, doc_rows = refs[at : at + 4]
-    at += 4
+    cotangent, stream_low, vectors, doc_cols, doc_rows = refs[at : at + 5]
+    at += 5
     saved = [refs[at + SAVED * layer : at + SAVED * (layer + 1)] for layer in range(layers)]
     at += SAVED * layers
-    outs, (norm_ref, input_grad, input_low) = refs[at : at + n], refs[at + n : at + n + 3]
-    at += n + 3
+    outs, (norm_ref, input_grad) = refs[at : at + n], refs[at + n : at + n + 2]
+    stream_other, grad_other = refs[at + n + 2 : at + n + 4]
+    at += n + 4
     sums = refs[at : at + 5]
     at += 5
     recv = {}
@@ -1680,7 +1756,6 @@
     core = d % 2
     partner = {DP: flip(d, 1)}
     upper = [dim for dim in plans[0].dims if dim != MP]
-    mp_bits = bits_of(mp_size)
     tokens, features = low.shape
     half = features // 2
     own_rows = pl.ds(place(core, tokens), tokens)
@@ -1692,7 +1767,22 @@
     wide = w_a.shape[2]
     per_block = cols[0] // wide
 
-    greet(z, d, upper, mp_size, mp_bits)
+    across = {DP: flip(d, 1), MP: flip(z, 1)}
+    moved = core != z % 2
+    dp_size = 2 ** (len(upper) + 1)
+    greet_all(z, d, dp_size, mp_size, across, moved)
+
+    def trade(src, dst, at):
+        return pltpu.make_async_remote_copy(
+            src_ref=src, dst_ref=dst, send_sem=tile_sems.at[at], recv_sem=tile_sems.at[at + 1],
+            device_id=across, device_id_type=MESH,
+        )
+
+    trades = [
+        trade(stream_low, stream_other, 2 * (dp_size + mp_size) - 4),
+        trade(low, grad_other, 2 * (dp_size + mp_size) - 2),
+    ]
+    pl.when(moved)(trades[0].start)
 
     loads = {}
 
@@ -1932,9 +2022,7 @@
                 copy = pltpu.make_async_copy(grad, input_grad, out_sems.at[n])
                 copy.start()
                 loads["input_grad"] = copy
-                copy = pltpu.make_async_copy(low, input_low, out_sems.at[n + 1])
-                copy.start()
-                loads["input_low"] = copy
+                pl.when(moved)(trades[1].start)
 
     def weight(t, s):
         slab = work.slab(t)
@@ -1960,6 +2048,8 @@
         left = left_t.at[t % 2]
 
         def multiply(right, first, step):
+            step = 2 * step if cols[t] % (2 * step) == 0 else step
+
             def piece(at, carry):
                 here = pl.multiple_of(at * step, step)
                 there = pl.ds(pl.multiple_of(block * cols[t] + here, step), step)
@@ -2025,21 +2115,32 @@
         else:
             work.step(*step, finish)
 
-    pairs = [{DP: flip(d, bit)} for bit in [1] + upper]
-    pairs += [{MP: flip(z, bit)} for bit in mp_bits]
-    for at, to in enumerate(pairs):
-        exchange = pltpu.make_async_remote_copy(
-            src_ref=tiles.at[2 * at],
-            dst_ref=tiles.at[2 * at + 1],
-            send_sem=tile_sems.at[2 * at],
-            recv_sem=tile_sems.at[2 * at + 1],
-            device_id=to,
-            device_id_type=MESH,
-        )
-        exchange.start()
-        exchange.wait()
-        tiles[2 * at + 2] = tiles[2 * at] + tiles[2 * at + 1]
-    norm_ref[...] = tiles[2 * len(pairs)]
+    first = 0
+    sem = 0
+    for axis, me, size in ((DP, d, dp_size), (MP, z, mp_size)):
+        copies = []
+        for mask in range(1, size):
+            copies.append(
+                pltpu.make_async_remote_copy(
+                    src_ref=tiles.at[first],
+                    dst_ref=tiles.at[first + mask],
+                    send_sem=tile_sems.at[sem],
+                    recv_sem=tile_sems.at[sem + 1],
+                    device_id={axis: flip(me, mask)},
+                    device_id_type=MESH,
+                )
+            )
+            sem += 2
+        for copy in copies:
+            copy.start()
+        for copy in copies:
+            copy.wait()
+        total = tiles[first + flip_by(me, 0, size)]
+        for at in range(1, size):
+            total = total + tiles[first + flip_by(me, at, size)]
+        first += size
+        tiles[first] = total
+    norm_ref[...] = tiles[first]
 
     for s in (2, 3):
         pushed((0, "grads", s))
@@ -2050,7 +2151,8 @@
         if t >= 4:
             loads["out", t].wait()
     loads["input_grad"].wait()
-    loads["input_low"].wait()
+    for copy in trades:
+        pl.when(moved)(copy.wait)
 
 
 def backward_chain(plans, layers):
@@ -2084,7 +2186,7 @@
 
 
 def backward_all(
-    full, cotangent, vectors, docs, stored, plans, order, dp_size, mp_size, layers, vector_count,
+    full, cotangent, stream_low, vectors, docs, stored, plans, order, dp_size, mp_size, layers, vector_count,
     gain_rows, shift_rows,
 ):
     n = len(plans)
@@ -2098,7 +2200,6 @@
         for layer in reversed(range(layers))
         for kind in (3, 2, 1, 0)
     ] + [max(HD, features // dp_size)]
-    rounds = len(bits_of(dp_size)) + len(bits_of(mp_size))
     half_qkv = full[0].shape[1] // 2
     any_place = pl.BlockSpec(memory_space=pl.ANY)
     vmem = pl.BlockSpec(memory_space=pltpu.VMEM)
@@ -2106,6 +2207,7 @@
     out_shape += [
         jax.ShapeDtypeStruct((8, HD), f32),
         jax.ShapeDtypeStruct((tokens, features), f32),
+        jax.ShapeDtypeStruct((tokens, features), bf16),
         jax.ShapeDtypeStruct((tokens, features), bf16),
     ]
     slabs = (0, 1, 2, 3, 8)
@@ -2149,20 +2251,20 @@
         pltpu.VMEM((length, HD), f32),
         pltpu.VMEM((wides[8], features), f32),
         pltpu.VMEM((wides[8], units), f32),
-        pltpu.VMEM((2 * rounds + 1, 8, HD), f32),
+        pltpu.VMEM((dp_size + mp_size + 1, 8, HD), f32),
         pltpu.SemaphoreType.DMA((110,)),
         pltpu.SemaphoreType.DMA((2 * 11 * layers,)),
-        pltpu.SemaphoreType.DMA((n + 2,)),
-        pltpu.SemaphoreType.DMA((2 * rounds,)),
+        pltpu.SemaphoreType.DMA((n + 1,)),
+        pltpu.SemaphoreType.DMA((2 * (dp_size + mp_size),)),
         pltpu.SemaphoreType.DMA((total,)),
         pltpu.SemaphoreType.DMA((total,)),
         pltpu.SemaphoreType.REGULAR((4, len(plans[0].dims) + 1, 2)),
         pltpu.SemaphoreType.REGULAR((mp_size,)),
         pltpu.SemaphoreType.REGULAR((2,)),
     ]
-    operands = list(full[: 4 * layers]) + [cotangent, vectors]
+    operands = list(full[: 4 * layers]) + [cotangent, stream_low, vectors]
     operands += [docs.reshape(-1, 1), docs.reshape(1, -1)]
-    specs = [any_place] * (4 * layers + 1) + [vmem] * 3
+    specs = [any_place] * (4 * layers + 2) + [vmem] * 3
     for each in stored:
         operands += each
         specs += [any_place] * SAVED
@@ -2172,29 +2274,29 @@
         ),
         out_shape=out_shape,
         in_specs=specs,
-        out_specs=[any_place] * n + [vmem, any_place, any_place],
+        out_specs=[any_place] * n + [vmem] + [any_place] * 3,
         scratch_shapes=scratch,
         compiler_params=pltpu.CompilerParams(
             collective_id=1, has_side_effects=True, vmem_limit_bytes=63 * 2**20
         ),
     )(*operands)
-    return list(out[:n]), out[n], out[n + 1], out[n + 2]
+    return list(out[:n]), *out[n:]
 
 
 forward_table = (
-    116, 1, 22, 23, 188, 0, 189, 95, 118, 117, 97, 191, 119, 24, 190, 25, 3, 121, 94, 193, 5, 192,
-    194, 26, 27, 206, 2, 71, 99, 4, 195, 120, 29, 69, 11, 199, 123, 196, 96, 28, 30, 197, 122, 13,
-    70, 128, 31, 127, 73, 6, 7, 8, 98, 33, 34, 9, 129, 44, 203, 72, 10, 32, 77, 202, 14, 45, 134,
-    19, 125, 124, 207, 76, 18, 12, 100, 75, 204, 41, 205, 37, 126, 46, 35, 103, 74, 198, 79, 105,
-    20, 200, 107, 201, 16, 208, 47, 136, 102, 36, 209, 106, 104, 42, 78, 17, 15, 210, 39, 48, 112,
-    52, 38, 21, 211, 101, 51, 49, 82, 43, 83, 81, 212, 80, 135, 213, 50, 57, 54, 113, 214, 165,
-    53, 132, 85, 164, 163, 131, 215, 108, 65, 55, 40, 56, 216, 138, 133, 217, 87, 60, 58, 111, 84,
-    130, 91, 66, 218, 140, 61, 59, 114, 167, 90, 219, 86, 139, 171, 110, 166, 62, 88, 137, 92, 67,
-    170, 146, 63, 64, 145, 89, 109, 220, 68, 221, 222, 223, 141, 142, 224, 115, 169, 225, 226, 93,
-    168, 227, 228, 173, 229, 230, 172, 231, 232, 233, 143, 147, 144, 234, 148, 235, 152, 176, 236,
-    237, 153, 174, 175, 180, 151, 181, 238, 177, 149, 150, 239, 157, 154, 240, 179, 182, 158, 155,
-    156, 178, 184, 183, 159, 241, 242, 161, 160, 185, 243, 162, 244, 245, 246, 247, 187, 248, 249,
-    250, 186, 251, 252, 253, 254, 255,
+    22, 23, 0, 1, 188, 116, 24, 25, 2, 189, 3, 117, 27, 191, 26, 190, 94, 118, 4, 70, 95, 119, 71,
+    5, 192, 193, 121, 200, 97, 8, 96, 31, 195, 197, 194, 28, 9, 198, 99, 120, 98, 30, 100, 72, 73,
+    69, 196, 32, 6, 207, 127, 7, 104, 12, 74, 44, 16, 10, 199, 201, 128, 33, 105, 18, 13, 46, 208,
+    29, 112, 45, 40, 17, 11, 107, 203, 202, 75, 76, 83, 19, 77, 34, 125, 205, 47, 206, 122, 204,
+    39, 209, 52, 48, 20, 14, 103, 36, 15, 38, 79, 210, 106, 21, 78, 211, 212, 213, 126, 49, 41,
+    51, 35, 101, 214, 102, 54, 37, 80, 114, 81, 53, 129, 215, 50, 216, 82, 86, 164, 56, 165, 55,
+    123, 163, 124, 84, 87, 217, 42, 136, 65, 57, 91, 59, 61, 133, 111, 58, 85, 166, 138, 113, 139,
+    134, 66, 130, 43, 108, 60, 218, 90, 219, 88, 140, 62, 170, 135, 167, 171, 64, 109, 67, 92, 63,
+    220, 146, 110, 132, 131, 68, 168, 221, 89, 222, 223, 224, 225, 145, 226, 115, 227, 228, 229,
+    141, 142, 93, 173, 230, 231, 169, 148, 232, 233, 172, 147, 176, 234, 143, 144, 152, 151, 137,
+    235, 236, 237, 159, 177, 178, 175, 174, 181, 153, 180, 184, 238, 149, 150, 239, 240, 155, 157,
+    156, 182, 154, 160, 158, 185, 179, 241, 242, 243, 161, 183, 162, 244, 245, 246, 247, 248, 249,
+    186, 250, 251, 252, 187, 253, 254, 255,
 )
 backward_table = (
     0, 1, 2, 3, 4, 5, 6, 7, 8, 9, 10, 11, 12, 13, 14, 15, 16, 17, 87, 18, 19, 20, 21, 85, 96, 22,
@@ -2244,16 +2346,6 @@
     paired = pieces == 2 and dp_size % 2 == 0 and mp_size % 2 == 0
     if paired:
         moved = core != me_mp % 2
-        pairs = []
-        for d in range(dp_size):
-            for m in range(mp_size):
-                if d % 2 != m % 2:
-                    pairs.append((d * mp_size + m, (d ^ 1) * mp_size + (m ^ 1)))
-
-        def trade(values):
-            other = lax.ppermute(values, (DP, MP), pairs)
-            return jnp.where(moved, other, values)
-
         doc_rows = jnp.where(moved, swap(documents), documents)
         docs = lax.dynamic_index_in_dim(doc_rows, me_mp // 2, 0, False)
 
@@ -2271,9 +2363,6 @@
         first_slot = core * slots
     else:
         groups = [list(range(g * pieces, (g + 1) * pieces)) for g in range(mp_size // pieces)]
-
-        def trade(values):
-            return values
 
         docs = lax.dynamic_index_in_dim(documents, me_mp // pieces, 0, False)
 
@@ -2312,8 +2401,8 @@
     if paired and wide == lanes and bias_wide == lanes:
         shards = prepare_all(
             [
-                qkv_by_part, proj_weight, upper_weight, lower_weight, norm_gains, shift_params,
-                hidden_bias,
+                qkv_by_part, proj_weight, upper_weight, lower_weight, norm_gains,
+                shift_params.transpose(1, 0, 2), hidden_bias,
             ],
             small_rows,
         )
@@ -2340,14 +2429,13 @@
     tabled = dp_size == 8 and mp_size == 4 and layers == 2
     if paired:
         spread_order = forward_order(spreads, layers, forward_table if tabled else ())
-        full, stored, stream, stream_low, vectors = forward_all(
-            shards, inputs, docs, spreads, spread_order, dp_size, mp_size, layers,
+        full, stored, stream, stream_low, cotangent, vectors = forward_all(
+            shards, inputs, cotangent, docs, spreads, spread_order, dp_size, mp_size, layers,
             vector_count, gain_rows, shift_rows,
         )
     else:
         spread_order = step_order(spreads, (), lambda t, stage: t // 2 + stage)
         full = spread_all(shards, spreads, spread_order, dp_size, mp_size)
-    cotangent = trade(cotangent)
     if not paired:
         small_all = full[-1].reshape(dp_size, small_rows, mp_size, lanes).astype(f32)
         vectors = small_all[:, :vector_count, 0, :wide].transpose(1, 0, 2)
@@ -2373,8 +2461,6 @@
             )
             stream = middle + dot_cols(active, lower_w) + shifts[layer, 2]
     output_stream = stream
-    if paired:
-        stream_other = lax.ppermute(stream_low, (DP, MP), pairs)
 
     ways = []
     for layer in reversed(range(layers)):
@@ -2384,11 +2470,10 @@
         ways[-1] = (1,) + ways[-1]
         folds = [Rows(dims, mp_size, at == 8) for at, dims in enumerate(ways)]
         fold_order = backward_order(folds, layers, backward_table if tabled else ())
-        owned, norm_tile, input_grad, grad_low = backward_all(
-            full, cotangent, vectors, docs, stored, folds, fold_order, dp_size, mp_size, layers,
+        owned, norm_tile, input_grad, stream_other, grad_other = backward_all(
+            full, cotangent, stream_low, vectors, docs, stored, folds, fold_order, dp_size, mp_size, layers,
             vector_count, gain_rows, shift_rows,
         )
-        grad_other = lax.ppermute(grad_low, (DP, MP), pairs)
     else:
         grad_stream = cotangent.astype(f32)
         weight_grads = [None] * layers
@@ -2446,11 +2531,10 @@
         folds = [Fold(dims, mp_size) for dims in ways]
         fold_order = step_order(folds, (), lambda t, stage: t // 2 + stage)
         owned, norm_tile = fold_all(local, folds, fold_order, dp_size, mp_size, vector_count)
-    small_owned = owned.pop().astype(f32)
-    vector_owned = small_owned[:vector_count, :wide]
-    bias_owned = small_owned[vector_count : vector_count + layers, :bias_wide]
-    grad_norm = jnp.sqrt(jnp.sum(norm_tile))
-    factor = jnp.minimum(1.0, clip_bound / grad_norm)
+    small_owned = owned.pop()
+
+    def by_row(values):
+        return values.transpose(1, 0, 2)
 
     states = [qkv_by_part, qkv_moment.transpose(0, 2, 1, 3), qkv_square.transpose(0, 2, 1, 3)]
     states += [
@@ -2458,28 +2542,26 @@
         lower_weight, lower_moment, lower_square,
     ]
     ordered = [owned[4 * layer + kind] for kind in (3, 2, 1, 0) for layer in range(layers)]
+    small_states = [
+        hidden_bias, bias_moment, bias_square, norm_gains, gains_moment, gains_square,
+        by_row(shift_params), by_row(shifts_moment), by_row(shifts_square),
+    ]
+    if wide < lanes or bias_wide < lanes:
+        small_states = [padded(each) for each in small_states]
     streams = [output_stream, stream_other, input_grad, grad_other] if paired else []
-    matrices = list(adam_all(factor, moved, ordered, states, streams))
+    results = list(
+        adam_all(
+            ordered, states, small_owned, norm_tile, small_states, streams, vector_count, gain_rows
+        )
+    )
     if paired:
-        output_stream, input_grad = matrices[12:]
-        matrices = matrices[:12]
-    matrices[:3] = [each.transpose(0, 2, 1, 3) for each in matrices[:3]]
-    results = [output_stream, input_grad] + matrices
-    rest = (
-        (hidden_bias, bias_moment, bias_square, bias_owned),
-        (
-            norm_gains, gains_moment, gains_square,
-            vector_owned[: layers * gain_rows].reshape(layers, gain_rows, wide),
-        ),
-        (
-            shift_params, shifts_moment, shifts_square,
-            vector_owned[layers * gain_rows :].reshape(layers, shift_rows, wide),
-        ),
-    )
-    for at, group in enumerate(rest, 4):
-        results.extend(adam_update(*group, factor, group_rates[at], group_decays[at]))
-    results.append(grad_norm)
-    return tuple(results)
+        output_stream, input_grad = results[22:]
+    grad_norm = results[21][0, 0]
+    results[:3] = [each.transpose(0, 2, 1, 3) for each in results[:3]]
+    results[18:21] = [by_row(each) for each in results[18:21]]
+    results[12:15] = [each[:, :bias_wide] for each in results[12:15]]
+    results[15:21] = [each[:, :, :wide] for each in results[15:21]]
+    return (output_stream, input_grad, *results[:21], grad_norm)
 
 
 def fold_dims(line_first, line_second, layer):

time: 558 us -> 537 us (0.962)
  starting transfers between devices: 13.8 us -> 0.12 us
  Pallas kernels: 511 us -> 523 us
  waiting for transfers between devices: 9.04 us -> 0.01 us
  other arithmetic: 6.8 us -> 0.71 us
    pallas_call x1, Pallas kernels: 265 us -> 280 us  [backward_all(): pl.pallas_call(functools.partial(backward_kernel, plans, order, mp_size,...]
    ppermute x3 -> x0, starting transfers between devices: 13.7 us -> none  [the longest x1 7.07 us: program(): grad_other = lax.ppermute(grad_low, (DP, MP), pairs)]
    ppermute x3 -> x0, waiting for transfers between devices: 9.04 us -> none  [the longest x1 9.03 us: program(): grad_other = lax.ppermute(grad_low, (DP, MP), pairs)]
  transfers between devices with their start and end apart: 4 -> 1, of which waited for: 1 -> 0; matrix products, arithmetic and copies ran while one was open for 2% -> 0% of each run, Pallas kernels for 91% -> 1%
where the time goes in v5:
time: 537 us; the launch traced here: 527 us
  Pallas kernels  523 us (97%)
    pallas_call x1, Pallas kernels, backward_all(): pl.pallas_call(functools.partial(backward_kernel, plans, order, mp_size,...  280 us
    pallas_call x1, Pallas kernels, forward_all(): pl.pallas_call(functools.partial(forward_kernel, plans, order, mp_size, l...  229 us
    pallas_call x1, Pallas kernels, adam_all(): pl.pallas_call(functools.partial(adam_kernel, len(streams) // 2, vector_c...  10.9 us
  transfers between devices with their start and end apart: 1, of which 0 were waited for; matrix products, arithmetic and copies ran while one was open for 0% of the time, Pallas kernels for 1%

profile of v5, /device:TPU:1, one launch (start us, length us, event | category | flops | bytes accessed | tf_op | source)
XLA Modules:
  0.0 527.1 jit_solution(2530497556428862046)
XLA Ops:
  0.7 0.1 collective-permute-start
  0.8 2.9 shard_map.415
  3.7 0.0 collective-permute-done
  3.7 0.7 broadcast_select_fusion.refs_12_
  4.4 0.0 copy-start
  4.5 1.0 copy.48.refs_11_
  5.5 0.0 copy-done
  5.5 229.3 %shard_map.416 = (bf16[1024,3072]{1,0:T(8,128)(2,1)}, bf16[1024,1024]{1,0:T(8,128)(2,1)}, bf16[1024,4096]{1,0:T(8,128)(2,1)}, bf16[1024,4096]{1,0:T(8,128)(2,1)}...) custom-call(bf16[128,768]{1,0:T(8,128)(2,1)} %get-tuple-element.100., ...), custom_call_target="tpu_custom_call" | custom-call | tf_op jit(solution)/shard_map/pallas_call | solution.py:1381
  234.8 280.0 %shard_map.417 = (bf16[128,1024]{1,0:T(8,128)(2,1)}, bf16[128,1024]{1,0:T(8,128)(2,1)}, bf16[128,256]{1,0:T(8,128)(2,1)}, bf16[128,768]{1,0:T(8,128)(2,1)}, bf16...) custom-call(bf16[1024,3072]{1,0:T(8,128)(2,1)} %get-tuple-element.10, ...), custom_call_target="tpu_custom_call" | custom-call | tf_op jit(solution)/shard_map/pallas_call | solution.py:2271
  514.8 10.9 %shard_map.418 = (f32[2,3,128,256]{3,2,1,0:T(8,128)}, f32[2,3,128,256]{3,2,1,0:T(8,128)}, f32[2,3,128,256]{3,2,1,0:T(8,128)}, f32[2,256,128]{2,1,0:T(8,128)}, f3...) custom-call(bf16[128,768]{1,0:T(8,128)(2,1)} %get-tuple-element.138., ...), custom_call_target="tpu_custom_call" | custom-call | tf_op jit(solution)/shard_map/pallas_call | solution.py:929
  525.7 1.2 slice.3
Async XLA Ops:
  0.7 3.1 collective-permute-start
  4.4 1.0 copy-start

commit v6 on v5

--- a/solution.py
+++ b/solution.py
@@ -1068,6 +1068,8 @@
     )
     keep_back = pltpu.make_async_copy(cotangent, cotangent_out, trade_sems.at[5])
 
+    work.begin()
+
     @pl.when(moved)
     def _():
         trade.start()
@@ -1075,8 +1077,6 @@
     @pl.when(jnp.logical_not(moved))
     def _():
         keep.start()
-
-    work.begin()
 
     saves = []
 
@@ -2284,19 +2284,19 @@
 
 
 forward_table = (
-    22, 23, 0, 1, 188, 116, 24, 25, 2, 189, 3, 117, 27, 191, 26, 190, 94, 118, 4, 70, 95, 119, 71,
-    5, 192, 193, 121, 200, 97, 8, 96, 31, 195, 197, 194, 28, 9, 198, 99, 120, 98, 30, 100, 72, 73,
-    69, 196, 32, 6, 207, 127, 7, 104, 12, 74, 44, 16, 10, 199, 201, 128, 33, 105, 18, 13, 46, 208,
-    29, 112, 45, 40, 17, 11, 107, 203, 202, 75, 76, 83, 19, 77, 34, 125, 205, 47, 206, 122, 204,
-    39, 209, 52, 48, 20, 14, 103, 36, 15, 38, 79, 210, 106, 21, 78, 211, 212, 213, 126, 49, 41,
-    51, 35, 101, 214, 102, 54, 37, 80, 114, 81, 53, 129, 215, 50, 216, 82, 86, 164, 56, 165, 55,
-    123, 163, 124, 84, 87, 217, 42, 136, 65, 57, 91, 59, 61, 133, 111, 58, 85, 166, 138, 113, 139,
-    134, 66, 130, 43, 108, 60, 218, 90, 219, 88, 140, 62, 170, 135, 167, 171, 64, 109, 67, 92, 63,
-    220, 146, 110, 132, 131, 68, 168, 221, 89, 222, 223, 224, 225, 145, 226, 115, 227, 228, 229,
-    141, 142, 93, 173, 230, 231, 169, 148, 232, 233, 172, 147, 176, 234, 143, 144, 152, 151, 137,
-    235, 236, 237, 159, 177, 178, 175, 174, 181, 153, 180, 184, 238, 149, 150, 239, 240, 155, 157,
-    156, 182, 154, 160, 158, 185, 179, 241, 242, 243, 161, 183, 162, 244, 245, 246, 247, 248, 249,
-    186, 250, 251, 252, 187, 253, 254, 255,
+    95, 1, 23, 116, 0, 22, 188, 189, 3, 191, 71, 94, 97, 24, 25, 190, 2, 70, 192, 26, 193, 198, 5,
+    73, 96, 4, 11, 10, 118, 117, 99, 27, 7, 199, 98, 197, 194, 6, 72, 29, 69, 196, 195, 201, 119,
+    9, 8, 200, 101, 28, 75, 46, 45, 13, 207, 44, 32, 12, 107, 120, 202, 74, 30, 100, 105, 103, 47,
+    112, 206, 208, 19, 14, 203, 104, 31, 106, 34, 35, 121, 83, 51, 48, 205, 204, 77, 17, 128, 76,
+    15, 41, 20, 18, 16, 209, 49, 210, 21, 33, 52, 50, 57, 102, 84, 42, 82, 211, 212, 53, 213, 126,
+    78, 214, 37, 54, 129, 215, 36, 216, 79, 38, 55, 58, 108, 56, 40, 164, 114, 217, 66, 134, 127,
+    122, 80, 140, 39, 61, 165, 139, 81, 218, 124, 123, 85, 136, 43, 59, 109, 219, 60, 111, 138,
+    86, 163, 62, 113, 91, 90, 65, 142, 125, 141, 92, 167, 166, 87, 64, 63, 220, 135, 110, 130, 67,
+    145, 68, 221, 222, 223, 88, 115, 224, 225, 226, 146, 227, 228, 229, 89, 171, 144, 170, 230,
+    231, 168, 93, 143, 151, 232, 233, 152, 234, 169, 176, 148, 147, 235, 236, 133, 172, 237, 153,
+    159, 149, 154, 173, 150, 238, 239, 178, 240, 155, 157, 174, 179, 132, 184, 131, 156, 158, 175,
+    160, 161, 241, 137, 180, 242, 243, 162, 182, 244, 185, 183, 245, 177, 181, 246, 247, 248, 249,
+    187, 250, 251, 186, 252, 253, 254, 255,
 )
 backward_table = (
     0, 1, 2, 3, 4, 5, 6, 7, 8, 9, 10, 11, 12, 13, 14, 15, 16, 17, 87, 18, 19, 20, 21, 85, 96, 22,

time: 537 us -> 542 us (level)
    pallas_call x1, Pallas kernels: 280 us -> 288 us  [backward_all(): pl.pallas_call(functools.partial(backward_kernel, plans, order, mp_size,...]
where the time goes in v6:
time: 542 us; the launch traced here: 532 us
  Pallas kernels  528 us (97%)
    pallas_call x1, Pallas kernels, backward_all(): pl.pallas_call(functools.partial(backward_kernel, plans, order, mp_size,...  288 us
    pallas_call x1, Pallas kernels, forward_all(): pl.pallas_call(functools.partial(forward_kernel, plans, order, mp_size, l...  226 us
    pallas_call x1, Pallas kernels, adam_all(): pl.pallas_call(functools.partial(adam_kernel, len(streams) // 2, vector_c...  10.9 us
  transfers between devices with their start and end apart: 1, of which 0 were waited for; matrix products, arithmetic and copies ran while one was open for 0% of the time, Pallas kernels for 1%

profile of v6, /device:TPU:1, one launch (start us, length us, event | category | flops | bytes accessed | tf_op | source)
XLA Modules:
  0.0 532.0 jit_solution(16541114729042534989)
XLA Ops:
  0.7 0.1 collective-permute-start
  0.8 2.9 shard_map.415
  3.7 0.0 collective-permute-done
  3.7 0.7 broadcast_select_fusion.refs_12_
  4.4 0.0 copy-start
  4.5 1.0 copy.48.refs_11_
  5.5 0.0 copy-done
  5.5 225.9 %shard_map.416 = (bf16[1024,3072]{1,0:T(8,128)(2,1)}, bf16[1024,1024]{1,0:T(8,128)(2,1)}, bf16[1024,4096]{1,0:T(8,128)(2,1)}, bf16[1024,4096]{1,0:T(8,128)(2,1)}...) custom-call(bf16[128,768]{1,0:T(8,128)(2,1)} %get-tuple-element.100., ...), custom_call_target="tpu_custom_call" | custom-call | tf_op jit(solution)/shard_map/pallas_call | solution.py:1381
  231.3 288.3 %shard_map.417 = (bf16[128,1024]{1,0:T(8,128)(2,1)}, bf16[128,1024]{1,0:T(8,128)(2,1)}, bf16[128,256]{1,0:T(8,128)(2,1)}, bf16[128,768]{1,0:T(8,128)(2,1)}, bf16...) custom-call(bf16[1024,3072]{1,0:T(8,128)(2,1)} %get-tuple-element.10, ...), custom_call_target="tpu_custom_call" | custom-call | tf_op jit(solution)/shard_map/pallas_call | solution.py:2271
  519.6 10.9 %shard_map.418 = (f32[2,3,128,256]{3,2,1,0:T(8,128)}, f32[2,3,128,256]{3,2,1,0:T(8,128)}, f32[2,3,128,256]{3,2,1,0:T(8,128)}, f32[2,256,128]{2,1,0:T(8,128)}, f3...) custom-call(bf16[128,768]{1,0:T(8,128)(2,1)} %get-tuple-element.138., ...), custom_call_target="tpu_custom_call" | custom-call | tf_op jit(solution)/shard_map/pallas_call | solution.py:929
  530.5 1.2 slice.3
Async XLA Ops:
  0.7 3.1 collective-permute-start
  4.4 1.0 copy-start
